TPU v7x, 32 devices: a whole 2x2x4 slice. The times are simulated.
32 devices in a mesh: row: 4 (over y, core), box: 8 (over z, x).
Axes of the slice: x: 2, y: 2, z: 4, core: 2. Of those that a mesh axis runs over, the one named last changes fastest.
Arguments:
- solved: bfloat16 [2, 8192, 512], P(None, ('box', 'row')), may hold values from -6 to 6
- rhs: bfloat16 [4, 8192, 512], P('row', 'box'), may hold values from -6 to 6
- leaf_basis: bfloat16 [4, 3, 32, 256, 128], P('row', None, 'box'), may hold values from -0.375 to 0.375
- first_level: bfloat16 [4, 3, 8, 4, 4, 128, 128], P('row', None, 'box'), may hold values from -0.25 to 0.25
- second_level: bfloat16 [4, 3, 8, 8, 128, 128], P('row', None, 'box'), may hold values from -0.5 to 0.5
- third_level: bfloat16 [4, 3, 8, 8, 128, 128], P('row', None, 'box'), may hold values from -0.25 to 0.25
- fourth_level: bfloat16 [4, 3, 8, 2, 2, 128, 128], P('row', None, 'box'), may hold values from -0.375 to 0.375
- out_basis: bfloat16 [4, 3, 16, 512, 128], P('row', None, 'box'), may hold values from -0.5 to 0.5
Outputs:
- unknowns: bfloat16 [4, 8192, 512], P('row', 'box')
All inputs are finite; a program needn't handle non-finite values.
Results may differ from a plain program's by a relative error of at most 0.015.
Values may be sent and summed in bfloat16 or wider, within the bound.
No kernel may reach another device: no remote copies, remote signals or barrier semaphores. Data moves between devices by JAX's collectives and lax.ppermute only.
A program may use at most 128 MiB of HBM per device.

v0:
```python
import jax
import jax.numpy as jnp
from jax import lax
from jax.sharding import PartitionSpec as P


def leaf_levels(inputs, basis, first_mats, second_mats):
    stack_size, row_count, columns = inputs.shape
    leaf_count = basis.shape[1]
    leaf_rows = basis.shape[2]
    rank_size = basis.shape[3]
    slot_count = second_mats.shape[1]
    leaf_coef = jnp.einsum(
        "jlpr,jlpn->jlrn",
        basis,
        inputs.reshape(stack_size, leaf_count, leaf_rows, columns),
        preferred_element_type=jnp.float32,
    ).astype(jnp.bfloat16)
    mid_coef = jnp.einsum(
        "jskrq,jkqn->jsrn", first_mats, leaf_coef, preferred_element_type=jnp.float32
    ).astype(jnp.bfloat16)
    slot_mats = second_mats.reshape(stack_size, 4, slot_count // 4, rank_size, rank_size)
    slot_coef = jnp.einsum(
        "jstrq,jsqn->jstrn", slot_mats, mid_coef, preferred_element_type=jnp.float32
    ).astype(jnp.bfloat16)
    return slot_coef.reshape(stack_size, slot_count, rank_size, columns)


def outer_levels(received, third_mats, fourth_mats, outer_basis):
    stack_size, slot_count, rank_size, columns = received.shape
    grouped = received.reshape(stack_size, slot_count // 4, 4, rank_size, columns)
    group_mats = third_mats.reshape(stack_size, slot_count // 4, 4, rank_size, rank_size)
    group_coef = jnp.einsum(
        "jgkrq,jgkqn->jgrn", group_mats, grouped, preferred_element_type=jnp.float32
    ).astype(jnp.bfloat16)
    half_coef = jnp.einsum(
        "jhgrq,jgqn->jhrn", fourth_mats, group_coef, preferred_element_type=jnp.float32
    ).astype(jnp.bfloat16)
    result = jnp.einsum(
        "jhpr,jhrn->jhpn", outer_basis, half_coef, preferred_element_type=jnp.float32
    )
    return result.reshape(stack_size, -1, columns)


def on_device(
    solved, rhs, leaf_basis, first_level, second_level, third_level, fourth_level, out_basis
):
    gathered = lax.all_gather(solved, "row", axis=1, tiled=True)
    basis = leaf_basis[0]
    first_mats = first_level[0, :, 0]
    second_mats = second_level[0, :, 0]
    third_mats = third_level[0, :, 0]
    fourth_mats = fourth_level[0, :, 0]
    outer_basis = out_basis[0]
    coefs = leaf_levels(gathered, basis[:2], first_mats[:2], second_mats[:2])
    received = lax.all_to_all(coefs, "box", split_axis=1, concat_axis=1, tiled=True)
    both = outer_levels(received, third_mats[:2], fourth_mats[:2], outer_basis[:2])
    residual = rhs[0].astype(jnp.float32) - both[0] - both[1]
    residual_b = residual.astype(jnp.bfloat16)
    diag_coefs = leaf_levels(residual_b[None], basis[2:], first_mats[2:], second_mats[2:])
    diag_received = lax.all_to_all(diag_coefs, "box", split_axis=1, concat_axis=1, tiled=True)
    correction = outer_levels(diag_received, third_mats[2:], fourth_mats[2:], outer_basis[2:])[0]
    return (residual + correction).astype(jnp.bfloat16)[None]


def solution(mesh):
    placed = (
        P(None, ("box", "row"), None),
        P("row", "box", None),
        P("row", None, "box", None, None),
        P("row", None, "box", None, None, None, None),
        P("row", None, "box", None, None, None),
        P("row", None, "box", None, None, None),
        P("row", None, "box", None, None, None, None),
        P("row", None, "box", None, None),
    )
    return jax.shard_map(
        on_device, mesh=mesh, in_specs=placed, out_specs=P("row", "box", None), check_vma=False
    )
```

profile of v0, /device:TPU:0, one launch (start us, length us, event | category | flops | bytes accessed | tf_op | source)
XLA Modules:
  0.0 152.5 jit_solution(18275372139845090351)
XLA Ops:
  6.5 0.0 all-gather.2.cloned.1.call-start
  6.5 0.7 all-gather.2.cloned.1.call-update
  7.3 1.9 %slice.68 = bf16[1,2,1,8,128,128]{5,4,3,2,1,0:T(8,128)(2,1)} slice(bf16[1,3,1,8,128,128]{5,4,3,2,1,0:T(8,128)(2,1)} %param.12), slice={[0:1], [0:2], [0:1], [0:8], [0:128], [0:128]} | slice | bytes 1048576 | tf_op jit(solution)/shard_map/slice | solution.py:55
  9.1 25.1 %all-gather.2.cloned.1.call-done = bf16[2,1024,512]{2,1,0:T(8,128)(2,1)} async-done(((bf16[2,256,512]{2,1,0:T(8,128)(2,1)}), bf16[2,1024,512]{2,1,0:T(8,128)(2,1)}) %all-gather.2.cloned.1.call-update) | async-done | bytes 2097168 | tf_op jit(solution)/shard_map/all_gather | solution.py:48
  34.2 2.3 %fusion.3 = bf16[2,4,128,512,1]{3,2,1,4,0:T(8,128)(2,1)S(1)} fusion(bf16[2,4,256,512]{3,2,1,0:T(8,128)(2,1)} %bitcast.169, bf16[1,3,4,256,128]{4,3,2,1,0:T(8,128)(2,1)} %param.10), kind=kOutput, calls=%fused_computation.12 | convolution fusion | flops 268959744 | bytes 3670016 | tf_op jit(solution)/shard_map/jlpr,jlpn->jlrn/dot_general | solution.py:13
  36.5 2.7 %convolution_convert_fusion = bf16[2,4,512,2,128]{4,2,3,1,0:T(8,128)(2,1)S(1)} fusion(bf16[2,4,2,128,128]{4,3,2,1,0:T(8,128)(2,1)} %bitcast.170, bf16[2,4,128,512,1]{3,2,1,4,0:T(8,128)(2,1)S(1)} %fusion.3, bf16[1,3,1,4,4,128,128]{6,5,4,3,2,1,0:T(8,128)(2,1)} %param.11), kind=kOutput, calls=%fused_computation.9 | convolution fusion | flops 806879232 | bytes 4718592 | tf_op jit(solution)/shard_map/jstrq,jsqn->jstrn/dot_general | solution.py:23
  39.2 1.5 copy.9
  40.7 0.0 slice-start.1
  40.7 5.6 %all-to-all-start = ((bf16[2,8,128,512]{2,3,0,1:T(8,128)(2,1)}), bf16[2,8,128,512]{2,3,0,1:T(8,128)(2,1)S(1)}, u32[]{:S(2)}, u32[]{:S(2)}) async-start(bf16[2,8,128,512]{2,3,0,1:T(8,128)(2,1)} %copy.9), calls=%async_computation | async-start | bytes 4194304 | tf_op jit(solution)/shard_map/all_to_all | solution.py:56
  46.3 0.0 copy-start.3
  46.3 48.6 %all-to-all-done = bf16[2,8,128,512]{2,3,0,1:T(8,128)(2,1)S(1)} async-done(((bf16[2,8,128,512]{2,3,0,1:T(8,128)(2,1)}), bf16[2,8,128,512]{2,3,0,1:T(8,128)(2,1)S(1)}, u32[]{:S(2)}, u32[]{:S(2)}) %all-to-all-start) | async-done | bytes 2097184 | tf_op jit(solution)/shard_map/all_to_all | solution.py:56
  94.9 0.0 slice-done.1
  94.9 1.5 fusion.14
  96.4 0.0 copy-done.3
  96.4 4.0 %convolution_bitcast_fusion = f32[2,2,512,512]{3,2,1,0:T(8,128)} fusion(bf16[2,2,128,512,1]{2,3,1,4,0:T(8,128)(2,1)} %fusion.14, bf16[1,3,2,512,128]{4,3,2,1,0:T(8,128)(2,1)S(1)} %copy-done.3, bf16[1,3,1,2,2,128,128]{6,5,4,3,2,1,0:T(8,128)(2,1)} %param.14), kind=kOutput, calls=%fused_computation | convolution fusion | flops 402915328 | bytes 5505024 | tf_op jit(solution)/shard_map/jhpr,jhrn->jhpn/dot_general | solution.py:39
  100.4 0.0 copy-start.1
  100.4 2.8 %fusion.48 = (f32[1,2,512,512]{3,2,1,0:T(8,128)S(1)}, f32[1,2,512,512]{3,2,1,0:T(8,128)S(1)}) fusion(f32[2,2,512,512]{3,2,1,0:T(8,128)} %convolution_bitcast_fusion), kind=kLoop, calls=%fused_computation.48 | loop fusion | bytes 8388608 | tf_op jit(solution)/shard_map/slice | solution.py:58
  103.2 0.0 copy-start
  103.2 0.0 copy-done.1
  103.2 0.0 slice-start
  103.2 1.9 %fusion.17 = bf16[4,128,512,1]{1,2,0,3:T(8,128)(2,1)S(1)} fusion(f32[4,256,512]{2,1,0:T(8,128)S(1)} %bitcast.164, f32[4,256,512]{2,1,0:T(8,128)S(1)} %bitcast.163, bf16[1,3,4,256,128]{4,3,2,1,0:T(8,128)(2,1)} %param.10, bf16[4,256,512]{2,1,0:T(8,128)(2,1)S(1)} %bitcast.168), kind=kOutput, calls=%fused_computation.23 | convolution fusion | flops 136577024 | bytes 6029312 | tf_op jit(solution)/shard_map/jlpr,jlpn->jlrn/dot_general | solution.py:13
  105.1 0.0 copy-done
  105.1 0.0 slice-done
  105.1 0.0 slice-start.2
  105.2 2.8 %convolution_convert_fusion.2 = bf16[4,512,2,128]{3,1,2,0:T(8,128)(2,1)} fusion(bf16[4,2,128,128]{3,2,1,0:T(8,128)(2,1)S(1)} %bitcast.172, bf16[4,128,512,1]{1,2,0,3:T(8,128)(2,1)S(1)} %fusion.17, bf16[1,3,1,4,4,128,128]{6,5,4,3,2,1,0:T(8,128)(2,1)} %param.11), kind=kOutput, calls=%fused_computation.11 | convolution fusion | flops 403439616 | bytes 2359296 | tf_op jit(solution)/shard_map/jstrq,jsqn->jstrn/dot_general | solution.py:23
  108.0 3.6 %all-to-all-start.1 = ((bf16[1,8,128,512]{2,3,0,1:T(8,128)(2,1)}), bf16[1,8,128,512]{2,3,0,1:T(8,128)(2,1)S(1)}, u32[]{:S(2)}, u32[]{:S(2)}) async-start(bf16[1,8,128,512]{2,3,0,1:T(8,128)(2,1)} %bitcast.167), calls=%async_computation.1 | async-start | bytes 2097152 | tf_op jit(solution)/shard_map/all_to_all | solution.py:61
  111.6 25.9 %all-to-all-done.1 = bf16[1,8,128,512]{2,3,0,1:T(8,128)(2,1)S(1)} async-done(((bf16[1,8,128,512]{2,3,0,1:T(8,128)(2,1)}), bf16[1,8,128,512]{2,3,0,1:T(8,128)(2,1)S(1)}, u32[]{:S(2)}, u32[]{:S(2)}) %all-to-all-start.1) | async-done | bytes 1048608 | tf_op jit(solution)/shard_map/all_to_all | solution.py:61
  137.5 0.0 slice-done.2
  137.5 1.1 fusion.23
  138.7 0.0 copy-start.2
  138.7 3.1 %fusion.22 = f32[2,512,512]{1,2,0:T(8,128)} fusion(bf16[2,128,512,1]{1,2,0,3:T(8,128)(2,1)} %fusion.23, bf16[1,3,2,512,128]{4,3,2,1,0:T(8,128)(2,1)} %param.15, bf16[1,3,1,2,2,128,128]{6,5,4,3,2,1,0:T(8,128)(2,1)} %param.14), kind=kOutput, calls=%fused_computation.30 | convolution fusion | flops 201457664 | bytes 2752512 | tf_op jit(solution)/shard_map/jhpr,jhrn->jhpn/dot_general | solution.py:39
  141.8 0.0 copy-done.2
  141.8 3.8 %fusion = bf16[1,1024,512]{2,1,0:T(8,128)(2,1)} fusion(f32[2,512,512]{1,2,0:T(8,128)} %fusion.22, f32[1,2,512,512]{3,2,1,0:T(8,128)} %copy-done, f32[1,2,512,512]{3,2,1,0:T(8,128)S(1)} %get-tuple-element.5, bf16[1,1024,512]{2,1,0:T(8,128)(2,1)S(1)} %copy-done.2), kind=kLoop, calls=%fused_computation.2 | loop fusion | flops 2621440 | bytes 8388608 | tf_op jit(solution)/shard_map/convert_element_type | solution.py:63
Async XLA Ops:
  6.5 27.7 %all-gather.2.cloned.1.call-start = ((), (), s32[]{:S(2)}) async-start(), calls=%async_computation.2 | async-start | bytes 2621440 | tf_op jit(solution)/shard_map/all_gather | solution.py:48
  40.7 54.3 %slice-start.1 = ((bf16[1,3,1,8,128,128]{5,4,3,2,1,0:T(8,128)(2,1)}), bf16[1,2,1,8,128,128]{5,4,3,2,1,0:T(8,128)(2,1)S(1)}, s32[]{:S(2)}) async-start(bf16[1,3,1,8,128,128]{5,4,3,2,1,0:T(8,128)(2,1)} %param.13), calls=%async_computation.4 | async-start | bytes 1048576 | tf_op jit(solution)/shard_map/slice | solution.py:57
  40.7 54.3 %all-to-all-start = ((bf16[2,8,128,512]{2,3,0,1:T(8,128)(2,1)}), bf16[2,8,128,512]{2,3,0,1:T(8,128)(2,1)S(1)}, u32[]{:S(2)}, u32[]{:S(2)}) async-start(bf16[2,8,128,512]{2,3,0,1:T(8,128)(2,1)} %copy.9), calls=%async_computation | async-start | bytes 4194304 | tf_op jit(solution)/shard_map/all_to_all | solution.py:56
  46.3 50.1 %copy-start.3 = (bf16[1,3,2,512,128]{4,3,2,1,0:T(8,128)(2,1)S(1)}, bf16[1,3,2,512,128]{4,3,2,1,0:T(8,128)(2,1)}, u32[]{:S(2)}) copy-start(bf16[1,3,2,512,128]{4,3,2,1,0:T(8,128)(2,1)} %param.15) | copy-start | bytes 2359300
  100.4 2.8 %copy-start.1 = (bf16[1,1024,512]{2,1,0:T(8,128)(2,1)S(1)}, bf16[1,1024,512]{2,1,0:T(8,128)(2,1)}, u32[]{:S(2)}) copy-start(bf16[1,1024,512]{2,1,0:T(8,128)(2,1)} %param.9) | copy-start | bytes 3145732
  103.2 1.9 %copy-start = (f32[1,2,512,512]{3,2,1,0:T(8,128)}, f32[1,2,512,512]{3,2,1,0:T(8,128)S(1)}, u32[]{:S(2)}) copy-start(f32[1,2,512,512]{3,2,1,0:T(8,128)S(1)} %get-tuple-element.6) | copy-start | bytes 6291460
  103.2 1.9 %slice-start = ((bf16[1,3,1,8,128,128]{5,4,3,2,1,0:T(8,128)(2,1)}), bf16[1,1,1,8,128,128]{5,4,3,2,1,0:T(8,128)(2,1)S(1)}, s32[]{:S(2)}) async-start(bf16[1,3,1,8,128,128]{5,4,3,2,1,0:T(8,128)(2,1)} %param.12), calls=%async_computation.3 | async-start | bytes 524288 | tf_op jit(solution)/shard_map/slice | solution.py:60
  105.1 32.4 %slice-start.2 = ((bf16[1,3,1,8,128,128]{5,4,3,2,1,0:T(8,128)(2,1)}), bf16[1,1,1,8,128,128]{5,4,3,2,1,0:T(8,128)(2,1)S(1)}, s32[]{:S(2)}) async-start(bf16[1,3,1,8,128,128]{5,4,3,2,1,0:T(8,128)(2,1)} %param.13), calls=%async_computation.5 | async-start | bytes 524288 | tf_op jit(solution)/shard_map/slice | solution.py:62
  108.0 29.6 %all-to-all-start.1 = ((bf16[1,8,128,512]{2,3,0,1:T(8,128)(2,1)}), bf16[1,8,128,512]{2,3,0,1:T(8,128)(2,1)S(1)}, u32[]{:S(2)}, u32[]{:S(2)}) async-start(bf16[1,8,128,512]{2,3,0,1:T(8,128)(2,1)} %bitcast.167), calls=%async_computation.1 | async-start | bytes 2097152 | tf_op jit(solution)/shard_map/all_to_all | solution.py:61
  138.7 3.1 %copy-start.2 = (bf16[1,1024,512]{2,1,0:T(8,128)(2,1)S(1)}, bf16[1,1024,512]{2,1,0:T(8,128)(2,1)}, u32[]{:S(2)}) copy-start(bf16[1,1024,512]{2,1,0:T(8,128)(2,1)} %param.9) | copy-start | bytes 3145732
Sparse Core Ops, SparseCore 0:
  8.9 25.2 all-gather.1
where the time goes:
time: 153 us; the launch traced here: 152 us
  waiting for transfers between devices  100 us (65%)
  matrix products  19.4 us (13%)
  between operations  13.5 us (9%)
  starting transfers between devices  9.29 us (6%)
  local copies, waits for them, and re-layouts  6.16 us (4%)
  other arithmetic  3.82 us (2%)
    all_to_all x1, waiting for transfers between devices, on_device(): lax.all_to_all(coefs, 'box', split_axis=1, concat_axis=1, tiled=True)  48.6 us
    all_to_all x1, waiting for transfers between devices, on_device(): lax.all_to_all(diag_coefs, 'box', split_axis=1, concat_axis=1, tiled=True)  25.9 us
    all_gather x1, waiting for transfers between devices, on_device(): gathered = lax.all_gather(solved, 'row', axis=1, tiled=True)  25.1 us
    dot_general x2, matrix products, outer_levels(): jnp.einsum('jhpr,jhrn->jhpn', outer_basis, half_coef, preferred_element_t...  7.1 us
    all_to_all x1, starting transfers between devices, on_device(): lax.all_to_all(coefs, 'box', split_axis=1, concat_axis=1, tiled=True)  5.64 us
    dot_general x2, matrix products, leaf_levels(): jnp.einsum('jstrq,jsqn->jstrn', slot_mats, mid_coef, preferred_element_ty...  5.45 us
    dot_general x2, matrix products, leaf_levels(): jnp.einsum('jlpr,jlpn->jlrn', basis, inputs.reshape(stack_size, leaf_coun...  4.17 us
    convert_element_type x1, other arithmetic, on_device(): return (residual + correction).astype(jnp.bfloat16)[None]  3.82 us
  transfers between devices with their start and end apart: 3, of which 3 were waited for; matrix products, arithmetic and copies ran while one was open for 1% of the time, Pallas kernels for 0%

commit v1 on v0

v1 whole, which is shorter than its diff:
```python
import functools

import jax
import jax.numpy as jnp
from jax import lax
from jax.experimental import pallas as pl
from jax.experimental.pallas import tpu as pltpu
from jax.sharding import PartitionSpec as P

F32 = jnp.float32
BF16 = jnp.bfloat16
MIB = 1024 * 1024
CHUNKS = 1
VMEM = pl.BlockSpec(memory_space=pltpu.VMEM)


def dot(a, b):
    return jnp.dot(a, b, preferred_element_type=F32)


def dot_t(a, b):
    return lax.dot_general(a, b, (((0,), (0,)), ((), ())), preferred_element_type=F32)


def place(radix):
    box = lax.axis_index("box")
    return lax.div(box, radix), lax.rem(box, radix)


def wrap(value, size):
    return lax.rem(value + size, size)


def take(refs, *counts):
    refs, out = list(refs), []
    for count in counts:
        out.append(refs[:count])
        refs = refs[count:]
    return out


def pick_kernel(radix, groups, third, *outs):
    group, member = place(radix)
    at = 0
    for delta in range(1, groups):
        for i in range(radix):
            slot = wrap(group + delta, groups) * radix + jnp.bitwise_xor(member, i)
            for j in range(outs[at].shape[0]):
                outs[at][j] = third[0, j, 0, slot]
            at += 1


def leaf_order(row, leaves, row_size):
    per_leaf = row_size // leaves
    return [jnp.bitwise_xor(lax.div(row, per_leaf), t) for t in range(leaves)]


def column_weights(j, order, first, second, third_of, own, other, at):
    levels, radix = first.shape[3], first.shape[4]
    slots = second.shape[3]
    groups = slots // radix
    group, member = place(radix)

    def up(slot, matrix):
        level = lax.div(slot, slots // levels)
        return dot(matrix, jnp.concatenate([first[0, j, 0, level, k] for k in order], axis=1)).astype(BF16)

    for i in range(radix):
        box = jnp.bitwise_xor(member, i)
        slot = group * radix + box
        own[at, i] = up(slot, second[0, j, 0, slot])
        for delta in range(1, groups):
            slot = wrap(group - delta, groups) * radix + box
            mat = dot(third_of(delta, i, slot), second[0, j, 0, slot]).astype(BF16)
            other[at, i, delta - 1] = up(slot, mat)


def off_weights_kernel(radix, groups, offs, row_size, first, second, *refs):
    thirds, (own, other) = take(refs, (groups - 1) * radix, 2)
    order = leaf_order(lax.axis_index("row"), first.shape[4], row_size)
    for j in range(offs):
        column_weights(
            j, order, first, second, lambda delta, i, slot: thirds[(delta - 1) * radix + i][j], own, other, j
        )


def rest_weights_kernel(
    radix, groups, offs, first, second, fourth, out_basis, thirds, own, other, off_rows, last_rows
):
    column_weights(
        offs, range(first.shape[4]), first, second, lambda delta, i, slot: thirds[0, slot], own, other, 0
    )
    group, _ = place(radix)
    rank = fourth.shape[6]
    half_rows = out_basis.shape[3]
    for j in range(offs + 1):
        out, start = (off_rows, j * groups * rank) if j < offs else (last_rows, 0)
        for h in range(fourth.shape[3]):
            mats = [fourth[0, j, 0, h, wrap(group + delta, groups)] for delta in range(groups)]
            out[h * half_rows : (h + 1) * half_rows, start : start + groups * rank] = dot(
                out_basis[0, j, h], jnp.concatenate(mats, axis=1)
            ).astype(BF16)


def column_levels(leaf, own_mats, other_mats, own, other, at):
    radix, groups_less, rank, depth = other_mats.shape
    coef = dot(other_mats[...].reshape(radix * groups_less * rank, depth), leaf).astype(BF16)
    for i in range(radix):
        other[i][at] = coef[i * groups_less * rank : (i + 1) * groups_less * rank].reshape(
            groups_less, rank, coef.shape[1]
        )
    coef = dot(own_mats[...].reshape(radix * rank, depth), leaf).astype(BF16)
    for i in range(radix):
        own[i][at] = coef[i * rank : (i + 1) * rank]


def off_kernel(radix, pieces, span, basis, own_mats, other_mats, *refs):
    parts, own, other = take(refs, pieces, radix, radix)
    row = lax.axis_index("row")
    leaves, leaf_rows = basis.shape[2], basis.shape[3]
    rows = parts[0].shape[1]
    per_leaf = leaf_rows // rows
    order = leaf_order(row, leaves, pieces)
    for j in range(parts[0].shape[0]):
        leaf = []
        for t in range(leaves):
            total = None
            for u in range(per_leaf):
                start = jnp.bitwise_xor(lax.rem(row, per_leaf), u) * rows
                if per_leaf == 1:
                    mat = basis[0, j, order[t]]
                else:
                    mat = basis[0, j, order[t], pl.ds(pl.multiple_of(start, rows), rows)]
                ref = parts[t * per_leaf + u]
                data = ref[j, :, span] if ref.shape[2] > span.stop - span.start else ref[j]
                part = dot_t(mat, data)
                total = part if total is None else total + part
            leaf.append(total.astype(BF16))
        column_levels(jnp.concatenate(leaf, axis=0), own_mats.at[j], other_mats.at[j], own, other, j)


def group_coefs(j, at, own, crossed, third, radix):
    group, member = place(radix)
    mats = [third[0, j, 0, group * radix + jnp.bitwise_xor(member, i)] for i in range(radix)]
    total = dot(jnp.concatenate(mats, axis=1), jnp.concatenate([ref[at] for ref in own], axis=0))
    return [total.astype(BF16)] + [ref[at] for ref in crossed]


def middle_kernel(radix, groups, offs, span, third, rhs, basis, row_mats, own_mats, other_mats, *refs):
    own_in, crossed, (residual_ref,), own, other = take(refs, radix, groups - 1, 1, radix, radix)
    coefs = []
    for j in range(offs):
        coefs += group_coefs(j, j, own_in, crossed, third, radix)
    coefs = jnp.concatenate(coefs, axis=0)
    leaves, leaf_rows = basis.shape[2], basis.shape[3]
    leaf = []
    for k in range(leaves):
        rows = slice(k * leaf_rows, (k + 1) * leaf_rows)
        residual = rhs[0, rows, span].astype(F32) - dot(row_mats[rows], coefs)
        residual_ref[rows] = residual
        leaf.append(dot_t(basis[0, offs, k], residual.astype(BF16)).astype(BF16))
    column_levels(jnp.concatenate(leaf, axis=0), own_mats.at[0], other_mats.at[0], own, other, 0)


def last_kernel(radix, groups, offs, third, row_mats, residual, *refs):
    own_in, crossed, (out,) = take(refs, radix, groups - 1, 1)
    coefs = jnp.concatenate(group_coefs(offs, 0, own_in, crossed, third, radix), axis=0)
    out[0] = (residual[...] + dot(row_mats[...], coefs)).astype(BF16)


def on_device(
    row_size, box_size, solved, rhs, leaf_basis, first_level, second_level, third_level, fourth_level, out_basis
):
    radix = first_level.shape[4]
    groups = box_size // radix
    butterflies = leaf_basis.shape[1]
    offs = solved.shape[0]
    width = solved.shape[2] // CHUNKS
    rank = leaf_basis.shape[4]
    rows = rhs.shape[1]
    depth = radix * rank

    def over_row(array, mask):
        return lax.ppermute(array, "row", [(r, r ^ mask) for r in range(row_size)])

    def over_members(array, mask):
        pairs = [(b, (b // radix) * radix + ((b % radix) ^ mask)) for b in range(box_size)]
        return array if mask == 0 else lax.ppermute(array, "box", pairs)

    def over_groups(array, delta, mask=0):
        pairs = [
            (b, ((b // radix + delta) % groups) * radix + ((b % radix) ^ mask)) for b in range(box_size)
        ]
        return lax.ppermute(array, "box", pairs)

    def call(kernel, name, flops, outs, *args):
        outs = [jax.ShapeDtypeStruct(shape, dtype) for shape, dtype in outs]
        size = sum(a.size * a.dtype.itemsize for a in [*args, *outs])
        return pl.pallas_call(
            kernel,
            out_shape=outs,
            in_specs=[VMEM] * len(args),
            out_specs=[VMEM] * len(outs),
            compiler_params=pltpu.CompilerParams(vmem_limit_bytes=min(16 * MIB + 2 * size, 56 * MIB)),
            cost_estimate=pl.CostEstimate(flops=int(flops), bytes_accessed=int(size), transcendentals=0),
            name=name,
        )(*args)

    sent_count = (groups - 1) * radix
    shifts = [(delta, i) for delta in range(1, groups) for i in range(radix)]
    picked = call(
        functools.partial(pick_kernel, radix, groups),
        "pick_third",
        0,
        [((offs, rank, rank), BF16)] * sent_count,
        third_level,
    )
    thirds = [over_groups(a, *shift) for a, shift in zip(picked, shifts)]

    beside = over_row(solved, 1)
    chunks = []
    for c in range(CHUNKS):
        span = slice(c * width, (c + 1) * width)
        pieces = {0: solved, 1: beside}
        part = solved if CHUNKS == 1 else solved[:, :, span]
        for mask in range(2, row_size, 2):
            pieces[mask] = over_row(part, mask)
            if c == 0 and mask == 2:
                pieces[mask], *thirds[:3] = lax.optimization_barrier((pieces[mask], *thirds[:3]))
            pieces[mask + 1] = over_row(pieces[mask], 1)
        chunks.append((span, [pieces[mask] for mask in range(row_size)]))

    def column_mats(count):
        return [((count, radix, rank, depth), BF16), ((count, radix, groups - 1, rank, depth), BF16)]

    mats_flops = 2 * box_size * rank * rank * (depth + rank)
    own_mats, other_mats = call(
        functools.partial(off_weights_kernel, radix, groups, offs, row_size),
        "off_weights",
        offs * mats_flops,
        column_mats(offs),
        first_level,
        second_level,
        *thirds,
    )
    def levels_out(count):
        own = [((count, rank, width), BF16)] * radix
        return own + [((count, groups - 1, rank, width), BF16)] * radix

    def send(levels, beside=None):
        own, other = levels[:radix], levels[radix:]
        other = [over_members(a, i) for i, a in enumerate(other)]
        own = [over_members(a, i) for i, a in enumerate(own)]
        if beside is not None:
            _, last = lax.optimization_barrier((levels[radix], third_level[0, offs:, 0]))
            last = lax.all_to_all(last, "box", split_axis=1, concat_axis=1, tiled=True)
            other[0], last = lax.optimization_barrier((other[0], last))
            beside.append(last)
        crossed = []
        for delta in range(1, groups):
            total = sum(a[:, delta - 1].astype(F32) for a in other).astype(BF16)
            crossed.append(over_groups(total, groups - delta))
        return own + crossed

    column_flops = 2 * width * rank * (rows + box_size * depth)
    row_flops = 2 * width * rank * (depth + groups * rows)
    done, last_weights = [], None
    for span, pieces in chunks:
        levels = call(
            functools.partial(off_kernel, radix, row_size, span),
            "off_levels",
            offs * column_flops,
            levels_out(offs),
            leaf_basis,
            own_mats,
            other_mats,
            *pieces,
        )
        if last_weights is None:
            thirds_last = []
            received = send(levels, thirds_last)
            last_weights = call(
                functools.partial(rest_weights_kernel, radix, groups, offs),
                "rest_weights",
                mats_flops + 2 * butterflies * rows * rank * groups * rank,
                column_mats(1) + [((rows, offs * groups * rank), BF16), ((rows, groups * rank), BF16)],
                first_level,
                second_level,
                fourth_level,
                out_basis,
                thirds_last[0],
            )
        else:
            received = send(levels)
        own_last, other_last, off_rows, last_rows = last_weights
        residual, *levels = call(
            functools.partial(middle_kernel, radix, groups, offs, span),
            "middle_levels",
            offs * row_flops + column_flops,
            [((rows, width), F32)] + levels_out(butterflies - offs),
            third_level,
            rhs,
            leaf_basis,
            off_rows,
            own_last,
            other_last,
            *received,
        )
        received = send(levels)
        done += call(
            functools.partial(last_kernel, radix, groups, offs),
            "last_levels",
            row_flops,
            [((1, rows, width), BF16)],
            third_level,
            last_rows,
            residual,
            *received,
        )
    return done[0] if CHUNKS == 1 else jnp.concatenate(done, axis=2)


def solution(mesh):
    placed = (
        P(None, ("box", "row"), None),
        P("row", "box", None),
        P("row", None, "box", None, None),
        P("row", None, "box", None, None, None, None),
        P("row", None, "box", None, None, None),
        P("row", None, "box", None, None, None),
        P("row", None, "box", None, None, None, None),
        P("row", None, "box", None, None),
    )
    return jax.shard_map(
        functools.partial(on_device, mesh.shape["row"], mesh.shape["box"]),
        mesh=mesh,
        in_specs=placed,
        out_specs=P("row", "box", None),
        check_vma=False,
    )
```

time: 153 us -> 99.9 us (0.65)
  waiting for transfers between devices: 100 us -> 33.6 us
  starting transfers between devices: 9.29 us -> 42.3 us
  matrix products: 19.4 us -> 0 us
  between operations: 13.5 us -> 0.17 us
  Pallas kernels: 0 us -> 9.71 us
  local copies, waits for them, and re-layouts: 6.16 us -> 12.2 us
  other arithmetic: 3.82 us -> 1.43 us
    all_to_all x2 -> x1, waiting for transfers between devices: 74.6 us -> 3.07 us  [send(): last = lax.all_to_all(last, 'box', split_axis=1, concat_axis=1, tiled=True)]
    ppermute x0 -> x21, starting transfers between devices: none -> 36.8 us  [the longest x12 18.4 us: over_members(): return array if mask == 0 else lax.ppermute(array, 'box', pairs)]
    ppermute x0 -> x21, waiting for transfers between devices: none -> 30.5 us  [the longest x12 21 us: over_members(): return array if mask == 0 else lax.ppermute(array, 'box', pairs)]
    all_gather x1 -> x0, waiting for transfers between devices: 25.1 us -> none  [on_device(): gathered = lax.all_gather(solved, 'row', axis=1, tiled=True)]
    dot_general x8 -> x0, matrix products: 19.4 us -> none  [the longest x2 7.1 us: outer_levels(): jnp.einsum('jhpr,jhrn->jhpn', outer_basis, half_coef, preferred_element_t...]
    unnamed x8 -> x40, local copies, waits for them, and re-layouts: 0.02 us -> 11.5 us
    pallas_call x0 -> x6, Pallas kernels: none -> 9.71 us  [call(): pl.pallas_call(kernel, out_shape=outs, in_specs=[VMEM] * len(args), out_s...]
    slice x8 -> x0, local copies, waits for them, and re-layouts: 4.66 us -> none  [the longest x1 2.75 us: on_device(): residual = rhs[0].astype(jnp.float32) - both[0] - both[1]]
  transfers between devices with their start and end apart: 3 -> 22, of which waited for: 3 -> 12; matrix products, arithmetic and copies ran while one was open for 1% -> 2% of each run, Pallas kernels for 0% -> 3%
where the time goes in v1:
time: 99.9 us; the launch traced here: 99.4 us
  starting transfers between devices  42.3 us (42%)
  waiting for transfers between devices  33.6 us (34%)
  local copies, waits for them, and re-layouts  12.2 us (12%)
  Pallas kernels  9.71 us (10%)
  other arithmetic  1.43 us (1%)
    ppermute x12, waiting for transfers between devices, over_members(): return array if mask == 0 else lax.ppermute(array, 'box', pairs)  21 us
    ppermute x12, starting transfers between devices, over_members(): return array if mask == 0 else lax.ppermute(array, 'box', pairs)  18.4 us
    ppermute x6, starting transfers between devices, over_groups(): return lax.ppermute(array, 'box', pairs)  15.5 us
    unnamed x40, local copies, waits for them, and re-layouts  11.5 us
    pallas_call x6, Pallas kernels, call(): pl.pallas_call(kernel, out_shape=outs, in_specs=[VMEM] * len(args), out_s...  9.71 us
    ppermute x6, waiting for transfers between devices, over_groups(): return lax.ppermute(array, 'box', pairs)  9.53 us
    all_to_all x1, starting transfers between devices, send(): last = lax.all_to_all(last, 'box', split_axis=1, concat_axis=1, tiled=True)  5.48 us
    all_to_all x1, waiting for transfers between devices, send(): last = lax.all_to_all(last, 'box', split_axis=1, concat_axis=1, tiled=True)  3.07 us
  transfers between devices with their start and end apart: 22, of which 12 were waited for; matrix products, arithmetic and copies ran while one was open for 2% of the time, Pallas kernels for 3%

profile of v1, /device:TPU:0, one launch (start us, length us, event | category | flops | bytes accessed | tf_op | source)
XLA Modules:
  0.0 99.4 jit_solution(2658038585745708731)
XLA Ops:
  0.0 3.0 %collective-permute-start = (bf16[2,256,512]{2,1,0:T(8,128)(2,1)}, bf16[2,256,512]{2,1,0:T(8,128)(2,1)S(1)}, u32[]{:S(2)}, u32[]{:S(2)}) collective-permute-start(bf16[2,256,512]{2,1,0:T(8,128)(2,1)} %refs_0_.1), channel_id=1, source_target_pairs={{0,16},{8,24},{16,0},{24,8},{1,17},{9,25},{17,1},{25,9},{2,18},{10... | collective-permute-start | bytes 1572872 | tf_op jit(solution)/shard_map/ppermute | solution.py:184
  3.0 1.1 %copy-done = bf16[1,3,1,8,128,128]{5,4,3,2,1,0:T(8,128)(2,1)S(1)} copy-done((bf16[1,3,1,8,128,128]{5,4,3,2,1,0:T(8,128)(2,1)S(1)}, bf16[1,3,1,8,128,128]{5,4,3,2,1,0:T(8,128)(2,1)}, u32[]{:S(2)}) %copy-start) | copy-done | bytes 786456
  4.1 2.7 %collective-permute-start.1 = (bf16[2,128,128]{2,1,0:T(8,128)(2,1)S(1)}, bf16[2,128,128]{2,1,0:T(8,128)(2,1)S(1)}, u32[]{:S(2)}, u32[]{:S(2)}) collective-permute-start(bf16[2,128,128]{2,1,0:T(8,128)(2,1)S(1)} %get-tuple-element.39), channel_id=1, source_target_pairs={{0,4},{1,5},{2,6},{3,7},{4,0},{5,1},{6,2},{7,3},{8,12},{9,13},{10,... | collective-permute-start | bytes 196616 | tf_op jit(solution)/shard_map/ppermute | solution.py:194
  6.8 1.3 %collective-permute-start.2 = (bf16[2,128,128]{2,1,0:T(8,128)(2,1)S(1)}, bf16[2,128,128]{2,1,0:T(8,128)(2,1)S(1)}, u32[]{:S(2)}, u32[]{:S(2)}) collective-permute-start(bf16[2,128,128]{2,1,0:T(8,128)(2,1)S(1)} %get-tuple-element.40), channel_id=1, source_target_pairs={{0,5},{1,4},{2,7},{3,6},{4,1},{5,0},{6,3},{7,2},{8,13},{9,12},{10,... | collective-permute-start | bytes 196616 | tf_op jit(solution)/shard_map/ppermute | solution.py:194
  8.0 3.6 %collective-permute-start.3 = (bf16[2,128,128]{2,1,0:T(8,128)(2,1)S(1)}, bf16[2,128,128]{2,1,0:T(8,128)(2,1)S(1)}, u32[]{:S(2)}, u32[]{:S(2)}) collective-permute-start(bf16[2,128,128]{2,1,0:T(8,128)(2,1)S(1)} %get-tuple-element.41), channel_id=1, source_target_pairs={{0,6},{1,7},{2,4},{3,5},{4,2},{5,3},{6,0},{7,1},{8,14},{9,15},{10,... | collective-permute-start | bytes 196616 | tf_op jit(solution)/shard_map/ppermute | solution.py:194
  11.6 0.0 collective-permute-start.5
  11.7 0.0 collective-permute-done.1.refs_0_
  11.7 4.0 %collective-permute-done.2.refs_1_ = bf16[2,128,128]{2,1,0:T(8,128)(2,1)S(1)} collective-permute-done((bf16[2,128,128]{2,1,0:T(8,128)(2,1)S(1)}, bf16[2,128,128]{2,1,0:T(8,128)(2,1)S(1)}, u32[]{:S(2)}, u32[]{:S(2)}) %collective-permute-start.2) | collective-permute-done | bytes 65568 | tf_op jit(solution)/shard_map/ppermute | solution.py:194
  15.7 0.0 collective-permute-done.3.refs_2_
  15.7 0.0 collective-permute-done.refs_2_
  15.7 4.2 %collective-permute-start.4 = (bf16[2,128,128]{2,1,0:T(8,128)(2,1)S(1)}, bf16[2,128,128]{2,1,0:T(8,128)(2,1)S(1)}, u32[]{:S(2)}, u32[]{:S(2)}) collective-permute-start(bf16[2,128,128]{2,1,0:T(8,128)(2,1)S(1)} %get-tuple-element.45), channel_id=1, source_target_pairs={{0,7},{1,6},{2,5},{3,4},{4,3},{5,2},{6,1},{7,0},{8,15},{9,14},{10,... | collective-permute-start | bytes 196616 | tf_op jit(solution)/shard_map/ppermute | solution.py:194
  19.9 0.7 slice_bitcast_fusion
  20.6 2.4 %collective-permute-done.4.refs_3_ = bf16[2,128,128]{2,1,0:T(8,128)(2,1)S(1)} collective-permute-done((bf16[2,128,128]{2,1,0:T(8,128)(2,1)S(1)}, bf16[2,128,128]{2,1,0:T(8,128)(2,1)S(1)}, u32[]{:S(2)}, u32[]{:S(2)}) %collective-permute-start.4) | collective-permute-done | bytes 65568 | tf_op jit(solution)/shard_map/ppermute | solution.py:194
  23.0 1.4 %copy-done.2 = bf16[1,3,1,4,4,128,128]{6,5,4,3,2,1,0:T(8,128)(2,1)S(1)} copy-done((bf16[1,3,1,4,4,128,128]{6,5,4,3,2,1,0:T(8,128)(2,1)S(1)}, bf16[1,3,1,4,4,128,128]{6,5,4,3,2,1,0:T(8,128)(2,1)}, u32[]{:S(2)}) %copy-start.2) | copy-done | bytes 1572888
  24.4 1.1 %copy-done.5 = bf16[1,3,1,8,128,128]{5,4,3,2,1,0:T(8,128)(2,1)S(1)} copy-done((bf16[1,3,1,8,128,128]{5,4,3,2,1,0:T(8,128)(2,1)S(1)}, bf16[1,3,1,8,128,128]{5,4,3,2,1,0:T(8,128)(2,1)}, u32[]{:S(2)}) %copy-start.5) | copy-done | bytes 786456
  25.5 1.8 %off_weights.1 = (bf16[2,4,128,512]{3,2,1,0:T(8,128)(2,1)S(1)}, bf16[2,4,1,128,512]{4,3,2,1,0:T(8,128)(2,1)S(1)}) custom-call(bf16[1,3,1,4,4,128,128]{6,5,4,3,2,1,0:T(8,128)(2,1)S(1)} %copy-done.2, bf16[1,3,1,8,128,128]{5,4,3,2,1,0:T(8,128)(2,1)S(1)} %copy-done.5, bf16[2,128,128]{2,1,0:T(8,128)(2,1)S(1)} %collective-permute-done.1.refs_0_, ...), custom_call_target="tpu_custom_call" | custom-call | flops 335544320 | bytes 4718592 | tf_op jit(solution)/shard_map/off_weights/pallas_call | solution.py:199
  27.3 0.0 collective-permute-done.6.refs_3_
  27.4 0.0 copy-start.6
  27.4 1.7 %off_levels.1 = (bf16[2,128,512]{2,1,0:T(8,128)(2,1)S(1)}, bf16[2,128,512]{2,1,0:T(8,128)(2,1)S(1)}, bf16[2,128,512]{2,1,0:T(8,128)(2,1)S(1)}, bf16[2,128,512]{2...) custom-call(bf16[1,3,4,256,128]{4,3,2,1,0:T(8,128)(2,1)S(1)} %copy-d, ...), custom_call_target="tpu_custom_call" | custom-call | flops 1342177280 | bytes 7077888 | tf_op jit(solution)/shard_map/off_levels/pallas_call | solution.py:199
  29.1 0.7 copy-done.11
  29.8 0.7 copy-done.13
  30.5 0.7 copy-done.14
  31.2 0.7 copy-done.15
  32.0 0.7 copy-done.16
  32.7 0.7 copy-done.17
  33.4 0.7 copy-done.18
  34.1 0.7 copy-done.19
  34.8 5.5 %all-to-all-start = ((bf16[1,8,128,128]{3,2,0,1:T(8,128)(2,1)}), bf16[1,8,128,128]{3,2,0,1:T(8,128)(2,1)S(1)}, u32[]{:S(2)}, u32[]{:S(2)}) async-start(bf16[1,8,128,128]{3,2,0,1:T(8,128)(2,1)} %slice_bitcast_fusion), calls=%async_computation | async-start | bytes 524288 | tf_op jit(solution)/shard_map/all_to_all | solution.py:256
  40.2 2.0 %collective-permute-start.10 = (bf16[2,1,128,512]{3,2,0,1:T(8,128)(2,1)}, bf16[2,1,128,512]{3,2,0,1:T(8,128)(2,1)}, u32[]{:S(2)}, u32[]{:S(2)}) collective-permute-start(bf16[2,1,128,512]{3,2,0,1:T(8,128)(2,1)} %bitcast.15), channel_id=1, source_target_pairs={{0,1},{1,0},{2,3},{3,2},{4,5},{5,4},{6,7},{7,6},{8,9},{9,8},{10,11... | collective-permute-start | bytes 786440 | tf_op jit(solution)/shard_map/ppermute | solution.py:188
  42.3 1.5 %collective-permute-start.11 = (bf16[2,1,128,512]{3,2,0,1:T(8,128)(2,1)}, bf16[2,1,128,512]{3,2,0,1:T(8,128)(2,1)}, u32[]{:S(2)}, u32[]{:S(2)}) collective-permute-start(bf16[2,1,128,512]{3,2,0,1:T(8,128)(2,1)} %bitcast.14), channel_id=1, source_target_pairs={{0,2},{1,3},{2,0},{3,1},{4,6},{5,7},{6,4},{7,5},{8,10},{9,11},{10,... | collective-permute-start | bytes 786440 | tf_op jit(solution)/shard_map/ppermute | solution.py:188
  43.7 0.0 collective-permute-start.12
  43.8 2.0 %collective-permute-start.7 = (bf16[2,128,512]{2,1,0:T(8,128)(2,1)}, bf16[2,128,512]{2,1,0:T(8,128)(2,1)}, u32[]{:S(2)}, u32[]{:S(2)}) collective-permute-start(bf16[2,128,512]{2,1,0:T(8,128)(2,1)} %copy-done.16), channel_id=1, source_target_pairs={{0,1},{1,0},{2,3},{3,2},{4,5},{5,4},{6,7},{7,6},{8,9},{9,8},{10,11... | collective-permute-start | bytes 786440 | tf_op jit(solution)/shard_map/ppermute | solution.py:188
  45.8 1.5 %collective-permute-start.8 = (bf16[2,128,512]{2,1,0:T(8,128)(2,1)}, bf16[2,128,512]{2,1,0:T(8,128)(2,1)}, u32[]{:S(2)}, u32[]{:S(2)}) collective-permute-start(bf16[2,128,512]{2,1,0:T(8,128)(2,1)} %copy-done.15), channel_id=1, source_target_pairs={{0,2},{1,3},{2,0},{3,1},{4,6},{5,7},{6,4},{7,5},{8,10},{9,11},{10,... | collective-permute-start | bytes 786440 | tf_op jit(solution)/shard_map/ppermute | solution.py:188
  47.2 3.1 %all-to-all-done = bf16[1,8,128,128]{3,2,0,1:T(8,128)(2,1)S(1)} async-done(((bf16[1,8,128,128]{3,2,0,1:T(8,128)(2,1)}), bf16[1,8,128,128]{3,2,0,1:T(8,128)(2,1)S(1)}, u32[]{:S(2)}, u32[]{:S(2)}) %all-to-all-start) | async-done | bytes 262176 | tf_op jit(solution)/shard_map/all_to_all | solution.py:256
  50.3 2.5 %collective-permute-done.10 = bf16[2,1,128,512]{3,2,0,1:T(8,128)(2,1)} collective-permute-done((bf16[2,1,128,512]{3,2,0,1:T(8,128)(2,1)}, bf16[2,1,128,512]{3,2,0,1:T(8,128)(2,1)}, u32[]{:S(2)}, u32[]{:S(2)}) %collective-permute-start.10) | collective-permute-done | bytes 262176 | tf_op jit(solution)/shard_map/ppermute | solution.py:188
  52.8 2.1 %collective-permute-start.9 = (bf16[2,128,512]{2,1,0:T(8,128)(2,1)}, bf16[2,128,512]{2,1,0:T(8,128)(2,1)S(1)}, u32[]{:S(2)}, u32[]{:S(2)}) collective-permute-start(bf16[2,128,512]{2,1,0:T(8,128)(2,1)} %copy-done.14), channel_id=1, source_target_pairs={{0,3},{1,2},{2,1},{3,0},{4,7},{5,6},{6,5},{7,4},{8,11},{9,10},{10,... | collective-permute-start | bytes 786440 | tf_op jit(solution)/shard_map/ppermute | solution.py:188
  54.9 0.0 collective-permute-done.11
  54.9 5.3 %collective-permute-done.12 = bf16[2,1,128,512]{3,2,0,1:T(8,128)(2,1)} collective-permute-done((bf16[2,1,128,512]{3,2,0,1:T(8,128)(2,1)}, bf16[2,1,128,512]{3,2,0,1:T(8,128)(2,1)}, u32[]{:S(2)}, u32[]{:S(2)}) %collective-permute-start.12) | collective-permute-done | bytes 262176 | tf_op jit(solution)/shard_map/ppermute | solution.py:188
  60.2 1.4 %fusion = bf16[2,128,512]{2,1,0:T(8,128)(2,1)S(1)} fusion(bf16[2,1,128,512]{3,2,0,1:T(8,128)(2,1)} %collective-permute-done.12, bf16[2,1,128,512]{3,2,0,1:T(8,128)(2,1)} %collective-permute-done.11, bf16[2,1,128,512]{3,2,0,1:T(8,128)(2,1)} %collective-permute-done.10, bf16[2,1,128,512]{3,2,1,0:T(8,128)(2,1)} %copy-done.13), kind=kLoop, calls=%fused_computation.1 | loop fusion | flops 1048576 | bytes 1310720 | tf_op jit(solution)/shard_map/add | solution.py:261
  61.6 0.0 copy-start.1
  61.6 0.0 copy-start.7
  61.6 2.8 %collective-permute-start.13 = (bf16[2,128,512]{2,1,0:T(8,128)(2,1)S(1)}, bf16[2,128,512]{2,1,0:T(8,128)(2,1)S(1)}, u32[]{:S(2)}, u32[]{:S(2)}) collective-permute-start(bf16[2,128,512]{2,1,0:T(8,128)(2,1)S(1)} %fusion), channel_id=1, source_target_pairs={{0,4},{1,5},{2,6},{3,7},{4,0},{5,1},{6,2},{7,3},{8,12},{9,13},{10,... | collective-permute-start | bytes 786440 | tf_op jit(solution)/shard_map/ppermute | solution.py:194
  64.4 1.1 %copy-done.8 = bf16[1,3,2,512,128]{4,3,2,1,0:T(8,128)(2,1)S(1)} copy-done((bf16[1,3,2,512,128]{4,3,2,1,0:T(8,128)(2,1)S(1)}, bf16[1,3,2,512,128]{4,3,2,1,0:T(8,128)(2,1)}, u32[]{:S(2)}) %copy-start.8) | copy-done | bytes 786456
  65.5 1.0 copy-done.10
  66.5 1.4 %rest_weights.1 = (bf16[1,4,128,512]{3,2,1,0:T(8,128)(2,1)S(1)}, bf16[1,4,1,128,512]{4,3,2,1,0:T(8,128)(2,1)S(1)}, bf16[1024,512]{1,0:T(8,128)(2,1)S(1)}, bf16[1024,256]{1,0:T(8,128)(2,1)S(1)}) custom-call(bf16[1,3,1,4,4,128,128]{6,5,4,3,2,1,0:T(8,128)(2,1)S(1)} %copy-done.3, bf16[1,3,1,8,128,128]{5,4,3,2,1,0:T(8,128)(2,1)S(1)} %copy-done.6, ...), custom_call_target="tpu_custom_call" | custom-call | flops 369098752 | bytes 6422528 | tf_op jit(solution)/shard_map/rest_weights/pallas_call | solution.py:199
  67.9 2.9 %collective-permute-done.8.refs_2_ = bf16[2,128,512]{2,1,0:T(8,128)(2,1)} collective-permute-done((bf16[2,128,512]{2,1,0:T(8,128)(2,1)}, bf16[2,128,512]{2,1,0:T(8,128)(2,1)}, u32[]{:S(2)}, u32[]{:S(2)}) %collective-permute-start.8) | collective-permute-done | bytes 262176 | tf_op jit(solution)/shard_map/ppermute | solution.py:188
  70.8 4.9 %collective-permute-done.9.refs_3_ = bf16[2,128,512]{2,1,0:T(8,128)(2,1)S(1)} collective-permute-done((bf16[2,128,512]{2,1,0:T(8,128)(2,1)}, bf16[2,128,512]{2,1,0:T(8,128)(2,1)S(1)}, u32[]{:S(2)}, u32[]{:S(2)}) %collective-permute-start.9) | collective-permute-done | bytes 262176 | tf_op jit(solution)/shard_map/ppermute | solution.py:188
  75.7 0.0 collective-permute-done.13.refs_4_
  75.8 3.2 %middle_levels.1 = (f32[1024,512]{1,0:T(8,128)S(1)}, bf16[1,128,512]{2,1,0:T(8,128)(2,1)S(1)}, bf16[1,128,512]{2,1,0:T(8,128)(2,1)S(1)}, bf16[1,128,512]{2,1,0:T...) custom-call(bf16[1,3,1,8,128,128]{5,4,3,2,1,0:T(8,128)(2,1)S(1)} %co, ...), custom_call_target="tpu_custom_call" | custom-call | flops 1342177280 | bytes 9175040 | tf_op jit(solution)/shard_map/middle_levels/pallas_call | solution.py:199
  79.0 1.4 %collective-permute-start.17 = (bf16[1,1,128,512]{3,2,1,0:T(8,128)(2,1)S(1)}, bf16[1,1,128,512]{3,2,1,0:T(8,128)(2,1)S(1)}, u32[]{:S(2)}, u32[]{:S(2)}) collective-permute-start(bf16[1,1,128,512]{3,2,1,0:T(8,128)(2,1)S(1)} %get-tuple-element.70), channel_id=1, source_target_pairs={{0,1},{1,0},{2,3},{3,2},{4,5},{5,4},{6,7},{7,6},{8,9},{9,8},{10,11... | collective-permute-start | bytes 393224 | tf_op jit(solution)/shard_map/ppermute | solution.py:188
  80.4 1.6 %collective-permute-start.18 = (bf16[1,1,128,512]{3,2,1,0:T(8,128)(2,1)S(1)}, bf16[1,1,128,512]{3,2,1,0:T(8,128)(2,1)S(1)}, u32[]{:S(2)}, u32[]{:S(2)}) collective-permute-start(bf16[1,1,128,512]{3,2,1,0:T(8,128)(2,1)S(1)} %get-tuple-element.71), channel_id=1, source_target_pairs={{0,2},{1,3},{2,0},{3,1},{4,6},{5,7},{6,4},{7,5},{8,10},{9,11},{10,... | collective-permute-start | bytes 393224 | tf_op jit(solution)/shard_map/ppermute | solution.py:188
  82.0 0.6 collective-permute-start.19
  82.5 1.3 %collective-permute-start.14 = (bf16[1,128,512]{2,1,0:T(8,128)(2,1)S(1)}, bf16[1,128,512]{2,1,0:T(8,128)(2,1)S(1)}, u32[]{:S(2)}, u32[]{:S(2)}) collective-permute-start(bf16[1,128,512]{2,1,0:T(8,128)(2,1)S(1)} %get-tuple-element.66), channel_id=1, source_target_pairs={{0,1},{1,0},{2,3},{3,2},{4,5},{5,4},{6,7},{7,6},{8,9},{9,8},{10,11... | collective-permute-start | bytes 393224 | tf_op jit(solution)/shard_map/ppermute | solution.py:188
  83.9 1.6 %collective-permute-start.15 = (bf16[1,128,512]{2,1,0:T(8,128)(2,1)S(1)}, bf16[1,128,512]{2,1,0:T(8,128)(2,1)S(1)}, u32[]{:S(2)}, u32[]{:S(2)}) collective-permute-start(bf16[1,128,512]{2,1,0:T(8,128)(2,1)S(1)} %get-tuple-element.67), channel_id=1, source_target_pairs={{0,2},{1,3},{2,0},{3,1},{4,6},{5,7},{6,4},{7,5},{8,10},{9,11},{10,... | collective-permute-start | bytes 393224 | tf_op jit(solution)/shard_map/ppermute | solution.py:188
  85.4 0.7 collective-permute-done.17
  86.1 2.8 %collective-permute-start.16 = (bf16[1,128,512]{2,1,0:T(8,128)(2,1)S(1)}, bf16[1,128,512]{2,1,0:T(8,128)(2,1)S(1)}, u32[]{:S(2)}, u32[]{:S(2)}) collective-permute-start(bf16[1,128,512]{2,1,0:T(8,128)(2,1)S(1)} %get-tuple-element.68), channel_id=1, source_target_pairs={{0,3},{1,2},{2,1},{3,0},{4,7},{5,6},{6,5},{7,4},{8,11},{9,10},{10,... | collective-permute-start | bytes 393224 | tf_op jit(solution)/shard_map/ppermute | solution.py:188
  89.0 0.7 collective-permute-done.19
  89.7 0.1 fusion.1
  89.8 1.0 collective-permute-start.20
  90.8 0.0 collective-permute-done.14.refs_1_
  90.8 2.5 %collective-permute-done.15.refs_2_ = bf16[1,128,512]{2,1,0:T(8,128)(2,1)S(1)} collective-permute-done((bf16[1,128,512]{2,1,0:T(8,128)(2,1)S(1)}, bf16[1,128,512]{2,1,0:T(8,128)(2,1)S(1)}, u32[]{:S(2)}, u32[]{:S(2)}) %collective-permute-start.15) | collective-permute-done | bytes 131104 | tf_op jit(solution)/shard_map/ppermute | solution.py:188
  93.3 1.4 %collective-permute-done.16.refs_3_ = bf16[1,128,512]{2,1,0:T(8,128)(2,1)S(1)} collective-permute-done((bf16[1,128,512]{2,1,0:T(8,128)(2,1)S(1)}, bf16[1,128,512]{2,1,0:T(8,128)(2,1)S(1)}, u32[]{:S(2)}, u32[]{:S(2)}) %collective-permute-start.16) | collective-permute-done | bytes 131104 | tf_op jit(solution)/shard_map/ppermute | solution.py:188
  94.7 3.1 %collective-permute-done.20.refs_4_ = bf16[1,128,512]{2,1,0:T(8,128)(2,1)S(1)} collective-permute-done((bf16[1,128,512]{2,1,0:T(8,128)(2,1)S(1)}, bf16[1,128,512]{2,1,0:T(8,128)(2,1)S(1)}, u32[]{:S(2)}, u32[]{:S(2)}) %collective-permute-start.20) | collective-permute-done | bytes 131104 | tf_op jit(solution)/shard_map/ppermute | solution.py:194
  97.8 1.6 %last_levels.1 = bf16[1,1024,512]{2,1,0:T(8,128)(2,1)} custom-call(bf16[1,3,1,8,128,128]{5,4,3,2,1,0:T(8,128)(2,1)S(1)} %copy-done.1, bf16[1024,256]{1,0:T(8,128)(2,1)S(1)} %get-tuple-element.52.row_mats, f32[1024,512]{1,0:T(8,128)S(1)} %get-tuple-element.64.residual, bf16[1,128,512]{2,1,0:T(8,128)(2,1)S(1)} %get-tuple-element.65.refs_0_, ...), custom_call_target="tpu_custom_call" | custom-call | flops 335544320 | bytes 5111808 | tf_op jit(solution)/shard_map/last_levels/pallas_call | solution.py:199
  (29 shorter events, 0.1 us)
Async XLA Ops:
  0.0 15.7 %collective-permute-start = (bf16[2,256,512]{2,1,0:T(8,128)(2,1)}, bf16[2,256,512]{2,1,0:T(8,128)(2,1)S(1)}, u32[]{:S(2)}, u32[]{:S(2)}) collective-permute-start(bf16[2,256,512]{2,1,0:T(8,128)(2,1)} %refs_0_.1), channel_id=1, source_target_pairs={{0,16},{8,24},{16,0},{24,8},{1,17},{9,25},{17,1},{25,9},{2,18},{10... | collective-permute-start | bytes 1572872 | tf_op jit(solution)/shard_map/ppermute | solution.py:184
  3.0 1.1 %copy-start = (bf16[1,3,1,8,128,128]{5,4,3,2,1,0:T(8,128)(2,1)S(1)}, bf16[1,3,1,8,128,128]{5,4,3,2,1,0:T(8,128)(2,1)}, u32[]{:S(2)}) copy-start(bf16[1,3,1,8,128,128]{5,4,3,2,1,0:T(8,128)(2,1)} %third.5) | copy-start | bytes 2359300
  4.1 23.2 %copy-start.4 = (bf16[1,3,4,256,128]{4,3,2,1,0:T(8,128)(2,1)S(1)}, bf16[1,3,4,256,128]{4,3,2,1,0:T(8,128)(2,1)}, u32[]{:S(2)}) copy-start(bf16[1,3,4,256,128]{4,3,2,1,0:T(8,128)(2,1)} %basis.3) | copy-start | bytes 2359300
  4.1 23.2 %copy-start.9 = (bf16[2,256,512]{2,1,0:T(8,128)(2,1)S(1)}, bf16[2,256,512]{2,1,0:T(8,128)(2,1)}, u32[]{:S(2)}) copy-start(bf16[2,256,512]{2,1,0:T(8,128)(2,1)} %refs_0_.1) | copy-start | bytes 1572868
  4.1 7.5 %collective-permute-start.1 = (bf16[2,128,128]{2,1,0:T(8,128)(2,1)S(1)}, bf16[2,128,128]{2,1,0:T(8,128)(2,1)S(1)}, u32[]{:S(2)}, u32[]{:S(2)}) collective-permute-start(bf16[2,128,128]{2,1,0:T(8,128)(2,1)S(1)} %get-tuple-element.39), channel_id=1, source_target_pairs={{0,4},{1,5},{2,6},{3,7},{4,0},{5,1},{6,2},{7,3},{8,12},{9,13},{10,... | collective-permute-start | bytes 196616 | tf_op jit(solution)/shard_map/ppermute | solution.py:194
  6.8 8.9 %collective-permute-start.2 = (bf16[2,128,128]{2,1,0:T(8,128)(2,1)S(1)}, bf16[2,128,128]{2,1,0:T(8,128)(2,1)S(1)}, u32[]{:S(2)}, u32[]{:S(2)}) collective-permute-start(bf16[2,128,128]{2,1,0:T(8,128)(2,1)S(1)} %get-tuple-element.40), channel_id=1, source_target_pairs={{0,5},{1,4},{2,7},{3,6},{4,1},{5,0},{6,3},{7,2},{8,13},{9,12},{10,... | collective-permute-start | bytes 196616 | tf_op jit(solution)/shard_map/ppermute | solution.py:194
  8.0 7.6 %collective-permute-start.3 = (bf16[2,128,128]{2,1,0:T(8,128)(2,1)S(1)}, bf16[2,128,128]{2,1,0:T(8,128)(2,1)S(1)}, u32[]{:S(2)}, u32[]{:S(2)}) collective-permute-start(bf16[2,128,128]{2,1,0:T(8,128)(2,1)S(1)} %get-tuple-element.41), channel_id=1, source_target_pairs={{0,6},{1,7},{2,4},{3,5},{4,2},{5,3},{6,0},{7,1},{8,14},{9,15},{10,... | collective-permute-start | bytes 196616 | tf_op jit(solution)/shard_map/ppermute | solution.py:194
  11.6 15.7 %collective-permute-start.5 = (bf16[2,256,512]{2,1,0:T(8,128)(2,1)}, bf16[2,256,512]{2,1,0:T(8,128)(2,1)S(1)}, u32[]{:S(2)}, u32[]{:S(2)}) collective-permute-start(bf16[2,256,512]{2,1,0:T(8,128)(2,1)} %refs_0_.1), channel_id=1, source_target_pairs={{0,8},{8,0},{16,24},{24,16},{1,9},{9,1},{17,25},{25,17},{2,10},{10... | collective-permute-start | bytes 1572872 | tf_op jit(solution)/shard_map/ppermute | solution.py:184
  15.7 11.7 %collective-permute-start.6 = (bf16[2,256,512]{2,1,0:T(8,128)(2,1)S(1)}, bf16[2,256,512]{2,1,0:T(8,128)(2,1)S(1)}, u32[]{:S(2)}, u32[]{:S(2)}) collective-permute-start(bf16[2,256,512]{2,1,0:T(8,128)(2,1)S(1)} %collective-permute-done.refs_2_), channel_id=1, source_target_pairs={{0,8},{8,0},{16,24},{24,16},{1,9},{9,1},{17,25},{25,17},{2,10},{10... | collective-permute-start | bytes 1572872 | tf_op jit(solution)/shard_map/ppermute | solution.py:184
  15.7 7.3 %collective-permute-start.4 = (bf16[2,128,128]{2,1,0:T(8,128)(2,1)S(1)}, bf16[2,128,128]{2,1,0:T(8,128)(2,1)S(1)}, u32[]{:S(2)}, u32[]{:S(2)}) collective-permute-start(bf16[2,128,128]{2,1,0:T(8,128)(2,1)S(1)} %get-tuple-element.45), channel_id=1, source_target_pairs={{0,7},{1,6},{2,5},{3,4},{4,3},{5,2},{6,1},{7,0},{8,15},{9,14},{10,... | collective-permute-start | bytes 196616 | tf_op jit(solution)/shard_map/ppermute | solution.py:194
  23.0 1.4 %copy-start.2 = (bf16[1,3,1,4,4,128,128]{6,5,4,3,2,1,0:T(8,128)(2,1)S(1)}, bf16[1,3,1,4,4,128,128]{6,5,4,3,2,1,0:T(8,128)(2,1)}, u32[]{:S(2)}) copy-start(bf16[1,3,1,4,4,128,128]{6,5,4,3,2,1,0:T(8,128)(2,1)} %first.3) | copy-start | bytes 4718596
  24.4 1.1 %copy-start.5 = (bf16[1,3,1,8,128,128]{5,4,3,2,1,0:T(8,128)(2,1)S(1)}, bf16[1,3,1,8,128,128]{5,4,3,2,1,0:T(8,128)(2,1)}, u32[]{:S(2)}) copy-start(bf16[1,3,1,8,128,128]{5,4,3,2,1,0:T(8,128)(2,1)} %second.3) | copy-start | bytes 2359300
  27.4 37.0 %copy-start.6 = (bf16[1,3,1,8,128,128]{5,4,3,2,1,0:T(8,128)(2,1)S(1)}, bf16[1,3,1,8,128,128]{5,4,3,2,1,0:T(8,128)(2,1)}, u32[]{:S(2)}) copy-start(bf16[1,3,1,8,128,128]{5,4,3,2,1,0:T(8,128)(2,1)} %second.3) | copy-start | bytes 2359300
  29.1 0.7 copy-start.11
  29.8 0.7 copy-start.13
  30.5 0.7 copy-start.14
  31.2 0.7 copy-start.15
  31.9 0.7 copy-start.16
  32.7 0.7 copy-start.17
  33.4 0.7 copy-start.18
  34.0 0.7 copy-start.19
  34.8 29.6 %copy-start.3 = (bf16[1,3,1,4,4,128,128]{6,5,4,3,2,1,0:T(8,128)(2,1)S(1)}, bf16[1,3,1,4,4,128,128]{6,5,4,3,2,1,0:T(8,128)(2,1)}, u32[]{:S(2)}) copy-start(bf16[1,3,1,4,4,128,128]{6,5,4,3,2,1,0:T(8,128)(2,1)} %first.3) | copy-start | bytes 4718596
  34.8 15.5 %all-to-all-start = ((bf16[1,8,128,128]{3,2,0,1:T(8,128)(2,1)}), bf16[1,8,128,128]{3,2,0,1:T(8,128)(2,1)S(1)}, u32[]{:S(2)}, u32[]{:S(2)}) async-start(bf16[1,8,128,128]{3,2,0,1:T(8,128)(2,1)} %slice_bitcast_fusion), calls=%async_computation | async-start | bytes 524288 | tf_op jit(solution)/shard_map/all_to_all | solution.py:256
  40.2 12.5 %collective-permute-start.10 = (bf16[2,1,128,512]{3,2,0,1:T(8,128)(2,1)}, bf16[2,1,128,512]{3,2,0,1:T(8,128)(2,1)}, u32[]{:S(2)}, u32[]{:S(2)}) collective-permute-start(bf16[2,1,128,512]{3,2,0,1:T(8,128)(2,1)} %bitcast.15), channel_id=1, source_target_pairs={{0,1},{1,0},{2,3},{3,2},{4,5},{5,4},{6,7},{7,6},{8,9},{9,8},{10,11... | collective-permute-start | bytes 786440 | tf_op jit(solution)/shard_map/ppermute | solution.py:188
  42.3 12.6 %collective-permute-start.11 = (bf16[2,1,128,512]{3,2,0,1:T(8,128)(2,1)}, bf16[2,1,128,512]{3,2,0,1:T(8,128)(2,1)}, u32[]{:S(2)}, u32[]{:S(2)}) collective-permute-start(bf16[2,1,128,512]{3,2,0,1:T(8,128)(2,1)} %bitcast.14), channel_id=1, source_target_pairs={{0,2},{1,3},{2,0},{3,1},{4,6},{5,7},{6,4},{7,5},{8,10},{9,11},{10,... | collective-permute-start | bytes 786440 | tf_op jit(solution)/shard_map/ppermute | solution.py:188
  43.7 16.5 %collective-permute-start.12 = (bf16[2,1,128,512]{3,2,0,1:T(8,128)(2,1)}, bf16[2,1,128,512]{3,2,0,1:T(8,128)(2,1)}, u32[]{:S(2)}, u32[]{:S(2)}) collective-permute-start(bf16[2,1,128,512]{3,2,0,1:T(8,128)(2,1)} %bitcast.13), channel_id=1, source_target_pairs={{0,3},{1,2},{2,1},{3,0},{4,7},{5,6},{6,5},{7,4},{8,11},{9,10},{10,... | collective-permute-start | bytes 786440 | tf_op jit(solution)/shard_map/ppermute | solution.py:188
  43.8 24.2 %collective-permute-start.7 = (bf16[2,128,512]{2,1,0:T(8,128)(2,1)}, bf16[2,128,512]{2,1,0:T(8,128)(2,1)}, u32[]{:S(2)}, u32[]{:S(2)}) collective-permute-start(bf16[2,128,512]{2,1,0:T(8,128)(2,1)} %copy-done.16), channel_id=1, source_target_pairs={{0,1},{1,0},{2,3},{3,2},{4,5},{5,4},{6,7},{7,6},{8,9},{9,8},{10,11... | collective-permute-start | bytes 786440 | tf_op jit(solution)/shard_map/ppermute | solution.py:188
  45.8 25.1 %collective-permute-start.8 = (bf16[2,128,512]{2,1,0:T(8,128)(2,1)}, bf16[2,128,512]{2,1,0:T(8,128)(2,1)}, u32[]{:S(2)}, u32[]{:S(2)}) collective-permute-start(bf16[2,128,512]{2,1,0:T(8,128)(2,1)} %copy-done.15), channel_id=1, source_target_pairs={{0,2},{1,3},{2,0},{3,1},{4,6},{5,7},{6,4},{7,5},{8,10},{9,11},{10,... | collective-permute-start | bytes 786440 | tf_op jit(solution)/shard_map/ppermute | solution.py:188
  52.8 23.0 %collective-permute-start.9 = (bf16[2,128,512]{2,1,0:T(8,128)(2,1)}, bf16[2,128,512]{2,1,0:T(8,128)(2,1)S(1)}, u32[]{:S(2)}, u32[]{:S(2)}) collective-permute-start(bf16[2,128,512]{2,1,0:T(8,128)(2,1)} %copy-done.14), channel_id=1, source_target_pairs={{0,3},{1,2},{2,1},{3,0},{4,7},{5,6},{6,5},{7,4},{8,11},{9,10},{10,... | collective-permute-start | bytes 786440 | tf_op jit(solution)/shard_map/ppermute | solution.py:188
  60.2 15.5 %copy-start.12 = (bf16[2,128,512]{2,1,0:T(8,128)(2,1)S(1)}, bf16[2,128,512]{2,1,0:T(8,128)(2,1)}, u32[]{:S(2)}) copy-start(bf16[2,128,512]{2,1,0:T(8,128)(2,1)} %copy-done.11) | copy-start | bytes 786436
  61.6 14.2 %copy-start.1 = (bf16[1,3,1,8,128,128]{5,4,3,2,1,0:T(8,128)(2,1)S(1)}, bf16[1,3,1,8,128,128]{5,4,3,2,1,0:T(8,128)(2,1)}, u32[]{:S(2)}) copy-start(bf16[1,3,1,8,128,128]{5,4,3,2,1,0:T(8,128)(2,1)} %third.5) | copy-start | bytes 2359300
  61.6 14.1 %copy-start.7 = (bf16[1,1024,512]{2,1,0:T(8,128)(2,1)S(1)}, bf16[1,1024,512]{2,1,0:T(8,128)(2,1)}, u32[]{:S(2)}) copy-start(bf16[1,1024,512]{2,1,0:T(8,128)(2,1)} %rhs.1) | copy-start | bytes 3145732
  61.6 14.1 %collective-permute-start.13 = (bf16[2,128,512]{2,1,0:T(8,128)(2,1)S(1)}, bf16[2,128,512]{2,1,0:T(8,128)(2,1)S(1)}, u32[]{:S(2)}, u32[]{:S(2)}) collective-permute-start(bf16[2,128,512]{2,1,0:T(8,128)(2,1)S(1)} %fusion), channel_id=1, source_target_pairs={{0,4},{1,5},{2,6},{3,7},{4,0},{5,1},{6,2},{7,3},{8,12},{9,13},{10,... | collective-permute-start | bytes 786440 | tf_op jit(solution)/shard_map/ppermute | solution.py:194
  64.4 1.1 %copy-start.8 = (bf16[1,3,2,512,128]{4,3,2,1,0:T(8,128)(2,1)S(1)}, bf16[1,3,2,512,128]{4,3,2,1,0:T(8,128)(2,1)}, u32[]{:S(2)}) copy-start(bf16[1,3,2,512,128]{4,3,2,1,0:T(8,128)(2,1)} %out_basis.1) | copy-start | bytes 2359300
  65.5 1.0 %copy-start.10 = (bf16[1,3,1,2,2,128,128]{6,5,4,3,2,1,0:T(8,128)(2,1)S(1)}, bf16[1,3,1,2,2,128,128]{6,5,4,3,2,1,0:T(8,128)(2,1)}, u32[]{:S(2)}) copy-start(bf16[1,3,1,2,2,128,128]{6,5,4,3,2,1,0:T(8,128)(2,1)} %fourth.1) | copy-start | bytes 1179652
  79.0 7.2 %collective-permute-start.17 = (bf16[1,1,128,512]{3,2,1,0:T(8,128)(2,1)S(1)}, bf16[1,1,128,512]{3,2,1,0:T(8,128)(2,1)S(1)}, u32[]{:S(2)}, u32[]{:S(2)}) collective-permute-start(bf16[1,1,128,512]{3,2,1,0:T(8,128)(2,1)S(1)} %get-tuple-element.70), channel_id=1, source_target_pairs={{0,1},{1,0},{2,3},{3,2},{4,5},{5,4},{6,7},{7,6},{8,9},{9,8},{10,11... | collective-permute-start | bytes 393224 | tf_op jit(solution)/shard_map/ppermute | solution.py:188
  80.4 8.6 %collective-permute-start.18 = (bf16[1,1,128,512]{3,2,1,0:T(8,128)(2,1)S(1)}, bf16[1,1,128,512]{3,2,1,0:T(8,128)(2,1)S(1)}, u32[]{:S(2)}, u32[]{:S(2)}) collective-permute-start(bf16[1,1,128,512]{3,2,1,0:T(8,128)(2,1)S(1)} %get-tuple-element.71), channel_id=1, source_target_pairs={{0,2},{1,3},{2,0},{3,1},{4,6},{5,7},{6,4},{7,5},{8,10},{9,11},{10,... | collective-permute-start | bytes 393224 | tf_op jit(solution)/shard_map/ppermute | solution.py:188
  82.0 7.8 %collective-permute-start.19 = (bf16[1,1,128,512]{3,2,1,0:T(8,128)(2,1)S(1)}, bf16[1,1,128,512]{3,2,1,0:T(8,128)(2,1)S(1)}, u32[]{:S(2)}, u32[]{:S(2)}) collective-permute-start(bf16[1,1,128,512]{3,2,1,0:T(8,128)(2,1)S(1)} %get-tuple-element.72), channel_id=1, source_target_pairs={{0,3},{1,2},{2,1},{3,0},{4,7},{5,6},{6,5},{7,4},{8,11},{9,10},{10,... | collective-permute-start | bytes 393224 | tf_op jit(solution)/shard_map/ppermute | solution.py:188
  82.5 8.3 %collective-permute-start.14 = (bf16[1,128,512]{2,1,0:T(8,128)(2,1)S(1)}, bf16[1,128,512]{2,1,0:T(8,128)(2,1)S(1)}, u32[]{:S(2)}, u32[]{:S(2)}) collective-permute-start(bf16[1,128,512]{2,1,0:T(8,128)(2,1)S(1)} %get-tuple-element.66), channel_id=1, source_target_pairs={{0,1},{1,0},{2,3},{3,2},{4,5},{5,4},{6,7},{7,6},{8,9},{9,8},{10,11... | collective-permute-start | bytes 393224 | tf_op jit(solution)/shard_map/ppermute | solution.py:188
  83.9 9.4 %collective-permute-start.15 = (bf16[1,128,512]{2,1,0:T(8,128)(2,1)S(1)}, bf16[1,128,512]{2,1,0:T(8,128)(2,1)S(1)}, u32[]{:S(2)}, u32[]{:S(2)}) collective-permute-start(bf16[1,128,512]{2,1,0:T(8,128)(2,1)S(1)} %get-tuple-element.67), channel_id=1, source_target_pairs={{0,2},{1,3},{2,0},{3,1},{4,6},{5,7},{6,4},{7,5},{8,10},{9,11},{10,... | collective-permute-start | bytes 393224 | tf_op jit(solution)/shard_map/ppermute | solution.py:188
  86.1 8.5 %collective-permute-start.16 = (bf16[1,128,512]{2,1,0:T(8,128)(2,1)S(1)}, bf16[1,128,512]{2,1,0:T(8,128)(2,1)S(1)}, u32[]{:S(2)}, u32[]{:S(2)}) collective-permute-start(bf16[1,128,512]{2,1,0:T(8,128)(2,1)S(1)} %get-tuple-element.68), channel_id=1, source_target_pairs={{0,3},{1,2},{2,1},{3,0},{4,7},{5,6},{6,5},{7,4},{8,11},{9,10},{10,... | collective-permute-start | bytes 393224 | tf_op jit(solution)/shard_map/ppermute | solution.py:188
  89.8 8.0 %collective-permute-start.20 = (bf16[1,128,512]{2,1,0:T(8,128)(2,1)S(1)}, bf16[1,128,512]{2,1,0:T(8,128)(2,1)S(1)}, u32[]{:S(2)}, u32[]{:S(2)}) collective-permute-start(bf16[1,128,512]{2,1,0:T(8,128)(2,1)S(1)} %fusion.1), channel_id=1, source_target_pairs={{0,4},{1,5},{2,6},{3,7},{4,0},{5,1},{6,2},{7,3},{8,12},{9,13},{10,... | collective-permute-start | bytes 393224 | tf_op jit(solution)/shard_map/ppermute | solution.py:194

commit v2 on v1

v2 whole, which is shorter than its diff:
```python
import functools

import jax
import jax.numpy as jnp
from jax import lax
from jax.experimental import pallas as pl
from jax.experimental.pallas import tpu as pltpu
from jax.sharding import PartitionSpec as P

F32 = jnp.float32
BF16 = jnp.bfloat16
MIB = 1024 * 1024
CHUNKS = 1
VMEM = pl.BlockSpec(memory_space=pltpu.VMEM)


def dot(a, b):
    return jnp.dot(a, b, preferred_element_type=F32)


def dot_t(a, b):
    return lax.dot_general(a, b, (((0,), (0,)), ((), ())), preferred_element_type=F32)


def place(radix):
    box = lax.axis_index("box")
    return lax.div(box, radix), lax.rem(box, radix)


def wrap(value, size):
    return lax.rem(value + size, size)


def take(refs, *counts):
    refs, out = list(refs), []
    for count in counts:
        out.append(refs[:count])
        refs = refs[count:]
    return out


def pick_kernel(radix, groups, offs, third, *outs):
    group, member = place(radix)
    at = 0
    for delta in range(1, groups):
        base = wrap(group + delta, groups) * radix
        for i in range(radix):
            for j in range(offs):
                outs[at][j] = third[0, j, 0, base + jnp.bitwise_xor(member, i)]
            at += 1
    for delta in range(1, groups):
        base = wrap(group + delta, groups) * radix
        for k in range(radix):
            outs[at][k] = third[0, offs, 0, base + k]
        at += 1


def leaf_order(row, leaves, row_size):
    per_leaf = row_size // leaves
    return [jnp.bitwise_xor(lax.div(row, per_leaf), t) for t in range(leaves)]


def weights_kernel(radix, groups, offs, row_size, first, second, fourth, out_basis, *outs):
    up_own, up_other, off_rows, last_rows = outs
    levels = first.shape[3]
    slots = second.shape[3]
    rank = fourth.shape[6]
    half_rows = out_basis.shape[3]
    group, member = place(radix)
    for j in range(first.shape[1]):
        order = leaf_order(lax.axis_index("row"), radix, row_size) if j < offs else range(radix)

        def up(slot):
            level = lax.div(slot, slots // levels)
            mats = jnp.concatenate([first[0, j, 0, level, k] for k in order], axis=1)
            return dot(second[0, j, 0, slot], mats).astype(BF16)

        for i in range(radix):
            box = jnp.bitwise_xor(member, i)
            up_own[j, i] = up(group * radix + box)
            for delta in range(1, groups):
                up_other[j, i, delta - 1] = up(wrap(group - delta, groups) * radix + box)
        out, start = (off_rows, j * groups * rank) if j < offs else (last_rows, 0)
        for h in range(fourth.shape[3]):
            mats = [fourth[0, j, 0, h, wrap(group + delta, groups)] for delta in range(groups)]
            out[h * half_rows : (h + 1) * half_rows, start : start + groups * rank] = dot(
                out_basis[0, j, h], jnp.concatenate(mats, axis=1)
            ).astype(BF16)


def other_mats(j, third_of, up_other):
    radix, less = up_other.shape[1], up_other.shape[2]
    mats = [dot(third_of(i, d), up_other[j, i, d]).astype(BF16) for i in range(radix) for d in range(less)]
    return jnp.concatenate(mats, axis=0)


def put_other(mats, leaf, other, at):
    coef = dot(mats, leaf).astype(BF16)
    for i, ref in enumerate(other):
        less, rank, width = ref.shape[1:]
        ref[at] = coef[i * less * rank : (i + 1) * less * rank].reshape(less, rank, width)


def put_own(mats, leaf, own, at):
    radix, rank, depth = mats.shape
    coef = dot(mats[...].reshape(radix * rank, depth), leaf).astype(BF16)
    tiles = leaf.shape[1] // rank
    for i, ref in enumerate(own):
        for c in range(tiles):
            ref[at * tiles + c] = coef[i * rank : (i + 1) * rank, c * rank : (c + 1) * rank]


def off_kernel(radix, groups, pieces, span, basis, up_other, *refs):
    thirds, parts, (leaf_ref,), other = take(refs, (groups - 1) * radix, pieces, 1, radix)
    row = lax.axis_index("row")
    leaves, leaf_rows = basis.shape[2], basis.shape[3]
    rows = parts[0].shape[1]
    per_leaf = leaf_rows // rows
    order = leaf_order(row, leaves, pieces)
    for j in range(parts[0].shape[0]):
        leaf = []
        for t in range(leaves):
            total = None
            for u in range(per_leaf):
                start = jnp.bitwise_xor(lax.rem(row, per_leaf), u) * rows
                if per_leaf == 1:
                    mat = basis[0, j, order[t]]
                else:
                    mat = basis[0, j, order[t], pl.ds(pl.multiple_of(start, rows), rows)]
                ref = parts[t * per_leaf + u]
                data = ref[j, :, span] if ref.shape[2] > span.stop - span.start else ref[j]
                part = dot_t(mat, data)
                total = part if total is None else total + part
            leaf.append(total.astype(BF16))
        leaf = jnp.concatenate(leaf, axis=0)
        leaf_ref[j] = leaf
        mats = other_mats(j, lambda i, d: thirds[d * radix + i][j], up_other)
        put_other(mats, leaf, other, j)


def own_kernel(radix, leaf, up_own, *refs):
    rides, own = take(refs, len(refs) - radix, radix)
    _, member = place(radix)
    offs = leaf.shape[0]
    for j in range(offs):
        put_own(up_own.at[j], leaf[j], own, j)
    for d, ride in enumerate(rides):
        for i, ref in enumerate(own):
            ref[ref.shape[0] - len(rides) + d] = ride[jnp.bitwise_xor(member, i)]


def group_coefs(j, at, tiles, own, crossed, third, radix):
    group, member = place(radix)
    mats = [third[0, j, 0, group * radix + jnp.bitwise_xor(member, i)] for i in range(radix)]
    slots = [jnp.concatenate([ref[at * tiles + c] for c in range(tiles)], axis=1) for ref in own]
    total = dot(jnp.concatenate(mats, axis=1), jnp.concatenate(slots, axis=0))
    return [total.astype(BF16)] + [ref[at] for ref in crossed]


def middle_kernel(radix, groups, offs, span, first_chunk, third, rhs, basis, row_mats, up_own, up_other, *refs):
    crossed, own_in, mats_in, (residual_ref,), own, other, mats_out = take(
        refs, groups - 1, radix, 0 if first_chunk else 1, 1, radix, radix, 1 if first_chunk else 0
    )
    rank = basis.shape[4]
    tiles = (span.stop - span.start) // rank
    if first_chunk:
        mats = other_mats(offs, lambda i, d: own_in[i][offs * tiles + d], up_other)
        mats_out[0][...] = mats
    else:
        mats = mats_in[0][...]
    coefs = []
    for j in range(offs):
        coefs += group_coefs(j, j, tiles, own_in, crossed, third, radix)
    coefs = jnp.concatenate(coefs, axis=0)
    leaves, leaf_rows = basis.shape[2], basis.shape[3]
    leaf = []
    for k in range(leaves):
        rows = slice(k * leaf_rows, (k + 1) * leaf_rows)
        residual = rhs[0, rows, span].astype(F32) - dot(row_mats[rows], coefs)
        residual_ref[rows] = residual
        leaf.append(dot_t(basis[0, offs, k], residual.astype(BF16)).astype(BF16))
    leaf = jnp.concatenate(leaf, axis=0)
    put_other(mats, leaf, other, 0)
    put_own(up_own.at[offs], leaf, own, 0)


def last_kernel(radix, groups, offs, third, row_mats, residual, *refs):
    crossed, own_in, (out,) = take(refs, groups - 1, radix, 1)
    tiles = residual.shape[1] // third.shape[5]
    coefs = jnp.concatenate(group_coefs(offs, 0, tiles, own_in, crossed, third, radix), axis=0)
    out[0] = (residual[...] + dot(row_mats[...], coefs)).astype(BF16)


def after(array, *others):
    return lax.optimization_barrier((array, *others))[0]


def on_device(
    row_size, box_size, solved, rhs, leaf_basis, first_level, second_level, third_level, fourth_level, out_basis
):
    radix = first_level.shape[4]
    groups = box_size // radix
    less = groups - 1
    butterflies = leaf_basis.shape[1]
    offs = solved.shape[0]
    width = solved.shape[2] // CHUNKS
    rank = leaf_basis.shape[4]
    rows = rhs.shape[1]
    depth = radix * rank
    tiles = width // rank

    def over_row(array, mask):
        return lax.ppermute(array, "row", [(r, r ^ mask) for r in range(row_size)])

    def over_members(array, mask):
        pairs = [(b, (b // radix) * radix + ((b % radix) ^ mask)) for b in range(box_size)]
        return array if mask == 0 else lax.ppermute(array, "box", pairs)

    def over_groups(array, delta, mask=0):
        pairs = [
            (b, ((b // radix + delta) % groups) * radix + ((b % radix) ^ mask)) for b in range(box_size)
        ]
        return lax.ppermute(array, "box", pairs)

    def call(kernel, name, flops, outs, *args):
        outs = [jax.ShapeDtypeStruct(shape, dtype) for shape, dtype in outs]
        size = sum(a.size * a.dtype.itemsize for a in [*args, *outs])
        return pl.pallas_call(
            kernel,
            out_shape=outs,
            in_specs=[VMEM] * len(args),
            out_specs=[VMEM] * len(outs),
            compiler_params=pltpu.CompilerParams(vmem_limit_bytes=min(16 * MIB + 2 * size, 56 * MIB)),
            cost_estimate=pl.CostEstimate(flops=int(flops), bytes_accessed=int(size), transcendentals=0),
            name=name,
        )(*args)

    picked = call(
        functools.partial(pick_kernel, radix, groups, offs),
        "pick_third",
        0,
        [((offs, rank, rank), BF16)] * (less * radix) + [((radix, rank, rank), BF16)] * less,
        third_level,
    )
    shifts = [(delta, i) for delta in range(1, groups) for i in range(radix)]
    thirds = [over_groups(a, *shift) for a, shift in zip(picked, shifts)]

    up_own, up_other, off_rows, last_rows = call(
        functools.partial(weights_kernel, radix, groups, offs, row_size),
        "weights",
        2 * butterflies * rank * (box_size * rank * depth + rows * groups * rank),
        [
            ((butterflies, radix, rank, depth), BF16),
            ((butterflies, radix, less, rank, depth), BF16),
            ((rows, offs * groups * rank), BF16),
            ((rows, groups * rank), BF16),
        ],
        first_level,
        second_level,
        fourth_level,
        out_basis,
    )

    beside = over_row(solved, 1)
    chunks, rides = [], None
    for c in range(CHUNKS):
        span = slice(c * width, (c + 1) * width)
        pieces = {0: solved, 1: beside}
        part = solved if CHUNKS == 1 else solved[:, :, span]
        for mask in range(2, row_size, 2):
            pieces[mask] = over_row(part, mask)
            if rides is None:
                pieces[mask] = after(pieces[mask], up_own, *thirds[: radix - 1])
                rides = [
                    over_groups(after(a, pieces[mask]), d + 1) for d, a in enumerate(picked[less * radix :])
                ]
            pieces[mask + 1] = over_row(pieces[mask], 1)
        chunks.append((span, [pieces[mask] for mask in range(row_size)]))

    def other_out(count):
        return [((count, less, rank, width), BF16)] * radix

    def own_out(count):
        return [((count, rank, rank), BF16)] * radix

    def add(other):
        other = [over_members(a, i) for i, a in enumerate(other)]
        return [sum(a[:, d].astype(F32) for a in other).astype(BF16) for d in range(less)]

    def send(own, sums):
        crossed = [over_groups(a, groups - 1 - d) for d, a in enumerate(sums)]
        return crossed + [over_members(after(a, *sums) if i else a, i) for i, a in enumerate(own)]

    other_flops = 2 * width * rank * radix * less * depth
    own_flops = 2 * width * rank * radix * depth
    leaf_flops = 2 * width * rank * rows
    row_flops = 2 * width * rank * (depth + groups * rows)
    done, mats = [], []
    for c, (span, pieces) in enumerate(chunks):
        leaf, *other = call(
            functools.partial(off_kernel, radix, groups, row_size, span),
            "off_levels",
            offs * (leaf_flops + other_flops),
            [((offs, depth, width), BF16)] + other_out(offs),
            leaf_basis,
            up_other,
            *thirds,
            *pieces,
        )
        own = call(
            functools.partial(own_kernel, radix),
            "own_levels",
            offs * own_flops,
            own_out(offs * tiles + (less if c == 0 else 0)),
            leaf,
            up_own,
            *(rides if c == 0 else []),
        )
        received = send(own, add(other))
        residual, *levels = call(
            functools.partial(middle_kernel, radix, groups, offs, span, c == 0),
            "middle_levels",
            offs * row_flops + leaf_flops + other_flops + own_flops,
            [((rows, width), F32)]
            + own_out(tiles)
            + other_out(1)
            + ([((radix * less * rank, depth), BF16)] if c == 0 else []),
            third_level,
            rhs,
            leaf_basis,
            off_rows,
            up_own,
            up_other,
            *received,
            *mats,
        )
        if c == 0:
            mats = [levels.pop()]
        received = send(levels[:radix], add(levels[radix:]))
        done += call(
            functools.partial(last_kernel, radix, groups, offs),
            "last_levels",
            row_flops,
            [((1, rows, width), BF16)],
            third_level,
            last_rows,
            residual,
            *received,
        )
    return done[0] if CHUNKS == 1 else jnp.concatenate(done, axis=2)


def solution(mesh):
    placed = (
        P(None, ("box", "row"), None),
        P("row", "box", None),
        P("row", None, "box", None, None),
        P("row", None, "box", None, None, None, None),
        P("row", None, "box", None, None, None),
        P("row", None, "box", None, None, None),
        P("row", None, "box", None, None, None, None),
        P("row", None, "box", None, None),
    )
    return jax.shard_map(
        functools.partial(on_device, mesh.shape["row"], mesh.shape["box"]),
        mesh=mesh,
        in_specs=placed,
        out_specs=P("row", "box", None),
        check_vma=False,
    )
```

time: 99.9 us -> 85.1 us (0.85)
  starting transfers between devices: 42.3 us -> 30 us
  waiting for transfers between devices: 33.6 us -> 41.3 us
  local copies, waits for them, and re-layouts: 12.2 us -> 5.82 us
  Pallas kernels: 9.71 us -> 7.34 us
  other arithmetic: 1.43 us -> 0.2 us
    ppermute x6 -> x7, waiting for transfers between devices: 9.53 us -> 31 us  [over_groups(): return lax.ppermute(array, 'box', pairs)]
    ppermute x12, waiting for transfers between devices: 21 us -> 10.3 us  [over_members(): return array if mask == 0 else lax.ppermute(array, 'box', pairs)]
    unnamed x40 -> x18, local copies, waits for them, and re-layouts: 11.5 us -> 5.82 us
    all_to_all x1 -> x0, starting transfers between devices: 5.48 us -> none  [send(): last = lax.all_to_all(last, 'box', split_axis=1, concat_axis=1, tiled=True)]
    ppermute x12, starting transfers between devices: 18.4 us -> 14.2 us  [over_members(): return array if mask == 0 else lax.ppermute(array, 'box', pairs)]
    ppermute x6 -> x7, starting transfers between devices: 15.5 us -> 12.3 us  [over_groups(): return lax.ppermute(array, 'box', pairs)]
    all_to_all x1 -> x0, waiting for transfers between devices: 3.07 us -> none  [send(): last = lax.all_to_all(last, 'box', split_axis=1, concat_axis=1, tiled=True)]
    pallas_call x6, Pallas kernels: 9.71 us -> 7.34 us  [call(): pl.pallas_call(kernel, out_shape=outs, in_specs=[VMEM] * len(args), out_s...]
  transfers between devices with their start and end apart: 22 -> 22, of which waited for: 12 -> 11; matrix products, arithmetic and copies ran while one was open for 2% -> 0% of each run, Pallas kernels for 3% -> 3%
where the time goes in v2:
time: 85.1 us; the launch traced here: 84.8 us
  waiting for transfers between devices  41.3 us (49%)
  starting transfers between devices  30 us (35%)
  Pallas kernels  7.34 us (9%)
  local copies, waits for them, and re-layouts  5.82 us (7%)
    ppermute x7, waiting for transfers between devices, over_groups(): return lax.ppermute(array, 'box', pairs)  31 us
    ppermute x12, starting transfers between devices, over_members(): return array if mask == 0 else lax.ppermute(array, 'box', pairs)  14.2 us
    ppermute x7, starting transfers between devices, over_groups(): return lax.ppermute(array, 'box', pairs)  12.3 us
    ppermute x12, waiting for transfers between devices, over_members(): return array if mask == 0 else lax.ppermute(array, 'box', pairs)  10.3 us
    pallas_call x6, Pallas kernels, call(): pl.pallas_call(kernel, out_shape=outs, in_specs=[VMEM] * len(args), out_s...  7.34 us
    unnamed x18, local copies, waits for them, and re-layouts  5.82 us
    ppermute x3, starting transfers between devices, over_row(): return lax.ppermute(array, 'row', [(r, r ^ mask) for r in range(row_size)])  3.54 us
  transfers between devices with their start and end apart: 22, of which 11 were waited for; matrix products, arithmetic and copies ran while one was open for 0% of the time, Pallas kernels for 3%

profile of v2, /device:TPU:0, one launch (start us, length us, event | category | flops | bytes accessed | tf_op | source)
XLA Modules:
  0.0 84.8 jit_solution(13956310661093072110)
XLA Ops:
  0.0 3.0 %collective-permute-start.5 = (bf16[2,256,512]{2,1,0:T(8,128)(2,1)}, bf16[2,256,512]{2,1,0:T(8,128)(2,1)S(1)}, u32[]{:S(2)}, u32[]{:S(2)}) collective-permute-start(bf16[2,256,512]{2,1,0:T(8,128)(2,1)} %refs_4_.1), channel_id=1, source_target_pairs={{0,16},{8,24},{16,0},{24,8},{1,17},{9,25},{17,1},{25,9},{2,18},{10... | collective-permute-start | bytes 1572872 | tf_op jit(solution)/shard_map/ppermute | solution.py:213
  3.0 0.0 copy-start
  3.0 1.1 %copy-done = bf16[1,3,1,8,128,128]{5,4,3,2,1,0:T(8,128)(2,1)S(1)} copy-done((bf16[1,3,1,8,128,128]{5,4,3,2,1,0:T(8,128)(2,1)S(1)}, bf16[1,3,1,8,128,128]{5,4,3,2,1,0:T(8,128)(2,1)}, u32[]{:S(2)}) %copy-start) | copy-done | bytes 786456
  4.1 2.7 %collective-permute-start = (bf16[2,128,128]{2,1,0:T(8,128)(2,1)S(1)}, bf16[2,128,128]{2,1,0:T(8,128)(2,1)S(1)}, u32[]{:S(2)}, u32[]{:S(2)}) collective-permute-start(bf16[2,128,128]{2,1,0:T(8,128)(2,1)S(1)} %get-tuple-element.44), channel_id=1, source_target_pairs={{0,4},{1,5},{2,6},{3,7},{4,0},{5,1},{6,2},{7,3},{8,12},{9,13},{10,... | collective-permute-start | bytes 196616 | tf_op jit(solution)/shard_map/ppermute | solution.py:223
  6.8 1.3 %collective-permute-start.1 = (bf16[2,128,128]{2,1,0:T(8,128)(2,1)S(1)}, bf16[2,128,128]{2,1,0:T(8,128)(2,1)S(1)}, u32[]{:S(2)}, u32[]{:S(2)}) collective-permute-start(bf16[2,128,128]{2,1,0:T(8,128)(2,1)S(1)} %get-tuple-element.45), channel_id=1, source_target_pairs={{0,5},{1,4},{2,7},{3,6},{4,1},{5,0},{6,3},{7,2},{8,13},{9,12},{10,... | collective-permute-start | bytes 196616 | tf_op jit(solution)/shard_map/ppermute | solution.py:223
  8.1 0.0 copy-start.2
  8.1 3.6 %collective-permute-start.2 = (bf16[2,128,128]{2,1,0:T(8,128)(2,1)S(1)}, bf16[2,128,128]{2,1,0:T(8,128)(2,1)S(1)}, u32[]{:S(2)}, u32[]{:S(2)}) collective-permute-start(bf16[2,128,128]{2,1,0:T(8,128)(2,1)S(1)} %get-tuple-element.46), channel_id=1, source_target_pairs={{0,6},{1,7},{2,4},{3,5},{4,2},{5,3},{6,0},{7,1},{8,14},{9,15},{10,... | collective-permute-start | bytes 196616 | tf_op jit(solution)/shard_map/ppermute | solution.py:223
  11.7 0.0 collective-permute-start.4
  11.7 1.4 %copy-done.3 = bf16[1,3,1,4,4,128,128]{6,5,4,3,2,1,0:T(8,128)(2,1)S(1)} copy-done((bf16[1,3,1,4,4,128,128]{6,5,4,3,2,1,0:T(8,128)(2,1)S(1)}, bf16[1,3,1,4,4,128,128]{6,5,4,3,2,1,0:T(8,128)(2,1)}, u32[]{:S(2)}) %copy-start.3) | copy-done | bytes 1572888
  13.1 0.0 copy-start.5
  13.1 1.1 %copy-done.5 = bf16[1,3,1,8,128,128]{5,4,3,2,1,0:T(8,128)(2,1)S(1)} copy-done((bf16[1,3,1,8,128,128]{5,4,3,2,1,0:T(8,128)(2,1)S(1)}, bf16[1,3,1,8,128,128]{5,4,3,2,1,0:T(8,128)(2,1)}, u32[]{:S(2)}) %copy-start.5) | copy-done | bytes 786456
  14.2 0.0 copy-start.6
  14.2 1.1 %copy-done.6 = bf16[1,3,2,512,128]{4,3,2,1,0:T(8,128)(2,1)S(1)} copy-done((bf16[1,3,2,512,128]{4,3,2,1,0:T(8,128)(2,1)S(1)}, bf16[1,3,2,512,128]{4,3,2,1,0:T(8,128)(2,1)}, u32[]{:S(2)}) %copy-start.6) | copy-done | bytes 786456
  15.3 1.0 %copy-done.8 = bf16[1,3,1,2,2,128,128]{6,5,4,3,2,1,0:T(8,128)(2,1)S(1)} copy-done((bf16[1,3,1,2,2,128,128]{6,5,4,3,2,1,0:T(8,128)(2,1)S(1)}, bf16[1,3,1,2,2,128,128]{6,5,4,3,2,1,0:T(8,128)(2,1)}, u32[]{:S(2)}) %copy-start.8) | copy-done | bytes 393240
  16.3 1.4 %weights.1 = (bf16[3,4,128,512]{3,2,1,0:T(8,128)(2,1)S(1)}, bf16[3,4,1,128,512]{4,3,2,1,0:T(8,128)(2,1)S(1)}, bf16[1024,512]{1,0:T(8,128)(2,1)S(1)}, bf16[1024,256]{1,0:T(8,128)(2,1)S(1)}) custom-call(bf16[1,3,1,4,4,128,128]{6,5,4,3,2,1,0:T(8,128)(2,1)S(1)} %copy-done.3, bf16[1,3,1,8,128,128]{5,4,3,2,1,0:T(8,128)(2,1)S(1)} %copy-done.5, ...), custom_call_target="tpu_custom_call" | custom-call | flops 603979776 | bytes 8257536 | tf_op jit(solution)/shard_map/weights/pallas_call | solution.py:228
  17.7 0.0 collective-permute-done.refs_0_
  17.7 0.0 collective-permute-done.1.refs_1_
  17.7 0.0 collective-permute-done.2.refs_2_
  17.8 0.0 collective-permute-done.5.refs_6_
  17.8 0.6 collective-permute-start.6
  18.3 1.5 %collective-permute-start.3 = (bf16[2,128,128]{2,1,0:T(8,128)(2,1)S(1)}, bf16[2,128,128]{2,1,0:T(8,128)(2,1)S(1)}, u32[]{:S(2)}, u32[]{:S(2)}) collective-permute-start(bf16[2,128,128]{2,1,0:T(8,128)(2,1)S(1)} %get-tuple-element.47), channel_id=1, source_target_pairs={{0,7},{1,6},{2,5},{3,4},{4,3},{5,2},{6,1},{7,0},{8,15},{9,14},{10,... | collective-permute-start | bytes 196616 | tf_op jit(solution)/shard_map/ppermute | solution.py:223
  19.9 5.4 %collective-permute-done.3.refs_3_ = bf16[2,128,128]{2,1,0:T(8,128)(2,1)S(1)} collective-permute-done((bf16[2,128,128]{2,1,0:T(8,128)(2,1)S(1)}, bf16[2,128,128]{2,1,0:T(8,128)(2,1)S(1)}, u32[]{:S(2)}, u32[]{:S(2)}) %collective-permute-start.3) | collective-permute-done | bytes 65568 | tf_op jit(solution)/shard_map/ppermute | solution.py:223
  25.3 0.0 collective-permute-done.4.refs_5_
  25.3 0.0 collective-permute-done.6.refs_7_
  25.3 0.0 copy-done.2
  25.3 0.0 copy-done.7
  25.3 1.3 %off_levels.1 = (bf16[2,512,512]{2,1,0:T(8,128)(2,1)S(1)}, bf16[2,1,128,512]{3,2,1,0:T(8,128)(2,1)S(1)}, bf16[2,1,128,512]{3,2,1,0:T(8,128)(2,1)S(1)}, bf16[2,1,...) custom-call(bf16[1,3,4,256,128]{4,3,2,1,0:T(8,128)(2,1)S(1)} %copy-done.2, ...), custom_call_target="tpu_custom_call" | custom-call | flops 805306368 | bytes 6815744 | tf_op jit(solution)/shard_map/off_levels/pallas_call | solution.py:228
  26.6 0.6 collective-permute-start.7
  27.2 0.0 collective-permute-start.8
  27.2 2.9 %collective-permute-start.9 = (bf16[2,1,128,512]{3,2,0,1:T(8,128)(2,1)S(1)}, bf16[2,1,128,512]{3,2,0,1:T(8,128)(2,1)S(1)}, u32[]{:S(2)}, u32[]{:S(2)}) collective-permute-start(bf16[2,1,128,512]{3,2,0,1:T(8,128)(2,1)S(1)} %bitcast.9), channel_id=1, source_target_pairs={{0,3},{1,2},{2,1},{3,0},{4,7},{5,6},{6,5},{7,4},{8,11},{9,10},{10,... | collective-permute-start | bytes 786440 | tf_op jit(solution)/shard_map/ppermute | solution.py:217
  30.2 0.0 collective-permute-start.11
  30.2 10.1 %collective-permute-done.11.refs_0_ = bf16[4,128,128]{2,1,0:T(8,128)(2,1)S(1)} collective-permute-done((bf16[4,128,128]{2,1,0:T(8,128)(2,1)S(1)}, bf16[4,128,128]{2,1,0:T(8,128)(2,1)S(1)}, u32[]{:S(2)}, u32[]{:S(2)}) %collective-permute-start.11) | collective-permute-done | bytes 131104 | tf_op jit(solution)/shard_map/ppermute | solution.py:223
  40.3 0.7 own_levels.1
  41.0 0.0 collective-permute-done.7
  41.0 0.0 collective-permute-done.8
  41.1 2.4 %collective-permute-done.9 = bf16[2,1,128,512]{3,2,0,1:T(8,128)(2,1)S(1)} collective-permute-done((bf16[2,1,128,512]{3,2,0,1:T(8,128)(2,1)S(1)}, bf16[2,1,128,512]{3,2,0,1:T(8,128)(2,1)S(1)}, u32[]{:S(2)}, u32[]{:S(2)}) %collective-permute-start.9) | collective-permute-done | bytes 262176 | tf_op jit(solution)/shard_map/ppermute | solution.py:217
  43.4 0.1 fusion
  43.6 1.3 %collective-permute-start.14 = (bf16[9,128,128]{2,1,0:T(8,128)(2,1)S(1)}, bf16[9,128,128]{2,1,0:T(8,128)(2,1)S(1)}, u32[]{:S(2)}, u32[]{:S(2)}) collective-permute-start(bf16[9,128,128]{2,1,0:T(8,128)(2,1)S(1)} %get-tuple-element.62), channel_id=1, source_target_pairs={{0,3},{1,2},{2,1},{3,0},{4,7},{5,6},{6,5},{7,4},{8,11},{9,10},{10,... | collective-permute-start | bytes 884744 | tf_op jit(solution)/shard_map/ppermute | solution.py:217
  44.8 0.8 collective-permute-start.13
  45.6 1.5 %collective-permute-start.12 = (bf16[9,128,128]{2,1,0:T(8,128)(2,1)S(1)}, bf16[9,128,128]{2,1,0:T(8,128)(2,1)S(1)}, u32[]{:S(2)}, u32[]{:S(2)}) collective-permute-start(bf16[9,128,128]{2,1,0:T(8,128)(2,1)S(1)} %get-tuple-element.58), channel_id=1, source_target_pairs={{0,1},{1,0},{2,3},{3,2},{4,5},{5,4},{6,7},{7,6},{8,9},{9,8},{10,11... | collective-permute-start | bytes 884744 | tf_op jit(solution)/shard_map/ppermute | solution.py:217
  47.1 1.0 %collective-permute-start.10 = (bf16[2,128,512]{2,1,0:T(8,128)(2,1)S(1)}, bf16[2,128,512]{2,1,0:T(8,128)(2,1)S(1)}, u32[]{:S(2)}, u32[]{:S(2)}) collective-permute-start(bf16[2,128,512]{2,1,0:T(8,128)(2,1)S(1)} %fusion), channel_id=1, source_target_pairs={{0,4},{1,5},{2,6},{3,7},{4,0},{5,1},{6,2},{7,3},{8,12},{9,13},{10,... | collective-permute-start | bytes 786440 | tf_op jit(solution)/shard_map/ppermute | solution.py:223
  48.2 13.9 %collective-permute-done.10.refs_0_ = bf16[2,128,512]{2,1,0:T(8,128)(2,1)S(1)} collective-permute-done((bf16[2,128,512]{2,1,0:T(8,128)(2,1)S(1)}, bf16[2,128,512]{2,1,0:T(8,128)(2,1)S(1)}, u32[]{:S(2)}, u32[]{:S(2)}) %collective-permute-start.10) | collective-permute-done | bytes 262176 | tf_op jit(solution)/shard_map/ppermute | solution.py:223
  62.1 0.0 collective-permute-done.14.refs_4_
  62.1 0.8 collective-permute-done.13.refs_3_
  62.9 0.0 collective-permute-done.12.refs_2_
  62.9 0.0 copy-done.1
  62.9 0.0 copy-done.4
  62.9 2.3 %middle_levels.1 = (f32[1024,512]{1,0:T(8,128)S(1)}, bf16[4,128,128]{2,1,0:T(8,128)(2,1)S(1)}, bf16[4,128,128]{2,1,0:T(8,128)(2,1)S(1)}, bf16[4,128,128]{2,1,0:T...) custom-call(bf16[1,3,1,8,128,128]{5,4,3,2,1,0:T(8,128)(2,1)S(1)} %co, ...), custom_call_target="tpu_custom_call" | custom-call | flops 1342177280 | bytes 11927552 | tf_op jit(solution)/shard_map/middle_levels/pallas_call | solution.py:228
  65.2 0.9 %collective-permute-start.15 = (bf16[1,1,128,512]{3,2,1,0:T(8,128)(2,1)S(1)}, bf16[1,1,128,512]{3,2,1,0:T(8,128)(2,1)S(1)}, u32[]{:S(2)}, u32[]{:S(2)}) collective-permute-start(bf16[1,1,128,512]{3,2,1,0:T(8,128)(2,1)S(1)} %get-tuple-element.65), channel_id=1, source_target_pairs={{0,1},{1,0},{2,3},{3,2},{4,5},{5,4},{6,7},{7,6},{8,9},{9,8},{10,11... | collective-permute-start | bytes 393224 | tf_op jit(solution)/shard_map/ppermute | solution.py:217
  66.1 1.3 %collective-permute-start.16 = (bf16[1,1,128,512]{3,2,1,0:T(8,128)(2,1)S(1)}, bf16[1,1,128,512]{3,2,1,0:T(8,128)(2,1)S(1)}, u32[]{:S(2)}, u32[]{:S(2)}) collective-permute-start(bf16[1,1,128,512]{3,2,1,0:T(8,128)(2,1)S(1)} %get-tuple-element.66), channel_id=1, source_target_pairs={{0,2},{1,3},{2,0},{3,1},{4,6},{5,7},{6,4},{7,5},{8,10},{9,11},{10,... | collective-permute-start | bytes 393224 | tf_op jit(solution)/shard_map/ppermute | solution.py:217
  67.4 1.3 %collective-permute-start.17 = (bf16[1,1,128,512]{3,2,1,0:T(8,128)(2,1)S(1)}, bf16[1,1,128,512]{3,2,1,0:T(8,128)(2,1)S(1)}, u32[]{:S(2)}, u32[]{:S(2)}) collective-permute-start(bf16[1,1,128,512]{3,2,1,0:T(8,128)(2,1)S(1)} %get-tuple-element.67), channel_id=1, source_target_pairs={{0,3},{1,2},{2,1},{3,0},{4,7},{5,6},{6,5},{7,4},{8,11},{9,10},{10,... | collective-permute-start | bytes 393224 | tf_op jit(solution)/shard_map/ppermute | solution.py:217
  68.7 1.9 %collective-permute-done.15 = bf16[1,1,128,512]{3,2,1,0:T(8,128)(2,1)S(1)} collective-permute-done((bf16[1,1,128,512]{3,2,1,0:T(8,128)(2,1)S(1)}, bf16[1,1,128,512]{3,2,1,0:T(8,128)(2,1)S(1)}, u32[]{:S(2)}, u32[]{:S(2)}) %collective-permute-start.15) | collective-permute-done | bytes 131104 | tf_op jit(solution)/shard_map/ppermute | solution.py:217
  70.7 0.4 collective-permute-done.16
  71.1 2.5 %collective-permute-done.17 = bf16[1,1,128,512]{3,2,1,0:T(8,128)(2,1)S(1)} collective-permute-done((bf16[1,1,128,512]{3,2,1,0:T(8,128)(2,1)S(1)}, bf16[1,1,128,512]{3,2,1,0:T(8,128)(2,1)S(1)}, u32[]{:S(2)}, u32[]{:S(2)}) %collective-permute-start.17) | collective-permute-done | bytes 131104 | tf_op jit(solution)/shard_map/ppermute | solution.py:217
  73.6 0.1 fusion.1
  73.7 1.7 %collective-permute-start.19 = (bf16[4,128,128]{2,1,0:T(8,128)(2,1)S(1)}, bf16[4,128,128]{2,1,0:T(8,128)(2,1)S(1)}, u32[]{:S(2)}, u32[]{:S(2)}) collective-permute-start(bf16[4,128,128]{2,1,0:T(8,128)(2,1)S(1)} %get-tuple-element.70), channel_id=1, source_target_pairs={{0,1},{1,0},{2,3},{3,2},{4,5},{5,4},{6,7},{7,6},{8,9},{9,8},{10,11... | collective-permute-start | bytes 393224 | tf_op jit(solution)/shard_map/ppermute | solution.py:217
  75.4 0.4 collective-permute-start.20
  75.8 1.4 %collective-permute-start.21 = (bf16[4,128,128]{2,1,0:T(8,128)(2,1)S(1)}, bf16[4,128,128]{2,1,0:T(8,128)(2,1)S(1)}, u32[]{:S(2)}, u32[]{:S(2)}) collective-permute-start(bf16[4,128,128]{2,1,0:T(8,128)(2,1)S(1)} %get-tuple-element.74), channel_id=1, source_target_pairs={{0,3},{1,2},{2,1},{3,0},{4,7},{5,6},{6,5},{7,4},{8,11},{9,10},{10,... | collective-permute-start | bytes 393224 | tf_op jit(solution)/shard_map/ppermute | solution.py:217
  77.2 2.2 %collective-permute-start.18 = (bf16[1,128,512]{2,1,0:T(8,128)(2,1)S(1)}, bf16[1,128,512]{2,1,0:T(8,128)(2,1)S(1)}, u32[]{:S(2)}, u32[]{:S(2)}) collective-permute-start(bf16[1,128,512]{2,1,0:T(8,128)(2,1)S(1)} %fusion.1), channel_id=1, source_target_pairs={{0,4},{1,5},{2,6},{3,7},{4,0},{5,1},{6,2},{7,3},{8,12},{9,13},{10,... | collective-permute-start | bytes 393224 | tf_op jit(solution)/shard_map/ppermute | solution.py:223
  79.4 0.0 collective-permute-done.19.refs_2_
  79.4 0.9 %collective-permute-done.20.refs_3_ = bf16[4,128,128]{2,1,0:T(8,128)(2,1)S(1)} collective-permute-done((bf16[4,128,128]{2,1,0:T(8,128)(2,1)S(1)}, bf16[4,128,128]{2,1,0:T(8,128)(2,1)S(1)}, u32[]{:S(2)}, u32[]{:S(2)}) %collective-permute-start.20) | collective-permute-done | bytes 131104 | tf_op jit(solution)/shard_map/ppermute | solution.py:217
  80.4 1.3 %collective-permute-done.21.refs_4_ = bf16[4,128,128]{2,1,0:T(8,128)(2,1)S(1)} collective-permute-done((bf16[4,128,128]{2,1,0:T(8,128)(2,1)S(1)}, bf16[4,128,128]{2,1,0:T(8,128)(2,1)S(1)}, u32[]{:S(2)}, u32[]{:S(2)}) %collective-permute-start.21) | collective-permute-done | bytes 131104 | tf_op jit(solution)/shard_map/ppermute | solution.py:217
  81.7 1.5 %collective-permute-done.18.refs_0_ = bf16[1,128,512]{2,1,0:T(8,128)(2,1)S(1)} collective-permute-done((bf16[1,128,512]{2,1,0:T(8,128)(2,1)S(1)}, bf16[1,128,512]{2,1,0:T(8,128)(2,1)S(1)}, u32[]{:S(2)}, u32[]{:S(2)}) %collective-permute-start.18) | collective-permute-done | bytes 131104 | tf_op jit(solution)/shard_map/ppermute | solution.py:223
  83.2 1.6 %last_levels.1 = bf16[1,1024,512]{2,1,0:T(8,128)(2,1)} custom-call(bf16[1,3,1,8,128,128]{5,4,3,2,1,0:T(8,128)(2,1)S(1)} %copy-done.1, bf16[1024,256]{1,0:T(8,128)(2,1)S(1)} %get-tuple-element.40.row_mats, f32[1024,512]{1,0:T(8,128)S(1)} %get-tuple-element.63.residual, bf16[1,128,512]{2,1,0:T(8,128)(2,1)S(1)} %collective-permute-done.18.refs_0_, ...), custom_call_target="tpu_custom_call" | custom-call | flops 335544320 | bytes 5111808 | tf_op jit(solution)/shard_map/last_levels/pallas_call | solution.py:228
  (6 shorter events, 0.0 us)
Async XLA Ops:
  0.0 17.8 %collective-permute-start.5 = (bf16[2,256,512]{2,1,0:T(8,128)(2,1)}, bf16[2,256,512]{2,1,0:T(8,128)(2,1)S(1)}, u32[]{:S(2)}, u32[]{:S(2)}) collective-permute-start(bf16[2,256,512]{2,1,0:T(8,128)(2,1)} %refs_4_.1), channel_id=1, source_target_pairs={{0,16},{8,24},{16,0},{24,8},{1,17},{9,25},{17,1},{25,9},{2,18},{10... | collective-permute-start | bytes 1572872 | tf_op jit(solution)/shard_map/ppermute | solution.py:213
  3.0 1.1 %copy-start = (bf16[1,3,1,8,128,128]{5,4,3,2,1,0:T(8,128)(2,1)S(1)}, bf16[1,3,1,8,128,128]{5,4,3,2,1,0:T(8,128)(2,1)}, u32[]{:S(2)}) copy-start(bf16[1,3,1,8,128,128]{5,4,3,2,1,0:T(8,128)(2,1)} %third.5) | copy-start | bytes 2359300
  4.1 13.6 %collective-permute-start = (bf16[2,128,128]{2,1,0:T(8,128)(2,1)S(1)}, bf16[2,128,128]{2,1,0:T(8,128)(2,1)S(1)}, u32[]{:S(2)}, u32[]{:S(2)}) collective-permute-start(bf16[2,128,128]{2,1,0:T(8,128)(2,1)S(1)} %get-tuple-element.44), channel_id=1, source_target_pairs={{0,4},{1,5},{2,6},{3,7},{4,0},{5,1},{6,2},{7,3},{8,12},{9,13},{10,... | collective-permute-start | bytes 196616 | tf_op jit(solution)/shard_map/ppermute | solution.py:223
  6.8 11.0 %collective-permute-start.1 = (bf16[2,128,128]{2,1,0:T(8,128)(2,1)S(1)}, bf16[2,128,128]{2,1,0:T(8,128)(2,1)S(1)}, u32[]{:S(2)}, u32[]{:S(2)}) collective-permute-start(bf16[2,128,128]{2,1,0:T(8,128)(2,1)S(1)} %get-tuple-element.45), channel_id=1, source_target_pairs={{0,5},{1,4},{2,7},{3,6},{4,1},{5,0},{6,3},{7,2},{8,13},{9,12},{10,... | collective-permute-start | bytes 196616 | tf_op jit(solution)/shard_map/ppermute | solution.py:223
  8.1 17.3 %copy-start.2 = (bf16[1,3,4,256,128]{4,3,2,1,0:T(8,128)(2,1)S(1)}, bf16[1,3,4,256,128]{4,3,2,1,0:T(8,128)(2,1)}, u32[]{:S(2)}) copy-start(bf16[1,3,4,256,128]{4,3,2,1,0:T(8,128)(2,1)} %basis.3) | copy-start | bytes 2359300
  8.1 9.7 %collective-permute-start.2 = (bf16[2,128,128]{2,1,0:T(8,128)(2,1)S(1)}, bf16[2,128,128]{2,1,0:T(8,128)(2,1)S(1)}, u32[]{:S(2)}, u32[]{:S(2)}) collective-permute-start(bf16[2,128,128]{2,1,0:T(8,128)(2,1)S(1)} %get-tuple-element.46), channel_id=1, source_target_pairs={{0,6},{1,7},{2,4},{3,5},{4,2},{5,3},{6,0},{7,1},{8,14},{9,15},{10,... | collective-permute-start | bytes 196616 | tf_op jit(solution)/shard_map/ppermute | solution.py:223
  11.7 13.7 %collective-permute-start.4 = (bf16[2,256,512]{2,1,0:T(8,128)(2,1)}, bf16[2,256,512]{2,1,0:T(8,128)(2,1)S(1)}, u32[]{:S(2)}, u32[]{:S(2)}) collective-permute-start(bf16[2,256,512]{2,1,0:T(8,128)(2,1)} %refs_4_.1), channel_id=1, source_target_pairs={{0,8},{8,0},{16,24},{24,16},{1,9},{9,1},{17,25},{25,17},{2,10},{10... | collective-permute-start | bytes 1572872 | tf_op jit(solution)/shard_map/ppermute | solution.py:213
  11.7 1.4 %copy-start.3 = (bf16[1,3,1,4,4,128,128]{6,5,4,3,2,1,0:T(8,128)(2,1)S(1)}, bf16[1,3,1,4,4,128,128]{6,5,4,3,2,1,0:T(8,128)(2,1)}, u32[]{:S(2)}) copy-start(bf16[1,3,1,4,4,128,128]{6,5,4,3,2,1,0:T(8,128)(2,1)} %first.1) | copy-start | bytes 4718596
  13.1 1.1 %copy-start.5 = (bf16[1,3,1,8,128,128]{5,4,3,2,1,0:T(8,128)(2,1)S(1)}, bf16[1,3,1,8,128,128]{5,4,3,2,1,0:T(8,128)(2,1)}, u32[]{:S(2)}) copy-start(bf16[1,3,1,8,128,128]{5,4,3,2,1,0:T(8,128)(2,1)} %second.1) | copy-start | bytes 2359300
  14.2 1.1 %copy-start.6 = (bf16[1,3,2,512,128]{4,3,2,1,0:T(8,128)(2,1)S(1)}, bf16[1,3,2,512,128]{4,3,2,1,0:T(8,128)(2,1)}, u32[]{:S(2)}) copy-start(bf16[1,3,2,512,128]{4,3,2,1,0:T(8,128)(2,1)} %out_basis.1) | copy-start | bytes 2359300
  15.3 1.0 %copy-start.8 = (bf16[1,3,1,2,2,128,128]{6,5,4,3,2,1,0:T(8,128)(2,1)S(1)}, bf16[1,3,1,2,2,128,128]{6,5,4,3,2,1,0:T(8,128)(2,1)}, u32[]{:S(2)}) copy-start(bf16[1,3,1,2,2,128,128]{6,5,4,3,2,1,0:T(8,128)(2,1)} %fourth.1) | copy-start | bytes 1179652
  16.3 9.0 %copy-start.7 = (bf16[2,256,512]{2,1,0:T(8,128)(2,1)S(1)}, bf16[2,256,512]{2,1,0:T(8,128)(2,1)}, u32[]{:S(2)}) copy-start(bf16[2,256,512]{2,1,0:T(8,128)(2,1)} %refs_4_.1) | copy-start | bytes 1572868
  17.8 7.5 %collective-permute-start.6 = (bf16[2,256,512]{2,1,0:T(8,128)(2,1)S(1)}, bf16[2,256,512]{2,1,0:T(8,128)(2,1)S(1)}, u32[]{:S(2)}, u32[]{:S(2)}) collective-permute-start(bf16[2,256,512]{2,1,0:T(8,128)(2,1)S(1)} %collective-permute-done.5.refs_6_), channel_id=1, source_target_pairs={{0,8},{8,0},{16,24},{24,16},{1,9},{9,1},{17,25},{25,17},{2,10},{10... | collective-permute-start | bytes 1572872 | tf_op jit(solution)/shard_map/ppermute | solution.py:213
  18.3 7.0 %collective-permute-start.3 = (bf16[2,128,128]{2,1,0:T(8,128)(2,1)S(1)}, bf16[2,128,128]{2,1,0:T(8,128)(2,1)S(1)}, u32[]{:S(2)}, u32[]{:S(2)}) collective-permute-start(bf16[2,128,128]{2,1,0:T(8,128)(2,1)S(1)} %get-tuple-element.47), channel_id=1, source_target_pairs={{0,7},{1,6},{2,5},{3,4},{4,3},{5,2},{6,1},{7,0},{8,15},{9,14},{10,... | collective-permute-start | bytes 196616 | tf_op jit(solution)/shard_map/ppermute | solution.py:223
  26.6 14.4 %collective-permute-start.7 = (bf16[2,1,128,512]{3,2,0,1:T(8,128)(2,1)S(1)}, bf16[2,1,128,512]{3,2,0,1:T(8,128)(2,1)S(1)}, u32[]{:S(2)}, u32[]{:S(2)}) collective-permute-start(bf16[2,1,128,512]{3,2,0,1:T(8,128)(2,1)S(1)} %bitcast.11), channel_id=1, source_target_pairs={{0,1},{1,0},{2,3},{3,2},{4,5},{5,4},{6,7},{7,6},{8,9},{9,8},{10,11... | collective-permute-start | bytes 786440 | tf_op jit(solution)/shard_map/ppermute | solution.py:217
  27.2 13.8 %collective-permute-start.8 = (bf16[2,1,128,512]{3,2,0,1:T(8,128)(2,1)S(1)}, bf16[2,1,128,512]{3,2,0,1:T(8,128)(2,1)S(1)}, u32[]{:S(2)}, u32[]{:S(2)}) collective-permute-start(bf16[2,1,128,512]{3,2,0,1:T(8,128)(2,1)S(1)} %bitcast.10), channel_id=1, source_target_pairs={{0,2},{1,3},{2,0},{3,1},{4,6},{5,7},{6,4},{7,5},{8,10},{9,11},{10,... | collective-permute-start | bytes 786440 | tf_op jit(solution)/shard_map/ppermute | solution.py:217
  27.2 16.2 %collective-permute-start.9 = (bf16[2,1,128,512]{3,2,0,1:T(8,128)(2,1)S(1)}, bf16[2,1,128,512]{3,2,0,1:T(8,128)(2,1)S(1)}, u32[]{:S(2)}, u32[]{:S(2)}) collective-permute-start(bf16[2,1,128,512]{3,2,0,1:T(8,128)(2,1)S(1)} %bitcast.9), channel_id=1, source_target_pairs={{0,3},{1,2},{2,1},{3,0},{4,7},{5,6},{6,5},{7,4},{8,11},{9,10},{10,... | collective-permute-start | bytes 786440 | tf_op jit(solution)/shard_map/ppermute | solution.py:217
  30.2 10.1 %collective-permute-start.11 = (bf16[4,128,128]{2,1,0:T(8,128)(2,1)S(1)}, bf16[4,128,128]{2,1,0:T(8,128)(2,1)S(1)}, u32[]{:S(2)}, u32[]{:S(2)}) collective-permute-start(bf16[4,128,128]{2,1,0:T(8,128)(2,1)S(1)} %get-tuple-element.55), channel_id=1, source_target_pairs={{0,4},{1,5},{2,6},{3,7},{4,0},{5,1},{6,2},{7,3},{8,12},{9,13},{10,... | collective-permute-start | bytes 393224 | tf_op jit(solution)/shard_map/ppermute | solution.py:223
  40.3 22.6 %copy-start.1 = (bf16[1,3,1,8,128,128]{5,4,3,2,1,0:T(8,128)(2,1)S(1)}, bf16[1,3,1,8,128,128]{5,4,3,2,1,0:T(8,128)(2,1)}, u32[]{:S(2)}) copy-start(bf16[1,3,1,8,128,128]{5,4,3,2,1,0:T(8,128)(2,1)} %third.5) | copy-start | bytes 2359300
  40.3 22.6 %copy-start.4 = (bf16[1,1024,512]{2,1,0:T(8,128)(2,1)S(1)}, bf16[1,1024,512]{2,1,0:T(8,128)(2,1)}, u32[]{:S(2)}) copy-start(bf16[1,1024,512]{2,1,0:T(8,128)(2,1)} %rhs.1) | copy-start | bytes 3145732
  43.6 18.5 %collective-permute-start.14 = (bf16[9,128,128]{2,1,0:T(8,128)(2,1)S(1)}, bf16[9,128,128]{2,1,0:T(8,128)(2,1)S(1)}, u32[]{:S(2)}, u32[]{:S(2)}) collective-permute-start(bf16[9,128,128]{2,1,0:T(8,128)(2,1)S(1)} %get-tuple-element.62), channel_id=1, source_target_pairs={{0,3},{1,2},{2,1},{3,0},{4,7},{5,6},{6,5},{7,4},{8,11},{9,10},{10,... | collective-permute-start | bytes 884744 | tf_op jit(solution)/shard_map/ppermute | solution.py:217
  44.8 18.0 %collective-permute-start.13 = (bf16[9,128,128]{2,1,0:T(8,128)(2,1)S(1)}, bf16[9,128,128]{2,1,0:T(8,128)(2,1)S(1)}, u32[]{:S(2)}, u32[]{:S(2)}) collective-permute-start(bf16[9,128,128]{2,1,0:T(8,128)(2,1)S(1)} %get-tuple-element.60), channel_id=1, source_target_pairs={{0,2},{1,3},{2,0},{3,1},{4,6},{5,7},{6,4},{7,5},{8,10},{9,11},{10,... | collective-permute-start | bytes 884744 | tf_op jit(solution)/shard_map/ppermute | solution.py:217
  45.6 17.2 %collective-permute-start.12 = (bf16[9,128,128]{2,1,0:T(8,128)(2,1)S(1)}, bf16[9,128,128]{2,1,0:T(8,128)(2,1)S(1)}, u32[]{:S(2)}, u32[]{:S(2)}) collective-permute-start(bf16[9,128,128]{2,1,0:T(8,128)(2,1)S(1)} %get-tuple-element.58), channel_id=1, source_target_pairs={{0,1},{1,0},{2,3},{3,2},{4,5},{5,4},{6,7},{7,6},{8,9},{9,8},{10,11... | collective-permute-start | bytes 884744 | tf_op jit(solution)/shard_map/ppermute | solution.py:217
  47.1 15.0 %collective-permute-start.10 = (bf16[2,128,512]{2,1,0:T(8,128)(2,1)S(1)}, bf16[2,128,512]{2,1,0:T(8,128)(2,1)S(1)}, u32[]{:S(2)}, u32[]{:S(2)}) collective-permute-start(bf16[2,128,512]{2,1,0:T(8,128)(2,1)S(1)} %fusion), channel_id=1, source_target_pairs={{0,4},{1,5},{2,6},{3,7},{4,0},{5,1},{6,2},{7,3},{8,12},{9,13},{10,... | collective-permute-start | bytes 786440 | tf_op jit(solution)/shard_map/ppermute | solution.py:223
  65.2 5.5 %collective-permute-start.15 = (bf16[1,1,128,512]{3,2,1,0:T(8,128)(2,1)S(1)}, bf16[1,1,128,512]{3,2,1,0:T(8,128)(2,1)S(1)}, u32[]{:S(2)}, u32[]{:S(2)}) collective-permute-start(bf16[1,1,128,512]{3,2,1,0:T(8,128)(2,1)S(1)} %get-tuple-element.65), channel_id=1, source_target_pairs={{0,1},{1,0},{2,3},{3,2},{4,5},{5,4},{6,7},{7,6},{8,9},{9,8},{10,11... | collective-permute-start | bytes 393224 | tf_op jit(solution)/shard_map/ppermute | solution.py:217
  66.1 5.0 %collective-permute-start.16 = (bf16[1,1,128,512]{3,2,1,0:T(8,128)(2,1)S(1)}, bf16[1,1,128,512]{3,2,1,0:T(8,128)(2,1)S(1)}, u32[]{:S(2)}, u32[]{:S(2)}) collective-permute-start(bf16[1,1,128,512]{3,2,1,0:T(8,128)(2,1)S(1)} %get-tuple-element.66), channel_id=1, source_target_pairs={{0,2},{1,3},{2,0},{3,1},{4,6},{5,7},{6,4},{7,5},{8,10},{9,11},{10,... | collective-permute-start | bytes 393224 | tf_op jit(solution)/shard_map/ppermute | solution.py:217
  67.4 6.2 %collective-permute-start.17 = (bf16[1,1,128,512]{3,2,1,0:T(8,128)(2,1)S(1)}, bf16[1,1,128,512]{3,2,1,0:T(8,128)(2,1)S(1)}, u32[]{:S(2)}, u32[]{:S(2)}) collective-permute-start(bf16[1,1,128,512]{3,2,1,0:T(8,128)(2,1)S(1)} %get-tuple-element.67), channel_id=1, source_target_pairs={{0,3},{1,2},{2,1},{3,0},{4,7},{5,6},{6,5},{7,4},{8,11},{9,10},{10,... | collective-permute-start | bytes 393224 | tf_op jit(solution)/shard_map/ppermute | solution.py:217
  73.7 5.8 %collective-permute-start.19 = (bf16[4,128,128]{2,1,0:T(8,128)(2,1)S(1)}, bf16[4,128,128]{2,1,0:T(8,128)(2,1)S(1)}, u32[]{:S(2)}, u32[]{:S(2)}) collective-permute-start(bf16[4,128,128]{2,1,0:T(8,128)(2,1)S(1)} %get-tuple-element.70), channel_id=1, source_target_pairs={{0,1},{1,0},{2,3},{3,2},{4,5},{5,4},{6,7},{7,6},{8,9},{9,8},{10,11... | collective-permute-start | bytes 393224 | tf_op jit(solution)/shard_map/ppermute | solution.py:217
  75.4 5.0 %collective-permute-start.20 = (bf16[4,128,128]{2,1,0:T(8,128)(2,1)S(1)}, bf16[4,128,128]{2,1,0:T(8,128)(2,1)S(1)}, u32[]{:S(2)}, u32[]{:S(2)}) collective-permute-start(bf16[4,128,128]{2,1,0:T(8,128)(2,1)S(1)} %get-tuple-element.72), channel_id=1, source_target_pairs={{0,2},{1,3},{2,0},{3,1},{4,6},{5,7},{6,4},{7,5},{8,10},{9,11},{10,... | collective-permute-start | bytes 393224 | tf_op jit(solution)/shard_map/ppermute | solution.py:217
  75.8 5.9 %collective-permute-start.21 = (bf16[4,128,128]{2,1,0:T(8,128)(2,1)S(1)}, bf16[4,128,128]{2,1,0:T(8,128)(2,1)S(1)}, u32[]{:S(2)}, u32[]{:S(2)}) collective-permute-start(bf16[4,128,128]{2,1,0:T(8,128)(2,1)S(1)} %get-tuple-element.74), channel_id=1, source_target_pairs={{0,3},{1,2},{2,1},{3,0},{4,7},{5,6},{6,5},{7,4},{8,11},{9,10},{10,... | collective-permute-start | bytes 393224 | tf_op jit(solution)/shard_map/ppermute | solution.py:217
  77.2 6.0 %collective-permute-start.18 = (bf16[1,128,512]{2,1,0:T(8,128)(2,1)S(1)}, bf16[1,128,512]{2,1,0:T(8,128)(2,1)S(1)}, u32[]{:S(2)}, u32[]{:S(2)}) collective-permute-start(bf16[1,128,512]{2,1,0:T(8,128)(2,1)S(1)} %fusion.1), channel_id=1, source_target_pairs={{0,4},{1,5},{2,6},{3,7},{4,0},{5,1},{6,2},{7,3},{8,12},{9,13},{10,... | collective-permute-start | bytes 393224 | tf_op jit(solution)/shard_map/ppermute | solution.py:223

commit v3 on v2

--- a/solution.py
+++ b/solution.py
@@ -10,7 +10,7 @@
 F32 = jnp.float32
 BF16 = jnp.bfloat16
 MIB = 1024 * 1024
-CHUNKS = 1
+MASKS = (1, 2)
 VMEM = pl.BlockSpec(memory_space=pltpu.VMEM)
 
 
@@ -94,29 +94,23 @@
     return jnp.concatenate(mats, axis=0)
 
 
-def put_other(mats, leaf, other, at):
-    coef = dot(mats, leaf).astype(BF16)
-    for i, ref in enumerate(other):
-        less, rank, width = ref.shape[1:]
-        ref[at] = coef[i * less * rank : (i + 1) * less * rank].reshape(less, rank, width)
-
-
-def put_own(mats, leaf, own, at):
-    radix, rank, depth = mats.shape
-    coef = dot(mats[...].reshape(radix * rank, depth), leaf).astype(BF16)
+def put_own(mats, members, leaf, own, at):
+    rank = mats.shape[1]
+    coef = dot(jnp.concatenate([mats[i] for i in members], axis=0), leaf).astype(BF16)
     tiles = leaf.shape[1] // rank
     for i, ref in enumerate(own):
         for c in range(tiles):
             ref[at * tiles + c] = coef[i * rank : (i + 1) * rank, c * rank : (c + 1) * rank]
 
 
-def off_kernel(radix, groups, pieces, span, basis, up_other, *refs):
-    thirds, parts, (leaf_ref,), other = take(refs, (groups - 1) * radix, pieces, 1, radix)
+def off_kernel(radix, groups, pieces, basis, up_other, *refs):
+    thirds, parts, (leaf_ref,), outs = take(refs, (groups - 1) * radix, pieces, 1, 3 * len(MASKS))
     row = lax.axis_index("row")
-    leaves, leaf_rows = basis.shape[2], basis.shape[3]
+    leaves, leaf_rows, rank = basis.shape[2], basis.shape[3], basis.shape[4]
     rows = parts[0].shape[1]
     per_leaf = leaf_rows // rows
     order = leaf_order(row, leaves, pieces)
+    less = groups - 1
     for j in range(parts[0].shape[0]):
         leaf = []
         for t in range(leaves):
@@ -127,26 +121,48 @@
                     mat = basis[0, j, order[t]]
                 else:
                     mat = basis[0, j, order[t], pl.ds(pl.multiple_of(start, rows), rows)]
-                ref = parts[t * per_leaf + u]
-                data = ref[j, :, span] if ref.shape[2] > span.stop - span.start else ref[j]
-                part = dot_t(mat, data)
+                part = dot_t(mat, parts[t * per_leaf + u][j])
                 total = part if total is None else total + part
             leaf.append(total.astype(BF16))
         leaf = jnp.concatenate(leaf, axis=0)
         leaf_ref[j] = leaf
         mats = other_mats(j, lambda i, d: thirds[d * radix + i][j], up_other)
-        put_other(mats, leaf, other, j)
-
-
-def own_kernel(radix, leaf, up_own, *refs):
-    rides, own = take(refs, len(refs) - radix, radix)
-    _, member = place(radix)
-    offs = leaf.shape[0]
+        coef = dot(mats, leaf).astype(BF16)
+        width = coef.shape[1] // len(MASKS)
+        for c, mask in enumerate(MASKS):
+            blocks = [
+                coef[i * less * rank : (i + 1) * less * rank, c * width : (c + 1) * width].reshape(less, rank, width)
+                for i in range(radix)
+            ]
+            outs[3 * c][j] = blocks[0]
+            outs[3 * c + 1][j] = blocks[3 - mask]
+            outs[3 * c + 2][j, 0] = blocks[mask]
+            outs[3 * c + 2][j, 1] = blocks[3]
+
+
+def own_kernel(members, leaf, up_own, *refs):
+    rides, own = take(refs, len(refs) - len(members), len(members))
+    _, member = place(up_own.shape[1])
+    for j in range(leaf.shape[0]):
+        put_own(up_own.at[j], members, leaf[j], own, j)
+    for d, ride in enumerate(rides):
+        for i, ref in zip(members, own):
+            ref[ref.shape[0] - len(rides) + d] = ride[jnp.bitwise_xor(member, i)]
+
+
+def stage_kernel(keep, got, out):
+    out[...] = (keep[...].astype(F32) + got[:, 1].astype(F32)).astype(BF16)
+
+
+def total_kernel(*refs):
+    halves, outs = refs[: 3 * len(MASKS)], refs[3 * len(MASKS) :]
+    offs, less, rank, width = halves[0].shape
     for j in range(offs):
-        put_own(up_own.at[j], leaf[j], own, j)
-    for d, ride in enumerate(rides):
-        for i, ref in enumerate(own):
-            ref[ref.shape[0] - len(rides) + d] = ride[jnp.bitwise_xor(member, i)]
+        for d in range(less):
+            for c in range(len(MASKS)):
+                keep, got, last = halves[3 * c : 3 * c + 3]
+                total = keep[j, d].astype(F32) + got[j, 0, d].astype(F32) + last[j, d].astype(F32)
+                outs[d][j, :, c * width : (c + 1) * width] = total.astype(BF16)
 
 
 def group_coefs(j, at, tiles, own, crossed, third, radix):
@@ -157,17 +173,18 @@
     return [total.astype(BF16)] + [ref[at] for ref in crossed]
 
 
-def middle_kernel(radix, groups, offs, span, first_chunk, third, rhs, basis, row_mats, up_own, up_other, *refs):
-    crossed, own_in, mats_in, (residual_ref,), own, other, mats_out = take(
-        refs, groups - 1, radix, 0 if first_chunk else 1, 1, radix, radix, 1 if first_chunk else 0
-    )
+def middle_kernel(radix, groups, offs, third, rhs, basis, row_mats, up_own, up_other, *refs):
+    less = groups - 1
+    crossed, own_in, rides, (residual_ref,), own, other = take(refs, less, radix, less, 1, radix, radix)
     rank = basis.shape[4]
-    tiles = (span.stop - span.start) // rank
-    if first_chunk:
-        mats = other_mats(offs, lambda i, d: own_in[i][offs * tiles + d], up_other)
-        mats_out[0][...] = mats
-    else:
-        mats = mats_in[0][...]
+    tiles = rhs.shape[2] // rank
+    _, member = place(radix)
+
+    def third_of(i, d):
+        if i == 0:
+            return rides[d][member]
+        return own_in[i][offs * tiles + d]
+
     coefs = []
     for j in range(offs):
         coefs += group_coefs(j, j, tiles, own_in, crossed, third, radix)
@@ -176,12 +193,14 @@
     leaf = []
     for k in range(leaves):
         rows = slice(k * leaf_rows, (k + 1) * leaf_rows)
-        residual = rhs[0, rows, span].astype(F32) - dot(row_mats[rows], coefs)
+        residual = rhs[0, rows].astype(F32) - dot(row_mats[rows], coefs)
         residual_ref[rows] = residual
         leaf.append(dot_t(basis[0, offs, k], residual.astype(BF16)).astype(BF16))
     leaf = jnp.concatenate(leaf, axis=0)
-    put_other(mats, leaf, other, 0)
-    put_own(up_own.at[offs], leaf, own, 0)
+    coef = dot(other_mats(offs, third_of, up_other), leaf).astype(BF16)
+    for i, ref in enumerate(other):
+        ref[0] = coef[i * less * rank : (i + 1) * less * rank].reshape(ref.shape[1:])
+    put_own(up_own.at[offs], range(radix), leaf, own, 0)
 
 
 def last_kernel(radix, groups, offs, third, row_mats, residual, *refs):
@@ -203,11 +222,12 @@
     less = groups - 1
     butterflies = leaf_basis.shape[1]
     offs = solved.shape[0]
-    width = solved.shape[2] // CHUNKS
+    columns = solved.shape[2]
+    width = columns // len(MASKS)
     rank = leaf_basis.shape[4]
     rows = rhs.shape[1]
     depth = radix * rank
-    tiles = width // rank
+    tiles = columns // rank
 
     def over_row(array, mask):
         return lax.ppermute(array, "row", [(r, r ^ mask) for r in range(row_size)])
@@ -261,93 +281,85 @@
         out_basis,
     )
 
-    beside = over_row(solved, 1)
-    chunks, rides = [], None
-    for c in range(CHUNKS):
-        span = slice(c * width, (c + 1) * width)
-        pieces = {0: solved, 1: beside}
-        part = solved if CHUNKS == 1 else solved[:, :, span]
-        for mask in range(2, row_size, 2):
-            pieces[mask] = over_row(part, mask)
-            if rides is None:
-                pieces[mask] = after(pieces[mask], up_own, *thirds[: radix - 1])
-                rides = [
-                    over_groups(after(a, pieces[mask]), d + 1) for d, a in enumerate(picked[less * radix :])
-                ]
-            pieces[mask + 1] = over_row(pieces[mask], 1)
-        chunks.append((span, [pieces[mask] for mask in range(row_size)]))
-
-    def other_out(count):
-        return [((count, less, rank, width), BF16)] * radix
-
-    def own_out(count):
-        return [((count, rank, rank), BF16)] * radix
-
-    def add(other):
-        other = [over_members(a, i) for i, a in enumerate(other)]
-        return [sum(a[:, d].astype(F32) for a in other).astype(BF16) for d in range(less)]
-
-    def send(own, sums):
-        crossed = [over_groups(a, groups - 1 - d) for d, a in enumerate(sums)]
-        return crossed + [over_members(after(a, *sums) if i else a, i) for i, a in enumerate(own)]
-
-    other_flops = 2 * width * rank * radix * less * depth
-    own_flops = 2 * width * rank * radix * depth
-    leaf_flops = 2 * width * rank * rows
-    row_flops = 2 * width * rank * (depth + groups * rows)
-    done, mats = [], []
-    for c, (span, pieces) in enumerate(chunks):
-        leaf, *other = call(
-            functools.partial(off_kernel, radix, groups, row_size, span),
-            "off_levels",
-            offs * (leaf_flops + other_flops),
-            [((offs, depth, width), BF16)] + other_out(offs),
-            leaf_basis,
-            up_other,
-            *thirds,
-            *pieces,
-        )
-        own = call(
-            functools.partial(own_kernel, radix),
-            "own_levels",
-            offs * own_flops,
-            own_out(offs * tiles + (less if c == 0 else 0)),
-            leaf,
-            up_own,
-            *(rides if c == 0 else []),
-        )
-        received = send(own, add(other))
-        residual, *levels = call(
-            functools.partial(middle_kernel, radix, groups, offs, span, c == 0),
-            "middle_levels",
-            offs * row_flops + leaf_flops + other_flops + own_flops,
-            [((rows, width), F32)]
-            + own_out(tiles)
-            + other_out(1)
-            + ([((radix * less * rank, depth), BF16)] if c == 0 else []),
-            third_level,
-            rhs,
-            leaf_basis,
-            off_rows,
-            up_own,
-            up_other,
-            *received,
-            *mats,
-        )
-        if c == 0:
-            mats = [levels.pop()]
-        received = send(levels[:radix], add(levels[radix:]))
-        done += call(
-            functools.partial(last_kernel, radix, groups, offs),
-            "last_levels",
-            row_flops,
-            [((1, rows, width), BF16)],
-            third_level,
-            last_rows,
-            residual,
-            *received,
-        )
-    return done[0] if CHUNKS == 1 else jnp.concatenate(done, axis=2)
+    shifts = [(delta, i) for delta in range(1, groups) for i in range(radix)]
+    thirds = [over_groups(a, *shift) for a, shift in zip(picked, shifts)]
+    pieces = {0: solved, 1: over_row(after(solved, thirds[0]), 1)}
+    for mask in range(2, row_size, 2):
+        pieces[mask] = after(over_row(solved, mask), up_own, *thirds)
+        pieces[mask + 1] = over_row(pieces[mask], 1)
+    rides = [over_groups(after(a, pieces[2]), d + 1) for d, a in enumerate(picked[less * radix :])]
+    pieces = [pieces[mask] for mask in range(row_size)]
+
+    ride_shape = ((offs * tiles + less, rank, rank), BF16)
+    part = (offs, less, rank, width)
+    other_flops = 2 * columns * rank * radix * less * depth
+    own_flops = 2 * columns * rank * radix * depth
+    leaf_flops = 2 * columns * rank * rows
+    row_flops = 2 * columns * rank * (depth + groups * rows)
+
+    leaf, *others = call(
+        functools.partial(off_kernel, radix, groups, row_size),
+        "off_levels",
+        offs * (leaf_flops + other_flops),
+        [((offs, depth, columns), BF16)]
+        + [(part, BF16), (part, BF16), ((offs, 2, less, rank, width), BF16)] * len(MASKS),
+        leaf_basis,
+        up_other,
+        *thirds,
+        *pieces,
+    )
+    halves = []
+    for c, mask in enumerate(MASKS):
+        keep, wait, sent = others[3 * c : 3 * c + 3]
+        got = over_members(sent, mask)
+        (staged,) = call(stage_kernel, "stage", 0, [(part, BF16)], wait, after(got, *rides) if c else got)
+        halves += [keep, got, over_members(staged, 3 - mask)]
+    sums = call(total_kernel, "total", 0, [((offs, rank, columns), BF16)] * less, *halves)
+    crossed = [over_groups(a, groups - 1 - d) for d, a in enumerate(sums)]
+    own = call(
+        functools.partial(own_kernel, range(radix)),
+        "own_levels",
+        offs * own_flops,
+        [ride_shape] * radix,
+        after(leaf, *sums),
+        up_own,
+        *rides,
+    )
+    own = [over_members(a, i) for i, a in enumerate(own)]
+
+    residual, *levels = call(
+        functools.partial(middle_kernel, radix, groups, offs),
+        "middle_levels",
+        offs * row_flops + leaf_flops + other_flops + own_flops,
+        [((rows, columns), F32)]
+        + [((tiles, rank, rank), BF16)] * radix
+        + [((1, less, rank, columns), BF16)] * radix,
+        third_level,
+        rhs,
+        leaf_basis,
+        off_rows,
+        up_own,
+        up_other,
+        *crossed,
+        *own,
+        *rides,
+    )
+    own, other = levels[:radix], levels[radix:]
+    other = [over_members(a, i) for i, a in enumerate(other)]
+    sums = [sum(a[:, d].astype(F32) for a in other).astype(BF16) for d in range(less)]
+    crossed = [over_groups(a, groups - 1 - d) for d, a in enumerate(sums)]
+    own = [over_members(after(a, *sums) if i else a, i) for i, a in enumerate(own)]
+    return call(
+        functools.partial(last_kernel, radix, groups, offs),
+        "last_levels",
+        row_flops,
+        [((1, rows, columns), BF16)],
+        third_level,
+        last_rows,
+        residual,
+        *crossed,
+        *own,
+    )[0]
 
 
 def solution(mesh):

time: 85.1 us -> 85.5 us (level)
  starting transfers between devices: 30 us -> 32.8 us
  waiting for transfers between devices: 41.3 us -> 38.8 us
    ppermute x7, waiting for transfers between devices: 31 us -> 17 us  [over_groups(): return lax.ppermute(array, 'box', pairs)]
    ppermute x12 -> x13, waiting for transfers between devices: 10.3 us -> 19.8 us  [over_members(): return array if mask == 0 else lax.ppermute(array, 'box', pairs)]
    ppermute x7, starting transfers between devices: 12.3 us -> 14.5 us  [over_groups(): return lax.ppermute(array, 'box', pairs)]
    ppermute x3, waiting for transfers between devices: 0.01 us -> 1.98 us  [over_row(): return lax.ppermute(array, 'row', [(r, r ^ mask) for r in range(row_size)])]
    ppermute x12 -> x13, starting transfers between devices: 14.2 us -> 15.3 us  [over_members(): return array if mask == 0 else lax.ppermute(array, 'box', pairs)]
    pallas_call x6 -> x9, Pallas kernels: 7.34 us -> 7.52 us  [call(): pl.pallas_call(kernel, out_shape=outs, in_specs=[VMEM] * len(args), out_s...]
  transfers between devices with their start and end apart: 22 -> 23, of which waited for: 11 -> 15; matrix products, arithmetic and copies ran while one was open for 0% -> 0% of each run, Pallas kernels for 3% -> 2%
where the time goes in v3:
time: 85.5 us; the launch traced here: 85.2 us
  waiting for transfers between devices  38.8 us (45%)
  starting transfers between devices  32.8 us (38%)
  Pallas kernels  7.52 us (9%)
  local copies, waits for them, and re-layouts  5.86 us (7%)
    ppermute x13, waiting for transfers between devices, over_members(): return array if mask == 0 else lax.ppermute(array, 'box', pairs)  19.8 us
    ppermute x7, waiting for transfers between devices, over_groups(): return lax.ppermute(array, 'box', pairs)  17 us
    ppermute x13, starting transfers between devices, over_members(): return array if mask == 0 else lax.ppermute(array, 'box', pairs)  15.3 us
    ppermute x7, starting transfers between devices, over_groups(): return lax.ppermute(array, 'box', pairs)  14.5 us
    pallas_call x9, Pallas kernels, call(): pl.pallas_call(kernel, out_shape=outs, in_specs=[VMEM] * len(args), out_s...  7.52 us
    unnamed x18, local copies, waits for them, and re-layouts  5.86 us
    ppermute x3, starting transfers between devices, over_row(): return lax.ppermute(array, 'row', [(r, r ^ mask) for r in range(row_size)])  3.04 us
    ppermute x3, waiting for transfers between devices, over_row(): return lax.ppermute(array, 'row', [(r, r ^ mask) for r in range(row_size)])  1.98 us
  transfers between devices with their start and end apart: 23, of which 15 were waited for; matrix products, arithmetic and copies ran while one was open for 0% of the time, Pallas kernels for 2%

profile of v3, /device:TPU:0, one launch (start us, length us, event | category | flops | bytes accessed | tf_op | source)
XLA Modules:
  0.0 85.2 jit_solution(5399113320399267482)
XLA Ops:
  0.0 3.0 %collective-permute-start.5 = (bf16[2,256,512]{2,1,0:T(8,128)(2,1)}, bf16[2,256,512]{2,1,0:T(8,128)(2,1)S(1)}, u32[]{:S(2)}, u32[]{:S(2)}) collective-permute-start(bf16[2,256,512]{2,1,0:T(8,128)(2,1)} %refs_4_.1), channel_id=1, source_target_pairs={{0,16},{8,24},{16,0},{24,8},{1,17},{9,25},{17,1},{25,9},{2,18},{10... | collective-permute-start | bytes 1572872 | tf_op jit(solution)/shard_map/ppermute | solution.py:233
  3.0 1.1 %copy-done = bf16[1,3,1,8,128,128]{5,4,3,2,1,0:T(8,128)(2,1)S(1)} copy-done((bf16[1,3,1,8,128,128]{5,4,3,2,1,0:T(8,128)(2,1)S(1)}, bf16[1,3,1,8,128,128]{5,4,3,2,1,0:T(8,128)(2,1)}, u32[]{:S(2)}) %copy-start) | copy-done | bytes 786456
  4.1 2.7 %collective-permute-start = (bf16[2,128,128]{2,1,0:T(8,128)(2,1)S(1)}, bf16[2,128,128]{2,1,0:T(8,128)(2,1)S(1)}, u32[]{:S(2)}, u32[]{:S(2)}) collective-permute-start(bf16[2,128,128]{2,1,0:T(8,128)(2,1)S(1)} %get-tuple-element.46), channel_id=1, source_target_pairs={{0,4},{1,5},{2,6},{3,7},{4,0},{5,1},{6,2},{7,3},{8,12},{9,13},{10,... | collective-permute-start | bytes 196616 | tf_op jit(solution)/shard_map/ppermute | solution.py:243
  6.8 1.3 %collective-permute-start.1 = (bf16[2,128,128]{2,1,0:T(8,128)(2,1)S(1)}, bf16[2,128,128]{2,1,0:T(8,128)(2,1)S(1)}, u32[]{:S(2)}, u32[]{:S(2)}) collective-permute-start(bf16[2,128,128]{2,1,0:T(8,128)(2,1)S(1)} %get-tuple-element.47), channel_id=1, source_target_pairs={{0,5},{1,4},{2,7},{3,6},{4,1},{5,0},{6,3},{7,2},{8,13},{9,12},{10,... | collective-permute-start | bytes 196616 | tf_op jit(solution)/shard_map/ppermute | solution.py:243
  8.1 3.6 %collective-permute-start.2 = (bf16[2,128,128]{2,1,0:T(8,128)(2,1)S(1)}, bf16[2,128,128]{2,1,0:T(8,128)(2,1)S(1)}, u32[]{:S(2)}, u32[]{:S(2)}) collective-permute-start(bf16[2,128,128]{2,1,0:T(8,128)(2,1)S(1)} %get-tuple-element.48), channel_id=1, source_target_pairs={{0,6},{1,7},{2,4},{3,5},{4,2},{5,3},{6,0},{7,1},{8,14},{9,15},{10,... | collective-permute-start | bytes 196616 | tf_op jit(solution)/shard_map/ppermute | solution.py:243
  11.7 0.2 collective-permute-start.3
  11.9 1.4 %copy-done.3 = bf16[1,3,1,4,4,128,128]{6,5,4,3,2,1,0:T(8,128)(2,1)S(1)} copy-done((bf16[1,3,1,4,4,128,128]{6,5,4,3,2,1,0:T(8,128)(2,1)S(1)}, bf16[1,3,1,4,4,128,128]{6,5,4,3,2,1,0:T(8,128)(2,1)}, u32[]{:S(2)}) %copy-start.3) | copy-done | bytes 1572888
  13.3 1.1 %copy-done.5 = bf16[1,3,1,8,128,128]{5,4,3,2,1,0:T(8,128)(2,1)S(1)} copy-done((bf16[1,3,1,8,128,128]{5,4,3,2,1,0:T(8,128)(2,1)S(1)}, bf16[1,3,1,8,128,128]{5,4,3,2,1,0:T(8,128)(2,1)}, u32[]{:S(2)}) %copy-start.5) | copy-done | bytes 786456
  14.4 1.1 %copy-done.6 = bf16[1,3,2,512,128]{4,3,2,1,0:T(8,128)(2,1)S(1)} copy-done((bf16[1,3,2,512,128]{4,3,2,1,0:T(8,128)(2,1)S(1)}, bf16[1,3,2,512,128]{4,3,2,1,0:T(8,128)(2,1)}, u32[]{:S(2)}) %copy-start.6) | copy-done | bytes 786456
  15.6 1.0 %copy-done.8 = bf16[1,3,1,2,2,128,128]{6,5,4,3,2,1,0:T(8,128)(2,1)S(1)} copy-done((bf16[1,3,1,2,2,128,128]{6,5,4,3,2,1,0:T(8,128)(2,1)S(1)}, bf16[1,3,1,2,2,128,128]{6,5,4,3,2,1,0:T(8,128)(2,1)}, u32[]{:S(2)}) %copy-start.8) | copy-done | bytes 393240
  16.6 1.4 %weights.1 = (bf16[3,4,128,512]{3,2,1,0:T(8,128)(2,1)S(1)}, bf16[3,4,1,128,512]{4,3,2,1,0:T(8,128)(2,1)S(1)}, bf16[1024,512]{1,0:T(8,128)(2,1)S(1)}, bf16[1024,256]{1,0:T(8,128)(2,1)S(1)}) custom-call(bf16[1,3,1,4,4,128,128]{6,5,4,3,2,1,0:T(8,128)(2,1)S(1)} %copy-done.3, bf16[1,3,1,8,128,128]{5,4,3,2,1,0:T(8,128)(2,1)S(1)} %copy-done.5, ...), custom_call_target="tpu_custom_call" | custom-call | flops 603979776 | bytes 8257536 | tf_op jit(solution)/shard_map/weights/pallas_call | solution.py:248
  18.0 0.0 collective-permute-done.refs_0_
  18.0 0.0 copy-done.7
  18.0 0.1 collective-permute-start.4
  18.1 0.0 collective-permute-done.1.refs_1_
  18.1 0.0 collective-permute-done.2.refs_2_
  18.1 0.6 collective-permute-done.3.refs_3_
  18.7 0.0 collective-permute-done.5.refs_6_
  18.7 0.0 collective-permute-start.6
  18.7 1.2 %collective-permute-done.4.refs_5_ = bf16[2,256,512]{2,1,0:T(8,128)(2,1)S(1)} collective-permute-done((bf16[2,256,512]{2,1,0:T(8,128)(2,1)S(1)}, bf16[2,256,512]{2,1,0:T(8,128)(2,1)S(1)}, u32[]{:S(2)}, u32[]{:S(2)}) %collective-permute-start.4) | collective-permute-done | bytes 524320 | tf_op jit(solution)/shard_map/ppermute | solution.py:233
  20.0 0.7 collective-permute-done.6.refs_7_
  20.7 0.0 copy-done.2
  20.7 1.3 %off_levels.1 = (bf16[2,512,512]{2,1,0:T(8,128)(2,1)S(1)}, bf16[2,1,128,256]{3,2,1,0:T(8,128)(2,1)S(1)}, bf16[2,1,128,256]{3,2,1,0:T(8,128)(2,1)S(1)}, bf16[2,2,...) custom-call(bf16[1,3,4,256,128]{4,3,2,1,0:T(8,128)(2,1)S(1)} %copy-d, ...), custom_call_target="tpu_custom_call" | custom-call | flops 805306368 | bytes 6815744 | tf_op jit(solution)/shard_map/off_levels/pallas_call | solution.py:248
  22.0 1.5 %collective-permute-start.7 = (bf16[2,2,1,128,256]{4,3,2,1,0:T(8,128)(2,1)S(1)}, bf16[2,2,1,128,256]{4,3,2,1,0:T(8,128)(2,1)S(1)}, u32[]{:S(2)}, u32[]{:S(2)}) collective-permute-start(bf16[2,2,1,128,256]{4,3,2,1,0:T(8,128)(2,1)S(1)} %get-tuple-element.53), channel_id=1, source_target_pairs={{0,1},{1,0},{2,3},{3,2},{4,5},{5,4},{6,7},{7,6},{8,9},{9,8},{10,11... | collective-permute-start | bytes 786440 | tf_op jit(solution)/shard_map/ppermute | solution.py:237
  23.5 0.7 collective-permute-start.9
  24.2 3.5 %collective-permute-start.10 = (bf16[4,128,128]{2,1,0:T(8,128)(2,1)S(1)}, bf16[4,128,128]{2,1,0:T(8,128)(2,1)S(1)}, u32[]{:S(2)}, u32[]{:S(2)}) collective-permute-start(bf16[4,128,128]{2,1,0:T(8,128)(2,1)S(1)} %get-tuple-element.59), channel_id=1, source_target_pairs={{0,4},{1,5},{2,6},{3,7},{4,0},{5,1},{6,2},{7,3},{8,12},{9,13},{10,... | collective-permute-start | bytes 393224 | tf_op jit(solution)/shard_map/ppermute | solution.py:243
  27.7 2.7 %collective-permute-done.7.got.refs_1_ = bf16[2,2,1,128,256]{4,3,2,1,0:T(8,128)(2,1)S(1)} collective-permute-done((bf16[2,2,1,128,256]{4,3,2,1,0:T(8,128)(2,1)S(1)}, bf16[2,2,1,128,256]{4,3,2,1,0:T(8,128)(2,1)S(1)}, u32[]{:S(2)}, u32[]{:S(2)}) %collective-permute-start.7) | collective-permute-done | bytes 262176 | tf_op jit(solution)/shard_map/ppermute | solution.py:237
  30.5 1.6 %collective-permute-start.8 = (bf16[2,1,128,256]{3,2,1,0:T(8,128)(2,1)S(1)}, bf16[2,1,128,256]{3,2,1,0:T(8,128)(2,1)S(1)}, u32[]{:S(2)}, u32[]{:S(2)}) collective-permute-start(bf16[2,1,128,256]{3,2,1,0:T(8,128)(2,1)S(1)} %stage.2), channel_id=1, source_target_pairs={{0,2},{1,3},{2,0},{3,1},{4,6},{5,7},{6,4},{7,5},{8,10},{9,11},{10,... | collective-permute-start | bytes 393224 | tf_op jit(solution)/shard_map/ppermute | solution.py:237
  32.0 1.7 %collective-permute-done.10.refs_0_.refs_5_ = bf16[4,128,128]{2,1,0:T(8,128)(2,1)S(1)} collective-permute-done((bf16[4,128,128]{2,1,0:T(8,128)(2,1)S(1)}, bf16[4,128,128]{2,1,0:T(8,128)(2,1)S(1)}, u32[]{:S(2)}, u32[]{:S(2)}) %collective-permute-start.10) | collective-permute-done | bytes 131104 | tf_op jit(solution)/shard_map/ppermute | solution.py:243
  33.7 1.8 %collective-permute-done.9.got.refs_4_ = bf16[2,2,1,128,256]{4,3,2,1,0:T(8,128)(2,1)S(1)} collective-permute-done((bf16[2,2,1,128,256]{4,3,2,1,0:T(8,128)(2,1)S(1)}, bf16[2,2,1,128,256]{4,3,2,1,0:T(8,128)(2,1)S(1)}, u32[]{:S(2)}, u32[]{:S(2)}) %collective-permute-start.9) | collective-permute-done | bytes 262176 | tf_op jit(solution)/shard_map/ppermute | solution.py:237
  35.6 0.6 collective-permute-start.11
  36.1 1.1 %collective-permute-done.8.refs_2_ = bf16[2,1,128,256]{3,2,1,0:T(8,128)(2,1)S(1)} collective-permute-done((bf16[2,1,128,256]{3,2,1,0:T(8,128)(2,1)S(1)}, bf16[2,1,128,256]{3,2,1,0:T(8,128)(2,1)S(1)}, u32[]{:S(2)}, u32[]{:S(2)}) %collective-permute-start.8) | collective-permute-done | bytes 131104 | tf_op jit(solution)/shard_map/ppermute | solution.py:237
  37.2 3.4 %collective-permute-done.11.refs_5_ = bf16[2,1,128,256]{3,2,1,0:T(8,128)(2,1)S(1)} collective-permute-done((bf16[2,1,128,256]{3,2,1,0:T(8,128)(2,1)S(1)}, bf16[2,1,128,256]{3,2,1,0:T(8,128)(2,1)S(1)}, u32[]{:S(2)}, u32[]{:S(2)}) %collective-permute-start.11) | collective-permute-done | bytes 131104 | tf_op jit(solution)/shard_map/ppermute | solution.py:237
  40.6 0.1 total.1
  40.7 0.0 copy-start.1
  40.7 0.0 copy-start.4
  40.7 0.7 own_levels.1
  41.4 0.6 collective-permute-start.13
  42.0 3.3 %collective-permute-start.14 = (bf16[9,128,128]{2,1,0:T(8,128)(2,1)S(1)}, bf16[9,128,128]{2,1,0:T(8,128)(2,1)S(1)}, u32[]{:S(2)}, u32[]{:S(2)}) collective-permute-start(bf16[9,128,128]{2,1,0:T(8,128)(2,1)S(1)} %get-tuple-element.65), channel_id=1, source_target_pairs={{0,2},{1,3},{2,0},{3,1},{4,6},{5,7},{6,4},{7,5},{8,10},{9,11},{10,... | collective-permute-start | bytes 884744 | tf_op jit(solution)/shard_map/ppermute | solution.py:237
  45.3 0.0 collective-permute-start.15
  45.3 1.7 %collective-permute-start.12 = (bf16[2,128,512]{2,1,0:T(8,128)(2,1)S(1)}, bf16[2,128,512]{2,1,0:T(8,128)(2,1)S(1)}, u32[]{:S(2)}, u32[]{:S(2)}) collective-permute-start(bf16[2,128,512]{2,1,0:T(8,128)(2,1)S(1)} %total.1), channel_id=1, source_target_pairs={{0,4},{1,5},{2,6},{3,7},{4,0},{5,1},{6,2},{7,3},{8,12},{9,13},{10,... | collective-permute-start | bytes 786440 | tf_op jit(solution)/shard_map/ppermute | solution.py:243
  47.0 13.1 %collective-permute-done.12.refs_0_ = bf16[2,128,512]{2,1,0:T(8,128)(2,1)S(1)} collective-permute-done((bf16[2,128,512]{2,1,0:T(8,128)(2,1)S(1)}, bf16[2,128,512]{2,1,0:T(8,128)(2,1)S(1)}, u32[]{:S(2)}, u32[]{:S(2)}) %collective-permute-start.12) | collective-permute-done | bytes 262176 | tf_op jit(solution)/shard_map/ppermute | solution.py:243
  60.2 0.0 collective-permute-done.13.refs_2_
  60.2 0.0 collective-permute-done.14.refs_3_
  60.2 0.9 %collective-permute-done.15.refs_4_ = bf16[9,128,128]{2,1,0:T(8,128)(2,1)S(1)} collective-permute-done((bf16[9,128,128]{2,1,0:T(8,128)(2,1)S(1)}, bf16[9,128,128]{2,1,0:T(8,128)(2,1)S(1)}, u32[]{:S(2)}, u32[]{:S(2)}) %collective-permute-start.15) | collective-permute-done | bytes 294944 | tf_op jit(solution)/shard_map/ppermute | solution.py:237
  61.1 0.0 copy-done.1
  61.1 0.0 copy-done.4
  61.1 2.3 %middle_levels.1 = (f32[1024,512]{1,0:T(8,128)S(1)}, bf16[4,128,128]{2,1,0:T(8,128)(2,1)S(1)}, bf16[4,128,128]{2,1,0:T(8,128)(2,1)S(1)}, bf16[4,128,128]{2,1,0:T...) custom-call(bf16[1,3,1,8,128,128]{5,4,3,2,1,0:T(8,128)(2,1)S(1)} %co, ...), custom_call_target="tpu_custom_call" | custom-call | flops 1342177280 | bytes 11534336 | tf_op jit(solution)/shard_map/middle_levels/pallas_call | solution.py:248
  63.4 1.3 %collective-permute-start.16 = (bf16[1,1,128,512]{3,2,1,0:T(8,128)(2,1)S(1)}, bf16[1,1,128,512]{3,2,1,0:T(8,128)(2,1)S(1)}, u32[]{:S(2)}, u32[]{:S(2)}) collective-permute-start(bf16[1,1,128,512]{3,2,1,0:T(8,128)(2,1)S(1)} %get-tuple-element.69), channel_id=1, source_target_pairs={{0,1},{1,0},{2,3},{3,2},{4,5},{5,4},{6,7},{7,6},{8,9},{9,8},{10,11... | collective-permute-start | bytes 393224 | tf_op jit(solution)/shard_map/ppermute | solution.py:237
  64.7 1.1 %collective-permute-start.17 = (bf16[1,1,128,512]{3,2,1,0:T(8,128)(2,1)S(1)}, bf16[1,1,128,512]{3,2,1,0:T(8,128)(2,1)S(1)}, u32[]{:S(2)}, u32[]{:S(2)}) collective-permute-start(bf16[1,1,128,512]{3,2,1,0:T(8,128)(2,1)S(1)} %get-tuple-element.70), channel_id=1, source_target_pairs={{0,2},{1,3},{2,0},{3,1},{4,6},{5,7},{6,4},{7,5},{8,10},{9,11},{10,... | collective-permute-start | bytes 393224 | tf_op jit(solution)/shard_map/ppermute | solution.py:237
  65.8 1.2 %collective-permute-start.18 = (bf16[1,1,128,512]{3,2,1,0:T(8,128)(2,1)S(1)}, bf16[1,1,128,512]{3,2,1,0:T(8,128)(2,1)S(1)}, u32[]{:S(2)}, u32[]{:S(2)}) collective-permute-start(bf16[1,1,128,512]{3,2,1,0:T(8,128)(2,1)S(1)} %get-tuple-element.71), channel_id=1, source_target_pairs={{0,3},{1,2},{2,1},{3,0},{4,7},{5,6},{6,5},{7,4},{8,11},{9,10},{10,... | collective-permute-start | bytes 393224 | tf_op jit(solution)/shard_map/ppermute | solution.py:237
  67.0 1.5 %collective-permute-done.16 = bf16[1,1,128,512]{3,2,1,0:T(8,128)(2,1)S(1)} collective-permute-done((bf16[1,1,128,512]{3,2,1,0:T(8,128)(2,1)S(1)}, bf16[1,1,128,512]{3,2,1,0:T(8,128)(2,1)S(1)}, u32[]{:S(2)}, u32[]{:S(2)}) %collective-permute-start.16) | collective-permute-done | bytes 131104 | tf_op jit(solution)/shard_map/ppermute | solution.py:237
  68.5 1.2 %collective-permute-done.17 = bf16[1,1,128,512]{3,2,1,0:T(8,128)(2,1)S(1)} collective-permute-done((bf16[1,1,128,512]{3,2,1,0:T(8,128)(2,1)S(1)}, bf16[1,1,128,512]{3,2,1,0:T(8,128)(2,1)S(1)}, u32[]{:S(2)}, u32[]{:S(2)}) %collective-permute-start.17) | collective-permute-done | bytes 131104 | tf_op jit(solution)/shard_map/ppermute | solution.py:237
  69.7 3.0 %collective-permute-done.18 = bf16[1,1,128,512]{3,2,1,0:T(8,128)(2,1)S(1)} collective-permute-done((bf16[1,1,128,512]{3,2,1,0:T(8,128)(2,1)S(1)}, bf16[1,1,128,512]{3,2,1,0:T(8,128)(2,1)S(1)}, u32[]{:S(2)}, u32[]{:S(2)}) %collective-permute-start.18) | collective-permute-done | bytes 131104 | tf_op jit(solution)/shard_map/ppermute | solution.py:237
  72.7 0.1 fusion
  72.7 0.1 collective-permute-start.20
  72.8 1.8 %collective-permute-start.21 = (bf16[4,128,128]{2,1,0:T(8,128)(2,1)S(1)}, bf16[4,128,128]{2,1,0:T(8,128)(2,1)S(1)}, u32[]{:S(2)}, u32[]{:S(2)}) collective-permute-start(bf16[4,128,128]{2,1,0:T(8,128)(2,1)S(1)} %get-tuple-element.76), channel_id=1, source_target_pairs={{0,2},{1,3},{2,0},{3,1},{4,6},{5,7},{6,4},{7,5},{8,10},{9,11},{10,... | collective-permute-start | bytes 393224 | tf_op jit(solution)/shard_map/ppermute | solution.py:237
  74.6 1.6 %collective-permute-start.22 = (bf16[4,128,128]{2,1,0:T(8,128)(2,1)S(1)}, bf16[4,128,128]{2,1,0:T(8,128)(2,1)S(1)}, u32[]{:S(2)}, u32[]{:S(2)}) collective-permute-start(bf16[4,128,128]{2,1,0:T(8,128)(2,1)S(1)} %get-tuple-element.78), channel_id=1, source_target_pairs={{0,3},{1,2},{2,1},{3,0},{4,7},{5,6},{6,5},{7,4},{8,11},{9,10},{10,... | collective-permute-start | bytes 393224 | tf_op jit(solution)/shard_map/ppermute | solution.py:237
  76.3 1.6 %collective-permute-start.19 = (bf16[1,128,512]{2,1,0:T(8,128)(2,1)S(1)}, bf16[1,128,512]{2,1,0:T(8,128)(2,1)S(1)}, u32[]{:S(2)}, u32[]{:S(2)}) collective-permute-start(bf16[1,128,512]{2,1,0:T(8,128)(2,1)S(1)} %fusion), channel_id=1, source_target_pairs={{0,4},{1,5},{2,6},{3,7},{4,0},{5,1},{6,2},{7,3},{8,12},{9,13},{10,... | collective-permute-start | bytes 393224 | tf_op jit(solution)/shard_map/ppermute | solution.py:243
  77.9 0.0 collective-permute-done.20.refs_2_
  77.9 0.0 collective-permute-done.21.refs_3_
  77.9 4.1 %collective-permute-done.22.refs_4_ = bf16[4,128,128]{2,1,0:T(8,128)(2,1)S(1)} collective-permute-done((bf16[4,128,128]{2,1,0:T(8,128)(2,1)S(1)}, bf16[4,128,128]{2,1,0:T(8,128)(2,1)S(1)}, u32[]{:S(2)}, u32[]{:S(2)}) %collective-permute-start.22) | collective-permute-done | bytes 131104 | tf_op jit(solution)/shard_map/ppermute | solution.py:237
  82.0 1.5 %collective-permute-done.19.refs_0_ = bf16[1,128,512]{2,1,0:T(8,128)(2,1)S(1)} collective-permute-done((bf16[1,128,512]{2,1,0:T(8,128)(2,1)S(1)}, bf16[1,128,512]{2,1,0:T(8,128)(2,1)S(1)}, u32[]{:S(2)}, u32[]{:S(2)}) %collective-permute-start.19) | collective-permute-done | bytes 131104 | tf_op jit(solution)/shard_map/ppermute | solution.py:243
  83.6 1.6 %last_levels.1 = bf16[1,1024,512]{2,1,0:T(8,128)(2,1)} custom-call(bf16[1,3,1,8,128,128]{5,4,3,2,1,0:T(8,128)(2,1)S(1)} %copy-done.1, bf16[1024,256]{1,0:T(8,128)(2,1)S(1)} %get-tuple-element.42.row_mats, f32[1024,512]{1,0:T(8,128)S(1)} %get-tuple-element.67.residual, bf16[1,128,512]{2,1,0:T(8,128)(2,1)S(1)} %collective-permute-done.19.refs_0_, ...), custom_call_target="tpu_custom_call" | custom-call | flops 335544320 | bytes 5111808 | tf_op jit(solution)/shard_map/last_levels/pallas_call | solution.py:248
  (10 shorter events, 0.1 us)
Async XLA Ops:
  0.0 18.7 %collective-permute-start.5 = (bf16[2,256,512]{2,1,0:T(8,128)(2,1)}, bf16[2,256,512]{2,1,0:T(8,128)(2,1)S(1)}, u32[]{:S(2)}, u32[]{:S(2)}) collective-permute-start(bf16[2,256,512]{2,1,0:T(8,128)(2,1)} %refs_4_.1), channel_id=1, source_target_pairs={{0,16},{8,24},{16,0},{24,8},{1,17},{9,25},{17,1},{25,9},{2,18},{10... | collective-permute-start | bytes 1572872 | tf_op jit(solution)/shard_map/ppermute | solution.py:233
  3.0 1.1 %copy-start = (bf16[1,3,1,8,128,128]{5,4,3,2,1,0:T(8,128)(2,1)S(1)}, bf16[1,3,1,8,128,128]{5,4,3,2,1,0:T(8,128)(2,1)}, u32[]{:S(2)}) copy-start(bf16[1,3,1,8,128,128]{5,4,3,2,1,0:T(8,128)(2,1)} %third.5) | copy-start | bytes 2359300
  4.1 13.8 %collective-permute-start = (bf16[2,128,128]{2,1,0:T(8,128)(2,1)S(1)}, bf16[2,128,128]{2,1,0:T(8,128)(2,1)S(1)}, u32[]{:S(2)}, u32[]{:S(2)}) collective-permute-start(bf16[2,128,128]{2,1,0:T(8,128)(2,1)S(1)} %get-tuple-element.46), channel_id=1, source_target_pairs={{0,4},{1,5},{2,6},{3,7},{4,0},{5,1},{6,2},{7,3},{8,12},{9,13},{10,... | collective-permute-start | bytes 196616 | tf_op jit(solution)/shard_map/ppermute | solution.py:243
  6.8 11.3 %collective-permute-start.1 = (bf16[2,128,128]{2,1,0:T(8,128)(2,1)S(1)}, bf16[2,128,128]{2,1,0:T(8,128)(2,1)S(1)}, u32[]{:S(2)}, u32[]{:S(2)}) collective-permute-start(bf16[2,128,128]{2,1,0:T(8,128)(2,1)S(1)} %get-tuple-element.47), channel_id=1, source_target_pairs={{0,5},{1,4},{2,7},{3,6},{4,1},{5,0},{6,3},{7,2},{8,13},{9,12},{10,... | collective-permute-start | bytes 196616 | tf_op jit(solution)/shard_map/ppermute | solution.py:243
  8.1 10.0 %collective-permute-start.2 = (bf16[2,128,128]{2,1,0:T(8,128)(2,1)S(1)}, bf16[2,128,128]{2,1,0:T(8,128)(2,1)S(1)}, u32[]{:S(2)}, u32[]{:S(2)}) collective-permute-start(bf16[2,128,128]{2,1,0:T(8,128)(2,1)S(1)} %get-tuple-element.48), channel_id=1, source_target_pairs={{0,6},{1,7},{2,4},{3,5},{4,2},{5,3},{6,0},{7,1},{8,14},{9,15},{10,... | collective-permute-start | bytes 196616 | tf_op jit(solution)/shard_map/ppermute | solution.py:243
  11.7 9.1 %copy-start.2 = (bf16[1,3,4,256,128]{4,3,2,1,0:T(8,128)(2,1)S(1)}, bf16[1,3,4,256,128]{4,3,2,1,0:T(8,128)(2,1)}, u32[]{:S(2)}) copy-start(bf16[1,3,4,256,128]{4,3,2,1,0:T(8,128)(2,1)} %basis.3) | copy-start | bytes 2359300
  11.7 7.1 %collective-permute-start.3 = (bf16[2,128,128]{2,1,0:T(8,128)(2,1)S(1)}, bf16[2,128,128]{2,1,0:T(8,128)(2,1)S(1)}, u32[]{:S(2)}, u32[]{:S(2)}) collective-permute-start(bf16[2,128,128]{2,1,0:T(8,128)(2,1)S(1)} %get-tuple-element.49), channel_id=1, source_target_pairs={{0,7},{1,6},{2,5},{3,4},{4,3},{5,2},{6,1},{7,0},{8,15},{9,14},{10,... | collective-permute-start | bytes 196616 | tf_op jit(solution)/shard_map/ppermute | solution.py:243
  11.8 1.4 %copy-start.3 = (bf16[1,3,1,4,4,128,128]{6,5,4,3,2,1,0:T(8,128)(2,1)S(1)}, bf16[1,3,1,4,4,128,128]{6,5,4,3,2,1,0:T(8,128)(2,1)}, u32[]{:S(2)}) copy-start(bf16[1,3,1,4,4,128,128]{6,5,4,3,2,1,0:T(8,128)(2,1)} %first.1) | copy-start | bytes 4718596
  13.3 1.1 %copy-start.5 = (bf16[1,3,1,8,128,128]{5,4,3,2,1,0:T(8,128)(2,1)S(1)}, bf16[1,3,1,8,128,128]{5,4,3,2,1,0:T(8,128)(2,1)}, u32[]{:S(2)}) copy-start(bf16[1,3,1,8,128,128]{5,4,3,2,1,0:T(8,128)(2,1)} %second.1) | copy-start | bytes 2359300
  14.4 1.1 %copy-start.6 = (bf16[1,3,2,512,128]{4,3,2,1,0:T(8,128)(2,1)S(1)}, bf16[1,3,2,512,128]{4,3,2,1,0:T(8,128)(2,1)}, u32[]{:S(2)}) copy-start(bf16[1,3,2,512,128]{4,3,2,1,0:T(8,128)(2,1)} %out_basis.1) | copy-start | bytes 2359300
  15.6 1.0 %copy-start.8 = (bf16[1,3,1,2,2,128,128]{6,5,4,3,2,1,0:T(8,128)(2,1)S(1)}, bf16[1,3,1,2,2,128,128]{6,5,4,3,2,1,0:T(8,128)(2,1)}, u32[]{:S(2)}) copy-start(bf16[1,3,1,2,2,128,128]{6,5,4,3,2,1,0:T(8,128)(2,1)} %fourth.1) | copy-start | bytes 1179652
  16.6 1.4 %copy-start.7 = (bf16[2,256,512]{2,1,0:T(8,128)(2,1)S(1)}, bf16[2,256,512]{2,1,0:T(8,128)(2,1)}, u32[]{:S(2)}) copy-start(bf16[2,256,512]{2,1,0:T(8,128)(2,1)} %refs_4_.1) | copy-start | bytes 1572868
  18.0 2.0 %collective-permute-start.4 = (bf16[2,256,512]{2,1,0:T(8,128)(2,1)S(1)}, bf16[2,256,512]{2,1,0:T(8,128)(2,1)S(1)}, u32[]{:S(2)}, u32[]{:S(2)}) collective-permute-start(bf16[2,256,512]{2,1,0:T(8,128)(2,1)S(1)} %copy-done.7), channel_id=1, source_target_pairs={{0,8},{8,0},{16,24},{24,16},{1,9},{9,1},{17,25},{25,17},{2,10},{10... | collective-permute-start | bytes 1572872 | tf_op jit(solution)/shard_map/ppermute | solution.py:233
  18.7 2.0 %collective-permute-start.6 = (bf16[2,256,512]{2,1,0:T(8,128)(2,1)S(1)}, bf16[2,256,512]{2,1,0:T(8,128)(2,1)S(1)}, u32[]{:S(2)}, u32[]{:S(2)}) collective-permute-start(bf16[2,256,512]{2,1,0:T(8,128)(2,1)S(1)} %collective-permute-done.5.refs_6_), channel_id=1, source_target_pairs={{0,8},{8,0},{16,24},{24,16},{1,9},{9,1},{17,25},{25,17},{2,10},{10... | collective-permute-start | bytes 1572872 | tf_op jit(solution)/shard_map/ppermute | solution.py:233
  22.0 8.4 %collective-permute-start.7 = (bf16[2,2,1,128,256]{4,3,2,1,0:T(8,128)(2,1)S(1)}, bf16[2,2,1,128,256]{4,3,2,1,0:T(8,128)(2,1)S(1)}, u32[]{:S(2)}, u32[]{:S(2)}) collective-permute-start(bf16[2,2,1,128,256]{4,3,2,1,0:T(8,128)(2,1)S(1)} %get-tuple-element.53), channel_id=1, source_target_pairs={{0,1},{1,0},{2,3},{3,2},{4,5},{5,4},{6,7},{7,6},{8,9},{9,8},{10,11... | collective-permute-start | bytes 786440 | tf_op jit(solution)/shard_map/ppermute | solution.py:237
  23.5 12.0 %collective-permute-start.9 = (bf16[2,2,1,128,256]{4,3,2,1,0:T(8,128)(2,1)S(1)}, bf16[2,2,1,128,256]{4,3,2,1,0:T(8,128)(2,1)S(1)}, u32[]{:S(2)}, u32[]{:S(2)}) collective-permute-start(bf16[2,2,1,128,256]{4,3,2,1,0:T(8,128)(2,1)S(1)} %get-tuple-element.56), channel_id=1, source_target_pairs={{0,2},{1,3},{2,0},{3,1},{4,6},{5,7},{6,4},{7,5},{8,10},{9,11},{10,... | collective-permute-start | bytes 786440 | tf_op jit(solution)/shard_map/ppermute | solution.py:237
  24.2 9.5 %collective-permute-start.10 = (bf16[4,128,128]{2,1,0:T(8,128)(2,1)S(1)}, bf16[4,128,128]{2,1,0:T(8,128)(2,1)S(1)}, u32[]{:S(2)}, u32[]{:S(2)}) collective-permute-start(bf16[4,128,128]{2,1,0:T(8,128)(2,1)S(1)} %get-tuple-element.59), channel_id=1, source_target_pairs={{0,4},{1,5},{2,6},{3,7},{4,0},{5,1},{6,2},{7,3},{8,12},{9,13},{10,... | collective-permute-start | bytes 393224 | tf_op jit(solution)/shard_map/ppermute | solution.py:243
  30.5 6.8 %collective-permute-start.8 = (bf16[2,1,128,256]{3,2,1,0:T(8,128)(2,1)S(1)}, bf16[2,1,128,256]{3,2,1,0:T(8,128)(2,1)S(1)}, u32[]{:S(2)}, u32[]{:S(2)}) collective-permute-start(bf16[2,1,128,256]{3,2,1,0:T(8,128)(2,1)S(1)} %stage.2), channel_id=1, source_target_pairs={{0,2},{1,3},{2,0},{3,1},{4,6},{5,7},{6,4},{7,5},{8,10},{9,11},{10,... | collective-permute-start | bytes 393224 | tf_op jit(solution)/shard_map/ppermute | solution.py:237
  35.6 5.0 %collective-permute-start.11 = (bf16[2,1,128,256]{3,2,1,0:T(8,128)(2,1)S(1)}, bf16[2,1,128,256]{3,2,1,0:T(8,128)(2,1)S(1)}, u32[]{:S(2)}, u32[]{:S(2)}) collective-permute-start(bf16[2,1,128,256]{3,2,1,0:T(8,128)(2,1)S(1)} %stage.3), channel_id=1, source_target_pairs={{0,1},{1,0},{2,3},{3,2},{4,5},{5,4},{6,7},{7,6},{8,9},{9,8},{10,11... | collective-permute-start | bytes 393224 | tf_op jit(solution)/shard_map/ppermute | solution.py:237
  40.7 20.4 %copy-start.1 = (bf16[1,3,1,8,128,128]{5,4,3,2,1,0:T(8,128)(2,1)S(1)}, bf16[1,3,1,8,128,128]{5,4,3,2,1,0:T(8,128)(2,1)}, u32[]{:S(2)}) copy-start(bf16[1,3,1,8,128,128]{5,4,3,2,1,0:T(8,128)(2,1)} %third.5) | copy-start | bytes 2359300
  40.7 20.4 %copy-start.4 = (bf16[1,1024,512]{2,1,0:T(8,128)(2,1)S(1)}, bf16[1,1024,512]{2,1,0:T(8,128)(2,1)}, u32[]{:S(2)}) copy-start(bf16[1,1024,512]{2,1,0:T(8,128)(2,1)} %rhs.1) | copy-start | bytes 3145732
  41.4 18.7 %collective-permute-start.13 = (bf16[9,128,128]{2,1,0:T(8,128)(2,1)S(1)}, bf16[9,128,128]{2,1,0:T(8,128)(2,1)S(1)}, u32[]{:S(2)}, u32[]{:S(2)}) collective-permute-start(bf16[9,128,128]{2,1,0:T(8,128)(2,1)S(1)} %get-tuple-element.64), channel_id=1, source_target_pairs={{0,1},{1,0},{2,3},{3,2},{4,5},{5,4},{6,7},{7,6},{8,9},{9,8},{10,11... | collective-permute-start | bytes 884744 | tf_op jit(solution)/shard_map/ppermute | solution.py:237
  42.0 18.2 %collective-permute-start.14 = (bf16[9,128,128]{2,1,0:T(8,128)(2,1)S(1)}, bf16[9,128,128]{2,1,0:T(8,128)(2,1)S(1)}, u32[]{:S(2)}, u32[]{:S(2)}) collective-permute-start(bf16[9,128,128]{2,1,0:T(8,128)(2,1)S(1)} %get-tuple-element.65), channel_id=1, source_target_pairs={{0,2},{1,3},{2,0},{3,1},{4,6},{5,7},{6,4},{7,5},{8,10},{9,11},{10,... | collective-permute-start | bytes 884744 | tf_op jit(solution)/shard_map/ppermute | solution.py:237
  45.3 15.8 %collective-permute-start.15 = (bf16[9,128,128]{2,1,0:T(8,128)(2,1)S(1)}, bf16[9,128,128]{2,1,0:T(8,128)(2,1)S(1)}, u32[]{:S(2)}, u32[]{:S(2)}) collective-permute-start(bf16[9,128,128]{2,1,0:T(8,128)(2,1)S(1)} %get-tuple-element.66), channel_id=1, source_target_pairs={{0,3},{1,2},{2,1},{3,0},{4,7},{5,6},{6,5},{7,4},{8,11},{9,10},{10,... | collective-permute-start | bytes 884744 | tf_op jit(solution)/shard_map/ppermute | solution.py:237
  45.3 14.9 %collective-permute-start.12 = (bf16[2,128,512]{2,1,0:T(8,128)(2,1)S(1)}, bf16[2,128,512]{2,1,0:T(8,128)(2,1)S(1)}, u32[]{:S(2)}, u32[]{:S(2)}) collective-permute-start(bf16[2,128,512]{2,1,0:T(8,128)(2,1)S(1)} %total.1), channel_id=1, source_target_pairs={{0,4},{1,5},{2,6},{3,7},{4,0},{5,1},{6,2},{7,3},{8,12},{9,13},{10,... | collective-permute-start | bytes 786440 | tf_op jit(solution)/shard_map/ppermute | solution.py:243
  63.4 5.0 %collective-permute-start.16 = (bf16[1,1,128,512]{3,2,1,0:T(8,128)(2,1)S(1)}, bf16[1,1,128,512]{3,2,1,0:T(8,128)(2,1)S(1)}, u32[]{:S(2)}, u32[]{:S(2)}) collective-permute-start(bf16[1,1,128,512]{3,2,1,0:T(8,128)(2,1)S(1)} %get-tuple-element.69), channel_id=1, source_target_pairs={{0,1},{1,0},{2,3},{3,2},{4,5},{5,4},{6,7},{7,6},{8,9},{9,8},{10,11... | collective-permute-start | bytes 393224 | tf_op jit(solution)/shard_map/ppermute | solution.py:237
  64.7 5.0 %collective-permute-start.17 = (bf16[1,1,128,512]{3,2,1,0:T(8,128)(2,1)S(1)}, bf16[1,1,128,512]{3,2,1,0:T(8,128)(2,1)S(1)}, u32[]{:S(2)}, u32[]{:S(2)}) collective-permute-start(bf16[1,1,128,512]{3,2,1,0:T(8,128)(2,1)S(1)} %get-tuple-element.70), channel_id=1, source_target_pairs={{0,2},{1,3},{2,0},{3,1},{4,6},{5,7},{6,4},{7,5},{8,10},{9,11},{10,... | collective-permute-start | bytes 393224 | tf_op jit(solution)/shard_map/ppermute | solution.py:237
  65.8 6.9 %collective-permute-start.18 = (bf16[1,1,128,512]{3,2,1,0:T(8,128)(2,1)S(1)}, bf16[1,1,128,512]{3,2,1,0:T(8,128)(2,1)S(1)}, u32[]{:S(2)}, u32[]{:S(2)}) collective-permute-start(bf16[1,1,128,512]{3,2,1,0:T(8,128)(2,1)S(1)} %get-tuple-element.71), channel_id=1, source_target_pairs={{0,3},{1,2},{2,1},{3,0},{4,7},{5,6},{6,5},{7,4},{8,11},{9,10},{10,... | collective-permute-start | bytes 393224 | tf_op jit(solution)/shard_map/ppermute | solution.py:237
  72.7 5.2 %collective-permute-start.20 = (bf16[4,128,128]{2,1,0:T(8,128)(2,1)S(1)}, bf16[4,128,128]{2,1,0:T(8,128)(2,1)S(1)}, u32[]{:S(2)}, u32[]{:S(2)}) collective-permute-start(bf16[4,128,128]{2,1,0:T(8,128)(2,1)S(1)} %get-tuple-element.74), channel_id=1, source_target_pairs={{0,1},{1,0},{2,3},{3,2},{4,5},{5,4},{6,7},{7,6},{8,9},{9,8},{10,11... | collective-permute-start | bytes 393224 | tf_op jit(solution)/shard_map/ppermute | solution.py:237
  72.8 5.1 %collective-permute-start.21 = (bf16[4,128,128]{2,1,0:T(8,128)(2,1)S(1)}, bf16[4,128,128]{2,1,0:T(8,128)(2,1)S(1)}, u32[]{:S(2)}, u32[]{:S(2)}) collective-permute-start(bf16[4,128,128]{2,1,0:T(8,128)(2,1)S(1)} %get-tuple-element.76), channel_id=1, source_target_pairs={{0,2},{1,3},{2,0},{3,1},{4,6},{5,7},{6,4},{7,5},{8,10},{9,11},{10,... | collective-permute-start | bytes 393224 | tf_op jit(solution)/shard_map/ppermute | solution.py:237
  74.6 7.4 %collective-permute-start.22 = (bf16[4,128,128]{2,1,0:T(8,128)(2,1)S(1)}, bf16[4,128,128]{2,1,0:T(8,128)(2,1)S(1)}, u32[]{:S(2)}, u32[]{:S(2)}) collective-permute-start(bf16[4,128,128]{2,1,0:T(8,128)(2,1)S(1)} %get-tuple-element.78), channel_id=1, source_target_pairs={{0,3},{1,2},{2,1},{3,0},{4,7},{5,6},{6,5},{7,4},{8,11},{9,10},{10,... | collective-permute-start | bytes 393224 | tf_op jit(solution)/shard_map/ppermute | solution.py:237
  76.3 7.3 %collective-permute-start.19 = (bf16[1,128,512]{2,1,0:T(8,128)(2,1)S(1)}, bf16[1,128,512]{2,1,0:T(8,128)(2,1)S(1)}, u32[]{:S(2)}, u32[]{:S(2)}) collective-permute-start(bf16[1,128,512]{2,1,0:T(8,128)(2,1)S(1)} %fusion), channel_id=1, source_target_pairs={{0,4},{1,5},{2,6},{3,7},{4,0},{5,1},{6,2},{7,3},{8,12},{9,13},{10,... | collective-permute-start | bytes 393224 | tf_op jit(solution)/shard_map/ppermute | solution.py:243

commit v4 on v3

--- a/solution.py
+++ b/solution.py
@@ -10,7 +10,6 @@
 F32 = jnp.float32
 BF16 = jnp.bfloat16
 MIB = 1024 * 1024
-MASKS = (1, 2)
 VMEM = pl.BlockSpec(memory_space=pltpu.VMEM)
 
 
@@ -103,8 +102,17 @@
             ref[at * tiles + c] = coef[i * rank : (i + 1) * rank, c * rank : (c + 1) * rank]
 
 
+def put_other(mats, leaf, other, at, member):
+    radix, _, less, rank, width = other.shape
+    coef = dot(mats, leaf).astype(BF16)
+    for i in range(radix):
+        part = coef[i * less * rank : (i + 1) * less * rank]
+        other[jnp.bitwise_xor(member, i), at] = part.reshape(less, rank, width)
+
+
 def off_kernel(radix, groups, pieces, basis, up_other, *refs):
-    thirds, parts, (leaf_ref,), outs = take(refs, (groups - 1) * radix, pieces, 1, 3 * len(MASKS))
+    thirds, parts, (leaf_ref, other) = take(refs, (groups - 1) * radix, pieces, 2)
+    _, member = place(radix)
     row = lax.axis_index("row")
     leaves, leaf_rows, rank = basis.shape[2], basis.shape[3], basis.shape[4]
     rows = parts[0].shape[1]
@@ -127,17 +135,7 @@
         leaf = jnp.concatenate(leaf, axis=0)
         leaf_ref[j] = leaf
         mats = other_mats(j, lambda i, d: thirds[d * radix + i][j], up_other)
-        coef = dot(mats, leaf).astype(BF16)
-        width = coef.shape[1] // len(MASKS)
-        for c, mask in enumerate(MASKS):
-            blocks = [
-                coef[i * less * rank : (i + 1) * less * rank, c * width : (c + 1) * width].reshape(less, rank, width)
-                for i in range(radix)
-            ]
-            outs[3 * c][j] = blocks[0]
-            outs[3 * c + 1][j] = blocks[3 - mask]
-            outs[3 * c + 2][j, 0] = blocks[mask]
-            outs[3 * c + 2][j, 1] = blocks[3]
+        put_other(mats, leaf, other, j, member)
 
 
 def own_kernel(members, leaf, up_own, *refs):
@@ -150,21 +148,6 @@
             ref[ref.shape[0] - len(rides) + d] = ride[jnp.bitwise_xor(member, i)]
 
 
-def stage_kernel(keep, got, out):
-    out[...] = (keep[...].astype(F32) + got[:, 1].astype(F32)).astype(BF16)
-
-
-def total_kernel(*refs):
-    halves, outs = refs[: 3 * len(MASKS)], refs[3 * len(MASKS) :]
-    offs, less, rank, width = halves[0].shape
-    for j in range(offs):
-        for d in range(less):
-            for c in range(len(MASKS)):
-                keep, got, last = halves[3 * c : 3 * c + 3]
-                total = keep[j, d].astype(F32) + got[j, 0, d].astype(F32) + last[j, d].astype(F32)
-                outs[d][j, :, c * width : (c + 1) * width] = total.astype(BF16)
-
-
 def group_coefs(j, at, tiles, own, crossed, third, radix):
     group, member = place(radix)
     mats = [third[0, j, 0, group * radix + jnp.bitwise_xor(member, i)] for i in range(radix)]
@@ -175,7 +158,7 @@
 
 def middle_kernel(radix, groups, offs, third, rhs, basis, row_mats, up_own, up_other, *refs):
     less = groups - 1
-    crossed, own_in, rides, (residual_ref,), own, other = take(refs, less, radix, less, 1, radix, radix)
+    crossed, own_in, rides, (residual_ref, other), own = take(refs, less, radix, less, 2, radix)
     rank = basis.shape[4]
     tiles = rhs.shape[2] // rank
     _, member = place(radix)
@@ -197,9 +180,7 @@
         residual_ref[rows] = residual
         leaf.append(dot_t(basis[0, offs, k], residual.astype(BF16)).astype(BF16))
     leaf = jnp.concatenate(leaf, axis=0)
-    coef = dot(other_mats(offs, third_of, up_other), leaf).astype(BF16)
-    for i, ref in enumerate(other):
-        ref[0] = coef[i * less * rank : (i + 1) * less * rank].reshape(ref.shape[1:])
+    put_other(other_mats(offs, third_of, up_other), leaf, other, 0, member)
     put_own(up_own.at[offs], range(radix), leaf, own, 0)
 
 
@@ -223,7 +204,6 @@
     butterflies = leaf_basis.shape[1]
     offs = solved.shape[0]
     columns = solved.shape[2]
-    width = columns // len(MASKS)
     rank = leaf_basis.shape[4]
     rows = rhs.shape[1]
     depth = radix * rank
@@ -262,9 +242,6 @@
         [((offs, rank, rank), BF16)] * (less * radix) + [((radix, rank, rank), BF16)] * less,
         third_level,
     )
-    shifts = [(delta, i) for delta in range(1, groups) for i in range(radix)]
-    thirds = [over_groups(a, *shift) for a, shift in zip(picked, shifts)]
-
     up_own, up_other, off_rows, last_rows = call(
         functools.partial(weights_kernel, radix, groups, offs, row_size),
         "weights",
@@ -291,49 +268,46 @@
     pieces = [pieces[mask] for mask in range(row_size)]
 
     ride_shape = ((offs * tiles + less, rank, rank), BF16)
-    part = (offs, less, rank, width)
     other_flops = 2 * columns * rank * radix * less * depth
     own_flops = 2 * columns * rank * radix * depth
     leaf_flops = 2 * columns * rank * rows
     row_flops = 2 * columns * rank * (depth + groups * rows)
 
-    leaf, *others = call(
+    def add(other):
+        index_groups = [list(range(g * radix, (g + 1) * radix)) for g in range(groups)]
+        total = lax.psum_scatter(other, "box", scatter_dimension=0, axis_index_groups=index_groups)
+        return [over_groups(total[:, d], less - d) for d in range(less)], total
+
+    leaf, other = call(
         functools.partial(off_kernel, radix, groups, row_size),
         "off_levels",
         offs * (leaf_flops + other_flops),
         [((offs, depth, columns), BF16)]
-        + [(part, BF16), (part, BF16), ((offs, 2, less, rank, width), BF16)] * len(MASKS),
+        + [((radix, offs, less, rank, columns), BF16)],
         leaf_basis,
         up_other,
         *thirds,
         *pieces,
     )
-    halves = []
-    for c, mask in enumerate(MASKS):
-        keep, wait, sent = others[3 * c : 3 * c + 3]
-        got = over_members(sent, mask)
-        (staged,) = call(stage_kernel, "stage", 0, [(part, BF16)], wait, after(got, *rides) if c else got)
-        halves += [keep, got, over_members(staged, 3 - mask)]
-    sums = call(total_kernel, "total", 0, [((offs, rank, columns), BF16)] * less, *halves)
-    crossed = [over_groups(a, groups - 1 - d) for d, a in enumerate(sums)]
+    crossed, total = add(other)
     own = call(
         functools.partial(own_kernel, range(radix)),
         "own_levels",
         offs * own_flops,
         [ride_shape] * radix,
-        after(leaf, *sums),
+        after(leaf, total),
         up_own,
         *rides,
     )
     own = [over_members(a, i) for i, a in enumerate(own)]
 
-    residual, *levels = call(
+    residual, other, *own = call(
         functools.partial(middle_kernel, radix, groups, offs),
         "middle_levels",
         offs * row_flops + leaf_flops + other_flops + own_flops,
         [((rows, columns), F32)]
-        + [((tiles, rank, rank), BF16)] * radix
-        + [((1, less, rank, columns), BF16)] * radix,
+        + [((radix, 1, less, rank, columns), BF16)]
+        + [((tiles, rank, rank), BF16)] * radix,
         third_level,
         rhs,
         leaf_basis,
@@ -344,11 +318,8 @@
         *own,
         *rides,
     )
-    own, other = levels[:radix], levels[radix:]
-    other = [over_members(a, i) for i, a in enumerate(other)]
-    sums = [sum(a[:, d].astype(F32) for a in other).astype(BF16) for d in range(less)]
-    crossed = [over_groups(a, groups - 1 - d) for d, a in enumerate(sums)]
-    own = [over_members(after(a, *sums) if i else a, i) for i, a in enumerate(own)]
+    crossed, total = add(other)
+    own = [over_members(after(a, total) if i else a, i) for i, a in enumerate(own)]
     return call(
         functools.partial(last_kernel, radix, groups, offs),
         "last_levels",

time: 85.5 us -> 138 us (1.61)
  waiting for transfers between devices: 38.8 us -> 67 us
  local copies, waits for them, and re-layouts: 5.86 us -> 20.6 us
  between operations: 0.14 us -> 13.6 us
  starting transfers between devices: 32.8 us -> 26.9 us
  Pallas kernels: 7.52 us -> 9.39 us
    reduce_scatter x0 -> x2, waiting for transfers between devices: none -> 39.9 us  [add(): lax.psum_scatter(other, 'box', scatter_dimension=0, axis_index_groups=ind...]
    unnamed x18 -> x50, local copies, waits for them, and re-layouts: 5.86 us -> 20.6 us
    ppermute x13 -> x6, waiting for transfers between devices: 19.8 us -> 5.82 us  [over_members(): return array if mask == 0 else lax.ppermute(array, 'box', pairs)]
    ppermute x13 -> x6, starting transfers between devices: 15.3 us -> 6.98 us  [over_members(): return array if mask == 0 else lax.ppermute(array, 'box', pairs)]
    ppermute x7, starting transfers between devices: 14.5 us -> 16.8 us  [over_groups(): return lax.ppermute(array, 'box', pairs)]
    ppermute x7, waiting for transfers between devices: 17 us -> 19.3 us  [over_groups(): return lax.ppermute(array, 'box', pairs)]
    pallas_call x9 -> x6, Pallas kernels: 7.52 us -> 9.39 us  [call(): pl.pallas_call(kernel, out_shape=outs, in_specs=[VMEM] * len(args), out_s...]
  transfers between devices with their start and end apart: 23 -> 18, of which waited for: 15 -> 10; matrix products, arithmetic and copies ran while one was open for 0% -> 0% of each run, Pallas kernels for 2% -> 2%
where the time goes in v4:
time: 138 us; the launch traced here: 137 us
  waiting for transfers between devices  67 us (49%)
  starting transfers between devices  26.9 us (19%)
  local copies, waits for them, and re-layouts  20.6 us (15%)
  between operations  13.6 us (10%)
  Pallas kernels  9.39 us (7%)
    reduce_scatter x2, waiting for transfers between devices, add(): lax.psum_scatter(other, 'box', scatter_dimension=0, axis_index_groups=ind...  39.9 us
    unnamed x50, local copies, waits for them, and re-layouts  20.6 us
    ppermute x7, waiting for transfers between devices, over_groups(): return lax.ppermute(array, 'box', pairs)  19.3 us
    ppermute x7, starting transfers between devices, over_groups(): return lax.ppermute(array, 'box', pairs)  16.8 us
    pallas_call x6, Pallas kernels, call(): pl.pallas_call(kernel, out_shape=outs, in_specs=[VMEM] * len(args), out_s...  9.39 us
    ppermute x6, starting transfers between devices, over_members(): return array if mask == 0 else lax.ppermute(array, 'box', pairs)  6.98 us
    ppermute x6, waiting for transfers between devices, over_members(): return array if mask == 0 else lax.ppermute(array, 'box', pairs)  5.82 us
    ppermute x3, starting transfers between devices, over_row(): return lax.ppermute(array, 'row', [(r, r ^ mask) for r in range(row_size)])  3.04 us
  transfers between devices with their start and end apart: 18, of which 10 were waited for; matrix products, arithmetic and copies ran while one was open for 0% of the time, Pallas kernels for 2%

profile of v4, /device:TPU:0, one launch (start us, length us, event | category | flops | bytes accessed | tf_op | source)
XLA Modules:
  0.0 137.4 jit_solution(14850682165619064774)
XLA Ops:
  6.5 3.0 %collective-permute-start.5 = (bf16[2,256,512]{2,1,0:T(8,128)(2,1)}, bf16[2,256,512]{2,1,0:T(8,128)(2,1)S(1)}, u32[]{:S(2)}, u32[]{:S(2)}) collective-permute-start(bf16[2,256,512]{2,1,0:T(8,128)(2,1)} %refs_4_.1), channel_id=1, source_target_pairs={{0,16},{8,24},{16,0},{24,8},{1,17},{9,25},{17,1},{25,9},{2,18},{10... | collective-permute-start | bytes 1572872 | tf_op jit(solution)/shard_map/ppermute | solution.py:213
  9.5 1.1 copy-done
  10.7 2.7 %collective-permute-start = (bf16[2,128,128]{2,1,0:T(8,128)(2,1)S(1)}, bf16[2,128,128]{2,1,0:T(8,128)(2,1)S(1)}, u32[]{:S(2)}, u32[]{:S(2)}) collective-permute-start(bf16[2,128,128]{2,1,0:T(8,128)(2,1)S(1)} %get-tuple-element.36), channel_id=1, source_target_pairs={{0,4},{1,5},{2,6},{3,7},{4,0},{5,1},{6,2},{7,3},{8,12},{9,13},{10,... | collective-permute-start | bytes 196616 | tf_op jit(solution)/shard_map/ppermute | solution.py:223
  13.3 1.3 collective-permute-start.1
  14.6 3.6 %collective-permute-start.2 = (bf16[2,128,128]{2,1,0:T(8,128)(2,1)S(1)}, bf16[2,128,128]{2,1,0:T(8,128)(2,1)S(1)}, u32[]{:S(2)}, u32[]{:S(2)}) collective-permute-start(bf16[2,128,128]{2,1,0:T(8,128)(2,1)S(1)} %get-tuple-element.38), channel_id=1, source_target_pairs={{0,6},{1,7},{2,4},{3,5},{4,2},{5,3},{6,0},{7,1},{8,14},{9,15},{10,... | collective-permute-start | bytes 196616 | tf_op jit(solution)/shard_map/ppermute | solution.py:223
  18.2 0.2 collective-permute-start.3
  18.4 1.4 %copy-done.7 = bf16[1,3,1,4,4,128,128]{6,5,4,3,2,1,0:T(8,128)(2,1)S(1)} copy-done((bf16[1,3,1,4,4,128,128]{6,5,4,3,2,1,0:T(8,128)(2,1)S(1)}, bf16[1,3,1,4,4,128,128]{6,5,4,3,2,1,0:T(8,128)(2,1)}, u32[]{:S(2)}) %copy-start.7) | copy-done | bytes 1572888
  19.8 1.1 copy-done.14
  21.0 1.1 copy-done.15
  22.1 1.0 copy-done.20
  23.1 1.4 %weights.1 = (bf16[3,4,128,512]{3,2,1,0:T(8,128)(2,1)S(1)}, bf16[3,4,1,128,512]{4,3,2,1,0:T(8,128)(2,1)S(1)}, bf16[1024,512]{1,0:T(8,128)(2,1)S(1)}, bf16[1024,256]{1,0:T(8,128)(2,1)S(1)}) custom-call(bf16[1,3,1,4,4,128,128]{6,5,4,3,2,1,0:T(8,128)(2,1)S(1)} %copy-done.7, bf16[1,3,1,8,128,128]{5,4,3,2,1,0:T(8,128)(2,1)S(1)} %copy-done.14, ...), custom_call_target="tpu_custom_call" | custom-call | flops 603979776 | bytes 8257536 | tf_op jit(solution)/shard_map/weights/pallas_call | solution.py:228
  24.5 0.0 copy-start.2
  24.5 0.0 copy-start.12
  24.5 0.0 collective-permute-done.refs_0_
  24.5 0.1 collective-permute-start.4
  24.6 0.0 collective-permute-done.1.refs_1_
  24.6 0.0 collective-permute-done.2.refs_2_
  24.6 0.6 collective-permute-done.3.refs_3_
  25.3 0.0 collective-permute-done.5.refs_6_
  25.3 0.0 collective-permute-start.6
  25.3 1.3 collective-permute-done.4.refs_5_
  26.5 0.7 collective-permute-done.6.refs_7_
  27.3 1.3 off_levels.1
  28.6 1.0 copy-done.8
  29.6 1.0 copy-done.9
  30.6 0.0 reduce-scatter.3.cloned.1.call-update
  30.6 0.0 copy-start.1
  30.6 0.0 reduce-scatter.5.cloned.1.call-start
  30.6 3.2 %collective-permute-start.8 = (bf16[4,128,128]{2,1,0:T(8,128)(2,1)S(1)}, bf16[4,128,128]{2,1,0:T(8,128)(2,1)S(1)}, u32[]{:S(2)}, u32[]{:S(2)}) collective-permute-start(bf16[4,128,128]{2,1,0:T(8,128)(2,1)S(1)} %get-tuple-element.45), channel_id=1, source_target_pairs={{0,4},{1,5},{2,6},{3,7},{4,0},{5,1},{6,2},{7,3},{8,12},{9,13},{10,... | collective-permute-start | bytes 393224 | tf_op jit(solution)/shard_map/ppermute | solution.py:223
  33.9 6.7 %collective-permute-done.8.refs_0_.refs_5_ = bf16[4,128,128]{2,1,0:T(8,128)(2,1)S(1)} collective-permute-done((bf16[4,128,128]{2,1,0:T(8,128)(2,1)S(1)}, bf16[4,128,128]{2,1,0:T(8,128)(2,1)S(1)}, u32[]{:S(2)}, u32[]{:S(2)}) %collective-permute-start.8) | collective-permute-done | bytes 131104 | tf_op jit(solution)/shard_map/ppermute | solution.py:223
  40.6 1.2 copy-done.10
  41.8 1.6 %own_levels.1 = (bf16[9,128,128]{2,1,0:T(8,128)(2,1)S(1)}, bf16[9,128,128]{2,1,0:T(8,128)(2,1)}, bf16[9,128,128]{2,1,0:T(8,128)(2,1)}, bf16[9,128,128]{2,1,0:T(8,128)(2,1)}) custom-call(bf16[2,512,512]{2,1,0:T(8,128)(2,1)S(1)} %copy-done.10, bf16[3,4,128,512]{3,2,1,0:T(8,128)(2,1)S(1)} %get-tuple-element.34.up_own, ...), custom_call_target="tpu_custom_call" | custom-call | flops 536870912 | bytes 3932160 | tf_op jit(solution)/shard_map/own_levels/pallas_call | solution.py:228
  43.4 0.7 copy-done.21
  44.1 0.9 collective-permute-start.9
  45.1 0.3 collective-permute-start.10
  45.3 2.3 %collective-permute-start.11 = (bf16[9,128,128]{2,1,0:T(8,128)(2,1)}, bf16[9,128,128]{2,1,0:T(8,128)(2,1)}, u32[]{:S(2)}, u32[]{:S(2)}) collective-permute-start(bf16[9,128,128]{2,1,0:T(8,128)(2,1)} %get-tuple-element.49), channel_id=1, source_target_pairs={{0,3},{1,2},{2,1},{3,0},{4,7},{5,6},{6,5},{7,4},{8,11},{9,10},{10,... | collective-permute-start | bytes 884744 | tf_op jit(solution)/shard_map/ppermute | solution.py:217
  47.6 20.4 %reduce-scatter.3.cloned.1.call-done = bf16[1,2,1,128,512]{4,3,1,2,0:T(8,128)(2,1)} async-done(((bf16[4,2,1,128,512]{4,3,1,2,0:T(8,128)(2,1)}), bf16[1,2,1,128,512]{4,3,1,2,0:T(8,128)(2,1)}) %reduce-scatter.3.cloned.1.call-update) | async-done | bytes 262160 | tf_op jit(solution)/shard_map/reduce_scatter | solution.py:278
  68.0 3.7 %collective-permute-start.7 = (bf16[2,128,512]{2,1,0:T(8,128)(2,1)}, bf16[2,128,512]{2,1,0:T(8,128)(2,1)S(1)}, u32[]{:S(2)}, u32[]{:S(2)}) collective-permute-start(bf16[2,128,512]{2,1,0:T(8,128)(2,1)} %bitcast.5), channel_id=1, source_target_pairs={{0,4},{1,5},{2,6},{3,7},{4,0},{5,1},{6,2},{7,3},{8,12},{9,13},{10,... | collective-permute-start | bytes 786440 | tf_op jit(solution)/shard_map/ppermute | solution.py:223
  71.6 0.0 collective-permute-done.9.refs_2_
  71.7 0.0 collective-permute-done.10.refs_3_
  71.7 0.0 collective-permute-done.11.refs_4_
  71.7 11.9 %collective-permute-done.7.refs_0_ = bf16[2,128,512]{2,1,0:T(8,128)(2,1)S(1)} collective-permute-done((bf16[2,128,512]{2,1,0:T(8,128)(2,1)}, bf16[2,128,512]{2,1,0:T(8,128)(2,1)S(1)}, u32[]{:S(2)}, u32[]{:S(2)}) %collective-permute-start.7) | collective-permute-done | bytes 262176 | tf_op jit(solution)/shard_map/ppermute | solution.py:223
  83.6 1.4 %copy-done.3 = bf16[3,4,1,128,512]{4,3,2,1,0:T(8,128)(2,1)S(1)} copy-done((bf16[3,4,1,128,512]{4,3,2,1,0:T(8,128)(2,1)S(1)}, bf16[3,4,1,128,512]{4,3,2,1,0:T(8,128)(2,1)}, u32[]{:S(2)}) %copy-start.3) | copy-done | bytes 1572888
  85.0 1.2 copy-done.11
  86.2 1.2 copy-done.13
  87.5 1.0 copy-done.22
  88.4 3.5 %middle_levels.1 = (f32[1024,512]{1,0:T(8,128)S(1)}, bf16[4,1,1,128,512]{4,3,2,1,0:T(8,128)(2,1)S(1)}, bf16[4,128,128]{2,1,0:T(8,128)(2,1)S(1)}, bf16[4,128,128]...) custom-call(bf16[1,3,1,8,128,128]{5,4,3,2,1,0:T(8,128)(2,1)S(1)} %copy-done.1, ...), custom_call_target="tpu_custom_call" | custom-call | flops 1342177280 | bytes 11534336 | tf_op jit(solution)/shard_map/middle_levels/pallas_call | solution.py:228
  91.9 1.3 copy-done.5
  93.2 0.8 copy-done.19
  94.0 0.7 copy-done.23
  94.7 0.6 copy-done.24
  95.3 0.0 reduce-scatter.5.cloned.1.call-update
  95.3 19.5 %reduce-scatter.5.cloned.1.call-done = bf16[1,1,1,128,512]{4,3,2,1,0:T(8,128)(2,1)} async-done(((bf16[4,1,1,128,512]{4,3,2,1,0:T(8,128)(2,1)}), bf16[1,1,1,128,512]{4,3,2,1,0:T(8,128)(2,1)}) %reduce-scatter.5.cloned.1.call-update) | async-done | bytes 131088 | tf_op jit(solution)/shard_map/reduce_scatter | solution.py:278
  114.8 0.1 collective-permute-start.13
  115.0 0.9 collective-permute-start.14
  115.9 2.4 %collective-permute-start.15 = (bf16[4,128,128]{2,1,0:T(8,128)(2,1)S(1)}, bf16[4,128,128]{2,1,0:T(8,128)(2,1)S(1)}, u32[]{:S(2)}, u32[]{:S(2)}) collective-permute-start(bf16[4,128,128]{2,1,0:T(8,128)(2,1)S(1)} %get-tuple-element.58), channel_id=1, source_target_pairs={{0,3},{1,2},{2,1},{3,0},{4,7},{5,6},{6,5},{7,4},{8,11},{9,10},{10,... | collective-permute-start | bytes 393224 | tf_op jit(solution)/shard_map/ppermute | solution.py:217
  118.3 2.2 %collective-permute-start.12 = (bf16[1,128,512]{2,1,0:T(8,128)(2,1)}, bf16[1,128,512]{2,1,0:T(8,128)(2,1)S(1)}, u32[]{:S(2)}, u32[]{:S(2)}) collective-permute-start(bf16[1,128,512]{2,1,0:T(8,128)(2,1)} %bitcast.6), channel_id=1, source_target_pairs={{0,4},{1,5},{2,6},{3,7},{4,0},{5,1},{6,2},{7,3},{8,12},{9,13},{10,... | collective-permute-start | bytes 393224 | tf_op jit(solution)/shard_map/ppermute | solution.py:223
  120.5 0.3 collective-permute-done.13.refs_2_
  120.8 1.9 %collective-permute-done.14.refs_3_ = bf16[4,128,128]{2,1,0:T(8,128)(2,1)S(1)} collective-permute-done((bf16[4,128,128]{2,1,0:T(8,128)(2,1)}, bf16[4,128,128]{2,1,0:T(8,128)(2,1)S(1)}, u32[]{:S(2)}, u32[]{:S(2)}) %collective-permute-start.14) | collective-permute-done | bytes 131104 | tf_op jit(solution)/shard_map/ppermute | solution.py:217
  122.7 3.6 %collective-permute-done.15.refs_4_ = bf16[4,128,128]{2,1,0:T(8,128)(2,1)S(1)} collective-permute-done((bf16[4,128,128]{2,1,0:T(8,128)(2,1)S(1)}, bf16[4,128,128]{2,1,0:T(8,128)(2,1)S(1)}, u32[]{:S(2)}, u32[]{:S(2)}) %collective-permute-start.15) | collective-permute-done | bytes 131104 | tf_op jit(solution)/shard_map/ppermute | solution.py:217
  126.3 0.0 collective-permute-done.12.refs_0_
  126.3 1.6 %copy-done.6 = f32[1024,512]{1,0:T(8,128)S(1)} copy-done((f32[1024,512]{1,0:T(8,128)S(1)}, f32[1024,512]{1,0:T(8,128)}, u32[]{:S(2)}) %copy-start.6) | copy-done | bytes 2097176
  127.9 1.0 copy-done.18
  129.0 1.6 %last_levels.1 = bf16[1,1024,512]{2,1,0:T(8,128)(2,1)} custom-call(bf16[1,3,1,8,128,128]{5,4,3,2,1,0:T(8,128)(2,1)S(1)} %copy-done.1, bf16[1024,256]{1,0:T(8,128)(2,1)S(1)} %copy-done.18, f32[1024,512]{1,0:T(8,128)S(1)} %copy-done.6, bf16[1,128,512]{2,1,0:T(8,128)(2,1)S(1)} %collective-permute-done.12.refs_0_, ...), custom_call_target="tpu_custom_call" | custom-call | flops 335544320 | bytes 5111808 | tf_op jit(solution)/shard_map/last_levels/pallas_call | solution.py:228
  (30 shorter events, 0.1 us)
Async XLA Ops:
  6.5 61.5 %reduce-scatter.3.cloned.1.call-start = ((), (), s32[]{:S(2)}) async-start(), calls=%async_computation.2 | async-start | bytes 1310720 | tf_op jit(solution)/shard_map/reduce_scatter | solution.py:278
  6.5 18.7 %collective-permute-start.5 = (bf16[2,256,512]{2,1,0:T(8,128)(2,1)}, bf16[2,256,512]{2,1,0:T(8,128)(2,1)S(1)}, u32[]{:S(2)}, u32[]{:S(2)}) collective-permute-start(bf16[2,256,512]{2,1,0:T(8,128)(2,1)} %refs_4_.1), channel_id=1, source_target_pairs={{0,16},{8,24},{16,0},{24,8},{1,17},{9,25},{17,1},{25,9},{2,18},{10... | collective-permute-start | bytes 1572872 | tf_op jit(solution)/shard_map/ppermute | solution.py:213
  9.5 1.1 copy-start
  10.7 13.9 %collective-permute-start = (bf16[2,128,128]{2,1,0:T(8,128)(2,1)S(1)}, bf16[2,128,128]{2,1,0:T(8,128)(2,1)S(1)}, u32[]{:S(2)}, u32[]{:S(2)}) collective-permute-start(bf16[2,128,128]{2,1,0:T(8,128)(2,1)S(1)} %get-tuple-element.36), channel_id=1, source_target_pairs={{0,4},{1,5},{2,6},{3,7},{4,0},{5,1},{6,2},{7,3},{8,12},{9,13},{10,... | collective-permute-start | bytes 196616 | tf_op jit(solution)/shard_map/ppermute | solution.py:223
  13.3 11.3 %collective-permute-start.1 = (bf16[2,128,128]{2,1,0:T(8,128)(2,1)S(1)}, bf16[2,128,128]{2,1,0:T(8,128)(2,1)S(1)}, u32[]{:S(2)}, u32[]{:S(2)}) collective-permute-start(bf16[2,128,128]{2,1,0:T(8,128)(2,1)S(1)} %get-tuple-element.37), channel_id=1, source_target_pairs={{0,5},{1,4},{2,7},{3,6},{4,1},{5,0},{6,3},{7,2},{8,13},{9,12},{10,... | collective-permute-start | bytes 196616 | tf_op jit(solution)/shard_map/ppermute | solution.py:223
  14.6 10.1 %collective-permute-start.2 = (bf16[2,128,128]{2,1,0:T(8,128)(2,1)S(1)}, bf16[2,128,128]{2,1,0:T(8,128)(2,1)S(1)}, u32[]{:S(2)}, u32[]{:S(2)}) collective-permute-start(bf16[2,128,128]{2,1,0:T(8,128)(2,1)S(1)} %get-tuple-element.38), channel_id=1, source_target_pairs={{0,6},{1,7},{2,4},{3,5},{4,2},{5,3},{6,0},{7,1},{8,14},{9,15},{10,... | collective-permute-start | bytes 196616 | tf_op jit(solution)/shard_map/ppermute | solution.py:223
  18.2 9.1 %copy-start.4 = (bf16[1,3,4,256,128]{4,3,2,1,0:T(8,128)(2,1)S(1)}, bf16[1,3,4,256,128]{4,3,2,1,0:T(8,128)(2,1)}, u32[]{:S(2)}) copy-start(bf16[1,3,4,256,128]{4,3,2,1,0:T(8,128)(2,1)} %basis.3) | copy-start | bytes 2359300
  18.2 7.1 %collective-permute-start.3 = (bf16[2,128,128]{2,1,0:T(8,128)(2,1)S(1)}, bf16[2,128,128]{2,1,0:T(8,128)(2,1)S(1)}, u32[]{:S(2)}, u32[]{:S(2)}) collective-permute-start(bf16[2,128,128]{2,1,0:T(8,128)(2,1)S(1)} %get-tuple-element.39), channel_id=1, source_target_pairs={{0,7},{1,6},{2,5},{3,4},{4,3},{5,2},{6,1},{7,0},{8,15},{9,14},{10,... | collective-permute-start | bytes 196616 | tf_op jit(solution)/shard_map/ppermute | solution.py:223
  18.4 1.4 %copy-start.7 = (bf16[1,3,1,4,4,128,128]{6,5,4,3,2,1,0:T(8,128)(2,1)S(1)}, bf16[1,3,1,4,4,128,128]{6,5,4,3,2,1,0:T(8,128)(2,1)}, u32[]{:S(2)}) copy-start(bf16[1,3,1,4,4,128,128]{6,5,4,3,2,1,0:T(8,128)(2,1)} %first.1) | copy-start | bytes 4718596
  19.8 1.1 copy-start.14
  21.0 1.1 copy-start.15
  22.1 1.0 copy-start.20
  23.1 1.4 %copy-start.16 = (bf16[2,256,512]{2,1,0:T(8,128)(2,1)S(1)}, bf16[2,256,512]{2,1,0:T(8,128)(2,1)}, u32[]{:S(2)}) copy-start(bf16[2,256,512]{2,1,0:T(8,128)(2,1)} %refs_4_.1) | copy-start | bytes 1572868
  24.5 4.1 %copy-start.2 = (bf16[3,4,1,128,512]{4,3,2,1,0:T(8,128)(2,1)}, bf16[3,4,1,128,512]{4,3,2,1,0:T(8,128)(2,1)S(1)}, u32[]{:S(2)}) copy-start(bf16[3,4,1,128,512]{4,3,2,1,0:T(8,128)(2,1)S(1)} %get-tuple-element.35.up_other) | copy-start | bytes 4718596
  24.5 4.1 %copy-start.12 = (bf16[1024,512]{1,0:T(8,128)(2,1)}, bf16[1024,512]{1,0:T(8,128)(2,1)S(1)}, u32[]{:S(2)}) copy-start(bf16[1024,512]{1,0:T(8,128)(2,1)S(1)} %get-tuple-element.33.row_mats) | copy-start | bytes 3145732
  24.5 4.1 %copy-start.17 = (bf16[1024,256]{1,0:T(8,128)(2,1)}, bf16[1024,256]{1,0:T(8,128)(2,1)S(1)}, u32[]{:S(2)}) copy-start(bf16[1024,256]{1,0:T(8,128)(2,1)S(1)} %get-tuple-element.32.row_mats) | copy-start | bytes 1572868
  24.5 2.0 %collective-permute-start.4 = (bf16[2,256,512]{2,1,0:T(8,128)(2,1)S(1)}, bf16[2,256,512]{2,1,0:T(8,128)(2,1)S(1)}, u32[]{:S(2)}, u32[]{:S(2)}) collective-permute-start(bf16[2,256,512]{2,1,0:T(8,128)(2,1)S(1)} %copy-done.16), channel_id=1, source_target_pairs={{0,8},{8,0},{16,24},{24,16},{1,9},{9,1},{17,25},{25,17},{2,10},{10... | collective-permute-start | bytes 1572872 | tf_op jit(solution)/shard_map/ppermute | solution.py:213
  25.3 2.0 %collective-permute-start.6 = (bf16[2,256,512]{2,1,0:T(8,128)(2,1)S(1)}, bf16[2,256,512]{2,1,0:T(8,128)(2,1)S(1)}, u32[]{:S(2)}, u32[]{:S(2)}) collective-permute-start(bf16[2,256,512]{2,1,0:T(8,128)(2,1)S(1)} %collective-permute-done.5.refs_6_), channel_id=1, source_target_pairs={{0,8},{8,0},{16,24},{24,16},{1,9},{9,1},{17,25},{25,17},{2,10},{10... | collective-permute-start | bytes 1572872 | tf_op jit(solution)/shard_map/ppermute | solution.py:213
  28.6 1.0 copy-start.8
  29.6 1.0 copy-start.9
  30.6 53.0 %copy-start.1 = (bf16[1,3,1,8,128,128]{5,4,3,2,1,0:T(8,128)(2,1)S(1)}, bf16[1,3,1,8,128,128]{5,4,3,2,1,0:T(8,128)(2,1)}, u32[]{:S(2)}) copy-start(bf16[1,3,1,8,128,128]{5,4,3,2,1,0:T(8,128)(2,1)} %third.5) | copy-start | bytes 2359300
  30.6 84.2 %reduce-scatter.5.cloned.1.call-start = ((), (), s32[]{:S(2)}) async-start(), calls=%async_computation.3 | async-start | bytes 655360 | tf_op jit(solution)/shard_map/reduce_scatter | solution.py:278
  30.6 9.9 %collective-permute-start.8 = (bf16[4,128,128]{2,1,0:T(8,128)(2,1)S(1)}, bf16[4,128,128]{2,1,0:T(8,128)(2,1)S(1)}, u32[]{:S(2)}, u32[]{:S(2)}) collective-permute-start(bf16[4,128,128]{2,1,0:T(8,128)(2,1)S(1)} %get-tuple-element.45), channel_id=1, source_target_pairs={{0,4},{1,5},{2,6},{3,7},{4,0},{5,1},{6,2},{7,3},{8,12},{9,13},{10,... | collective-permute-start | bytes 393224 | tf_op jit(solution)/shard_map/ppermute | solution.py:223
  40.6 1.2 copy-start.10
  43.4 0.7 copy-start.21
  44.1 27.5 %collective-permute-start.9 = (bf16[9,128,128]{2,1,0:T(8,128)(2,1)}, bf16[9,128,128]{2,1,0:T(8,128)(2,1)}, u32[]{:S(2)}, u32[]{:S(2)}) collective-permute-start(bf16[9,128,128]{2,1,0:T(8,128)(2,1)} %get-tuple-element.47), channel_id=1, source_target_pairs={{0,1},{1,0},{2,3},{3,2},{4,5},{5,4},{6,7},{7,6},{8,9},{9,8},{10,11... | collective-permute-start | bytes 884744 | tf_op jit(solution)/shard_map/ppermute | solution.py:217
  45.1 26.6 %collective-permute-start.10 = (bf16[9,128,128]{2,1,0:T(8,128)(2,1)}, bf16[9,128,128]{2,1,0:T(8,128)(2,1)}, u32[]{:S(2)}, u32[]{:S(2)}) collective-permute-start(bf16[9,128,128]{2,1,0:T(8,128)(2,1)} %get-tuple-element.48), channel_id=1, source_target_pairs={{0,2},{1,3},{2,0},{3,1},{4,6},{5,7},{6,4},{7,5},{8,10},{9,11},{10,... | collective-permute-start | bytes 884744 | tf_op jit(solution)/shard_map/ppermute | solution.py:217
  45.3 26.3 %collective-permute-start.11 = (bf16[9,128,128]{2,1,0:T(8,128)(2,1)}, bf16[9,128,128]{2,1,0:T(8,128)(2,1)}, u32[]{:S(2)}, u32[]{:S(2)}) collective-permute-start(bf16[9,128,128]{2,1,0:T(8,128)(2,1)} %get-tuple-element.49), channel_id=1, source_target_pairs={{0,3},{1,2},{2,1},{3,0},{4,7},{5,6},{6,5},{7,4},{8,11},{9,10},{10,... | collective-permute-start | bytes 884744 | tf_op jit(solution)/shard_map/ppermute | solution.py:217
  68.0 15.6 %collective-permute-start.7 = (bf16[2,128,512]{2,1,0:T(8,128)(2,1)}, bf16[2,128,512]{2,1,0:T(8,128)(2,1)S(1)}, u32[]{:S(2)}, u32[]{:S(2)}) collective-permute-start(bf16[2,128,512]{2,1,0:T(8,128)(2,1)} %bitcast.5), channel_id=1, source_target_pairs={{0,4},{1,5},{2,6},{3,7},{4,0},{5,1},{6,2},{7,3},{8,12},{9,13},{10,... | collective-permute-start | bytes 786440 | tf_op jit(solution)/shard_map/ppermute | solution.py:223
  83.6 1.4 %copy-start.3 = (bf16[3,4,1,128,512]{4,3,2,1,0:T(8,128)(2,1)S(1)}, bf16[3,4,1,128,512]{4,3,2,1,0:T(8,128)(2,1)}, u32[]{:S(2)}) copy-start(bf16[3,4,1,128,512]{4,3,2,1,0:T(8,128)(2,1)} %copy-done.2) | copy-start | bytes 4718596
  85.0 1.2 copy-start.11
  86.2 1.2 copy-start.13
  87.5 1.0 copy-start.22
  91.9 1.3 copy-start.5
  93.2 0.8 copy-start.19
  94.0 0.7 copy-start.23
  94.7 0.6 copy-start.24
  114.8 6.0 %collective-permute-start.13 = (bf16[4,128,128]{2,1,0:T(8,128)(2,1)}, bf16[4,128,128]{2,1,0:T(8,128)(2,1)S(1)}, u32[]{:S(2)}, u32[]{:S(2)}) collective-permute-start(bf16[4,128,128]{2,1,0:T(8,128)(2,1)} %copy-done.24), channel_id=1, source_target_pairs={{0,1},{1,0},{2,3},{3,2},{4,5},{5,4},{6,7},{7,6},{8,9},{9,8},{10,11... | collective-permute-start | bytes 393224 | tf_op jit(solution)/shard_map/ppermute | solution.py:217
  115.0 7.7 %collective-permute-start.14 = (bf16[4,128,128]{2,1,0:T(8,128)(2,1)}, bf16[4,128,128]{2,1,0:T(8,128)(2,1)S(1)}, u32[]{:S(2)}, u32[]{:S(2)}) collective-permute-start(bf16[4,128,128]{2,1,0:T(8,128)(2,1)} %copy-done.23), channel_id=1, source_target_pairs={{0,2},{1,3},{2,0},{3,1},{4,6},{5,7},{6,4},{7,5},{8,10},{9,11},{10,... | collective-permute-start | bytes 393224 | tf_op jit(solution)/shard_map/ppermute | solution.py:217
  115.9 10.4 %collective-permute-start.15 = (bf16[4,128,128]{2,1,0:T(8,128)(2,1)S(1)}, bf16[4,128,128]{2,1,0:T(8,128)(2,1)S(1)}, u32[]{:S(2)}, u32[]{:S(2)}) collective-permute-start(bf16[4,128,128]{2,1,0:T(8,128)(2,1)S(1)} %get-tuple-element.58), channel_id=1, source_target_pairs={{0,3},{1,2},{2,1},{3,0},{4,7},{5,6},{6,5},{7,4},{8,11},{9,10},{10,... | collective-permute-start | bytes 393224 | tf_op jit(solution)/shard_map/ppermute | solution.py:217
  118.3 8.0 %collective-permute-start.12 = (bf16[1,128,512]{2,1,0:T(8,128)(2,1)}, bf16[1,128,512]{2,1,0:T(8,128)(2,1)S(1)}, u32[]{:S(2)}, u32[]{:S(2)}) collective-permute-start(bf16[1,128,512]{2,1,0:T(8,128)(2,1)} %bitcast.6), channel_id=1, source_target_pairs={{0,4},{1,5},{2,6},{3,7},{4,0},{5,1},{6,2},{7,3},{8,12},{9,13},{10,... | collective-permute-start | bytes 393224 | tf_op jit(solution)/shard_map/ppermute | solution.py:223
  126.3 1.6 %copy-start.6 = (f32[1024,512]{1,0:T(8,128)S(1)}, f32[1024,512]{1,0:T(8,128)}, u32[]{:S(2)}) copy-start(f32[1024,512]{1,0:T(8,128)} %copy-done.5) | copy-start | bytes 6291460
  127.9 1.0 copy-start.18
Sparse Core Ops, SparseCore 0:
  30.7 37.2 reduce-scatter.2
  95.5 19.3 reduce-scatter.4

commit v5 on v4

--- a/solution.py
+++ b/solution.py
@@ -38,20 +38,23 @@
     return out
 
 
-def pick_kernel(radix, groups, offs, third, *outs):
-    group, member = place(radix)
+def pick_kernel(radix, groups, third, *outs):
+    group, _ = place(radix)
     at = 0
-    for delta in range(1, groups):
-        base = wrap(group + delta, groups) * radix
-        for i in range(radix):
-            for j in range(offs):
-                outs[at][j] = third[0, j, 0, base + jnp.bitwise_xor(member, i)]
+    for j in range(third.shape[1]):
+        for delta in range(1, groups):
+            base = wrap(group + delta, groups) * radix
+            for k in range(radix):
+                outs[at][k] = third[0, j, 0, base + k]
             at += 1
-    for delta in range(1, groups):
-        base = wrap(group + delta, groups) * radix
-        for k in range(radix):
-            outs[at][k] = third[0, offs, 0, base + k]
-        at += 1
+
+
+def share_kernel(radix, *refs):
+    rides, outs = take(refs, len(refs) - radix + 1, radix - 1)
+    _, member = place(radix)
+    for d, ride in enumerate(rides):
+        for i, ref in enumerate(outs):
+            ref[d] = ride[jnp.bitwise_xor(member, i + 1)]
 
 
 def leaf_order(row, leaves, row_size):
@@ -102,75 +105,86 @@
             ref[at * tiles + c] = coef[i * rank : (i + 1) * rank, c * rank : (c + 1) * rank]
 
 
-def put_other(mats, leaf, other, at, member):
-    radix, _, less, rank, width = other.shape
-    coef = dot(mats, leaf).astype(BF16)
-    for i in range(radix):
-        part = coef[i * less * rank : (i + 1) * less * rank]
-        other[jnp.bitwise_xor(member, i), at] = part.reshape(less, rank, width)
-
-
-def off_kernel(radix, groups, pieces, basis, up_other, *refs):
-    thirds, parts, (leaf_ref, other) = take(refs, (groups - 1) * radix, pieces, 2)
+def off_kernel(j, radix, groups, pieces, basis, up_other, *refs):
+    rides, shared, parts, (leaf_ref, keep, wait, sent) = take(refs, groups - 1, radix - 1, pieces, 4)
+    row = lax.axis_index("row")
     _, member = place(radix)
-    row = lax.axis_index("row")
     leaves, leaf_rows, rank = basis.shape[2], basis.shape[3], basis.shape[4]
-    rows = parts[0].shape[1]
+    rows = parts[0].shape[-2]
     per_leaf = leaf_rows // rows
     order = leaf_order(row, leaves, pieces)
     less = groups - 1
-    for j in range(parts[0].shape[0]):
-        leaf = []
-        for t in range(leaves):
-            total = None
-            for u in range(per_leaf):
-                start = jnp.bitwise_xor(lax.rem(row, per_leaf), u) * rows
-                if per_leaf == 1:
-                    mat = basis[0, j, order[t]]
-                else:
-                    mat = basis[0, j, order[t], pl.ds(pl.multiple_of(start, rows), rows)]
-                part = dot_t(mat, parts[t * per_leaf + u][j])
-                total = part if total is None else total + part
-            leaf.append(total.astype(BF16))
-        leaf = jnp.concatenate(leaf, axis=0)
-        leaf_ref[j] = leaf
-        mats = other_mats(j, lambda i, d: thirds[d * radix + i][j], up_other)
-        put_other(mats, leaf, other, j, member)
-
-
-def own_kernel(members, leaf, up_own, *refs):
-    rides, own = take(refs, len(refs) - len(members), len(members))
-    _, member = place(up_own.shape[1])
-    for j in range(leaf.shape[0]):
-        put_own(up_own.at[j], members, leaf[j], own, j)
+    leaf = []
+    for t in range(leaves):
+        total = None
+        for u in range(per_leaf):
+            start = jnp.bitwise_xor(lax.rem(row, per_leaf), u) * rows
+            if per_leaf == 1:
+                mat = basis[0, j, order[t]]
+            else:
+                mat = basis[0, j, order[t], pl.ds(pl.multiple_of(start, rows), rows)]
+            ref = parts[t * per_leaf + u]
+            part = dot_t(mat, ref[j] if ref.shape[0] > 1 else ref[0])
+            total = part if total is None else total + part
+        leaf.append(total.astype(BF16))
+    leaf = jnp.concatenate(leaf, axis=0)
+    leaf_ref[...] = leaf
+    mats = other_mats(j, lambda i, d: rides[d][member] if i == 0 else shared[i - 1][d], up_other)
+    coef = dot(mats, leaf).astype(BF16)
+    blocks = [
+        coef[i * less * rank : (i + 1) * less * rank].reshape(less, rank, coef.shape[1]) for i in range(radix)
+    ]
+    keep[...] = blocks[0]
+    wait[...] = blocks[2]
+    sent[0] = blocks[1]
+    sent[1] = blocks[3]
+
+
+def own_kernel(j, radix, leaf, up_own, *refs):
+    rides, own = take(refs, len(refs) - radix, radix)
+    _, member = place(radix)
+    put_own(up_own.at[j], range(radix), leaf[...], own, 0)
     for d, ride in enumerate(rides):
-        for i, ref in zip(members, own):
+        for i, ref in enumerate(own):
             ref[ref.shape[0] - len(rides) + d] = ride[jnp.bitwise_xor(member, i)]
 
 
-def group_coefs(j, at, tiles, own, crossed, third, radix):
+def stage_kernel(wait, got, out):
+    out[...] = (wait[...].astype(F32) + got[1].astype(F32)).astype(BF16)
+
+
+def total_kernel(keep, got, last, *outs):
+    for d, out in enumerate(outs):
+        out[...] = (keep[d].astype(F32) + got[0, d].astype(F32) + last[d].astype(F32)).astype(BF16)
+
+
+def group_coefs(j, own, crossed, third, radix):
+    rank = third.shape[5]
+    tiles = crossed[0].shape[-1] // rank
     group, member = place(radix)
     mats = [third[0, j, 0, group * radix + jnp.bitwise_xor(member, i)] for i in range(radix)]
-    slots = [jnp.concatenate([ref[at * tiles + c] for c in range(tiles)], axis=1) for ref in own]
+    slots = [jnp.concatenate([ref[c] for c in range(tiles)], axis=1) for ref in own]
     total = dot(jnp.concatenate(mats, axis=1), jnp.concatenate(slots, axis=0))
-    return [total.astype(BF16)] + [ref[at] for ref in crossed]
+    return [total.astype(BF16)] + [ref[...] for ref in crossed]
 
 
 def middle_kernel(radix, groups, offs, third, rhs, basis, row_mats, up_own, up_other, *refs):
     less = groups - 1
-    crossed, own_in, rides, (residual_ref, other), own = take(refs, less, radix, less, 2, radix)
+    crossed, own_in, rides, (residual_ref,), own, other = take(
+        refs, offs * less, offs * radix, less, 1, radix, radix
+    )
     rank = basis.shape[4]
     tiles = rhs.shape[2] // rank
     _, member = place(radix)
 
     def third_of(i, d):
-        if i == 0:
-            return rides[d][member]
-        return own_in[i][offs * tiles + d]
+        return rides[d][member] if i == 0 else own_in[(offs - 1) * radix + i][tiles + d]
 
     coefs = []
     for j in range(offs):
-        coefs += group_coefs(j, j, tiles, own_in, crossed, third, radix)
+        coefs += group_coefs(
+            j, own_in[j * radix : (j + 1) * radix], crossed[j * less : (j + 1) * less], third, radix
+        )
     coefs = jnp.concatenate(coefs, axis=0)
     leaves, leaf_rows = basis.shape[2], basis.shape[3]
     leaf = []
@@ -180,14 +194,15 @@
         residual_ref[rows] = residual
         leaf.append(dot_t(basis[0, offs, k], residual.astype(BF16)).astype(BF16))
     leaf = jnp.concatenate(leaf, axis=0)
-    put_other(other_mats(offs, third_of, up_other), leaf, other, 0, member)
+    coef = dot(other_mats(offs, third_of, up_other), leaf).astype(BF16)
+    for i, ref in enumerate(other):
+        ref[...] = coef[i * less * rank : (i + 1) * less * rank].reshape(ref.shape)
     put_own(up_own.at[offs], range(radix), leaf, own, 0)
 
 
 def last_kernel(radix, groups, offs, third, row_mats, residual, *refs):
     crossed, own_in, (out,) = take(refs, groups - 1, radix, 1)
-    tiles = residual.shape[1] // third.shape[5]
-    coefs = jnp.concatenate(group_coefs(offs, 0, tiles, own_in, crossed, third, radix), axis=0)
+    coefs = jnp.concatenate(group_coefs(offs, own_in, crossed, third, radix), axis=0)
     out[0] = (residual[...] + dot(row_mats[...], coefs)).astype(BF16)
 
 
@@ -231,17 +246,19 @@
             in_specs=[VMEM] * len(args),
             out_specs=[VMEM] * len(outs),
             compiler_params=pltpu.CompilerParams(vmem_limit_bytes=min(16 * MIB + 2 * size, 56 * MIB)),
-            cost_estimate=pl.CostEstimate(flops=int(flops), bytes_accessed=int(size), transcendentals=0),
+            cost_estimate=pl.CostEstimate(flops=int(flops), bytes_accessed=0, transcendentals=0),
             name=name,
         )(*args)
 
     picked = call(
-        functools.partial(pick_kernel, radix, groups, offs),
+        functools.partial(pick_kernel, radix, groups),
         "pick_third",
         0,
-        [((offs, rank, rank), BF16)] * (less * radix) + [((radix, rank, rank), BF16)] * less,
+        [((radix, rank, rank), BF16)] * (butterflies * less),
         third_level,
     )
+    picked = [picked[j * less : (j + 1) * less] for j in range(butterflies)]
+
     up_own, up_other, off_rows, last_rows = call(
         functools.partial(weights_kernel, radix, groups, offs, row_size),
         "weights",
@@ -258,56 +275,74 @@
         out_basis,
     )
 
-    shifts = [(delta, i) for delta in range(1, groups) for i in range(radix)]
-    thirds = [over_groups(a, *shift) for a, shift in zip(picked, shifts)]
-    pieces = {0: solved, 1: over_row(after(solved, thirds[0]), 1)}
-    for mask in range(2, row_size, 2):
-        pieces[mask] = after(over_row(solved, mask), up_own, *thirds)
-        pieces[mask + 1] = over_row(pieces[mask], 1)
-    rides = [over_groups(after(a, pieces[2]), d + 1) for d, a in enumerate(picked[less * radix :])]
-    pieces = [pieces[mask] for mask in range(row_size)]
-
-    ride_shape = ((offs * tiles + less, rank, rank), BF16)
+    part = (less, rank, columns)
     other_flops = 2 * columns * rank * radix * less * depth
     own_flops = 2 * columns * rank * radix * depth
     leaf_flops = 2 * columns * rank * rows
     row_flops = 2 * columns * rank * (depth + groups * rows)
 
-    def add(other):
-        index_groups = [list(range(g * radix, (g + 1) * radix)) for g in range(groups)]
-        total = lax.psum_scatter(other, "box", scatter_dimension=0, axis_index_groups=index_groups)
-        return [over_groups(total[:, d], less - d) for d in range(less)], total
-
-    leaf, other = call(
-        functools.partial(off_kernel, radix, groups, row_size),
-        "off_levels",
-        offs * (leaf_flops + other_flops),
-        [((offs, depth, columns), BF16)]
-        + [((radix, offs, less, rank, columns), BF16)],
-        leaf_basis,
-        up_other,
-        *thirds,
-        *pieces,
-    )
-    crossed, total = add(other)
-    own = call(
-        functools.partial(own_kernel, range(radix)),
-        "own_levels",
-        offs * own_flops,
-        [ride_shape] * radix,
-        after(leaf, total),
-        up_own,
-        *rides,
-    )
-    own = [over_members(a, i) for i, a in enumerate(own)]
-
-    residual, other, *own = call(
+    beside = over_row(solved, 1)
+
+    def fetch(j, *come):
+        rides = [over_groups(after(a, *come), d + 1) for d, a in enumerate(picked[j])]
+        far = []
+        if j < offs:
+            far = [over_row(after(solved[j : j + 1], *come[:row_size]), mask) for mask in range(2, row_size, 2)]
+        return rides, far
+
+    rides, far = fetch(0)
+    held = [up_own]
+    crossed, owns = [], []
+    for j in range(offs):
+        far = [after(a, *held, *rides) for a in far]
+        shared = call(
+            functools.partial(share_kernel, radix),
+            "share",
+            0,
+            [((less, rank, rank), BF16)] * (radix - 1),
+            *[after(a, *held) for a in rides],
+        )
+        shared = [over_members(a, i + 1) for i, a in enumerate(shared)]
+        pieces = [solved, beside]
+        for a in far:
+            pieces += [a, over_row(a, 1)]
+        leaf, keep, wait, sent = call(
+            functools.partial(off_kernel, j, radix, groups, row_size),
+            "off_levels",
+            leaf_flops + other_flops,
+            [((depth, columns), BF16), (part, BF16), (part, BF16), ((2, *part), BF16)],
+            leaf_basis,
+            up_other,
+            *rides,
+            *shared,
+            *pieces,
+        )
+        rides, far = fetch(j + 1, *far, *rides, *shared)
+        final = j == offs - 1
+        got = over_members(after(sent, *(owns[0][2:] if final else [])), 1)
+        (staged,) = call(stage_kernel, "stage", 0, [(part, BF16)], wait, after(got, *rides, *far))
+        last = over_members(staged, 2)
+        sums = call(total_kernel, "total", 0, [(part[1:], BF16)] * less, keep, got, after(last, *crossed))
+        crossed += [over_groups(a, less - d) for d, a in enumerate(sums)]
+        own = call(
+            functools.partial(own_kernel, j, radix),
+            "own_levels",
+            own_flops,
+            [((tiles + (less if final else 0), rank, rank), BF16)] * radix,
+            after(leaf, got) if final else leaf,
+            up_own,
+            *(rides if final else []),
+        )
+        owns.append([own[0], own[1]] + [over_members(a, i) for i, a in enumerate(own) if i > 1])
+        held = [staged]
+    for own in owns:
+        own[1] = over_members(after(own[1], got), 1)
+
+    residual, *levels = call(
         functools.partial(middle_kernel, radix, groups, offs),
         "middle_levels",
         offs * row_flops + leaf_flops + other_flops + own_flops,
-        [((rows, columns), F32)]
-        + [((radix, 1, less, rank, columns), BF16)]
-        + [((tiles, rank, rank), BF16)] * radix,
+        [((rows, columns), F32)] + [((tiles, rank, rank), BF16)] * radix + [(part, BF16)] * radix,
         third_level,
         rhs,
         leaf_basis,
@@ -315,11 +350,14 @@
         up_own,
         up_other,
         *crossed,
-        *own,
+        *[a for own in owns for a in own],
         *rides,
     )
-    crossed, total = add(other)
-    own = [over_members(after(a, total) if i else a, i) for i, a in enumerate(own)]
+    own, other = levels[:radix], levels[radix:]
+    other = [over_members(a, i) for i, a in enumerate(other)]
+    sums = [sum(a[d].astype(F32) for a in other).astype(BF16) for d in range(less)]
+    crossed = [over_groups(a, less - d) for d, a in enumerate(sums)]
+    own = [over_members(after(a, *sums) if i else a, i) for i, a in enumerate(own)]
     return call(
         functools.partial(last_kernel, radix, groups, offs),
         "last_levels",

time: 138 us -> 96.4 us (0.70)
  waiting for transfers between devices: 67 us -> 48.3 us
  local copies, waits for them, and re-layouts: 20.6 us -> 4.74 us
  between operations: 13.6 us -> 0.18 us
  starting transfers between devices: 26.9 us -> 35 us
  Pallas kernels: 9.39 us -> 7.9 us
    reduce_scatter x2 -> x0, waiting for transfers between devices: 39.9 us -> none  [add(): lax.psum_scatter(other, 'box', scatter_dimension=0, axis_index_groups=ind...]
    ppermute x6 -> x22, waiting for transfers between devices: 5.82 us -> 33.9 us  [over_members(): return array if mask == 0 else lax.ppermute(array, 'box', pairs)]
    unnamed x50 -> x16, local copies, waits for them, and re-layouts: 20.6 us -> 3.56 us
    ppermute x6 -> x22, starting transfers between devices: 6.98 us -> 20.9 us  [over_members(): return array if mask == 0 else lax.ppermute(array, 'box', pairs)]
    ppermute x7 -> x6, starting transfers between devices: 16.8 us -> 10.5 us  [over_groups(): return lax.ppermute(array, 'box', pairs)]
    ppermute x7 -> x6, waiting for transfers between devices: 19.3 us -> 14.4 us  [over_groups(): return lax.ppermute(array, 'box', pairs)]
    ppermute x3 -> x5, waiting for transfers between devices: 2.01 us -> 0.01 us  [over_row(): return lax.ppermute(array, 'row', [(r, r ^ mask) for r in range(row_size)])]
    pallas_call x6 -> x14, Pallas kernels: 9.39 us -> 7.9 us  [call(): pl.pallas_call(kernel, out_shape=outs, in_specs=[VMEM] * len(args), out_s...]
  transfers between devices with their start and end apart: 18 -> 33, of which waited for: 10 -> 22; matrix products, arithmetic and copies ran while one was open for 0% -> 0% of each run, Pallas kernels for 2% -> 4%
where the time goes in v5:
time: 96.4 us; the launch traced here: 96.2 us
  waiting for transfers between devices  48.3 us (50%)
  starting transfers between devices  35 us (36%)
  Pallas kernels  7.9 us (8%)
  local copies, waits for them, and re-layouts  4.74 us (5%)
    ppermute x22, waiting for transfers between devices, over_members(): return array if mask == 0 else lax.ppermute(array, 'box', pairs)  33.9 us
    ppermute x22, starting transfers between devices, over_members(): return array if mask == 0 else lax.ppermute(array, 'box', pairs)  20.9 us
    ppermute x6, waiting for transfers between devices, over_groups(): return lax.ppermute(array, 'box', pairs)  14.4 us
    ppermute x6, starting transfers between devices, over_groups(): return lax.ppermute(array, 'box', pairs)  10.5 us
    pallas_call x14, Pallas kernels, call(): pl.pallas_call(kernel, out_shape=outs, in_specs=[VMEM] * len(args), out_s...  7.9 us
    ppermute x5, starting transfers between devices, over_row(): return lax.ppermute(array, 'row', [(r, r ^ mask) for r in range(row_size)])  3.61 us
    unnamed x16, local copies, waits for them, and re-layouts  3.56 us
  transfers between devices with their start and end apart: 33, of which 22 were waited for; matrix products, arithmetic and copies ran while one was open for 0% of the time, Pallas kernels for 4%

profile of v5, /device:TPU:0, one launch (start us, length us, event | category | flops | bytes accessed | tf_op | source)
XLA Modules:
  0.0 96.2 jit_solution(7495819043687159520)
XLA Ops:
  0.0 1.2 %fusion.1 = (bf16[1,256,512]{2,1,0:T(8,128)(2,1)S(1)}, bf16[1,256,512]{2,1,0:T(8,128)(2,1)S(1)}) fusion(bf16[2,256,512]{2,1,0:T(8,128)(2,1)} %refs_4_.3), kind=kLoop, calls=%fused_computation.2 | loop fusion | bytes 1048576 | tf_op jit(solution)/shard_map/slice | solution.py:290
  1.2 3.0 %collective-permute-start.5 = (bf16[1,256,512]{2,1,0:T(8,128)(2,1)S(1)}, bf16[1,256,512]{2,1,0:T(8,128)(2,1)S(1)}, u32[]{:S(2)}, u32[]{:S(2)}) collective-permute-start(bf16[1,256,512]{2,1,0:T(8,128)(2,1)S(1)} %get-tuple-element.116), channel_id=1, source_target_pairs={{0,16},{8,24},{16,0},{24,8},{1,17},{9,25},{17,1},{25,9},{2,18},{10... | collective-permute-start | bytes 786440 | tf_op jit(solution)/shard_map/ppermute | solution.py:228
  4.3 0.0 copy-start.1
  4.3 2.7 %collective-permute-start = (bf16[4,128,128]{2,1,0:T(8,128)(2,1)S(1)}, bf16[4,128,128]{2,1,0:T(8,128)(2,1)S(1)}, u32[]{:S(2)}, u32[]{:S(2)}) collective-permute-start(bf16[4,128,128]{2,1,0:T(8,128)(2,1)S(1)} %get-tuple-element.64), channel_id=1, source_target_pairs={{0,4},{1,5},{2,6},{3,7},{4,0},{5,1},{6,2},{7,3},{8,12},{9,13},{10,... | collective-permute-start | bytes 393224 | tf_op jit(solution)/shard_map/ppermute | solution.py:238
  6.9 1.4 %copy-done.3 = bf16[1,3,1,4,4,128,128]{6,5,4,3,2,1,0:T(8,128)(2,1)S(1)} copy-done((bf16[1,3,1,4,4,128,128]{6,5,4,3,2,1,0:T(8,128)(2,1)S(1)}, bf16[1,3,1,4,4,128,128]{6,5,4,3,2,1,0:T(8,128)(2,1)}, u32[]{:S(2)}) %copy-start.3) | copy-done | bytes 1572888
  8.4 1.1 %copy-done.6 = bf16[1,3,2,512,128]{4,3,2,1,0:T(8,128)(2,1)S(1)} copy-done((bf16[1,3,2,512,128]{4,3,2,1,0:T(8,128)(2,1)S(1)}, bf16[1,3,2,512,128]{4,3,2,1,0:T(8,128)(2,1)}, u32[]{:S(2)}) %copy-start.6) | copy-done | bytes 786456
  9.5 1.0 %copy-done.7 = bf16[1,3,1,2,2,128,128]{6,5,4,3,2,1,0:T(8,128)(2,1)S(1)} copy-done((bf16[1,3,1,2,2,128,128]{6,5,4,3,2,1,0:T(8,128)(2,1)S(1)}, bf16[1,3,1,2,2,128,128]{6,5,4,3,2,1,0:T(8,128)(2,1)}, u32[]{:S(2)}) %copy-start.7) | copy-done | bytes 393240
  10.5 1.4 %weights.1 = (bf16[3,4,128,512]{3,2,1,0:T(8,128)(2,1)S(1)}, bf16[3,4,1,128,512]{4,3,2,1,0:T(8,128)(2,1)S(1)}, bf16[1024,512]{1,0:T(8,128)(2,1)S(1)}, bf16[1024,256]{1,0:T(8,128)(2,1)S(1)}) custom-call(bf16[1,3,1,4,4,128,128]{6,5,4,3,2,1,0:T(8,128)(2,1)S(1)} %copy-done.3, bf16[1,3,1,8,128,128]{5,4,3,2,1,0:T(8,128)(2,1)S(1)} %copy-done.5, ...), custom_call_target="tpu_custom_call" | custom-call | flops 603979776 | tf_op jit(solution)/shard_map/weights/pallas_call | solution.py:243
  11.9 2.1 %collective-permute-done.refs_0_ = bf16[4,128,128]{2,1,0:T(8,128)(2,1)S(1)} collective-permute-done((bf16[4,128,128]{2,1,0:T(8,128)(2,1)S(1)}, bf16[4,128,128]{2,1,0:T(8,128)(2,1)S(1)}, u32[]{:S(2)}, u32[]{:S(2)}) %collective-permute-start) | collective-permute-done | bytes 131104 | tf_op jit(solution)/shard_map/ppermute | solution.py:238
  14.0 1.6 %collective-permute-start.1 = (bf16[1,128,128]{2,1,0:T(8,128)(2,1)S(1)}, bf16[1,128,128]{2,1,0:T(8,128)(2,1)S(1)}, u32[]{:S(2)}, u32[]{:S(2)}) collective-permute-start(bf16[1,128,128]{2,1,0:T(8,128)(2,1)S(1)} %get-tuple-element.66), channel_id=1, source_target_pairs={{0,1},{1,0},{2,3},{3,2},{4,5},{5,4},{6,7},{7,6},{8,9},{9,8},{10,11... | collective-permute-start | bytes 98312 | tf_op jit(solution)/shard_map/ppermute | solution.py:232
  15.5 0.7 collective-permute-start.2
  16.3 1.3 %collective-permute-start.3 = (bf16[1,128,128]{2,1,0:T(8,128)(2,1)S(1)}, bf16[1,128,128]{2,1,0:T(8,128)(2,1)S(1)}, u32[]{:S(2)}, u32[]{:S(2)}) collective-permute-start(bf16[1,128,128]{2,1,0:T(8,128)(2,1)S(1)} %get-tuple-element.68), channel_id=1, source_target_pairs={{0,3},{1,2},{2,1},{3,0},{4,7},{5,6},{6,5},{7,4},{8,11},{9,10},{10,... | collective-permute-start | bytes 98312 | tf_op jit(solution)/shard_map/ppermute | solution.py:232
  17.5 0.4 collective-permute-done.1.refs_1_
  18.0 1.5 %collective-permute-done.2.refs_2_ = bf16[1,128,128]{2,1,0:T(8,128)(2,1)S(1)} collective-permute-done((bf16[1,128,128]{2,1,0:T(8,128)(2,1)S(1)}, bf16[1,128,128]{2,1,0:T(8,128)(2,1)S(1)}, u32[]{:S(2)}, u32[]{:S(2)}) %collective-permute-start.2) | collective-permute-done | bytes 32800 | tf_op jit(solution)/shard_map/ppermute | solution.py:232
  19.5 0.5 collective-permute-start.9
  20.0 1.1 %collective-permute-done.3.refs_3_ = bf16[1,128,128]{2,1,0:T(8,128)(2,1)S(1)} collective-permute-done((bf16[1,128,128]{2,1,0:T(8,128)(2,1)S(1)}, bf16[1,128,128]{2,1,0:T(8,128)(2,1)S(1)}, u32[]{:S(2)}, u32[]{:S(2)}) %collective-permute-start.3) | collective-permute-done | bytes 32800 | tf_op jit(solution)/shard_map/ppermute | solution.py:232
  21.1 0.8 off_levels.2
  21.9 0.6 collective-permute-start.7
  22.5 3.4 %collective-permute-start.8 = (bf16[4,128,128]{2,1,0:T(8,128)(2,1)S(1)}, bf16[4,128,128]{2,1,0:T(8,128)(2,1)S(1)}, u32[]{:S(2)}, u32[]{:S(2)}) collective-permute-start(bf16[4,128,128]{2,1,0:T(8,128)(2,1)S(1)} %get-tuple-element.74), channel_id=1, source_target_pairs={{0,4},{1,5},{2,6},{3,7},{4,0},{5,1},{6,2},{7,3},{8,12},{9,13},{10,... | collective-permute-start | bytes 393224 | tf_op jit(solution)/shard_map/ppermute | solution.py:238
  25.8 4.9 %collective-permute-done.8.refs_0_ = bf16[4,128,128]{2,1,0:T(8,128)(2,1)S(1)} collective-permute-done((bf16[4,128,128]{2,1,0:T(8,128)(2,1)S(1)}, bf16[4,128,128]{2,1,0:T(8,128)(2,1)S(1)}, u32[]{:S(2)}, u32[]{:S(2)}) %collective-permute-start.8) | collective-permute-done | bytes 131104 | tf_op jit(solution)/shard_map/ppermute | solution.py:238
  30.8 0.1 collective-permute-start.15
  30.9 0.4 own_levels.2
  31.3 0.1 collective-permute-start.16
  31.4 2.9 %collective-permute-start.17 = (bf16[4,128,128]{2,1,0:T(8,128)(2,1)S(1)}, bf16[4,128,128]{2,1,0:T(8,128)(2,1)S(1)}, u32[]{:S(2)}, u32[]{:S(2)}) collective-permute-start(bf16[4,128,128]{2,1,0:T(8,128)(2,1)S(1)} %get-tuple-element.86), channel_id=1, source_target_pairs={{0,3},{1,2},{2,1},{3,0},{4,7},{5,6},{6,5},{7,4},{8,11},{9,10},{10,... | collective-permute-start | bytes 393224 | tf_op jit(solution)/shard_map/ppermute | solution.py:232
  34.4 0.6 collective-permute-start.12
  35.0 0.1 collective-permute-start.13
  35.0 3.6 %collective-permute-done.12.refs_1_ = bf16[1,128,128]{2,1,0:T(8,128)(2,1)S(1)} collective-permute-done((bf16[1,128,128]{2,1,0:T(8,128)(2,1)S(1)}, bf16[1,128,128]{2,1,0:T(8,128)(2,1)S(1)}, u32[]{:S(2)}, u32[]{:S(2)}) %collective-permute-start.12) | collective-permute-done | bytes 32800 | tf_op jit(solution)/shard_map/ppermute | solution.py:232
  38.7 2.5 %collective-permute-done.13.refs_2_ = bf16[1,128,128]{2,1,0:T(8,128)(2,1)S(1)} collective-permute-done((bf16[1,128,128]{2,1,0:T(8,128)(2,1)S(1)}, bf16[1,128,128]{2,1,0:T(8,128)(2,1)S(1)}, u32[]{:S(2)}, u32[]{:S(2)}) %collective-permute-start.13) | collective-permute-done | bytes 32800 | tf_op jit(solution)/shard_map/ppermute | solution.py:232
  41.2 2.3 %collective-permute-done.14.refs_3_ = bf16[1,128,128]{2,1,0:T(8,128)(2,1)S(1)} collective-permute-done((bf16[1,128,128]{2,1,0:T(8,128)(2,1)S(1)}, bf16[1,128,128]{2,1,0:T(8,128)(2,1)S(1)}, u32[]{:S(2)}, u32[]{:S(2)}) %collective-permute-start.14) | collective-permute-done | bytes 32800 | tf_op jit(solution)/shard_map/ppermute | solution.py:232
  43.5 0.7 off_levels.3
  44.3 0.6 collective-permute-start.18
  44.9 0.0 collective-permute-start.10
  44.9 3.3 %collective-permute-start.19 = (bf16[4,128,128]{2,1,0:T(8,128)(2,1)S(1)}, bf16[4,128,128]{2,1,0:T(8,128)(2,1)S(1)}, u32[]{:S(2)}, u32[]{:S(2)}) collective-permute-start(bf16[4,128,128]{2,1,0:T(8,128)(2,1)S(1)} %get-tuple-element.90), channel_id=1, source_target_pairs={{0,4},{1,5},{2,6},{3,7},{4,0},{5,1},{6,2},{7,3},{8,12},{9,13},{10,... | collective-permute-start | bytes 393224 | tf_op jit(solution)/shard_map/ppermute | solution.py:238
  48.2 3.1 %collective-permute-done.10.last = bf16[1,128,512]{2,1,0:T(8,128)(2,1)S(1)} collective-permute-done((bf16[1,128,512]{2,1,0:T(8,128)(2,1)S(1)}, bf16[1,128,512]{2,1,0:T(8,128)(2,1)S(1)}, u32[]{:S(2)}, u32[]{:S(2)}) %collective-permute-start.10) | collective-permute-done | bytes 131104 | tf_op jit(solution)/shard_map/ppermute | solution.py:232
  51.2 0.1 total.2
  51.3 0.3 collective-permute-start.11
  51.6 2.6 %collective-permute-done.19.refs_0_.refs_10_ = bf16[4,128,128]{2,1,0:T(8,128)(2,1)S(1)} collective-permute-done((bf16[4,128,128]{2,1,0:T(8,128)(2,1)S(1)}, bf16[4,128,128]{2,1,0:T(8,128)(2,1)S(1)}, u32[]{:S(2)}, u32[]{:S(2)}) %collective-permute-start.19) | collective-permute-done | bytes 131104 | tf_op jit(solution)/shard_map/ppermute | solution.py:238
  54.2 0.6 collective-permute-start.20
  54.8 0.4 own_levels.3
  55.2 1.0 collective-permute-start.23
  56.2 1.9 %collective-permute-start.24 = (bf16[5,128,128]{2,1,0:T(8,128)(2,1)S(1)}, bf16[5,128,128]{2,1,0:T(8,128)(2,1)S(1)}, u32[]{:S(2)}, u32[]{:S(2)}) collective-permute-start(bf16[5,128,128]{2,1,0:T(8,128)(2,1)S(1)} %get-tuple-element.101), channel_id=1, source_target_pairs={{0,2},{1,3},{2,0},{3,1},{4,6},{5,7},{6,4},{7,5},{8,10},{9,11},{10,... | collective-permute-start | bytes 491528 | tf_op jit(solution)/shard_map/ppermute | solution.py:232
  58.1 0.7 collective-permute-start.25
  58.8 1.2 %collective-permute-start.22 = (bf16[4,128,128]{2,1,0:T(8,128)(2,1)S(1)}, bf16[4,128,128]{2,1,0:T(8,128)(2,1)S(1)}, u32[]{:S(2)}, u32[]{:S(2)}) collective-permute-start(bf16[4,128,128]{2,1,0:T(8,128)(2,1)S(1)} %get-tuple-element.95), channel_id=1, source_target_pairs={{0,1},{1,0},{2,3},{3,2},{4,5},{5,4},{6,7},{7,6},{8,9},{9,8},{10,11... | collective-permute-start | bytes 393224 | tf_op jit(solution)/shard_map/ppermute | solution.py:232
  60.0 2.5 %collective-permute-done.20.last = bf16[1,128,512]{2,1,0:T(8,128)(2,1)S(1)} collective-permute-done((bf16[1,128,512]{2,1,0:T(8,128)(2,1)S(1)}, bf16[1,128,512]{2,1,0:T(8,128)(2,1)S(1)}, u32[]{:S(2)}, u32[]{:S(2)}) %collective-permute-start.20) | collective-permute-done | bytes 131104 | tf_op jit(solution)/shard_map/ppermute | solution.py:232
  62.5 0.1 total.3
  62.6 0.9 collective-permute-start.21
  63.5 1.4 %collective-permute-done.22.refs_3_ = bf16[4,128,128]{2,1,0:T(8,128)(2,1)S(1)} collective-permute-done((bf16[4,128,128]{2,1,0:T(8,128)(2,1)S(1)}, bf16[4,128,128]{2,1,0:T(8,128)(2,1)S(1)}, u32[]{:S(2)}, u32[]{:S(2)}) %collective-permute-start.22) | collective-permute-done | bytes 131104 | tf_op jit(solution)/shard_map/ppermute | solution.py:232
  64.9 0.2 collective-permute-done.24.refs_8_
  65.1 2.4 %collective-permute-done.25.refs_9_ = bf16[5,128,128]{2,1,0:T(8,128)(2,1)S(1)} collective-permute-done((bf16[5,128,128]{2,1,0:T(8,128)(2,1)S(1)}, bf16[5,128,128]{2,1,0:T(8,128)(2,1)S(1)}, u32[]{:S(2)}, u32[]{:S(2)}) %collective-permute-start.25) | collective-permute-done | bytes 163872 | tf_op jit(solution)/shard_map/ppermute | solution.py:232
  67.5 2.4 %collective-permute-done.21.refs_1_ = bf16[128,512]{1,0:T(8,128)(2,1)S(1)} collective-permute-done((bf16[128,512]{1,0:T(8,128)(2,1)S(1)}, bf16[128,512]{1,0:T(8,128)(2,1)S(1)}, u32[]{:S(2)}, u32[]{:S(2)}) %collective-permute-start.21) | collective-permute-done | bytes 131104 | tf_op jit(solution)/shard_map/ppermute | solution.py:238
  69.9 2.3 %middle_levels.1 = (f32[1024,512]{1,0:T(8,128)S(1)}, bf16[4,128,128]{2,1,0:T(8,128)(2,1)S(1)}, bf16[4,128,128]{2,1,0:T(8,128)(2,1)S(1)}, bf16[4,128,128]{2,1,0:T...) custom-call(bf16[1,3,1,8,128,128]{5,4,3,2,1,0:T(8,128)(2,1)S(1)} %co, ...), custom_call_target="tpu_custom_call" | custom-call | flops 1342177280 | tf_op jit(solution)/shard_map/middle_levels/pallas_call | solution.py:243
  72.2 1.4 %collective-permute-start.26 = (bf16[1,128,512]{2,1,0:T(8,128)(2,1)S(1)}, bf16[1,128,512]{2,1,0:T(8,128)(2,1)S(1)}, u32[]{:S(2)}, u32[]{:S(2)}) collective-permute-start(bf16[1,128,512]{2,1,0:T(8,128)(2,1)S(1)} %get-tuple-element.105), channel_id=1, source_target_pairs={{0,1},{1,0},{2,3},{3,2},{4,5},{5,4},{6,7},{7,6},{8,9},{9,8},{10,11... | collective-permute-start | bytes 393224 | tf_op jit(solution)/shard_map/ppermute | solution.py:232
  73.6 2.2 %collective-permute-start.28 = (bf16[1,128,512]{2,1,0:T(8,128)(2,1)S(1)}, bf16[1,128,512]{2,1,0:T(8,128)(2,1)S(1)}, u32[]{:S(2)}, u32[]{:S(2)}) collective-permute-start(bf16[1,128,512]{2,1,0:T(8,128)(2,1)S(1)} %get-tuple-element.107), channel_id=1, source_target_pairs={{0,3},{1,2},{2,1},{3,0},{4,7},{5,6},{6,5},{7,4},{8,11},{9,10},{10,... | collective-permute-start | bytes 393224 | tf_op jit(solution)/shard_map/ppermute | solution.py:232
  75.8 2.7 %collective-permute-done.26 = bf16[1,128,512]{2,1,0:T(8,128)(2,1)S(1)} collective-permute-done((bf16[1,128,512]{2,1,0:T(8,128)(2,1)S(1)}, bf16[1,128,512]{2,1,0:T(8,128)(2,1)S(1)}, u32[]{:S(2)}, u32[]{:S(2)}) %collective-permute-start.26) | collective-permute-done | bytes 131104 | tf_op jit(solution)/shard_map/ppermute | solution.py:232
  78.5 2.9 %collective-permute-done.27 = bf16[1,128,512]{2,1,0:T(8,128)(2,1)S(1)} collective-permute-done((bf16[1,128,512]{2,1,0:T(8,128)(2,1)S(1)}, bf16[1,128,512]{2,1,0:T(8,128)(2,1)S(1)}, u32[]{:S(2)}, u32[]{:S(2)}) %collective-permute-start.27) | collective-permute-done | bytes 131104 | tf_op jit(solution)/shard_map/ppermute | solution.py:232
  81.4 2.8 %collective-permute-done.28 = bf16[1,128,512]{2,1,0:T(8,128)(2,1)S(1)} collective-permute-done((bf16[1,128,512]{2,1,0:T(8,128)(2,1)S(1)}, bf16[1,128,512]{2,1,0:T(8,128)(2,1)S(1)}, u32[]{:S(2)}, u32[]{:S(2)}) %collective-permute-start.28) | collective-permute-done | bytes 131104 | tf_op jit(solution)/shard_map/ppermute | solution.py:232
  84.2 0.1 fusion
  84.3 1.3 %collective-permute-start.30 = (bf16[4,128,128]{2,1,0:T(8,128)(2,1)S(1)}, bf16[4,128,128]{2,1,0:T(8,128)(2,1)S(1)}, u32[]{:S(2)}, u32[]{:S(2)}) collective-permute-start(bf16[4,128,128]{2,1,0:T(8,128)(2,1)S(1)} %get-tuple-element.110), channel_id=1, source_target_pairs={{0,1},{1,0},{2,3},{3,2},{4,5},{5,4},{6,7},{7,6},{8,9},{9,8},{10,11... | collective-permute-start | bytes 393224 | tf_op jit(solution)/shard_map/ppermute | solution.py:232
  85.6 2.3 %collective-permute-start.32 = (bf16[4,128,128]{2,1,0:T(8,128)(2,1)S(1)}, bf16[4,128,128]{2,1,0:T(8,128)(2,1)S(1)}, u32[]{:S(2)}, u32[]{:S(2)}) collective-permute-start(bf16[4,128,128]{2,1,0:T(8,128)(2,1)S(1)} %get-tuple-element.114), channel_id=1, source_target_pairs={{0,3},{1,2},{2,1},{3,0},{4,7},{5,6},{6,5},{7,4},{8,11},{9,10},{10,... | collective-permute-start | bytes 393224 | tf_op jit(solution)/shard_map/ppermute | solution.py:232
  87.9 1.5 %collective-permute-done.30.refs_2_ = bf16[4,128,128]{2,1,0:T(8,128)(2,1)S(1)} collective-permute-done((bf16[4,128,128]{2,1,0:T(8,128)(2,1)S(1)}, bf16[4,128,128]{2,1,0:T(8,128)(2,1)S(1)}, u32[]{:S(2)}, u32[]{:S(2)}) %collective-permute-start.30) | collective-permute-done | bytes 131104 | tf_op jit(solution)/shard_map/ppermute | solution.py:232
  89.3 1.2 %collective-permute-done.31.refs_3_ = bf16[4,128,128]{2,1,0:T(8,128)(2,1)S(1)} collective-permute-done((bf16[4,128,128]{2,1,0:T(8,128)(2,1)S(1)}, bf16[4,128,128]{2,1,0:T(8,128)(2,1)S(1)}, u32[]{:S(2)}, u32[]{:S(2)}) %collective-permute-start.31) | collective-permute-done | bytes 131104 | tf_op jit(solution)/shard_map/ppermute | solution.py:232
  90.5 1.7 %collective-permute-done.32.refs_4_ = bf16[4,128,128]{2,1,0:T(8,128)(2,1)S(1)} collective-permute-done((bf16[4,128,128]{2,1,0:T(8,128)(2,1)S(1)}, bf16[4,128,128]{2,1,0:T(8,128)(2,1)S(1)}, u32[]{:S(2)}, u32[]{:S(2)}) %collective-permute-start.32) | collective-permute-done | bytes 131104 | tf_op jit(solution)/shard_map/ppermute | solution.py:232
  92.2 2.4 %collective-permute-done.29.refs_0_ = bf16[128,512]{1,0:T(8,128)(2,1)S(1)} collective-permute-done((bf16[128,512]{1,0:T(8,128)(2,1)S(1)}, bf16[128,512]{1,0:T(8,128)(2,1)S(1)}, u32[]{:S(2)}, u32[]{:S(2)}) %collective-permute-start.29) | collective-permute-done | bytes 131104 | tf_op jit(solution)/shard_map/ppermute | solution.py:238
  94.6 1.6 %last_levels.1 = bf16[1,1024,512]{2,1,0:T(8,128)(2,1)} custom-call(bf16[1,3,1,8,128,128]{5,4,3,2,1,0:T(8,128)(2,1)S(1)} %copy-done, bf16[1024,256]{1,0:T(8,128)(2,1)S(1)} %get-tuple-element.60.row_mats, f32[1024,512]{1,0:T(8,128)S(1)} %get-tuple-element.103.residual, bf16[128,512]{1,0:T(8,128)(2,1)S(1)} %collective-permute-done.29.refs_0_, ...), custom_call_target="tpu_custom_call" | custom-call | flops 335544320 | tf_op jit(solution)/shard_map/last_levels/pallas_call | solution.py:243
  (34 shorter events, 0.2 us)
Async XLA Ops:
  0.0 4.2 %copy-start = (bf16[1,3,1,8,128,128]{5,4,3,2,1,0:T(8,128)(2,1)S(1)}, bf16[1,3,1,8,128,128]{5,4,3,2,1,0:T(8,128)(2,1)}, u32[]{:S(2)}) copy-start(bf16[1,3,1,8,128,128]{5,4,3,2,1,0:T(8,128)(2,1)} %third.5) | copy-start | bytes 2359300
  0.0 6.9 %copy-start.5 = (bf16[1,3,1,8,128,128]{5,4,3,2,1,0:T(8,128)(2,1)S(1)}, bf16[1,3,1,8,128,128]{5,4,3,2,1,0:T(8,128)(2,1)}, u32[]{:S(2)}) copy-start(bf16[1,3,1,8,128,128]{5,4,3,2,1,0:T(8,128)(2,1)} %second.1) | copy-start | bytes 2359300
  1.2 12.8 %collective-permute-start.5 = (bf16[1,256,512]{2,1,0:T(8,128)(2,1)S(1)}, bf16[1,256,512]{2,1,0:T(8,128)(2,1)S(1)}, u32[]{:S(2)}, u32[]{:S(2)}) collective-permute-start(bf16[1,256,512]{2,1,0:T(8,128)(2,1)S(1)} %get-tuple-element.116), channel_id=1, source_target_pairs={{0,16},{8,24},{16,0},{24,8},{1,17},{9,25},{17,1},{25,9},{2,18},{10... | collective-permute-start | bytes 786440 | tf_op jit(solution)/shard_map/ppermute | solution.py:228
  4.2 16.9 %collective-permute-start.4 = (bf16[2,256,512]{2,1,0:T(8,128)(2,1)}, bf16[2,256,512]{2,1,0:T(8,128)(2,1)S(1)}, u32[]{:S(2)}, u32[]{:S(2)}) collective-permute-start(bf16[2,256,512]{2,1,0:T(8,128)(2,1)} %refs_4_.3), channel_id=1, source_target_pairs={{0,8},{8,0},{16,24},{24,16},{1,9},{9,1},{17,25},{25,17},{2,10},{10... | collective-permute-start | bytes 1572872 | tf_op jit(solution)/shard_map/ppermute | solution.py:228
  4.3 16.8 %copy-start.1 = (bf16[1,3,4,256,128]{4,3,2,1,0:T(8,128)(2,1)S(1)}, bf16[1,3,4,256,128]{4,3,2,1,0:T(8,128)(2,1)}, u32[]{:S(2)}) copy-start(bf16[1,3,4,256,128]{4,3,2,1,0:T(8,128)(2,1)} %basis.5) | copy-start | bytes 2359300
  4.3 16.8 %copy-start.2 = (bf16[2,256,512]{2,1,0:T(8,128)(2,1)S(1)}, bf16[2,256,512]{2,1,0:T(8,128)(2,1)}, u32[]{:S(2)}) copy-start(bf16[2,256,512]{2,1,0:T(8,128)(2,1)} %refs_4_.3) | copy-start | bytes 1572868
  4.3 9.7 %collective-permute-start = (bf16[4,128,128]{2,1,0:T(8,128)(2,1)S(1)}, bf16[4,128,128]{2,1,0:T(8,128)(2,1)S(1)}, u32[]{:S(2)}, u32[]{:S(2)}) collective-permute-start(bf16[4,128,128]{2,1,0:T(8,128)(2,1)S(1)} %get-tuple-element.64), channel_id=1, source_target_pairs={{0,4},{1,5},{2,6},{3,7},{4,0},{5,1},{6,2},{7,3},{8,12},{9,13},{10,... | collective-permute-start | bytes 393224 | tf_op jit(solution)/shard_map/ppermute | solution.py:238
  6.9 1.4 %copy-start.3 = (bf16[1,3,1,4,4,128,128]{6,5,4,3,2,1,0:T(8,128)(2,1)S(1)}, bf16[1,3,1,4,4,128,128]{6,5,4,3,2,1,0:T(8,128)(2,1)}, u32[]{:S(2)}) copy-start(bf16[1,3,1,4,4,128,128]{6,5,4,3,2,1,0:T(8,128)(2,1)} %first.1) | copy-start | bytes 4718596
  8.3 1.1 %copy-start.6 = (bf16[1,3,2,512,128]{4,3,2,1,0:T(8,128)(2,1)S(1)}, bf16[1,3,2,512,128]{4,3,2,1,0:T(8,128)(2,1)}, u32[]{:S(2)}) copy-start(bf16[1,3,2,512,128]{4,3,2,1,0:T(8,128)(2,1)} %out_basis.1) | copy-start | bytes 2359300
  9.5 1.0 %copy-start.7 = (bf16[1,3,1,2,2,128,128]{6,5,4,3,2,1,0:T(8,128)(2,1)S(1)}, bf16[1,3,1,2,2,128,128]{6,5,4,3,2,1,0:T(8,128)(2,1)}, u32[]{:S(2)}) copy-start(bf16[1,3,1,2,2,128,128]{6,5,4,3,2,1,0:T(8,128)(2,1)} %fourth.1) | copy-start | bytes 1179652
  14.0 7.1 %collective-permute-start.6 = (bf16[1,256,512]{2,1,0:T(8,128)(2,1)S(1)}, bf16[1,256,512]{2,1,0:T(8,128)(2,1)S(1)}, u32[]{:S(2)}, u32[]{:S(2)}) collective-permute-start(bf16[1,256,512]{2,1,0:T(8,128)(2,1)S(1)} %collective-permute-done.5.refs_6_), channel_id=1, source_target_pairs={{0,8},{8,0},{16,24},{24,16},{1,9},{9,1},{17,25},{25,17},{2,10},{10... | collective-permute-start | bytes 786440 | tf_op jit(solution)/shard_map/ppermute | solution.py:228
  14.0 4.0 %collective-permute-start.1 = (bf16[1,128,128]{2,1,0:T(8,128)(2,1)S(1)}, bf16[1,128,128]{2,1,0:T(8,128)(2,1)S(1)}, u32[]{:S(2)}, u32[]{:S(2)}) collective-permute-start(bf16[1,128,128]{2,1,0:T(8,128)(2,1)S(1)} %get-tuple-element.66), channel_id=1, source_target_pairs={{0,1},{1,0},{2,3},{3,2},{4,5},{5,4},{6,7},{7,6},{8,9},{9,8},{10,11... | collective-permute-start | bytes 98312 | tf_op jit(solution)/shard_map/ppermute | solution.py:232
  15.5 3.9 %collective-permute-start.2 = (bf16[1,128,128]{2,1,0:T(8,128)(2,1)S(1)}, bf16[1,128,128]{2,1,0:T(8,128)(2,1)S(1)}, u32[]{:S(2)}, u32[]{:S(2)}) collective-permute-start(bf16[1,128,128]{2,1,0:T(8,128)(2,1)S(1)} %get-tuple-element.67), channel_id=1, source_target_pairs={{0,2},{1,3},{2,0},{3,1},{4,6},{5,7},{6,4},{7,5},{8,10},{9,11},{10,... | collective-permute-start | bytes 98312 | tf_op jit(solution)/shard_map/ppermute | solution.py:232
  16.3 4.8 %collective-permute-start.3 = (bf16[1,128,128]{2,1,0:T(8,128)(2,1)S(1)}, bf16[1,128,128]{2,1,0:T(8,128)(2,1)S(1)}, u32[]{:S(2)}, u32[]{:S(2)}) collective-permute-start(bf16[1,128,128]{2,1,0:T(8,128)(2,1)S(1)} %get-tuple-element.68), channel_id=1, source_target_pairs={{0,3},{1,2},{2,1},{3,0},{4,7},{5,6},{6,5},{7,4},{8,11},{9,10},{10,... | collective-permute-start | bytes 98312 | tf_op jit(solution)/shard_map/ppermute | solution.py:232
  19.5 11.3 %collective-permute-start.9 = (bf16[1,256,512]{2,1,0:T(8,128)(2,1)S(1)}, bf16[1,256,512]{2,1,0:T(8,128)(2,1)S(1)}, u32[]{:S(2)}, u32[]{:S(2)}) collective-permute-start(bf16[1,256,512]{2,1,0:T(8,128)(2,1)S(1)} %get-tuple-element.75), channel_id=1, source_target_pairs={{0,16},{8,24},{16,0},{24,8},{1,17},{9,25},{17,1},{25,9},{2,18},{10... | collective-permute-start | bytes 786440 | tf_op jit(solution)/shard_map/ppermute | solution.py:228
  21.9 8.9 %collective-permute-start.7 = (bf16[2,1,128,512]{3,2,1,0:T(8,128)(2,1)S(1)}, bf16[2,1,128,512]{3,2,1,0:T(8,128)(2,1)S(1)}, u32[]{:S(2)}, u32[]{:S(2)}) collective-permute-start(bf16[2,1,128,512]{3,2,1,0:T(8,128)(2,1)S(1)} %get-tuple-element.71), channel_id=1, source_target_pairs={{0,1},{1,0},{2,3},{3,2},{4,5},{5,4},{6,7},{7,6},{8,9},{9,8},{10,11... | collective-permute-start | bytes 786440 | tf_op jit(solution)/shard_map/ppermute | solution.py:232
  22.5 8.3 %collective-permute-start.8 = (bf16[4,128,128]{2,1,0:T(8,128)(2,1)S(1)}, bf16[4,128,128]{2,1,0:T(8,128)(2,1)S(1)}, u32[]{:S(2)}, u32[]{:S(2)}) collective-permute-start(bf16[4,128,128]{2,1,0:T(8,128)(2,1)S(1)} %get-tuple-element.74), channel_id=1, source_target_pairs={{0,4},{1,5},{2,6},{3,7},{4,0},{5,1},{6,2},{7,3},{8,12},{9,13},{10,... | collective-permute-start | bytes 393224 | tf_op jit(solution)/shard_map/ppermute | solution.py:238
  30.8 12.7 %collective-permute-start.15 = (bf16[1,256,512]{2,1,0:T(8,128)(2,1)S(1)}, bf16[1,256,512]{2,1,0:T(8,128)(2,1)S(1)}, u32[]{:S(2)}, u32[]{:S(2)}) collective-permute-start(bf16[1,256,512]{2,1,0:T(8,128)(2,1)S(1)} %collective-permute-done.9.refs_6_), channel_id=1, source_target_pairs={{0,8},{8,0},{16,24},{24,16},{1,9},{9,1},{17,25},{25,17},{2,10},{10... | collective-permute-start | bytes 786440 | tf_op jit(solution)/shard_map/ppermute | solution.py:228
  31.3 12.9 %collective-permute-start.16 = (bf16[4,128,128]{2,1,0:T(8,128)(2,1)S(1)}, bf16[4,128,128]{2,1,0:T(8,128)(2,1)S(1)}, u32[]{:S(2)}, u32[]{:S(2)}) collective-permute-start(bf16[4,128,128]{2,1,0:T(8,128)(2,1)S(1)} %get-tuple-element.85), channel_id=1, source_target_pairs={{0,2},{1,3},{2,0},{3,1},{4,6},{5,7},{6,4},{7,5},{8,10},{9,11},{10,... | collective-permute-start | bytes 393224 | tf_op jit(solution)/shard_map/ppermute | solution.py:232
  31.4 12.8 %collective-permute-start.17 = (bf16[4,128,128]{2,1,0:T(8,128)(2,1)S(1)}, bf16[4,128,128]{2,1,0:T(8,128)(2,1)S(1)}, u32[]{:S(2)}, u32[]{:S(2)}) collective-permute-start(bf16[4,128,128]{2,1,0:T(8,128)(2,1)S(1)} %get-tuple-element.86), channel_id=1, source_target_pairs={{0,3},{1,2},{2,1},{3,0},{4,7},{5,6},{6,5},{7,4},{8,11},{9,10},{10,... | collective-permute-start | bytes 393224 | tf_op jit(solution)/shard_map/ppermute | solution.py:232
  34.4 4.3 %collective-permute-start.12 = (bf16[1,128,128]{2,1,0:T(8,128)(2,1)S(1)}, bf16[1,128,128]{2,1,0:T(8,128)(2,1)S(1)}, u32[]{:S(2)}, u32[]{:S(2)}) collective-permute-start(bf16[1,128,128]{2,1,0:T(8,128)(2,1)S(1)} %get-tuple-element.78), channel_id=1, source_target_pairs={{0,1},{1,0},{2,3},{3,2},{4,5},{5,4},{6,7},{7,6},{8,9},{9,8},{10,11... | collective-permute-start | bytes 98312 | tf_op jit(solution)/shard_map/ppermute | solution.py:232
  35.0 6.2 %collective-permute-start.13 = (bf16[1,128,128]{2,1,0:T(8,128)(2,1)S(1)}, bf16[1,128,128]{2,1,0:T(8,128)(2,1)S(1)}, u32[]{:S(2)}, u32[]{:S(2)}) collective-permute-start(bf16[1,128,128]{2,1,0:T(8,128)(2,1)S(1)} %get-tuple-element.79), channel_id=1, source_target_pairs={{0,2},{1,3},{2,0},{3,1},{4,6},{5,7},{6,4},{7,5},{8,10},{9,11},{10,... | collective-permute-start | bytes 98312 | tf_op jit(solution)/shard_map/ppermute | solution.py:232
  38.7 4.8 %collective-permute-start.14 = (bf16[1,128,128]{2,1,0:T(8,128)(2,1)S(1)}, bf16[1,128,128]{2,1,0:T(8,128)(2,1)S(1)}, u32[]{:S(2)}, u32[]{:S(2)}) collective-permute-start(bf16[1,128,128]{2,1,0:T(8,128)(2,1)S(1)} %get-tuple-element.80), channel_id=1, source_target_pairs={{0,3},{1,2},{2,1},{3,0},{4,7},{5,6},{6,5},{7,4},{8,11},{9,10},{10,... | collective-permute-start | bytes 98312 | tf_op jit(solution)/shard_map/ppermute | solution.py:232
  44.3 9.9 %collective-permute-start.18 = (bf16[2,1,128,512]{3,2,1,0:T(8,128)(2,1)S(1)}, bf16[2,1,128,512]{3,2,1,0:T(8,128)(2,1)S(1)}, u32[]{:S(2)}, u32[]{:S(2)}) collective-permute-start(bf16[2,1,128,512]{3,2,1,0:T(8,128)(2,1)S(1)} %get-tuple-element.87), channel_id=1, source_target_pairs={{0,1},{1,0},{2,3},{3,2},{4,5},{5,4},{6,7},{7,6},{8,9},{9,8},{10,11... | collective-permute-start | bytes 786440 | tf_op jit(solution)/shard_map/ppermute | solution.py:232
  44.9 6.4 %collective-permute-start.10 = (bf16[1,128,512]{2,1,0:T(8,128)(2,1)S(1)}, bf16[1,128,512]{2,1,0:T(8,128)(2,1)S(1)}, u32[]{:S(2)}, u32[]{:S(2)}) collective-permute-start(bf16[1,128,512]{2,1,0:T(8,128)(2,1)S(1)} %stage.2), channel_id=1, source_target_pairs={{0,2},{1,3},{2,0},{3,1},{4,6},{5,7},{6,4},{7,5},{8,10},{9,11},{10,... | collective-permute-start | bytes 393224 | tf_op jit(solution)/shard_map/ppermute | solution.py:232
  44.9 9.3 %collective-permute-start.19 = (bf16[4,128,128]{2,1,0:T(8,128)(2,1)S(1)}, bf16[4,128,128]{2,1,0:T(8,128)(2,1)S(1)}, u32[]{:S(2)}, u32[]{:S(2)}) collective-permute-start(bf16[4,128,128]{2,1,0:T(8,128)(2,1)S(1)} %get-tuple-element.90), channel_id=1, source_target_pairs={{0,4},{1,5},{2,6},{3,7},{4,0},{5,1},{6,2},{7,3},{8,12},{9,13},{10,... | collective-permute-start | bytes 393224 | tf_op jit(solution)/shard_map/ppermute | solution.py:238
  51.3 7.5 %collective-permute-start.11 = (bf16[128,512]{1,0:T(8,128)(2,1)S(1)}, bf16[128,512]{1,0:T(8,128)(2,1)S(1)}, u32[]{:S(2)}, u32[]{:S(2)}) collective-permute-start(bf16[128,512]{1,0:T(8,128)(2,1)S(1)} %total.2), channel_id=1, source_target_pairs={{0,4},{1,5},{2,6},{3,7},{4,0},{5,1},{6,2},{7,3},{8,12},{9,13},{10,... | collective-permute-start | bytes 393224 | tf_op jit(solution)/shard_map/ppermute | solution.py:238
  54.2 15.7 %copy-start.4 = (bf16[1,1024,512]{2,1,0:T(8,128)(2,1)S(1)}, bf16[1,1024,512]{2,1,0:T(8,128)(2,1)}, u32[]{:S(2)}) copy-start(bf16[1,1024,512]{2,1,0:T(8,128)(2,1)} %rhs.1) | copy-start | bytes 3145732
  54.2 8.3 %collective-permute-start.20 = (bf16[1,128,512]{2,1,0:T(8,128)(2,1)S(1)}, bf16[1,128,512]{2,1,0:T(8,128)(2,1)S(1)}, u32[]{:S(2)}, u32[]{:S(2)}) collective-permute-start(bf16[1,128,512]{2,1,0:T(8,128)(2,1)S(1)} %stage.3), channel_id=1, source_target_pairs={{0,2},{1,3},{2,0},{3,1},{4,6},{5,7},{6,4},{7,5},{8,10},{9,11},{10,... | collective-permute-start | bytes 393224 | tf_op jit(solution)/shard_map/ppermute | solution.py:232
  55.2 9.7 %collective-permute-start.23 = (bf16[5,128,128]{2,1,0:T(8,128)(2,1)S(1)}, bf16[5,128,128]{2,1,0:T(8,128)(2,1)S(1)}, u32[]{:S(2)}, u32[]{:S(2)}) collective-permute-start(bf16[5,128,128]{2,1,0:T(8,128)(2,1)S(1)} %get-tuple-element.100), channel_id=1, source_target_pairs={{0,1},{1,0},{2,3},{3,2},{4,5},{5,4},{6,7},{7,6},{8,9},{9,8},{10,11... | collective-permute-start | bytes 491528 | tf_op jit(solution)/shard_map/ppermute | solution.py:232
  56.2 8.9 %collective-permute-start.24 = (bf16[5,128,128]{2,1,0:T(8,128)(2,1)S(1)}, bf16[5,128,128]{2,1,0:T(8,128)(2,1)S(1)}, u32[]{:S(2)}, u32[]{:S(2)}) collective-permute-start(bf16[5,128,128]{2,1,0:T(8,128)(2,1)S(1)} %get-tuple-element.101), channel_id=1, source_target_pairs={{0,2},{1,3},{2,0},{3,1},{4,6},{5,7},{6,4},{7,5},{8,10},{9,11},{10,... | collective-permute-start | bytes 491528 | tf_op jit(solution)/shard_map/ppermute | solution.py:232
  58.1 9.4 %collective-permute-start.25 = (bf16[5,128,128]{2,1,0:T(8,128)(2,1)S(1)}, bf16[5,128,128]{2,1,0:T(8,128)(2,1)S(1)}, u32[]{:S(2)}, u32[]{:S(2)}) collective-permute-start(bf16[5,128,128]{2,1,0:T(8,128)(2,1)S(1)} %get-tuple-element.102), channel_id=1, source_target_pairs={{0,3},{1,2},{2,1},{3,0},{4,7},{5,6},{6,5},{7,4},{8,11},{9,10},{10,... | collective-permute-start | bytes 491528 | tf_op jit(solution)/shard_map/ppermute | solution.py:232
  58.8 6.1 %collective-permute-start.22 = (bf16[4,128,128]{2,1,0:T(8,128)(2,1)S(1)}, bf16[4,128,128]{2,1,0:T(8,128)(2,1)S(1)}, u32[]{:S(2)}, u32[]{:S(2)}) collective-permute-start(bf16[4,128,128]{2,1,0:T(8,128)(2,1)S(1)} %get-tuple-element.95), channel_id=1, source_target_pairs={{0,1},{1,0},{2,3},{3,2},{4,5},{5,4},{6,7},{7,6},{8,9},{9,8},{10,11... | collective-permute-start | bytes 393224 | tf_op jit(solution)/shard_map/ppermute | solution.py:232
  62.6 7.3 %collective-permute-start.21 = (bf16[128,512]{1,0:T(8,128)(2,1)S(1)}, bf16[128,512]{1,0:T(8,128)(2,1)S(1)}, u32[]{:S(2)}, u32[]{:S(2)}) collective-permute-start(bf16[128,512]{1,0:T(8,128)(2,1)S(1)} %total.3), channel_id=1, source_target_pairs={{0,4},{1,5},{2,6},{3,7},{4,0},{5,1},{6,2},{7,3},{8,12},{9,13},{10,... | collective-permute-start | bytes 393224 | tf_op jit(solution)/shard_map/ppermute | solution.py:238
  72.2 6.3 %collective-permute-start.26 = (bf16[1,128,512]{2,1,0:T(8,128)(2,1)S(1)}, bf16[1,128,512]{2,1,0:T(8,128)(2,1)S(1)}, u32[]{:S(2)}, u32[]{:S(2)}) collective-permute-start(bf16[1,128,512]{2,1,0:T(8,128)(2,1)S(1)} %get-tuple-element.105), channel_id=1, source_target_pairs={{0,1},{1,0},{2,3},{3,2},{4,5},{5,4},{6,7},{7,6},{8,9},{9,8},{10,11... | collective-permute-start | bytes 393224 | tf_op jit(solution)/shard_map/ppermute | solution.py:232
  73.6 7.8 %collective-permute-start.27 = (bf16[1,128,512]{2,1,0:T(8,128)(2,1)S(1)}, bf16[1,128,512]{2,1,0:T(8,128)(2,1)S(1)}, u32[]{:S(2)}, u32[]{:S(2)}) collective-permute-start(bf16[1,128,512]{2,1,0:T(8,128)(2,1)S(1)} %get-tuple-element.106), channel_id=1, source_target_pairs={{0,2},{1,3},{2,0},{3,1},{4,6},{5,7},{6,4},{7,5},{8,10},{9,11},{10,... | collective-permute-start | bytes 393224 | tf_op jit(solution)/shard_map/ppermute | solution.py:232
  73.6 10.6 %collective-permute-start.28 = (bf16[1,128,512]{2,1,0:T(8,128)(2,1)S(1)}, bf16[1,128,512]{2,1,0:T(8,128)(2,1)S(1)}, u32[]{:S(2)}, u32[]{:S(2)}) collective-permute-start(bf16[1,128,512]{2,1,0:T(8,128)(2,1)S(1)} %get-tuple-element.107), channel_id=1, source_target_pairs={{0,3},{1,2},{2,1},{3,0},{4,7},{5,6},{6,5},{7,4},{8,11},{9,10},{10,... | collective-permute-start | bytes 393224 | tf_op jit(solution)/shard_map/ppermute | solution.py:232
  84.3 5.0 %collective-permute-start.30 = (bf16[4,128,128]{2,1,0:T(8,128)(2,1)S(1)}, bf16[4,128,128]{2,1,0:T(8,128)(2,1)S(1)}, u32[]{:S(2)}, u32[]{:S(2)}) collective-permute-start(bf16[4,128,128]{2,1,0:T(8,128)(2,1)S(1)} %get-tuple-element.110), channel_id=1, source_target_pairs={{0,1},{1,0},{2,3},{3,2},{4,5},{5,4},{6,7},{7,6},{8,9},{9,8},{10,11... | collective-permute-start | bytes 393224 | tf_op jit(solution)/shard_map/ppermute | solution.py:232
  85.6 5.0 %collective-permute-start.31 = (bf16[4,128,128]{2,1,0:T(8,128)(2,1)S(1)}, bf16[4,128,128]{2,1,0:T(8,128)(2,1)S(1)}, u32[]{:S(2)}, u32[]{:S(2)}) collective-permute-start(bf16[4,128,128]{2,1,0:T(8,128)(2,1)S(1)} %get-tuple-element.112), channel_id=1, source_target_pairs={{0,2},{1,3},{2,0},{3,1},{4,6},{5,7},{6,4},{7,5},{8,10},{9,11},{10,... | collective-permute-start | bytes 393224 | tf_op jit(solution)/shard_map/ppermute | solution.py:232
  85.6 6.6 %collective-permute-start.32 = (bf16[4,128,128]{2,1,0:T(8,128)(2,1)S(1)}, bf16[4,128,128]{2,1,0:T(8,128)(2,1)S(1)}, u32[]{:S(2)}, u32[]{:S(2)}) collective-permute-start(bf16[4,128,128]{2,1,0:T(8,128)(2,1)S(1)} %get-tuple-element.114), channel_id=1, source_target_pairs={{0,3},{1,2},{2,1},{3,0},{4,7},{5,6},{6,5},{7,4},{8,11},{9,10},{10,... | collective-permute-start | bytes 393224 | tf_op jit(solution)/shard_map/ppermute | solution.py:232
  87.9 6.7 %collective-permute-start.29 = (bf16[128,512]{1,0:T(8,128)(2,1)S(1)}, bf16[128,512]{1,0:T(8,128)(2,1)S(1)}, u32[]{:S(2)}, u32[]{:S(2)}) collective-permute-start(bf16[128,512]{1,0:T(8,128)(2,1)S(1)} %fusion), channel_id=1, source_target_pairs={{0,4},{1,5},{2,6},{3,7},{4,0},{5,1},{6,2},{7,3},{8,12},{9,13},{10,... | collective-permute-start | bytes 393224 | tf_op jit(solution)/shard_map/ppermute | solution.py:238

commit v6 on v4

v6 whole, which is shorter than its diff:
```python
import functools

import jax
import jax.numpy as jnp
from jax import lax
from jax.experimental import pallas as pl
from jax.experimental.pallas import tpu as pltpu
from jax.sharding import PartitionSpec as P

F32 = jnp.float32
BF16 = jnp.bfloat16
MIB = 1024 * 1024
VMEM = pl.BlockSpec(memory_space=pltpu.VMEM)


def dot(a, b):
    return jnp.dot(a, b, preferred_element_type=F32)


def dot_t(a, b):
    return lax.dot_general(a, b, (((0,), (0,)), ((), ())), preferred_element_type=F32)


def place(radix):
    box = lax.axis_index("box")
    return lax.div(box, radix), lax.rem(box, radix)


def wrap(value, size):
    return lax.rem(value + size, size)


def take(refs, *counts):
    refs, out = list(refs), []
    for count in counts:
        out.append(refs[:count])
        refs = refs[count:]
    return out


def pick_kernel(radix, groups, third, *outs):
    group, _ = place(radix)
    start = 0
    for at, out in enumerate(outs):
        base = wrap(group + at % (groups - 1) + 1, groups) * radix
        for j in range(out.shape[0]):
            for k in range(radix):
                out[j, k] = third[0, start + j, 0, base + k]
        start += out.shape[0] if at % (groups - 1) == groups - 2 else 0


def leaf_order(row, leaves, row_size):
    per_leaf = row_size // leaves
    return [jnp.bitwise_xor(lax.div(row, per_leaf), t) for t in range(leaves)]


def weights_kernel(radix, groups, offs, row_size, first, second, fourth, out_basis, *outs):
    up_own, up_other, off_rows, last_rows = outs
    levels = first.shape[3]
    slots = second.shape[3]
    rank = fourth.shape[6]
    half_rows = out_basis.shape[3]
    group, member = place(radix)
    for j in range(first.shape[1]):
        order = leaf_order(lax.axis_index("row"), radix, row_size) if j < offs else range(radix)

        def up(slot):
            level = lax.div(slot, slots // levels)
            mats = jnp.concatenate([first[0, j, 0, level, k] for k in order], axis=1)
            return dot(second[0, j, 0, slot], mats).astype(BF16)

        for i in range(radix):
            box = jnp.bitwise_xor(member, i)
            up_own[j, i] = up(group * radix + box)
            for delta in range(1, groups):
                up_other[j, i, delta - 1] = up(wrap(group - delta, groups) * radix + box)
        out, start = (off_rows, j * groups * rank) if j < offs else (last_rows, 0)
        for h in range(fourth.shape[3]):
            mats = [fourth[0, j, 0, h, wrap(group + delta, groups)] for delta in range(groups)]
            out[h * half_rows : (h + 1) * half_rows, start : start + groups * rank] = dot(
                out_basis[0, j, h], jnp.concatenate(mats, axis=1)
            ).astype(BF16)


def put_other(mats, leaf, other, at):
    radix, less, rank, depth = mats.shape
    coef = dot(mats[...].reshape(radix * less * rank, depth), leaf).astype(BF16)
    for i, ref in enumerate(other):
        ref[at] = coef[i * less * rank : (i + 1) * less * rank].reshape(ref.shape[1:])


def put_own(mats, leaf, own, at):
    radix, rank, depth = mats.shape
    coef = dot(mats[...].reshape(radix * rank, depth), leaf).astype(BF16)
    for i, ref in enumerate(own):
        ref[at] = coef[i * rank : (i + 1) * rank]


def off_kernel(radix, pieces, basis, up_other, *refs):
    parts, (leaf_ref,), other = take(refs, pieces, 1, radix)
    row = lax.axis_index("row")
    leaves, leaf_rows = basis.shape[2], basis.shape[3]
    rows = parts[0].shape[1]
    per_leaf = leaf_rows // rows
    order = leaf_order(row, leaves, pieces)
    for j in range(parts[0].shape[0]):
        leaf = []
        for t in range(leaves):
            total = None
            for u in range(per_leaf):
                start = jnp.bitwise_xor(lax.rem(row, per_leaf), u) * rows
                if per_leaf == 1:
                    mat = basis[0, j, order[t]]
                else:
                    mat = basis[0, j, order[t], pl.ds(pl.multiple_of(start, rows), rows)]
                part = dot_t(mat, parts[t * per_leaf + u][j])
                total = part if total is None else total + part
            leaf.append(total.astype(BF16))
        leaf = jnp.concatenate(leaf, axis=0)
        leaf_ref[j] = leaf
        put_other(up_other.at[j], leaf, other, j)


def own_kernel(leaf, up_own, *own):
    for j in range(leaf.shape[0]):
        put_own(up_own.at[j], leaf[j], own, j)


def sum_kernel(radix, *refs):
    got, thirds, outs = take(refs, radix, (len(refs) - radix) // 2, (len(refs) - radix) // 2)
    _, member = place(radix)
    for d, (third, out) in enumerate(zip(thirds, outs)):
        for j in range(out.shape[0]):
            mats = [third[j, jnp.bitwise_xor(member, i)] for i in range(radix)]
            slots = jnp.concatenate([ref[j, d] for ref in got], axis=0)
            out[j] = dot(jnp.concatenate(mats, axis=1), slots).astype(BF16)


def group_coefs(j, at, own, crossed, third, radix):
    group, member = place(radix)
    mats = [third[0, j, 0, group * radix + jnp.bitwise_xor(member, i)] for i in range(radix)]
    total = dot(jnp.concatenate(mats, axis=1), jnp.concatenate([ref[at] for ref in own], axis=0))
    return [total.astype(BF16)] + [ref[at] for ref in crossed]


def middle_kernel(radix, groups, offs, third, rhs, basis, row_mats, up_own, up_other, *refs):
    crossed, own_in, (residual_ref,), own, other = take(refs, groups - 1, radix, 1, radix, radix)
    coefs = []
    for j in range(offs):
        coefs += group_coefs(j, j, own_in, crossed, third, radix)
    coefs = jnp.concatenate(coefs, axis=0)
    leaves, leaf_rows = basis.shape[2], basis.shape[3]
    leaf = []
    for k in range(leaves):
        rows = slice(k * leaf_rows, (k + 1) * leaf_rows)
        residual = rhs[0, rows].astype(F32) - dot(row_mats[rows], coefs)
        residual_ref[rows] = residual
        leaf.append(dot_t(basis[0, offs, k], residual.astype(BF16)).astype(BF16))
    leaf = jnp.concatenate(leaf, axis=0)
    put_other(up_other.at[offs], leaf, other, 0)
    put_own(up_own.at[offs], leaf, own, 0)


def last_kernel(radix, groups, offs, third, row_mats, residual, *refs):
    crossed, own_in, (out,) = take(refs, groups - 1, radix, 1)
    coefs = jnp.concatenate(group_coefs(offs, 0, own_in, crossed, third, radix), axis=0)
    out[0] = (residual[...] + dot(row_mats[...], coefs)).astype(BF16)


def after(array, *others):
    return lax.optimization_barrier((array, *others))[0]


def on_device(
    row_size, box_size, solved, rhs, leaf_basis, first_level, second_level, third_level, fourth_level, out_basis
):
    radix = first_level.shape[4]
    groups = box_size // radix
    less = groups - 1
    butterflies = leaf_basis.shape[1]
    offs = solved.shape[0]
    columns = solved.shape[2]
    rank = leaf_basis.shape[4]
    rows = rhs.shape[1]
    depth = radix * rank

    def over_row(array, mask):
        return lax.ppermute(array, "row", [(r, r ^ mask) for r in range(row_size)])

    def over_members(array, mask):
        pairs = [(b, (b // radix) * radix + ((b % radix) ^ mask)) for b in range(box_size)]
        return array if mask == 0 else lax.ppermute(array, "box", pairs)

    def over_groups(array, delta, mask=0):
        pairs = [
            (b, ((b // radix + delta) % groups) * radix + ((b % radix) ^ mask)) for b in range(box_size)
        ]
        return lax.ppermute(array, "box", pairs)

    def call(kernel, name, flops, outs, *args):
        outs = [jax.ShapeDtypeStruct(shape, dtype) for shape, dtype in outs]
        size = sum(a.size * a.dtype.itemsize for a in [*args, *outs])
        return pl.pallas_call(
            kernel,
            out_shape=outs,
            in_specs=[VMEM] * len(args),
            out_specs=[VMEM] * len(outs),
            compiler_params=pltpu.CompilerParams(vmem_limit_bytes=min(16 * MIB + 2 * size, 56 * MIB)),
            cost_estimate=pl.CostEstimate(flops=int(flops), bytes_accessed=0, transcendentals=0),
            name=name,
        )(*args)

    picked = call(
        functools.partial(pick_kernel, radix, groups),
        "pick_third",
        0,
        [((offs, radix, rank, rank), BF16)] * less + [((butterflies - offs, radix, rank, rank), BF16)] * less,
        third_level,
    )
    thirds = [over_groups(a, d + 1) for d, a in enumerate(picked[:less])]
    thirds_last = [over_groups(after(a, *thirds), d + 1) for d, a in enumerate(picked[less:])]

    up_own, up_other, off_rows, last_rows = call(
        functools.partial(weights_kernel, radix, groups, offs, row_size),
        "weights",
        2 * butterflies * rank * (box_size * rank * depth + rows * groups * rank),
        [
            ((butterflies, radix, rank, depth), BF16),
            ((butterflies, radix, less, rank, depth), BF16),
            ((rows, offs * groups * rank), BF16),
            ((rows, groups * rank), BF16),
        ],
        first_level,
        second_level,
        fourth_level,
        out_basis,
    )

    pieces = [solved, over_row(solved, 1)]
    for mask in range(2, row_size, 2):
        far = after(over_row(solved, mask), up_own, *thirds)
        pieces += [far, over_row(far, 1)]

    other_flops = 2 * columns * rank * radix * less * depth
    own_flops = 2 * columns * rank * radix * depth
    leaf_flops = 2 * columns * rank * rows
    row_flops = 2 * columns * rank * (depth + groups * rows)

    def own_out(count):
        return [((count, rank, columns), BF16)] * radix

    def other_out(count):
        return [((count, less, rank, columns), BF16)] * radix

    def add(other, thirds):
        other = [over_members(a, i) for i, a in enumerate(other)]
        count = other[0].shape[0]
        sums = call(
            functools.partial(sum_kernel, radix),
            "sums",
            count * less * 2 * columns * rank * depth,
            [((count, rank, columns), BF16)] * less,
            *other,
            *thirds,
        )
        return sums, [over_groups(a, less - d) for d, a in enumerate(sums)]

    leaf, *other = call(
        functools.partial(off_kernel, radix, row_size),
        "off_levels",
        offs * (leaf_flops + other_flops),
        [((offs, depth, columns), BF16)] + other_out(offs),
        leaf_basis,
        up_other,
        *pieces,
    )
    own = call(own_kernel, "own_levels", offs * own_flops, own_out(offs), after(leaf, *thirds_last), up_own)
    sums, crossed = add(other, thirds)
    own = [over_members(after(a, *sums) if i else a, i) for i, a in enumerate(own)]

    residual, *levels = call(
        functools.partial(middle_kernel, radix, groups, offs),
        "middle_levels",
        offs * row_flops + leaf_flops + other_flops + own_flops,
        [((rows, columns), F32)] + own_out(1) + other_out(1),
        third_level,
        rhs,
        leaf_basis,
        off_rows,
        up_own,
        up_other,
        *crossed,
        *own,
    )
    own, other = levels[:radix], levels[radix:]
    sums, crossed = add(other, thirds_last)
    own = [over_members(after(a, *sums) if i else a, i) for i, a in enumerate(own)]
    return call(
        functools.partial(last_kernel, radix, groups, offs),
        "last_levels",
        row_flops,
        [((1, rows, columns), BF16)],
        third_level,
        last_rows,
        residual,
        *crossed,
        *own,
    )[0]


def solution(mesh):
    placed = (
        P(None, ("box", "row"), None),
        P("row", "box", None),
        P("row", None, "box", None, None),
        P("row", None, "box", None, None, None, None),
        P("row", None, "box", None, None, None),
        P("row", None, "box", None, None, None),
        P("row", None, "box", None, None, None, None),
        P("row", None, "box", None, None),
    )
    return jax.shard_map(
        functools.partial(on_device, mesh.shape["row"], mesh.shape["box"]),
        mesh=mesh,
        in_specs=placed,
        out_specs=P("row", "box", None),
        check_vma=False,
    )
```

time: 138 us -> 84.4 us (0.61)
  waiting for transfers between devices: 67 us -> 44.3 us
  local copies, waits for them, and re-layouts: 20.6 us -> 5.82 us
  between operations: 13.6 us -> 0.11 us
  Pallas kernels: 9.39 us -> 7.62 us
    reduce_scatter x2 -> x0, waiting for transfers between devices: 39.9 us -> none  [add(): lax.psum_scatter(other, 'box', scatter_dimension=0, axis_index_groups=ind...]
    ppermute x6 -> x12, waiting for transfers between devices: 5.82 us -> 23.3 us  [over_members(): return array if mask == 0 else lax.ppermute(array, 'box', pairs)]
    unnamed x50 -> x18, local copies, waits for them, and re-layouts: 20.6 us -> 5.82 us
    ppermute x7 -> x4, starting transfers between devices: 16.8 us -> 7.98 us  [over_groups(): return lax.ppermute(array, 'box', pairs)]
    ppermute x6 -> x12, starting transfers between devices: 6.98 us -> 15.3 us  [over_members(): return array if mask == 0 else lax.ppermute(array, 'box', pairs)]
    pallas_call x6 -> x8, Pallas kernels: 9.39 us -> 7.62 us  [call(): pl.pallas_call(kernel, out_shape=outs, in_specs=[VMEM] * len(args), out_s...]
    ppermute x7 -> x4, waiting for transfers between devices: 19.3 us -> 19.1 us  [over_groups(): return lax.ppermute(array, 'box', pairs)]
  transfers between devices with their start and end apart: 18 -> 19, of which waited for: 10 -> 12; matrix products, arithmetic and copies ran while one was open for 0% -> 0% of each run, Pallas kernels for 2% -> 3%
where the time goes in v6:
time: 84.4 us; the launch traced here: 84 us
  waiting for transfers between devices  44.3 us (52%)
  starting transfers between devices  26.2 us (31%)
  Pallas kernels  7.62 us (9%)
  local copies, waits for them, and re-layouts  5.82 us (7%)
    ppermute x12, waiting for transfers between devices, over_members(): return array if mask == 0 else lax.ppermute(array, 'box', pairs)  23.3 us
    ppermute x4, waiting for transfers between devices, over_groups(): return lax.ppermute(array, 'box', pairs)  19.1 us
    ppermute x12, starting transfers between devices, over_members(): return array if mask == 0 else lax.ppermute(array, 'box', pairs)  15.3 us
    ppermute x4, starting transfers between devices, over_groups(): return lax.ppermute(array, 'box', pairs)  7.98 us
    pallas_call x8, Pallas kernels, call(): pl.pallas_call(kernel, out_shape=outs, in_specs=[VMEM] * len(args), out_s...  7.62 us
    unnamed x18, local copies, waits for them, and re-layouts  5.82 us
    ppermute x3, starting transfers between devices, over_row(): return lax.ppermute(array, 'row', [(r, r ^ mask) for r in range(row_size)])  2.97 us
    ppermute x3, waiting for transfers between devices, over_row(): return lax.ppermute(array, 'row', [(r, r ^ mask) for r in range(row_size)])  1.91 us
  transfers between devices with their start and end apart: 19, of which 12 were waited for; matrix products, arithmetic and copies ran while one was open for 0% of the time, Pallas kernels for 3%

profile of v6, /device:TPU:0, one launch (start us, length us, event | category | flops | bytes accessed | tf_op | source)
XLA Modules:
  0.0 84.0 jit_solution(8465416666593633633)
XLA Ops:
  0.0 3.0 %collective-permute-start.1 = (bf16[2,256,512]{2,1,0:T(8,128)(2,1)}, bf16[2,256,512]{2,1,0:T(8,128)(2,1)S(1)}, u32[]{:S(2)}, u32[]{:S(2)}) collective-permute-start(bf16[2,256,512]{2,1,0:T(8,128)(2,1)} %refs_0_.1), channel_id=1, source_target_pairs={{0,16},{8,24},{16,0},{24,8},{1,17},{9,25},{17,1},{25,9},{2,18},{10... | collective-permute-start | bytes 1572872 | tf_op jit(solution)/shard_map/ppermute | solution.py:188
  3.0 0.0 copy-start
  3.0 1.1 %copy-done = bf16[1,3,1,8,128,128]{5,4,3,2,1,0:T(8,128)(2,1)S(1)} copy-done((bf16[1,3,1,8,128,128]{5,4,3,2,1,0:T(8,128)(2,1)S(1)}, bf16[1,3,1,8,128,128]{5,4,3,2,1,0:T(8,128)(2,1)}, u32[]{:S(2)}) %copy-start) | copy-done | bytes 786456
  4.1 0.0 copy-start.2
  4.1 2.7 %collective-permute-start.2 = (bf16[2,4,128,128]{3,2,1,0:T(8,128)(2,1)S(1)}, bf16[2,4,128,128]{3,2,1,0:T(8,128)(2,1)S(1)}, u32[]{:S(2)}, u32[]{:S(2)}) collective-permute-start(bf16[2,4,128,128]{3,2,1,0:T(8,128)(2,1)S(1)} %get-tuple-element.42), channel_id=1, source_target_pairs={{0,4},{1,5},{2,6},{3,7},{4,0},{5,1},{6,2},{7,3},{8,12},{9,13},{10,... | collective-permute-start | bytes 786440 | tf_op jit(solution)/shard_map/ppermute | solution.py:198
  6.8 0.0 collective-permute-start
  6.8 0.0 copy-start.3
  6.8 1.4 %copy-done.3 = bf16[1,3,1,4,4,128,128]{6,5,4,3,2,1,0:T(8,128)(2,1)S(1)} copy-done((bf16[1,3,1,4,4,128,128]{6,5,4,3,2,1,0:T(8,128)(2,1)S(1)}, bf16[1,3,1,4,4,128,128]{6,5,4,3,2,1,0:T(8,128)(2,1)}, u32[]{:S(2)}) %copy-start.3) | copy-done | bytes 1572888
  8.2 0.0 copy-start.5
  8.2 1.1 %copy-done.5 = bf16[1,3,1,8,128,128]{5,4,3,2,1,0:T(8,128)(2,1)S(1)} copy-done((bf16[1,3,1,8,128,128]{5,4,3,2,1,0:T(8,128)(2,1)S(1)}, bf16[1,3,1,8,128,128]{5,4,3,2,1,0:T(8,128)(2,1)}, u32[]{:S(2)}) %copy-start.5) | copy-done | bytes 786456
  9.3 0.0 copy-start.6
  9.3 1.1 %copy-done.6 = bf16[1,3,2,512,128]{4,3,2,1,0:T(8,128)(2,1)S(1)} copy-done((bf16[1,3,2,512,128]{4,3,2,1,0:T(8,128)(2,1)S(1)}, bf16[1,3,2,512,128]{4,3,2,1,0:T(8,128)(2,1)}, u32[]{:S(2)}) %copy-start.6) | copy-done | bytes 786456
  10.5 0.0 copy-start.8
  10.5 1.0 %copy-done.8 = bf16[1,3,1,2,2,128,128]{6,5,4,3,2,1,0:T(8,128)(2,1)S(1)} copy-done((bf16[1,3,1,2,2,128,128]{6,5,4,3,2,1,0:T(8,128)(2,1)S(1)}, bf16[1,3,1,2,2,128,128]{6,5,4,3,2,1,0:T(8,128)(2,1)}, u32[]{:S(2)}) %copy-start.8) | copy-done | bytes 393240
  11.5 0.0 copy-start.7
  11.5 1.4 %weights.1 = (bf16[3,4,128,512]{3,2,1,0:T(8,128)(2,1)S(1)}, bf16[3,4,1,128,512]{4,3,2,1,0:T(8,128)(2,1)S(1)}, bf16[1024,512]{1,0:T(8,128)(2,1)S(1)}, bf16[1024,256]{1,0:T(8,128)(2,1)S(1)}) custom-call(bf16[1,3,1,4,4,128,128]{6,5,4,3,2,1,0:T(8,128)(2,1)S(1)} %copy-done.3, bf16[1,3,1,8,128,128]{5,4,3,2,1,0:T(8,128)(2,1)S(1)} %copy-done.5, ...), custom_call_target="tpu_custom_call" | custom-call | flops 603979776 | tf_op jit(solution)/shard_map/weights/pallas_call | solution.py:203
  12.9 5.6 %collective-permute-done.2.refs_4_ = bf16[2,4,128,128]{3,2,1,0:T(8,128)(2,1)S(1)} collective-permute-done((bf16[2,4,128,128]{3,2,1,0:T(8,128)(2,1)S(1)}, bf16[2,4,128,128]{3,2,1,0:T(8,128)(2,1)S(1)}, u32[]{:S(2)}, u32[]{:S(2)}) %collective-permute-start.2) | collective-permute-done | bytes 262176 | tf_op jit(solution)/shard_map/ppermute | solution.py:198
  18.5 0.0 collective-permute-done.1.refs_2_
  18.5 0.0 collective-permute-start.3
  18.5 0.0 collective-permute-done.refs_1_
  18.5 1.9 %collective-permute-done.3.refs_3_ = bf16[2,256,512]{2,1,0:T(8,128)(2,1)S(1)} collective-permute-done((bf16[2,256,512]{2,1,0:T(8,128)(2,1)S(1)}, bf16[2,256,512]{2,1,0:T(8,128)(2,1)S(1)}, u32[]{:S(2)}, u32[]{:S(2)}) %collective-permute-start.3) | collective-permute-done | bytes 524320 | tf_op jit(solution)/shard_map/ppermute | solution.py:188
  20.4 0.0 copy-done.2
  20.4 0.0 copy-done.7
  20.4 1.2 %off_levels.1 = (bf16[2,512,512]{2,1,0:T(8,128)(2,1)S(1)}, bf16[2,1,128,512]{3,2,1,0:T(8,128)(2,1)S(1)}, bf16[2,1,128,512]{3,2,1,0:T(8,128)(2,1)S(1)}, bf16[2,1,...) custom-call(bf16[1,3,4,256,128]{4,3,2,1,0:T(8,128)(2,1)S(1)} %copy-done.2, ...), custom_call_target="tpu_custom_call" | custom-call | flops 805306368 | tf_op jit(solution)/shard_map/off_levels/pallas_call | solution.py:203
  21.6 1.6 %collective-permute-start.4 = (bf16[2,1,128,512]{3,2,1,0:T(8,128)(2,1)S(1)}, bf16[2,1,128,512]{3,2,1,0:T(8,128)(2,1)S(1)}, u32[]{:S(2)}, u32[]{:S(2)}) collective-permute-start(bf16[2,1,128,512]{3,2,1,0:T(8,128)(2,1)S(1)} %get-tuple-element.45), channel_id=1, source_target_pairs={{0,1},{1,0},{2,3},{3,2},{4,5},{5,4},{6,7},{7,6},{8,9},{9,8},{10,11... | collective-permute-start | bytes 786440 | tf_op jit(solution)/shard_map/ppermute | solution.py:192
  23.1 0.7 collective-permute-start.5
  23.8 1.3 %collective-permute-start.6 = (bf16[2,1,128,512]{3,2,1,0:T(8,128)(2,1)S(1)}, bf16[2,1,128,512]{3,2,1,0:T(8,128)(2,1)S(1)}, u32[]{:S(2)}, u32[]{:S(2)}) collective-permute-start(bf16[2,1,128,512]{3,2,1,0:T(8,128)(2,1)S(1)} %get-tuple-element.47), channel_id=1, source_target_pairs={{0,3},{1,2},{2,1},{3,0},{4,7},{5,6},{6,5},{7,4},{8,11},{9,10},{10,... | collective-permute-start | bytes 786440 | tf_op jit(solution)/shard_map/ppermute | solution.py:192
  25.1 2.1 %collective-permute-start.8 = (bf16[1,4,128,128]{3,2,1,0:T(8,128)(2,1)S(1)}, bf16[1,4,128,128]{3,2,1,0:T(8,128)(2,1)S(1)}, u32[]{:S(2)}, u32[]{:S(2)}) collective-permute-start(bf16[1,4,128,128]{3,2,1,0:T(8,128)(2,1)S(1)} %get-tuple-element.50), channel_id=1, source_target_pairs={{0,4},{1,5},{2,6},{3,7},{4,0},{5,1},{6,2},{7,3},{8,12},{9,13},{10,... | collective-permute-start | bytes 393224 | tf_op jit(solution)/shard_map/ppermute | solution.py:198
  27.2 10.6 %collective-permute-done.8.refs_4_ = bf16[1,4,128,128]{3,2,1,0:T(8,128)(2,1)S(1)} collective-permute-done((bf16[1,4,128,128]{3,2,1,0:T(8,128)(2,1)S(1)}, bf16[1,4,128,128]{3,2,1,0:T(8,128)(2,1)S(1)}, u32[]{:S(2)}, u32[]{:S(2)}) %collective-permute-start.8) | collective-permute-done | bytes 131104 | tf_op jit(solution)/shard_map/ppermute | solution.py:198
  37.8 0.0 copy-start.1
  37.8 0.0 copy-start.4
  37.8 0.7 own_levels.1
  38.5 0.0 collective-permute-done.4.refs_1_
  38.6 0.0 collective-permute-done.5.refs_2_
  38.6 1.0 %collective-permute-done.6.refs_3_ = bf16[2,1,128,512]{3,2,1,0:T(8,128)(2,1)S(1)} collective-permute-done((bf16[2,1,128,512]{3,2,1,0:T(8,128)(2,1)S(1)}, bf16[2,1,128,512]{3,2,1,0:T(8,128)(2,1)S(1)}, u32[]{:S(2)}, u32[]{:S(2)}) %collective-permute-start.6) | collective-permute-done | bytes 262176 | tf_op jit(solution)/shard_map/ppermute | solution.py:192
  39.6 0.3 sums.2
  39.9 1.5 %collective-permute-start.9 = (bf16[2,128,512]{2,1,0:T(8,128)(2,1)S(1)}, bf16[2,128,512]{2,1,0:T(8,128)(2,1)S(1)}, u32[]{:S(2)}, u32[]{:S(2)}) collective-permute-start(bf16[2,128,512]{2,1,0:T(8,128)(2,1)S(1)} %get-tuple-element.54), channel_id=1, source_target_pairs={{0,1},{1,0},{2,3},{3,2},{4,5},{5,4},{6,7},{7,6},{8,9},{9,8},{10,11... | collective-permute-start | bytes 786440 | tf_op jit(solution)/shard_map/ppermute | solution.py:192
  41.5 2.1 %collective-permute-start.10 = (bf16[2,128,512]{2,1,0:T(8,128)(2,1)S(1)}, bf16[2,128,512]{2,1,0:T(8,128)(2,1)S(1)}, u32[]{:S(2)}, u32[]{:S(2)}) collective-permute-start(bf16[2,128,512]{2,1,0:T(8,128)(2,1)S(1)} %get-tuple-element.56), channel_id=1, source_target_pairs={{0,2},{1,3},{2,0},{3,1},{4,6},{5,7},{6,4},{7,5},{8,10},{9,11},{10,... | collective-permute-start | bytes 786440 | tf_op jit(solution)/shard_map/ppermute | solution.py:192
  43.6 0.9 %collective-permute-start.11 = (bf16[2,128,512]{2,1,0:T(8,128)(2,1)S(1)}, bf16[2,128,512]{2,1,0:T(8,128)(2,1)S(1)}, u32[]{:S(2)}, u32[]{:S(2)}) collective-permute-start(bf16[2,128,512]{2,1,0:T(8,128)(2,1)S(1)} %get-tuple-element.58), channel_id=1, source_target_pairs={{0,3},{1,2},{2,1},{3,0},{4,7},{5,6},{6,5},{7,4},{8,11},{9,10},{10,... | collective-permute-start | bytes 786440 | tf_op jit(solution)/shard_map/ppermute | solution.py:192
  44.5 1.3 %collective-permute-start.7 = (bf16[2,128,512]{2,1,0:T(8,128)(2,1)S(1)}, bf16[2,128,512]{2,1,0:T(8,128)(2,1)S(1)}, u32[]{:S(2)}, u32[]{:S(2)}) collective-permute-start(bf16[2,128,512]{2,1,0:T(8,128)(2,1)S(1)} %sums.2), channel_id=1, source_target_pairs={{0,4},{1,5},{2,6},{3,7},{4,0},{5,1},{6,2},{7,3},{8,12},{9,13},{10,... | collective-permute-start | bytes 786440 | tf_op jit(solution)/shard_map/ppermute | solution.py:198
  45.8 1.4 %collective-permute-done.9.refs_2_ = bf16[2,128,512]{2,1,0:T(8,128)(2,1)S(1)} collective-permute-done((bf16[2,128,512]{2,1,0:T(8,128)(2,1)S(1)}, bf16[2,128,512]{2,1,0:T(8,128)(2,1)S(1)}, u32[]{:S(2)}, u32[]{:S(2)}) %collective-permute-start.9) | collective-permute-done | bytes 262176 | tf_op jit(solution)/shard_map/ppermute | solution.py:192
  47.2 9.3 %collective-permute-done.10.refs_3_ = bf16[2,128,512]{2,1,0:T(8,128)(2,1)S(1)} collective-permute-done((bf16[2,128,512]{2,1,0:T(8,128)(2,1)S(1)}, bf16[2,128,512]{2,1,0:T(8,128)(2,1)S(1)}, u32[]{:S(2)}, u32[]{:S(2)}) %collective-permute-start.10) | collective-permute-done | bytes 262176 | tf_op jit(solution)/shard_map/ppermute | solution.py:192
  56.4 4.8 %collective-permute-done.11.refs_4_ = bf16[2,128,512]{2,1,0:T(8,128)(2,1)S(1)} collective-permute-done((bf16[2,128,512]{2,1,0:T(8,128)(2,1)S(1)}, bf16[2,128,512]{2,1,0:T(8,128)(2,1)S(1)}, u32[]{:S(2)}, u32[]{:S(2)}) %collective-permute-start.11) | collective-permute-done | bytes 262176 | tf_op jit(solution)/shard_map/ppermute | solution.py:192
  61.3 0.0 collective-permute-done.7.refs_0_
  61.3 0.0 copy-done.1
  61.3 0.0 copy-done.4
  61.3 2.2 %middle_levels.1 = (f32[1024,512]{1,0:T(8,128)S(1)}, bf16[1,128,512]{2,1,0:T(8,128)(2,1)S(1)}, bf16[1,128,512]{2,1,0:T(8,128)(2,1)S(1)}, bf16[1,128,512]{2,1,0:T...) custom-call(bf16[1,3,1,8,128,128]{5,4,3,2,1,0:T(8,128)(2,1)S(1)} %co, ...), custom_call_target="tpu_custom_call" | custom-call | flops 1342177280 | tf_op jit(solution)/shard_map/middle_levels/pallas_call | solution.py:203
  63.5 0.6 collective-permute-start.12
  64.1 0.7 collective-permute-start.13
  64.8 2.2 %collective-permute-start.14 = (bf16[1,1,128,512]{3,2,1,0:T(8,128)(2,1)S(1)}, bf16[1,1,128,512]{3,2,1,0:T(8,128)(2,1)S(1)}, u32[]{:S(2)}, u32[]{:S(2)}) collective-permute-start(bf16[1,1,128,512]{3,2,1,0:T(8,128)(2,1)S(1)} %get-tuple-element.63), channel_id=1, source_target_pairs={{0,3},{1,2},{2,1},{3,0},{4,7},{5,6},{6,5},{7,4},{8,11},{9,10},{10,... | collective-permute-start | bytes 393224 | tf_op jit(solution)/shard_map/ppermute | solution.py:192
  67.0 2.9 %collective-permute-done.12.refs_1_ = bf16[1,1,128,512]{3,2,1,0:T(8,128)(2,1)S(1)} collective-permute-done((bf16[1,1,128,512]{3,2,1,0:T(8,128)(2,1)S(1)}, bf16[1,1,128,512]{3,2,1,0:T(8,128)(2,1)S(1)}, u32[]{:S(2)}, u32[]{:S(2)}) %collective-permute-start.12) | collective-permute-done | bytes 131104 | tf_op jit(solution)/shard_map/ppermute | solution.py:192
  69.9 0.0 collective-permute-done.13.refs_2_
  69.9 1.5 %collective-permute-done.14.refs_3_ = bf16[1,1,128,512]{3,2,1,0:T(8,128)(2,1)S(1)} collective-permute-done((bf16[1,1,128,512]{3,2,1,0:T(8,128)(2,1)S(1)}, bf16[1,1,128,512]{3,2,1,0:T(8,128)(2,1)S(1)}, u32[]{:S(2)}, u32[]{:S(2)}) %collective-permute-start.14) | collective-permute-done | bytes 131104 | tf_op jit(solution)/shard_map/ppermute | solution.py:192
  71.4 0.2 sums.3
  71.6 0.8 collective-permute-start.16
  72.4 1.3 %collective-permute-start.17 = (bf16[1,128,512]{2,1,0:T(8,128)(2,1)S(1)}, bf16[1,128,512]{2,1,0:T(8,128)(2,1)S(1)}, u32[]{:S(2)}, u32[]{:S(2)}) collective-permute-start(bf16[1,128,512]{2,1,0:T(8,128)(2,1)S(1)} %get-tuple-element.68), channel_id=1, source_target_pairs={{0,2},{1,3},{2,0},{3,1},{4,6},{5,7},{6,4},{7,5},{8,10},{9,11},{10,... | collective-permute-start | bytes 393224 | tf_op jit(solution)/shard_map/ppermute | solution.py:192
  73.7 1.4 %collective-permute-start.18 = (bf16[1,128,512]{2,1,0:T(8,128)(2,1)S(1)}, bf16[1,128,512]{2,1,0:T(8,128)(2,1)S(1)}, u32[]{:S(2)}, u32[]{:S(2)}) collective-permute-start(bf16[1,128,512]{2,1,0:T(8,128)(2,1)S(1)} %get-tuple-element.70), channel_id=1, source_target_pairs={{0,3},{1,2},{2,1},{3,0},{4,7},{5,6},{6,5},{7,4},{8,11},{9,10},{10,... | collective-permute-start | bytes 393224 | tf_op jit(solution)/shard_map/ppermute | solution.py:192
  75.2 2.0 %collective-permute-start.15 = (bf16[1,128,512]{2,1,0:T(8,128)(2,1)S(1)}, bf16[1,128,512]{2,1,0:T(8,128)(2,1)S(1)}, u32[]{:S(2)}, u32[]{:S(2)}) collective-permute-start(bf16[1,128,512]{2,1,0:T(8,128)(2,1)S(1)} %sums.3), channel_id=1, source_target_pairs={{0,4},{1,5},{2,6},{3,7},{4,0},{5,1},{6,2},{7,3},{8,12},{9,13},{10,... | collective-permute-start | bytes 393224 | tf_op jit(solution)/shard_map/ppermute | solution.py:198
  77.1 0.0 collective-permute-done.16.refs_2_
  77.1 0.5 collective-permute-done.17.refs_3_
  77.7 1.9 %collective-permute-done.18.refs_4_ = bf16[1,128,512]{2,1,0:T(8,128)(2,1)S(1)} collective-permute-done((bf16[1,128,512]{2,1,0:T(8,128)(2,1)S(1)}, bf16[1,128,512]{2,1,0:T(8,128)(2,1)S(1)}, u32[]{:S(2)}, u32[]{:S(2)}) %collective-permute-start.18) | collective-permute-done | bytes 131104 | tf_op jit(solution)/shard_map/ppermute | solution.py:192
  79.6 2.8 %collective-permute-done.15.refs_0_ = bf16[1,128,512]{2,1,0:T(8,128)(2,1)S(1)} collective-permute-done((bf16[1,128,512]{2,1,0:T(8,128)(2,1)S(1)}, bf16[1,128,512]{2,1,0:T(8,128)(2,1)S(1)}, u32[]{:S(2)}, u32[]{:S(2)}) %collective-permute-start.15) | collective-permute-done | bytes 131104 | tf_op jit(solution)/shard_map/ppermute | solution.py:198
  82.4 1.6 %last_levels.1 = bf16[1,1024,512]{2,1,0:T(8,128)(2,1)} custom-call(bf16[1,3,1,8,128,128]{5,4,3,2,1,0:T(8,128)(2,1)S(1)} %copy-done.1, bf16[1024,256]{1,0:T(8,128)(2,1)S(1)} %get-tuple-element.38.row_mats, f32[1024,512]{1,0:T(8,128)S(1)} %get-tuple-element.59.residual, bf16[1,128,512]{2,1,0:T(8,128)(2,1)S(1)} %collective-permute-done.15.refs_0_, ...), custom_call_target="tpu_custom_call" | custom-call | flops 335544320 | tf_op jit(solution)/shard_map/last_levels/pallas_call | solution.py:203
  (1 shorter events, 0.0 us)
Async XLA Ops:
  0.0 18.5 %collective-permute-start.1 = (bf16[2,256,512]{2,1,0:T(8,128)(2,1)}, bf16[2,256,512]{2,1,0:T(8,128)(2,1)S(1)}, u32[]{:S(2)}, u32[]{:S(2)}) collective-permute-start(bf16[2,256,512]{2,1,0:T(8,128)(2,1)} %refs_0_.1), channel_id=1, source_target_pairs={{0,16},{8,24},{16,0},{24,8},{1,17},{9,25},{17,1},{25,9},{2,18},{10... | collective-permute-start | bytes 1572872 | tf_op jit(solution)/shard_map/ppermute | solution.py:188
  3.0 1.1 %copy-start = (bf16[1,3,1,8,128,128]{5,4,3,2,1,0:T(8,128)(2,1)S(1)}, bf16[1,3,1,8,128,128]{5,4,3,2,1,0:T(8,128)(2,1)}, u32[]{:S(2)}) copy-start(bf16[1,3,1,8,128,128]{5,4,3,2,1,0:T(8,128)(2,1)} %third.5) | copy-start | bytes 2359300
  4.1 16.3 %copy-start.2 = (bf16[1,3,4,256,128]{4,3,2,1,0:T(8,128)(2,1)S(1)}, bf16[1,3,4,256,128]{4,3,2,1,0:T(8,128)(2,1)}, u32[]{:S(2)}) copy-start(bf16[1,3,4,256,128]{4,3,2,1,0:T(8,128)(2,1)} %basis.3) | copy-start | bytes 2359300
  4.1 14.3 %collective-permute-start.2 = (bf16[2,4,128,128]{3,2,1,0:T(8,128)(2,1)S(1)}, bf16[2,4,128,128]{3,2,1,0:T(8,128)(2,1)S(1)}, u32[]{:S(2)}, u32[]{:S(2)}) collective-permute-start(bf16[2,4,128,128]{3,2,1,0:T(8,128)(2,1)S(1)} %get-tuple-element.42), channel_id=1, source_target_pairs={{0,4},{1,5},{2,6},{3,7},{4,0},{5,1},{6,2},{7,3},{8,12},{9,13},{10,... | collective-permute-start | bytes 786440 | tf_op jit(solution)/shard_map/ppermute | solution.py:198
  6.8 11.7 %collective-permute-start = (bf16[2,256,512]{2,1,0:T(8,128)(2,1)}, bf16[2,256,512]{2,1,0:T(8,128)(2,1)S(1)}, u32[]{:S(2)}, u32[]{:S(2)}) collective-permute-start(bf16[2,256,512]{2,1,0:T(8,128)(2,1)} %refs_0_.1), channel_id=1, source_target_pairs={{0,8},{8,0},{16,24},{24,16},{1,9},{9,1},{17,25},{25,17},{2,10},{10... | collective-permute-start | bytes 1572872 | tf_op jit(solution)/shard_map/ppermute | solution.py:188
  6.8 1.4 %copy-start.3 = (bf16[1,3,1,4,4,128,128]{6,5,4,3,2,1,0:T(8,128)(2,1)S(1)}, bf16[1,3,1,4,4,128,128]{6,5,4,3,2,1,0:T(8,128)(2,1)}, u32[]{:S(2)}) copy-start(bf16[1,3,1,4,4,128,128]{6,5,4,3,2,1,0:T(8,128)(2,1)} %first.1) | copy-start | bytes 4718596
  8.2 1.1 %copy-start.5 = (bf16[1,3,1,8,128,128]{5,4,3,2,1,0:T(8,128)(2,1)S(1)}, bf16[1,3,1,8,128,128]{5,4,3,2,1,0:T(8,128)(2,1)}, u32[]{:S(2)}) copy-start(bf16[1,3,1,8,128,128]{5,4,3,2,1,0:T(8,128)(2,1)} %second.1) | copy-start | bytes 2359300
  9.3 1.1 %copy-start.6 = (bf16[1,3,2,512,128]{4,3,2,1,0:T(8,128)(2,1)S(1)}, bf16[1,3,2,512,128]{4,3,2,1,0:T(8,128)(2,1)}, u32[]{:S(2)}) copy-start(bf16[1,3,2,512,128]{4,3,2,1,0:T(8,128)(2,1)} %out_basis.1) | copy-start | bytes 2359300
  10.5 1.0 %copy-start.8 = (bf16[1,3,1,2,2,128,128]{6,5,4,3,2,1,0:T(8,128)(2,1)S(1)}, bf16[1,3,1,2,2,128,128]{6,5,4,3,2,1,0:T(8,128)(2,1)}, u32[]{:S(2)}) copy-start(bf16[1,3,1,2,2,128,128]{6,5,4,3,2,1,0:T(8,128)(2,1)} %fourth.1) | copy-start | bytes 1179652
  11.5 8.9 %copy-start.7 = (bf16[2,256,512]{2,1,0:T(8,128)(2,1)S(1)}, bf16[2,256,512]{2,1,0:T(8,128)(2,1)}, u32[]{:S(2)}) copy-start(bf16[2,256,512]{2,1,0:T(8,128)(2,1)} %refs_0_.1) | copy-start | bytes 1572868
  18.5 1.9 %collective-permute-start.3 = (bf16[2,256,512]{2,1,0:T(8,128)(2,1)S(1)}, bf16[2,256,512]{2,1,0:T(8,128)(2,1)S(1)}, u32[]{:S(2)}, u32[]{:S(2)}) collective-permute-start(bf16[2,256,512]{2,1,0:T(8,128)(2,1)S(1)} %collective-permute-done.1.refs_2_), channel_id=1, source_target_pairs={{0,8},{8,0},{16,24},{24,16},{1,9},{9,1},{17,25},{25,17},{2,10},{10... | collective-permute-start | bytes 1572872 | tf_op jit(solution)/shard_map/ppermute | solution.py:188
  21.6 17.0 %collective-permute-start.4 = (bf16[2,1,128,512]{3,2,1,0:T(8,128)(2,1)S(1)}, bf16[2,1,128,512]{3,2,1,0:T(8,128)(2,1)S(1)}, u32[]{:S(2)}, u32[]{:S(2)}) collective-permute-start(bf16[2,1,128,512]{3,2,1,0:T(8,128)(2,1)S(1)} %get-tuple-element.45), channel_id=1, source_target_pairs={{0,1},{1,0},{2,3},{3,2},{4,5},{5,4},{6,7},{7,6},{8,9},{9,8},{10,11... | collective-permute-start | bytes 786440 | tf_op jit(solution)/shard_map/ppermute | solution.py:192
  23.1 15.4 %collective-permute-start.5 = (bf16[2,1,128,512]{3,2,1,0:T(8,128)(2,1)S(1)}, bf16[2,1,128,512]{3,2,1,0:T(8,128)(2,1)S(1)}, u32[]{:S(2)}, u32[]{:S(2)}) collective-permute-start(bf16[2,1,128,512]{3,2,1,0:T(8,128)(2,1)S(1)} %get-tuple-element.46), channel_id=1, source_target_pairs={{0,2},{1,3},{2,0},{3,1},{4,6},{5,7},{6,4},{7,5},{8,10},{9,11},{10,... | collective-permute-start | bytes 786440 | tf_op jit(solution)/shard_map/ppermute | solution.py:192
  23.8 15.8 %collective-permute-start.6 = (bf16[2,1,128,512]{3,2,1,0:T(8,128)(2,1)S(1)}, bf16[2,1,128,512]{3,2,1,0:T(8,128)(2,1)S(1)}, u32[]{:S(2)}, u32[]{:S(2)}) collective-permute-start(bf16[2,1,128,512]{3,2,1,0:T(8,128)(2,1)S(1)} %get-tuple-element.47), channel_id=1, source_target_pairs={{0,3},{1,2},{2,1},{3,0},{4,7},{5,6},{6,5},{7,4},{8,11},{9,10},{10,... | collective-permute-start | bytes 786440 | tf_op jit(solution)/shard_map/ppermute | solution.py:192
  25.1 12.7 %collective-permute-start.8 = (bf16[1,4,128,128]{3,2,1,0:T(8,128)(2,1)S(1)}, bf16[1,4,128,128]{3,2,1,0:T(8,128)(2,1)S(1)}, u32[]{:S(2)}, u32[]{:S(2)}) collective-permute-start(bf16[1,4,128,128]{3,2,1,0:T(8,128)(2,1)S(1)} %get-tuple-element.50), channel_id=1, source_target_pairs={{0,4},{1,5},{2,6},{3,7},{4,0},{5,1},{6,2},{7,3},{8,12},{9,13},{10,... | collective-permute-start | bytes 393224 | tf_op jit(solution)/shard_map/ppermute | solution.py:198
  37.8 23.4 %copy-start.1 = (bf16[1,3,1,8,128,128]{5,4,3,2,1,0:T(8,128)(2,1)S(1)}, bf16[1,3,1,8,128,128]{5,4,3,2,1,0:T(8,128)(2,1)}, u32[]{:S(2)}) copy-start(bf16[1,3,1,8,128,128]{5,4,3,2,1,0:T(8,128)(2,1)} %third.5) | copy-start | bytes 2359300
  37.8 23.4 %copy-start.4 = (bf16[1,1024,512]{2,1,0:T(8,128)(2,1)S(1)}, bf16[1,1024,512]{2,1,0:T(8,128)(2,1)}, u32[]{:S(2)}) copy-start(bf16[1,1024,512]{2,1,0:T(8,128)(2,1)} %rhs.1) | copy-start | bytes 3145732
  39.9 7.3 %collective-permute-start.9 = (bf16[2,128,512]{2,1,0:T(8,128)(2,1)S(1)}, bf16[2,128,512]{2,1,0:T(8,128)(2,1)S(1)}, u32[]{:S(2)}, u32[]{:S(2)}) collective-permute-start(bf16[2,128,512]{2,1,0:T(8,128)(2,1)S(1)} %get-tuple-element.54), channel_id=1, source_target_pairs={{0,1},{1,0},{2,3},{3,2},{4,5},{5,4},{6,7},{7,6},{8,9},{9,8},{10,11... | collective-permute-start | bytes 786440 | tf_op jit(solution)/shard_map/ppermute | solution.py:192
  41.5 15.0 %collective-permute-start.10 = (bf16[2,128,512]{2,1,0:T(8,128)(2,1)S(1)}, bf16[2,128,512]{2,1,0:T(8,128)(2,1)S(1)}, u32[]{:S(2)}, u32[]{:S(2)}) collective-permute-start(bf16[2,128,512]{2,1,0:T(8,128)(2,1)S(1)} %get-tuple-element.56), channel_id=1, source_target_pairs={{0,2},{1,3},{2,0},{3,1},{4,6},{5,7},{6,4},{7,5},{8,10},{9,11},{10,... | collective-permute-start | bytes 786440 | tf_op jit(solution)/shard_map/ppermute | solution.py:192
  43.6 17.7 %collective-permute-start.11 = (bf16[2,128,512]{2,1,0:T(8,128)(2,1)S(1)}, bf16[2,128,512]{2,1,0:T(8,128)(2,1)S(1)}, u32[]{:S(2)}, u32[]{:S(2)}) collective-permute-start(bf16[2,128,512]{2,1,0:T(8,128)(2,1)S(1)} %get-tuple-element.58), channel_id=1, source_target_pairs={{0,3},{1,2},{2,1},{3,0},{4,7},{5,6},{6,5},{7,4},{8,11},{9,10},{10,... | collective-permute-start | bytes 786440 | tf_op jit(solution)/shard_map/ppermute | solution.py:192
  44.5 16.7 %collective-permute-start.7 = (bf16[2,128,512]{2,1,0:T(8,128)(2,1)S(1)}, bf16[2,128,512]{2,1,0:T(8,128)(2,1)S(1)}, u32[]{:S(2)}, u32[]{:S(2)}) collective-permute-start(bf16[2,128,512]{2,1,0:T(8,128)(2,1)S(1)} %sums.2), channel_id=1, source_target_pairs={{0,4},{1,5},{2,6},{3,7},{4,0},{5,1},{6,2},{7,3},{8,12},{9,13},{10,... | collective-permute-start | bytes 786440 | tf_op jit(solution)/shard_map/ppermute | solution.py:198
  63.5 6.4 %collective-permute-start.12 = (bf16[1,1,128,512]{3,2,1,0:T(8,128)(2,1)S(1)}, bf16[1,1,128,512]{3,2,1,0:T(8,128)(2,1)S(1)}, u32[]{:S(2)}, u32[]{:S(2)}) collective-permute-start(bf16[1,1,128,512]{3,2,1,0:T(8,128)(2,1)S(1)} %get-tuple-element.61), channel_id=1, source_target_pairs={{0,1},{1,0},{2,3},{3,2},{4,5},{5,4},{6,7},{7,6},{8,9},{9,8},{10,11... | collective-permute-start | bytes 393224 | tf_op jit(solution)/shard_map/ppermute | solution.py:192
  64.1 5.9 %collective-permute-start.13 = (bf16[1,1,128,512]{3,2,1,0:T(8,128)(2,1)S(1)}, bf16[1,1,128,512]{3,2,1,0:T(8,128)(2,1)S(1)}, u32[]{:S(2)}, u32[]{:S(2)}) collective-permute-start(bf16[1,1,128,512]{3,2,1,0:T(8,128)(2,1)S(1)} %get-tuple-element.62), channel_id=1, source_target_pairs={{0,2},{1,3},{2,0},{3,1},{4,6},{5,7},{6,4},{7,5},{8,10},{9,11},{10,... | collective-permute-start | bytes 393224 | tf_op jit(solution)/shard_map/ppermute | solution.py:192
  64.8 6.6 %collective-permute-start.14 = (bf16[1,1,128,512]{3,2,1,0:T(8,128)(2,1)S(1)}, bf16[1,1,128,512]{3,2,1,0:T(8,128)(2,1)S(1)}, u32[]{:S(2)}, u32[]{:S(2)}) collective-permute-start(bf16[1,1,128,512]{3,2,1,0:T(8,128)(2,1)S(1)} %get-tuple-element.63), channel_id=1, source_target_pairs={{0,3},{1,2},{2,1},{3,0},{4,7},{5,6},{6,5},{7,4},{8,11},{9,10},{10,... | collective-permute-start | bytes 393224 | tf_op jit(solution)/shard_map/ppermute | solution.py:192
  71.6 5.5 %collective-permute-start.16 = (bf16[1,128,512]{2,1,0:T(8,128)(2,1)S(1)}, bf16[1,128,512]{2,1,0:T(8,128)(2,1)S(1)}, u32[]{:S(2)}, u32[]{:S(2)}) collective-permute-start(bf16[1,128,512]{2,1,0:T(8,128)(2,1)S(1)} %get-tuple-element.66), channel_id=1, source_target_pairs={{0,1},{1,0},{2,3},{3,2},{4,5},{5,4},{6,7},{7,6},{8,9},{9,8},{10,11... | collective-permute-start | bytes 393224 | tf_op jit(solution)/shard_map/ppermute | solution.py:192
  72.4 5.3 %collective-permute-start.17 = (bf16[1,128,512]{2,1,0:T(8,128)(2,1)S(1)}, bf16[1,128,512]{2,1,0:T(8,128)(2,1)S(1)}, u32[]{:S(2)}, u32[]{:S(2)}) collective-permute-start(bf16[1,128,512]{2,1,0:T(8,128)(2,1)S(1)} %get-tuple-element.68), channel_id=1, source_target_pairs={{0,2},{1,3},{2,0},{3,1},{4,6},{5,7},{6,4},{7,5},{8,10},{9,11},{10,... | collective-permute-start | bytes 393224 | tf_op jit(solution)/shard_map/ppermute | solution.py:192
  73.7 5.9 %collective-permute-start.18 = (bf16[1,128,512]{2,1,0:T(8,128)(2,1)S(1)}, bf16[1,128,512]{2,1,0:T(8,128)(2,1)S(1)}, u32[]{:S(2)}, u32[]{:S(2)}) collective-permute-start(bf16[1,128,512]{2,1,0:T(8,128)(2,1)S(1)} %get-tuple-element.70), channel_id=1, source_target_pairs={{0,3},{1,2},{2,1},{3,0},{4,7},{5,6},{6,5},{7,4},{8,11},{9,10},{10,... | collective-permute-start | bytes 393224 | tf_op jit(solution)/shard_map/ppermute | solution.py:192
  75.2 7.3 %collective-permute-start.15 = (bf16[1,128,512]{2,1,0:T(8,128)(2,1)S(1)}, bf16[1,128,512]{2,1,0:T(8,128)(2,1)S(1)}, u32[]{:S(2)}, u32[]{:S(2)}) collective-permute-start(bf16[1,128,512]{2,1,0:T(8,128)(2,1)S(1)} %sums.3), channel_id=1, source_target_pairs={{0,4},{1,5},{2,6},{3,7},{4,0},{5,1},{6,2},{7,3},{8,12},{9,13},{10,... | collective-permute-start | bytes 393224 | tf_op jit(solution)/shard_map/ppermute | solution.py:198

commit v7 on v6

--- a/solution.py
+++ b/solution.py
@@ -10,6 +10,7 @@
 F32 = jnp.float32
 BF16 = jnp.bfloat16
 MIB = 1024 * 1024
+ACROSS, ALONG, BOTH = 1, 2, 3
 VMEM = pl.BlockSpec(memory_space=pltpu.VMEM)
 
 
@@ -49,13 +50,21 @@
         start += out.shape[0] if at % (groups - 1) == groups - 2 else 0
 
 
+def second_kernel(radix, groups, second, *outs):
+    group, member = place(radix)
+    for i, out in zip((ALONG, BOTH), outs):
+        for j in range(out.shape[0]):
+            for delta in range(groups):
+                out[j, delta] = second[0, j, 0, wrap(group - delta, groups) * radix + jnp.bitwise_xor(member, i)]
+
+
 def leaf_order(row, leaves, row_size):
     per_leaf = row_size // leaves
     return [jnp.bitwise_xor(lax.div(row, per_leaf), t) for t in range(leaves)]
 
 
 def weights_kernel(radix, groups, offs, row_size, first, second, fourth, out_basis, *outs):
-    up_own, up_other, off_rows, last_rows = outs
+    up_own, up_other, up_mid, off_rows, last_rows = outs
     levels = first.shape[3]
     slots = second.shape[3]
     rank = fourth.shape[6]
@@ -74,6 +83,11 @@
             up_own[j, i] = up(group * radix + box)
             for delta in range(1, groups):
                 up_other[j, i, delta - 1] = up(wrap(group - delta, groups) * radix + box)
+        if j < offs:
+            for delta in range(groups):
+                slot = wrap(group - delta, groups) * radix + jnp.bitwise_xor(member, ALONG)
+                level = lax.div(slot, slots // levels)
+                up_mid[j, delta] = jnp.concatenate([first[0, j, 0, level, k] for k in order], axis=1)
         out, start = (off_rows, j * groups * rank) if j < offs else (last_rows, 0)
         for h in range(fourth.shape[3]):
             mats = [fourth[0, j, 0, h, wrap(group + delta, groups)] for delta in range(groups)]
@@ -96,13 +110,14 @@
         ref[at] = coef[i * rank : (i + 1) * rank]
 
 
-def off_kernel(radix, pieces, basis, up_other, *refs):
-    parts, (leaf_ref,), other = take(refs, pieces, 1, radix)
+def off_kernel(pieces, basis, up_other, up_mid, *refs):
+    parts, (leaf_ref, keep, across, along) = take(refs, pieces, 4)
     row = lax.axis_index("row")
     leaves, leaf_rows = basis.shape[2], basis.shape[3]
     rows = parts[0].shape[1]
     per_leaf = leaf_rows // rows
     order = leaf_order(row, leaves, pieces)
+    less, rank, columns = keep.shape[1:]
     for j in range(parts[0].shape[0]):
         leaf = []
         for t in range(leaves):
@@ -118,16 +133,48 @@
             leaf.append(total.astype(BF16))
         leaf = jnp.concatenate(leaf, axis=0)
         leaf_ref[j] = leaf
-        put_other(up_other.at[j], leaf, other, j)
-
-
-def own_kernel(leaf, up_own, *own):
+        mats = [up_other[j, 0], up_other[j, ACROSS], up_mid[j, 1:]]
+        mats = jnp.concatenate([m.reshape(less * rank, m.shape[2]) for m in mats], axis=0)
+        coef = dot(mats, leaf).astype(BF16)
+        for i, ref in enumerate((keep, across, along)):
+            ref[j] = coef[i * less * rank : (i + 1) * less * rank].reshape(less, rank, columns)
+
+
+def own_kernel(leaf, up_own, up_mid, *own):
+    rank = up_mid.shape[2]
     for j in range(leaf.shape[0]):
-        put_own(up_own.at[j], leaf[j], own, j)
+        coef = dot(jnp.concatenate([up_own[j, 0], up_own[j, ACROSS], up_mid[j, 0]], axis=0), leaf[j]).astype(BF16)
+        for i, ref in enumerate(own):
+            ref[j] = coef[i * rank : (i + 1) * rank]
+
+
+def slots_of(got, second_along, second_both, j, delta):
+    keep, across, along, both = got
+    return jnp.concatenate(
+        [
+            keep,
+            across,
+            dot(second_along[j, delta], along).astype(BF16),
+            dot(second_both[j, delta], both).astype(BF16),
+        ],
+        axis=0,
+    )
+
+
+def off_sum_kernel(second_along, second_both, *refs):
+    got, thirds, outs = take(refs, 4, (len(refs) - 4) // 2, (len(refs) - 4) // 2)
+    radix = thirds[0].shape[1]
+    _, member = place(radix)
+    for d, (third, out) in enumerate(zip(thirds, outs)):
+        for j in range(out.shape[0]):
+            mats = [third[j, jnp.bitwise_xor(member, i)] for i in range(radix)]
+            slots = slots_of([ref[j, d] for ref in got], second_along, second_both, j, d + 1)
+            out[j] = dot(jnp.concatenate(mats, axis=1), slots).astype(BF16)
 
 
 def sum_kernel(radix, *refs):
     got, thirds, outs = take(refs, radix, (len(refs) - radix) // 2, (len(refs) - radix) // 2)
+    got = got[::-1]
     _, member = place(radix)
     for d, (third, out) in enumerate(zip(thirds, outs)):
         for j in range(out.shape[0]):
@@ -136,18 +183,20 @@
             out[j] = dot(jnp.concatenate(mats, axis=1), slots).astype(BF16)
 
 
-def group_coefs(j, at, own, crossed, third, radix):
+def group_coef(j, slots, third, radix):
     group, member = place(radix)
     mats = [third[0, j, 0, group * radix + jnp.bitwise_xor(member, i)] for i in range(radix)]
-    total = dot(jnp.concatenate(mats, axis=1), jnp.concatenate([ref[at] for ref in own], axis=0))
-    return [total.astype(BF16)] + [ref[at] for ref in crossed]
-
-
-def middle_kernel(radix, groups, offs, third, rhs, basis, row_mats, up_own, up_other, *refs):
+    return dot(jnp.concatenate(mats, axis=1), slots).astype(BF16)
+
+
+def middle_kernel(
+    radix, groups, offs, third, rhs, basis, row_mats, up_own, up_other, second_along, second_both, *refs
+):
     crossed, own_in, (residual_ref,), own, other = take(refs, groups - 1, radix, 1, radix, radix)
     coefs = []
     for j in range(offs):
-        coefs += group_coefs(j, j, own_in, crossed, third, radix)
+        slots = slots_of([ref[j] for ref in own_in], second_along, second_both, j, 0)
+        coefs += [group_coef(j, slots, third, radix)] + [ref[j] for ref in crossed]
     coefs = jnp.concatenate(coefs, axis=0)
     leaves, leaf_rows = basis.shape[2], basis.shape[3]
     leaf = []
@@ -163,7 +212,10 @@
 
 def last_kernel(radix, groups, offs, third, row_mats, residual, *refs):
     crossed, own_in, (out,) = take(refs, groups - 1, radix, 1)
-    coefs = jnp.concatenate(group_coefs(offs, 0, own_in, crossed, third, radix), axis=0)
+    own_in = own_in[::-1]
+    slots = jnp.concatenate([ref[0] for ref in own_in], axis=0)
+    coefs = [group_coef(offs, slots, third, radix)] + [ref[0] for ref in crossed]
+    coefs = jnp.concatenate(coefs, axis=0)
     out[0] = (residual[...] + dot(row_mats[...], coefs)).astype(BF16)
 
 
@@ -220,13 +272,14 @@
     thirds = [over_groups(a, d + 1) for d, a in enumerate(picked[:less])]
     thirds_last = [over_groups(after(a, *thirds), d + 1) for d, a in enumerate(picked[less:])]
 
-    up_own, up_other, off_rows, last_rows = call(
+    up_own, up_other, up_mid, off_rows, last_rows = call(
         functools.partial(weights_kernel, radix, groups, offs, row_size),
         "weights",
         2 * butterflies * rank * (box_size * rank * depth + rows * groups * rank),
         [
             ((butterflies, radix, rank, depth), BF16),
             ((butterflies, radix, less, rank, depth), BF16),
+            ((offs, groups, rank, depth), BF16),
             ((rows, offs * groups * rank), BF16),
             ((rows, groups * rank), BF16),
         ],
@@ -236,9 +289,18 @@
         out_basis,
     )
 
+    seconds = call(
+        functools.partial(second_kernel, radix, groups),
+        "pick_second",
+        0,
+        [((offs, groups, rank, rank), BF16)] * 2,
+        second_level,
+    )
+    seconds = [over_members(a, i) for i, a in zip((ALONG, BOTH), seconds)]
+
     pieces = [solved, over_row(solved, 1)]
     for mask in range(2, row_size, 2):
-        far = after(over_row(solved, mask), up_own, *thirds)
+        far = after(over_row(solved, mask), up_own, *thirds, *seconds)
         pieces += [far, over_row(far, 1)]
 
     other_flops = 2 * columns * rank * radix * less * depth
@@ -252,31 +314,43 @@
     def other_out(count):
         return [((count, less, rank, columns), BF16)] * radix
 
-    def add(other, thirds):
-        other = [over_members(a, i) for i, a in enumerate(other)]
-        count = other[0].shape[0]
-        sums = call(
-            functools.partial(sum_kernel, radix),
-            "sums",
-            count * less * 2 * columns * rank * depth,
-            [((count, rank, columns), BF16)] * less,
-            *other,
-            *thirds,
-        )
-        return sums, [over_groups(a, less - d) for d, a in enumerate(sums)]
-
-    leaf, *other = call(
-        functools.partial(off_kernel, radix, row_size),
+    def cross(sums):
+        return [over_groups(a, less - d) for d, a in enumerate(sums)]
+
+    leaf, keep, across, along = call(
+        functools.partial(off_kernel, row_size),
         "off_levels",
         offs * (leaf_flops + other_flops),
-        [((offs, depth, columns), BF16)] + other_out(offs),
+        [((offs, depth, columns), BF16)] + other_out(offs)[:3],
         leaf_basis,
         up_other,
+        up_mid,
         *pieces,
     )
-    own = call(own_kernel, "own_levels", offs * own_flops, own_out(offs), after(leaf, *thirds_last), up_own)
-    sums, crossed = add(other, thirds)
-    own = [over_members(after(a, *sums) if i else a, i) for i, a in enumerate(own)]
+    along = over_members(along, ALONG)
+    across = over_members(across, ACROSS)
+    both = over_members(after(along, across, *thirds_last), ACROSS)
+    own = call(own_kernel, "own_levels", offs * own_flops, own_out(offs)[:3], leaf, up_own, up_mid)
+    own_along = over_members(after(own[2], along), ALONG)
+    sums = call(
+        off_sum_kernel,
+        "off_sums",
+        offs * less * 2 * columns * rank * depth,
+        [((offs, rank, columns), BF16)] * less,
+        *seconds,
+        keep,
+        across,
+        along,
+        both,
+        *thirds,
+    )
+    crossed = cross(sums)
+    own = [
+        own[0],
+        over_members(after(own[1], both), ACROSS),
+        own_along,
+    ]
+    own.append(over_members(after(own_along, own[1], *sums), ACROSS))
 
     residual, *levels = call(
         functools.partial(middle_kernel, radix, groups, offs),
@@ -289,11 +363,21 @@
         off_rows,
         up_own,
         up_other,
+        *seconds,
         *crossed,
         *own,
     )
     own, other = levels[:radix], levels[radix:]
-    sums, crossed = add(other, thirds_last)
+    other = [over_members(a, i) for i, a in reversed(list(enumerate(other)))]
+    sums = call(
+        functools.partial(sum_kernel, radix),
+        "sums",
+        less * 2 * columns * rank * depth,
+        [((1, rank, columns), BF16)] * less,
+        *other,
+        *thirds_last,
+    )
+    crossed = cross(sums)
     own = [over_members(after(a, *sums) if i else a, i) for i, a in enumerate(own)]
     return call(
         functools.partial(last_kernel, radix, groups, offs),
@@ -304,7 +388,7 @@
         last_rows,
         residual,
         *crossed,
-        *own,
+        *own[::-1],
     )[0]
 
 

time: 84.4 us -> 80.7 us (0.956)
  waiting for transfers between devices: 44.3 us -> 39 us
  starting transfers between devices: 26.2 us -> 27.4 us
    ppermute x4, waiting for transfers between devices: 19.1 us -> 12.6 us  [over_groups(): return lax.ppermute(array, 'box', pairs)]
    ppermute x12 -> x14, waiting for transfers between devices: 23.3 us -> 24.6 us  [over_members(): return array if mask == 0 else lax.ppermute(array, 'box', pairs)]
    ppermute x12 -> x14, starting transfers between devices: 15.3 us -> 15.9 us  [over_members(): return array if mask == 0 else lax.ppermute(array, 'box', pairs)]
    pallas_call x8 -> x9, Pallas kernels: 7.62 us -> 7.94 us  [call(): pl.pallas_call(kernel, out_shape=outs, in_specs=[VMEM] * len(args), out_s...]
    unnamed x18 -> x20, local copies, waits for them, and re-layouts: 5.82 us -> 5.83 us
  transfers between devices with their start and end apart: 19 -> 21, of which waited for: 12 -> 14; matrix products, arithmetic and copies ran while one was open for 0% -> 0% of each run, Pallas kernels for 3% -> 3%
where the time goes in v7:
time: 80.7 us; the launch traced here: 80.4 us
  waiting for transfers between devices  39 us (48%)
  starting transfers between devices  27.4 us (34%)
  Pallas kernels  7.94 us (10%)
  local copies, waits for them, and re-layouts  5.83 us (7%)
    ppermute x14, waiting for transfers between devices, over_members(): return array if mask == 0 else lax.ppermute(array, 'box', pairs)  24.6 us
    ppermute x14, starting transfers between devices, over_members(): return array if mask == 0 else lax.ppermute(array, 'box', pairs)  15.9 us
    ppermute x4, waiting for transfers between devices, over_groups(): return lax.ppermute(array, 'box', pairs)  12.6 us
    ppermute x4, starting transfers between devices, over_groups(): return lax.ppermute(array, 'box', pairs)  8.59 us
    pallas_call x9, Pallas kernels, call(): pl.pallas_call(kernel, out_shape=outs, in_specs=[VMEM] * len(args), out_s...  7.94 us
    unnamed x20, local copies, waits for them, and re-layouts  5.83 us
    ppermute x3, starting transfers between devices, over_row(): return lax.ppermute(array, 'row', [(r, r ^ mask) for r in range(row_size)])  2.97 us
    ppermute x3, waiting for transfers between devices, over_row(): return lax.ppermute(array, 'row', [(r, r ^ mask) for r in range(row_size)])  1.9 us
  transfers between devices with their start and end apart: 21, of which 14 were waited for; matrix products, arithmetic and copies ran while one was open for 0% of the time, Pallas kernels for 3%

profile of v7, /device:TPU:0, one launch (start us, length us, event | category | flops | bytes accessed | tf_op | source)
XLA Modules:
  0.0 80.4 jit_solution(13868903560173696990)
XLA Ops:
  0.0 3.0 %collective-permute-start.3 = (bf16[2,256,512]{2,1,0:T(8,128)(2,1)}, bf16[2,256,512]{2,1,0:T(8,128)(2,1)S(1)}, u32[]{:S(2)}, u32[]{:S(2)}) collective-permute-start(bf16[2,256,512]{2,1,0:T(8,128)(2,1)} %refs_0_.1), channel_id=1, source_target_pairs={{0,16},{8,24},{16,0},{24,8},{1,17},{9,25},{17,1},{25,9},{2,18},{10... | collective-permute-start | bytes 1572872 | tf_op jit(solution)/shard_map/ppermute | solution.py:240
  3.0 1.1 %copy-done = bf16[1,3,1,8,128,128]{5,4,3,2,1,0:T(8,128)(2,1)S(1)} copy-done((bf16[1,3,1,8,128,128]{5,4,3,2,1,0:T(8,128)(2,1)S(1)}, bf16[1,3,1,8,128,128]{5,4,3,2,1,0:T(8,128)(2,1)}, u32[]{:S(2)}) %copy-start) | copy-done | bytes 786456
  4.1 0.0 copy-start.4
  4.1 2.7 %collective-permute-start.4 = (bf16[2,4,128,128]{3,2,1,0:T(8,128)(2,1)S(1)}, bf16[2,4,128,128]{3,2,1,0:T(8,128)(2,1)S(1)}, u32[]{:S(2)}, u32[]{:S(2)}) collective-permute-start(bf16[2,4,128,128]{3,2,1,0:T(8,128)(2,1)S(1)} %get-tuple-element.46), channel_id=1, source_target_pairs={{0,4},{1,5},{2,6},{3,7},{4,0},{5,1},{6,2},{7,3},{8,12},{9,13},{10,... | collective-permute-start | bytes 786440 | tf_op jit(solution)/shard_map/ppermute | solution.py:250
  6.8 1.1 %copy-done.3 = bf16[1,3,1,8,128,128]{5,4,3,2,1,0:T(8,128)(2,1)S(1)} copy-done((bf16[1,3,1,8,128,128]{5,4,3,2,1,0:T(8,128)(2,1)S(1)}, bf16[1,3,1,8,128,128]{5,4,3,2,1,0:T(8,128)(2,1)}, u32[]{:S(2)}) %copy-start.3) | copy-done | bytes 786456
  7.9 1.6 %collective-permute-start = (bf16[2,2,128,128]{3,2,1,0:T(8,128)(2,1)S(1)}, bf16[2,2,128,128]{3,2,1,0:T(8,128)(2,1)S(1)}, u32[]{:S(2)}, u32[]{:S(2)}) collective-permute-start(bf16[2,2,128,128]{3,2,1,0:T(8,128)(2,1)S(1)} %get-tuple-element.43), channel_id=1, source_target_pairs={{0,2},{1,3},{2,0},{3,1},{4,6},{5,7},{6,4},{7,5},{8,10},{9,11},{10,... | collective-permute-start | bytes 393224 | tf_op jit(solution)/shard_map/ppermute | solution.py:244
  9.6 0.0 copy-start.2
  9.6 1.4 %collective-permute-start.1 = (bf16[2,2,128,128]{3,2,1,0:T(8,128)(2,1)S(1)}, bf16[2,2,128,128]{3,2,1,0:T(8,128)(2,1)S(1)}, u32[]{:S(2)}, u32[]{:S(2)}) collective-permute-start(bf16[2,2,128,128]{3,2,1,0:T(8,128)(2,1)S(1)} %get-tuple-element.44), channel_id=1, source_target_pairs={{0,3},{1,2},{2,1},{3,0},{4,7},{5,6},{6,5},{7,4},{8,11},{9,10},{10,... | collective-permute-start | bytes 393224 | tf_op jit(solution)/shard_map/ppermute | solution.py:244
  11.0 0.0 collective-permute-start.2
  11.0 0.0 copy-done.4
  11.0 0.0 copy-start.5
  11.0 1.4 %copy-done.5 = bf16[1,3,1,4,4,128,128]{6,5,4,3,2,1,0:T(8,128)(2,1)S(1)} copy-done((bf16[1,3,1,4,4,128,128]{6,5,4,3,2,1,0:T(8,128)(2,1)S(1)}, bf16[1,3,1,4,4,128,128]{6,5,4,3,2,1,0:T(8,128)(2,1)}, u32[]{:S(2)}) %copy-start.5) | copy-done | bytes 1572888
  12.4 1.1 %copy-done.7 = bf16[1,3,2,512,128]{4,3,2,1,0:T(8,128)(2,1)S(1)} copy-done((bf16[1,3,2,512,128]{4,3,2,1,0:T(8,128)(2,1)S(1)}, bf16[1,3,2,512,128]{4,3,2,1,0:T(8,128)(2,1)}, u32[]{:S(2)}) %copy-start.7) | copy-done | bytes 786456
  13.5 1.0 %copy-done.9 = bf16[1,3,1,2,2,128,128]{6,5,4,3,2,1,0:T(8,128)(2,1)S(1)} copy-done((bf16[1,3,1,2,2,128,128]{6,5,4,3,2,1,0:T(8,128)(2,1)S(1)}, bf16[1,3,1,2,2,128,128]{6,5,4,3,2,1,0:T(8,128)(2,1)}, u32[]{:S(2)}) %copy-start.9) | copy-done | bytes 393240
  14.5 1.4 %weights.1 = (bf16[3,4,128,512]{3,2,1,0:T(8,128)(2,1)S(1)}, bf16[3,4,1,128,512]{4,3,2,1,0:T(8,128)(2,1)S(1)}, bf16[2,2,128,512]{3,2,1,0:T(8,128)(2,1)S(1)}, bf16...) custom-call(bf16[1,3,1,4,4,128,128]{6,5,4,3,2,1,0:T(8,128)(2,1)S(1)} %copy-done.5, ...), custom_call_target="tpu_custom_call" | custom-call | flops 603979776 | tf_op jit(solution)/shard_map/weights/pallas_call | solution.py:255
  15.9 0.4 collective-permute-done.second_along
  16.3 4.6 %collective-permute-done.1.second_both = bf16[2,2,128,128]{3,2,1,0:T(8,128)(2,1)S(1)} collective-permute-done((bf16[2,2,128,128]{3,2,1,0:T(8,128)(2,1)S(1)}, bf16[2,2,128,128]{3,2,1,0:T(8,128)(2,1)S(1)}, u32[]{:S(2)}, u32[]{:S(2)}) %collective-permute-start.1) | collective-permute-done | bytes 131104 | tf_op jit(solution)/shard_map/ppermute | solution.py:244
  20.9 0.0 collective-permute-done.4.refs_4_
  20.9 0.0 collective-permute-done.3.refs_2_
  20.9 0.0 collective-permute-start.5
  20.9 0.0 collective-permute-done.2.refs_1_
  21.0 1.9 %collective-permute-done.5.refs_3_ = bf16[2,256,512]{2,1,0:T(8,128)(2,1)S(1)} collective-permute-done((bf16[2,256,512]{2,1,0:T(8,128)(2,1)S(1)}, bf16[2,256,512]{2,1,0:T(8,128)(2,1)S(1)}, u32[]{:S(2)}, u32[]{:S(2)}) %collective-permute-start.5) | collective-permute-done | bytes 524320 | tf_op jit(solution)/shard_map/ppermute | solution.py:240
  22.8 0.0 copy-done.2
  22.8 0.0 copy-done.8
  22.9 1.0 %off_levels.1 = (bf16[2,512,512]{2,1,0:T(8,128)(2,1)S(1)}, bf16[2,1,128,512]{3,2,1,0:T(8,128)(2,1)S(1)}, bf16[2,1,128,512]{3,2,1,0:T(8,128)(2,1)S(1)}, bf16[2,1,128,512]{3,2,1,0:T(8,128)(2,1)S(1)}) custom-call(bf16[1,3,4,256,128]{4,3,2,1,0:T(8,128)(2,1)S(1)} %copy-done.2, bf16[3,4,1,128,512]{4,3,2,1,0:T(8,128)(2,1)S(1)} %get-tuple-element.42.up_other, ...), custom_call_target="tpu_custom_call" | custom-call | flops 805306368 | tf_op jit(solution)/shard_map/off_levels/pallas_call | solution.py:255
  23.9 0.9 %collective-permute-start.6 = (bf16[2,1,128,512]{3,2,1,0:T(8,128)(2,1)S(1)}, bf16[2,1,128,512]{3,2,1,0:T(8,128)(2,1)S(1)}, u32[]{:S(2)}, u32[]{:S(2)}) collective-permute-start(bf16[2,1,128,512]{3,2,1,0:T(8,128)(2,1)S(1)} %get-tuple-element.49), channel_id=1, source_target_pairs={{0,1},{1,0},{2,3},{3,2},{4,5},{5,4},{6,7},{7,6},{8,9},{9,8},{10,11... | collective-permute-start | bytes 786440 | tf_op jit(solution)/shard_map/ppermute | solution.py:244
  24.8 0.0 collective-permute-start.7
  24.8 2.8 %collective-permute-start.8 = (bf16[1,4,128,128]{3,2,1,0:T(8,128)(2,1)S(1)}, bf16[1,4,128,128]{3,2,1,0:T(8,128)(2,1)S(1)}, u32[]{:S(2)}, u32[]{:S(2)}) collective-permute-start(bf16[1,4,128,128]{3,2,1,0:T(8,128)(2,1)S(1)} %get-tuple-element.52), channel_id=1, source_target_pairs={{0,4},{1,5},{2,6},{3,7},{4,0},{5,1},{6,2},{7,3},{8,12},{9,13},{10,... | collective-permute-start | bytes 393224 | tf_op jit(solution)/shard_map/ppermute | solution.py:250
  27.5 5.9 %collective-permute-done.8.refs_4_ = bf16[1,4,128,128]{3,2,1,0:T(8,128)(2,1)S(1)} collective-permute-done((bf16[1,4,128,128]{3,2,1,0:T(8,128)(2,1)S(1)}, bf16[1,4,128,128]{3,2,1,0:T(8,128)(2,1)S(1)}, u32[]{:S(2)}, u32[]{:S(2)}) %collective-permute-start.8) | collective-permute-done | bytes 131104 | tf_op jit(solution)/shard_map/ppermute | solution.py:250
  33.5 0.0 collective-permute-done.6.refs_1_
  33.5 2.2 %collective-permute-done.7.refs_2_ = bf16[2,1,128,512]{3,2,1,0:T(8,128)(2,1)S(1)} collective-permute-done((bf16[2,1,128,512]{3,2,1,0:T(8,128)(2,1)S(1)}, bf16[2,1,128,512]{3,2,1,0:T(8,128)(2,1)S(1)}, u32[]{:S(2)}, u32[]{:S(2)}) %collective-permute-start.7) | collective-permute-done | bytes 262176 | tf_op jit(solution)/shard_map/ppermute | solution.py:244
  35.7 1.2 %collective-permute-start.9 = (bf16[2,1,128,512]{3,2,1,0:T(8,128)(2,1)S(1)}, bf16[2,1,128,512]{3,2,1,0:T(8,128)(2,1)S(1)}, u32[]{:S(2)}, u32[]{:S(2)}) collective-permute-start(bf16[2,1,128,512]{3,2,1,0:T(8,128)(2,1)S(1)} %collective-permute-done.7.refs_2_), channel_id=1, source_target_pairs={{0,1},{1,0},{2,3},{3,2},{4,5},{5,4},{6,7},{7,6},{8,9},{9,8},{10,11... | collective-permute-start | bytes 786440 | tf_op jit(solution)/shard_map/ppermute | solution.py:244
  36.9 0.6 own_levels.1
  37.4 0.0 copy-start.1
  37.4 0.0 copy-start.6
  37.5 1.4 %collective-permute-start.12 = (bf16[2,128,512]{2,1,0:T(8,128)(2,1)S(1)}, bf16[2,128,512]{2,1,0:T(8,128)(2,1)S(1)}, u32[]{:S(2)}, u32[]{:S(2)}) collective-permute-start(bf16[2,128,512]{2,1,0:T(8,128)(2,1)S(1)} %get-tuple-element.59), channel_id=1, source_target_pairs={{0,2},{1,3},{2,0},{3,1},{4,6},{5,7},{6,4},{7,5},{8,10},{9,11},{10,... | collective-permute-start | bytes 786440 | tf_op jit(solution)/shard_map/ppermute | solution.py:244
  38.8 4.1 %collective-permute-done.9.refs_3_ = bf16[2,1,128,512]{3,2,1,0:T(8,128)(2,1)S(1)} collective-permute-done((bf16[2,1,128,512]{3,2,1,0:T(8,128)(2,1)S(1)}, bf16[2,1,128,512]{3,2,1,0:T(8,128)(2,1)S(1)}, u32[]{:S(2)}, u32[]{:S(2)}) %collective-permute-start.9) | collective-permute-done | bytes 262176 | tf_op jit(solution)/shard_map/ppermute | solution.py:244
  43.0 1.1 %collective-permute-start.11 = (bf16[2,128,512]{2,1,0:T(8,128)(2,1)S(1)}, bf16[2,128,512]{2,1,0:T(8,128)(2,1)S(1)}, u32[]{:S(2)}, u32[]{:S(2)}) collective-permute-start(bf16[2,128,512]{2,1,0:T(8,128)(2,1)S(1)} %get-tuple-element.57), channel_id=1, source_target_pairs={{0,1},{1,0},{2,3},{3,2},{4,5},{5,4},{6,7},{7,6},{8,9},{9,8},{10,11... | collective-permute-start | bytes 786440 | tf_op jit(solution)/shard_map/ppermute | solution.py:244
  44.1 0.6 off_sums.1
  44.7 1.3 %collective-permute-start.10 = (bf16[2,128,512]{2,1,0:T(8,128)(2,1)S(1)}, bf16[2,128,512]{2,1,0:T(8,128)(2,1)S(1)}, u32[]{:S(2)}, u32[]{:S(2)}) collective-permute-start(bf16[2,128,512]{2,1,0:T(8,128)(2,1)S(1)} %off_sums.1), channel_id=1, source_target_pairs={{0,4},{1,5},{2,6},{3,7},{4,0},{5,1},{6,2},{7,3},{8,12},{9,13},{10,... | collective-permute-start | bytes 786440 | tf_op jit(solution)/shard_map/ppermute | solution.py:250
  46.0 0.0 collective-permute-done.12.refs_3_
  46.0 3.7 %collective-permute-done.11.refs_2_ = bf16[2,128,512]{2,1,0:T(8,128)(2,1)S(1)} collective-permute-done((bf16[2,128,512]{2,1,0:T(8,128)(2,1)S(1)}, bf16[2,128,512]{2,1,0:T(8,128)(2,1)S(1)}, u32[]{:S(2)}, u32[]{:S(2)}) %collective-permute-start.11) | collective-permute-done | bytes 262176 | tf_op jit(solution)/shard_map/ppermute | solution.py:244
  49.7 1.2 %collective-permute-start.13 = (bf16[2,128,512]{2,1,0:T(8,128)(2,1)S(1)}, bf16[2,128,512]{2,1,0:T(8,128)(2,1)S(1)}, u32[]{:S(2)}, u32[]{:S(2)}) collective-permute-start(bf16[2,128,512]{2,1,0:T(8,128)(2,1)S(1)} %collective-permute-done.12.refs_3_), channel_id=1, source_target_pairs={{0,1},{1,0},{2,3},{3,2},{4,5},{5,4},{6,7},{7,6},{8,9},{9,8},{10,11... | collective-permute-start | bytes 786440 | tf_op jit(solution)/shard_map/ppermute | solution.py:244
  50.9 6.4 %collective-permute-done.10.refs_0_ = bf16[2,128,512]{2,1,0:T(8,128)(2,1)S(1)} collective-permute-done((bf16[2,128,512]{2,1,0:T(8,128)(2,1)S(1)}, bf16[2,128,512]{2,1,0:T(8,128)(2,1)S(1)}, u32[]{:S(2)}, u32[]{:S(2)}) %collective-permute-start.10) | collective-permute-done | bytes 262176 | tf_op jit(solution)/shard_map/ppermute | solution.py:250
  57.3 0.0 collective-permute-done.13.refs_4_
  57.3 0.0 copy-done.1
  57.3 0.0 copy-done.6
  57.3 2.5 %middle_levels.1 = (f32[1024,512]{1,0:T(8,128)S(1)}, bf16[1,128,512]{2,1,0:T(8,128)(2,1)S(1)}, bf16[1,128,512]{2,1,0:T(8,128)(2,1)S(1)}, bf16[1,128,512]{2,1,0:T...) custom-call(bf16[1,3,1,8,128,128]{5,4,3,2,1,0:T(8,128)(2,1)S(1)} %co, ...), custom_call_target="tpu_custom_call" | custom-call | flops 1342177280 | tf_op jit(solution)/shard_map/middle_levels/pallas_call | solution.py:255
  59.8 0.9 %collective-permute-start.14 = (bf16[1,1,128,512]{3,2,1,0:T(8,128)(2,1)S(1)}, bf16[1,1,128,512]{3,2,1,0:T(8,128)(2,1)S(1)}, u32[]{:S(2)}, u32[]{:S(2)}) collective-permute-start(bf16[1,1,128,512]{3,2,1,0:T(8,128)(2,1)S(1)} %get-tuple-element.62), channel_id=1, source_target_pairs={{0,3},{1,2},{2,1},{3,0},{4,7},{5,6},{6,5},{7,4},{8,11},{9,10},{10,... | collective-permute-start | bytes 393224 | tf_op jit(solution)/shard_map/ppermute | solution.py:244
  60.6 1.7 %collective-permute-start.15 = (bf16[1,1,128,512]{3,2,1,0:T(8,128)(2,1)S(1)}, bf16[1,1,128,512]{3,2,1,0:T(8,128)(2,1)S(1)}, u32[]{:S(2)}, u32[]{:S(2)}) collective-permute-start(bf16[1,1,128,512]{3,2,1,0:T(8,128)(2,1)S(1)} %get-tuple-element.63), channel_id=1, source_target_pairs={{0,2},{1,3},{2,0},{3,1},{4,6},{5,7},{6,4},{7,5},{8,10},{9,11},{10,... | collective-permute-start | bytes 393224 | tf_op jit(solution)/shard_map/ppermute | solution.py:244
  62.3 1.0 %collective-permute-start.16 = (bf16[1,1,128,512]{3,2,1,0:T(8,128)(2,1)S(1)}, bf16[1,1,128,512]{3,2,1,0:T(8,128)(2,1)S(1)}, u32[]{:S(2)}, u32[]{:S(2)}) collective-permute-start(bf16[1,1,128,512]{3,2,1,0:T(8,128)(2,1)S(1)} %get-tuple-element.64), channel_id=1, source_target_pairs={{0,1},{1,0},{2,3},{3,2},{4,5},{5,4},{6,7},{7,6},{8,9},{9,8},{10,11... | collective-permute-start | bytes 393224 | tf_op jit(solution)/shard_map/ppermute | solution.py:244
  63.3 2.9 %collective-permute-done.14.refs_0_ = bf16[1,1,128,512]{3,2,1,0:T(8,128)(2,1)S(1)} collective-permute-done((bf16[1,1,128,512]{3,2,1,0:T(8,128)(2,1)S(1)}, bf16[1,1,128,512]{3,2,1,0:T(8,128)(2,1)S(1)}, u32[]{:S(2)}, u32[]{:S(2)}) %collective-permute-start.14) | collective-permute-done | bytes 131104 | tf_op jit(solution)/shard_map/ppermute | solution.py:244
  66.3 1.4 %collective-permute-done.15.refs_1_ = bf16[1,1,128,512]{3,2,1,0:T(8,128)(2,1)S(1)} collective-permute-done((bf16[1,1,128,512]{3,2,1,0:T(8,128)(2,1)S(1)}, bf16[1,1,128,512]{3,2,1,0:T(8,128)(2,1)S(1)}, u32[]{:S(2)}, u32[]{:S(2)}) %collective-permute-start.15) | collective-permute-done | bytes 131104 | tf_op jit(solution)/shard_map/ppermute | solution.py:244
  67.6 0.1 collective-permute-done.16.refs_2_
  67.7 0.2 sums.1
  67.9 0.9 %collective-permute-start.18 = (bf16[1,128,512]{2,1,0:T(8,128)(2,1)S(1)}, bf16[1,128,512]{2,1,0:T(8,128)(2,1)S(1)}, u32[]{:S(2)}, u32[]{:S(2)}) collective-permute-start(bf16[1,128,512]{2,1,0:T(8,128)(2,1)S(1)} %get-tuple-element.67), channel_id=1, source_target_pairs={{0,3},{1,2},{2,1},{3,0},{4,7},{5,6},{6,5},{7,4},{8,11},{9,10},{10,... | collective-permute-start | bytes 393224 | tf_op jit(solution)/shard_map/ppermute | solution.py:244
  68.8 2.1 %collective-permute-start.19 = (bf16[1,128,512]{2,1,0:T(8,128)(2,1)S(1)}, bf16[1,128,512]{2,1,0:T(8,128)(2,1)S(1)}, u32[]{:S(2)}, u32[]{:S(2)}) collective-permute-start(bf16[1,128,512]{2,1,0:T(8,128)(2,1)S(1)} %get-tuple-element.69), channel_id=1, source_target_pairs={{0,2},{1,3},{2,0},{3,1},{4,6},{5,7},{6,4},{7,5},{8,10},{9,11},{10,... | collective-permute-start | bytes 393224 | tf_op jit(solution)/shard_map/ppermute | solution.py:244
  70.8 0.6 collective-permute-start.20
  71.5 1.8 %collective-permute-start.17 = (bf16[1,128,512]{2,1,0:T(8,128)(2,1)S(1)}, bf16[1,128,512]{2,1,0:T(8,128)(2,1)S(1)}, u32[]{:S(2)}, u32[]{:S(2)}) collective-permute-start(bf16[1,128,512]{2,1,0:T(8,128)(2,1)S(1)} %sums.1), channel_id=1, source_target_pairs={{0,4},{1,5},{2,6},{3,7},{4,0},{5,1},{6,2},{7,3},{8,12},{9,13},{10,... | collective-permute-start | bytes 393224 | tf_op jit(solution)/shard_map/ppermute | solution.py:250
  73.3 2.6 %collective-permute-done.18.refs_1_ = bf16[1,128,512]{2,1,0:T(8,128)(2,1)S(1)} collective-permute-done((bf16[1,128,512]{2,1,0:T(8,128)(2,1)S(1)}, bf16[1,128,512]{2,1,0:T(8,128)(2,1)S(1)}, u32[]{:S(2)}, u32[]{:S(2)}) %collective-permute-start.18) | collective-permute-done | bytes 131104 | tf_op jit(solution)/shard_map/ppermute | solution.py:244
  75.9 2.6 %collective-permute-done.19.refs_2_ = bf16[1,128,512]{2,1,0:T(8,128)(2,1)S(1)} collective-permute-done((bf16[1,128,512]{2,1,0:T(8,128)(2,1)S(1)}, bf16[1,128,512]{2,1,0:T(8,128)(2,1)S(1)}, u32[]{:S(2)}, u32[]{:S(2)}) %collective-permute-start.19) | collective-permute-done | bytes 131104 | tf_op jit(solution)/shard_map/ppermute | solution.py:244
  78.5 0.0 collective-permute-done.20.refs_3_
  78.5 0.2 collective-permute-done.17.refs_0_
  78.7 1.6 %last_levels.1 = bf16[1,1024,512]{2,1,0:T(8,128)(2,1)} custom-call(bf16[1,3,1,8,128,128]{5,4,3,2,1,0:T(8,128)(2,1)S(1)} %copy-done.1, bf16[1024,256]{1,0:T(8,128)(2,1)S(1)} %get-tuple-element.39.row_mats, f32[1024,512]{1,0:T(8,128)S(1)} %get-tuple-element.61.residual, bf16[1,128,512]{2,1,0:T(8,128)(2,1)S(1)} %collective-permute-done.17.refs_0_, ...), custom_call_target="tpu_custom_call" | custom-call | flops 335544320 | tf_op jit(solution)/shard_map/last_levels/pallas_call | solution.py:255
  (7 shorter events, 0.1 us)
Async XLA Ops:
  0.0 20.9 %collective-permute-start.3 = (bf16[2,256,512]{2,1,0:T(8,128)(2,1)}, bf16[2,256,512]{2,1,0:T(8,128)(2,1)S(1)}, u32[]{:S(2)}, u32[]{:S(2)}) collective-permute-start(bf16[2,256,512]{2,1,0:T(8,128)(2,1)} %refs_0_.1), channel_id=1, source_target_pairs={{0,16},{8,24},{16,0},{24,8},{1,17},{9,25},{17,1},{25,9},{2,18},{10... | collective-permute-start | bytes 1572872 | tf_op jit(solution)/shard_map/ppermute | solution.py:240
  3.0 1.1 %copy-start = (bf16[1,3,1,8,128,128]{5,4,3,2,1,0:T(8,128)(2,1)S(1)}, bf16[1,3,1,8,128,128]{5,4,3,2,1,0:T(8,128)(2,1)}, u32[]{:S(2)}) copy-start(bf16[1,3,1,8,128,128]{5,4,3,2,1,0:T(8,128)(2,1)} %third.5) | copy-start | bytes 2359300
  4.1 6.9 %copy-start.4 = (bf16[1,3,1,8,128,128]{5,4,3,2,1,0:T(8,128)(2,1)S(1)}, bf16[1,3,1,8,128,128]{5,4,3,2,1,0:T(8,128)(2,1)}, u32[]{:S(2)}) copy-start(bf16[1,3,1,8,128,128]{5,4,3,2,1,0:T(8,128)(2,1)} %second.3) | copy-start | bytes 2359300
  4.1 16.8 %collective-permute-start.4 = (bf16[2,4,128,128]{3,2,1,0:T(8,128)(2,1)S(1)}, bf16[2,4,128,128]{3,2,1,0:T(8,128)(2,1)S(1)}, u32[]{:S(2)}, u32[]{:S(2)}) collective-permute-start(bf16[2,4,128,128]{3,2,1,0:T(8,128)(2,1)S(1)} %get-tuple-element.46), channel_id=1, source_target_pairs={{0,4},{1,5},{2,6},{3,7},{4,0},{5,1},{6,2},{7,3},{8,12},{9,13},{10,... | collective-permute-start | bytes 786440 | tf_op jit(solution)/shard_map/ppermute | solution.py:250
  6.8 1.1 %copy-start.3 = (bf16[1,3,1,8,128,128]{5,4,3,2,1,0:T(8,128)(2,1)S(1)}, bf16[1,3,1,8,128,128]{5,4,3,2,1,0:T(8,128)(2,1)}, u32[]{:S(2)}) copy-start(bf16[1,3,1,8,128,128]{5,4,3,2,1,0:T(8,128)(2,1)} %second.3) | copy-start | bytes 2359300
  7.9 8.4 %collective-permute-start = (bf16[2,2,128,128]{3,2,1,0:T(8,128)(2,1)S(1)}, bf16[2,2,128,128]{3,2,1,0:T(8,128)(2,1)S(1)}, u32[]{:S(2)}, u32[]{:S(2)}) collective-permute-start(bf16[2,2,128,128]{3,2,1,0:T(8,128)(2,1)S(1)} %get-tuple-element.43), channel_id=1, source_target_pairs={{0,2},{1,3},{2,0},{3,1},{4,6},{5,7},{6,4},{7,5},{8,10},{9,11},{10,... | collective-permute-start | bytes 393224 | tf_op jit(solution)/shard_map/ppermute | solution.py:244
  9.6 13.3 %copy-start.2 = (bf16[1,3,4,256,128]{4,3,2,1,0:T(8,128)(2,1)S(1)}, bf16[1,3,4,256,128]{4,3,2,1,0:T(8,128)(2,1)}, u32[]{:S(2)}) copy-start(bf16[1,3,4,256,128]{4,3,2,1,0:T(8,128)(2,1)} %basis.3) | copy-start | bytes 2359300
  9.6 11.3 %collective-permute-start.1 = (bf16[2,2,128,128]{3,2,1,0:T(8,128)(2,1)S(1)}, bf16[2,2,128,128]{3,2,1,0:T(8,128)(2,1)S(1)}, u32[]{:S(2)}, u32[]{:S(2)}) collective-permute-start(bf16[2,2,128,128]{3,2,1,0:T(8,128)(2,1)S(1)} %get-tuple-element.44), channel_id=1, source_target_pairs={{0,3},{1,2},{2,1},{3,0},{4,7},{5,6},{6,5},{7,4},{8,11},{9,10},{10,... | collective-permute-start | bytes 393224 | tf_op jit(solution)/shard_map/ppermute | solution.py:244
  11.0 10.0 %collective-permute-start.2 = (bf16[2,256,512]{2,1,0:T(8,128)(2,1)}, bf16[2,256,512]{2,1,0:T(8,128)(2,1)S(1)}, u32[]{:S(2)}, u32[]{:S(2)}) collective-permute-start(bf16[2,256,512]{2,1,0:T(8,128)(2,1)} %refs_0_.1), channel_id=1, source_target_pairs={{0,8},{8,0},{16,24},{24,16},{1,9},{9,1},{17,25},{25,17},{2,10},{10... | collective-permute-start | bytes 1572872 | tf_op jit(solution)/shard_map/ppermute | solution.py:240
  11.0 1.4 %copy-start.5 = (bf16[1,3,1,4,4,128,128]{6,5,4,3,2,1,0:T(8,128)(2,1)S(1)}, bf16[1,3,1,4,4,128,128]{6,5,4,3,2,1,0:T(8,128)(2,1)}, u32[]{:S(2)}) copy-start(bf16[1,3,1,4,4,128,128]{6,5,4,3,2,1,0:T(8,128)(2,1)} %first.1) | copy-start | bytes 4718596
  12.4 1.1 %copy-start.7 = (bf16[1,3,2,512,128]{4,3,2,1,0:T(8,128)(2,1)S(1)}, bf16[1,3,2,512,128]{4,3,2,1,0:T(8,128)(2,1)}, u32[]{:S(2)}) copy-start(bf16[1,3,2,512,128]{4,3,2,1,0:T(8,128)(2,1)} %out_basis.1) | copy-start | bytes 2359300
  13.5 1.0 %copy-start.9 = (bf16[1,3,1,2,2,128,128]{6,5,4,3,2,1,0:T(8,128)(2,1)S(1)}, bf16[1,3,1,2,2,128,128]{6,5,4,3,2,1,0:T(8,128)(2,1)}, u32[]{:S(2)}) copy-start(bf16[1,3,1,2,2,128,128]{6,5,4,3,2,1,0:T(8,128)(2,1)} %fourth.1) | copy-start | bytes 1179652
  14.5 8.3 %copy-start.8 = (bf16[2,256,512]{2,1,0:T(8,128)(2,1)S(1)}, bf16[2,256,512]{2,1,0:T(8,128)(2,1)}, u32[]{:S(2)}) copy-start(bf16[2,256,512]{2,1,0:T(8,128)(2,1)} %refs_0_.1) | copy-start | bytes 1572868
  20.9 1.9 %collective-permute-start.5 = (bf16[2,256,512]{2,1,0:T(8,128)(2,1)S(1)}, bf16[2,256,512]{2,1,0:T(8,128)(2,1)S(1)}, u32[]{:S(2)}, u32[]{:S(2)}) collective-permute-start(bf16[2,256,512]{2,1,0:T(8,128)(2,1)S(1)} %collective-permute-done.3.refs_2_), channel_id=1, source_target_pairs={{0,8},{8,0},{16,24},{24,16},{1,9},{9,1},{17,25},{25,17},{2,10},{10... | collective-permute-start | bytes 1572872 | tf_op jit(solution)/shard_map/ppermute | solution.py:240
  23.9 9.6 %collective-permute-start.6 = (bf16[2,1,128,512]{3,2,1,0:T(8,128)(2,1)S(1)}, bf16[2,1,128,512]{3,2,1,0:T(8,128)(2,1)S(1)}, u32[]{:S(2)}, u32[]{:S(2)}) collective-permute-start(bf16[2,1,128,512]{3,2,1,0:T(8,128)(2,1)S(1)} %get-tuple-element.49), channel_id=1, source_target_pairs={{0,1},{1,0},{2,3},{3,2},{4,5},{5,4},{6,7},{7,6},{8,9},{9,8},{10,11... | collective-permute-start | bytes 786440 | tf_op jit(solution)/shard_map/ppermute | solution.py:244
  24.8 10.9 %collective-permute-start.7 = (bf16[2,1,128,512]{3,2,1,0:T(8,128)(2,1)S(1)}, bf16[2,1,128,512]{3,2,1,0:T(8,128)(2,1)S(1)}, u32[]{:S(2)}, u32[]{:S(2)}) collective-permute-start(bf16[2,1,128,512]{3,2,1,0:T(8,128)(2,1)S(1)} %get-tuple-element.50), channel_id=1, source_target_pairs={{0,2},{1,3},{2,0},{3,1},{4,6},{5,7},{6,4},{7,5},{8,10},{9,11},{10,... | collective-permute-start | bytes 786440 | tf_op jit(solution)/shard_map/ppermute | solution.py:244
  24.8 8.7 %collective-permute-start.8 = (bf16[1,4,128,128]{3,2,1,0:T(8,128)(2,1)S(1)}, bf16[1,4,128,128]{3,2,1,0:T(8,128)(2,1)S(1)}, u32[]{:S(2)}, u32[]{:S(2)}) collective-permute-start(bf16[1,4,128,128]{3,2,1,0:T(8,128)(2,1)S(1)} %get-tuple-element.52), channel_id=1, source_target_pairs={{0,4},{1,5},{2,6},{3,7},{4,0},{5,1},{6,2},{7,3},{8,12},{9,13},{10,... | collective-permute-start | bytes 393224 | tf_op jit(solution)/shard_map/ppermute | solution.py:250
  35.7 7.3 %collective-permute-start.9 = (bf16[2,1,128,512]{3,2,1,0:T(8,128)(2,1)S(1)}, bf16[2,1,128,512]{3,2,1,0:T(8,128)(2,1)S(1)}, u32[]{:S(2)}, u32[]{:S(2)}) collective-permute-start(bf16[2,1,128,512]{3,2,1,0:T(8,128)(2,1)S(1)} %collective-permute-done.7.refs_2_), channel_id=1, source_target_pairs={{0,1},{1,0},{2,3},{3,2},{4,5},{5,4},{6,7},{7,6},{8,9},{9,8},{10,11... | collective-permute-start | bytes 786440 | tf_op jit(solution)/shard_map/ppermute | solution.py:244
  37.4 19.8 %copy-start.1 = (bf16[1,3,1,8,128,128]{5,4,3,2,1,0:T(8,128)(2,1)S(1)}, bf16[1,3,1,8,128,128]{5,4,3,2,1,0:T(8,128)(2,1)}, u32[]{:S(2)}) copy-start(bf16[1,3,1,8,128,128]{5,4,3,2,1,0:T(8,128)(2,1)} %third.5) | copy-start | bytes 2359300
  37.4 19.8 %copy-start.6 = (bf16[1,1024,512]{2,1,0:T(8,128)(2,1)S(1)}, bf16[1,1024,512]{2,1,0:T(8,128)(2,1)}, u32[]{:S(2)}) copy-start(bf16[1,1024,512]{2,1,0:T(8,128)(2,1)} %rhs.1) | copy-start | bytes 3145732
  37.5 8.5 %collective-permute-start.12 = (bf16[2,128,512]{2,1,0:T(8,128)(2,1)S(1)}, bf16[2,128,512]{2,1,0:T(8,128)(2,1)S(1)}, u32[]{:S(2)}, u32[]{:S(2)}) collective-permute-start(bf16[2,128,512]{2,1,0:T(8,128)(2,1)S(1)} %get-tuple-element.59), channel_id=1, source_target_pairs={{0,2},{1,3},{2,0},{3,1},{4,6},{5,7},{6,4},{7,5},{8,10},{9,11},{10,... | collective-permute-start | bytes 786440 | tf_op jit(solution)/shard_map/ppermute | solution.py:244
  43.0 6.7 %collective-permute-start.11 = (bf16[2,128,512]{2,1,0:T(8,128)(2,1)S(1)}, bf16[2,128,512]{2,1,0:T(8,128)(2,1)S(1)}, u32[]{:S(2)}, u32[]{:S(2)}) collective-permute-start(bf16[2,128,512]{2,1,0:T(8,128)(2,1)S(1)} %get-tuple-element.57), channel_id=1, source_target_pairs={{0,1},{1,0},{2,3},{3,2},{4,5},{5,4},{6,7},{7,6},{8,9},{9,8},{10,11... | collective-permute-start | bytes 786440 | tf_op jit(solution)/shard_map/ppermute | solution.py:244
  44.7 12.6 %collective-permute-start.10 = (bf16[2,128,512]{2,1,0:T(8,128)(2,1)S(1)}, bf16[2,128,512]{2,1,0:T(8,128)(2,1)S(1)}, u32[]{:S(2)}, u32[]{:S(2)}) collective-permute-start(bf16[2,128,512]{2,1,0:T(8,128)(2,1)S(1)} %off_sums.1), channel_id=1, source_target_pairs={{0,4},{1,5},{2,6},{3,7},{4,0},{5,1},{6,2},{7,3},{8,12},{9,13},{10,... | collective-permute-start | bytes 786440 | tf_op jit(solution)/shard_map/ppermute | solution.py:250
  49.7 7.6 %collective-permute-start.13 = (bf16[2,128,512]{2,1,0:T(8,128)(2,1)S(1)}, bf16[2,128,512]{2,1,0:T(8,128)(2,1)S(1)}, u32[]{:S(2)}, u32[]{:S(2)}) collective-permute-start(bf16[2,128,512]{2,1,0:T(8,128)(2,1)S(1)} %collective-permute-done.12.refs_3_), channel_id=1, source_target_pairs={{0,1},{1,0},{2,3},{3,2},{4,5},{5,4},{6,7},{7,6},{8,9},{9,8},{10,11... | collective-permute-start | bytes 786440 | tf_op jit(solution)/shard_map/ppermute | solution.py:244
  59.8 6.5 %collective-permute-start.14 = (bf16[1,1,128,512]{3,2,1,0:T(8,128)(2,1)S(1)}, bf16[1,1,128,512]{3,2,1,0:T(8,128)(2,1)S(1)}, u32[]{:S(2)}, u32[]{:S(2)}) collective-permute-start(bf16[1,1,128,512]{3,2,1,0:T(8,128)(2,1)S(1)} %get-tuple-element.62), channel_id=1, source_target_pairs={{0,3},{1,2},{2,1},{3,0},{4,7},{5,6},{6,5},{7,4},{8,11},{9,10},{10,... | collective-permute-start | bytes 393224 | tf_op jit(solution)/shard_map/ppermute | solution.py:244
  60.6 7.0 %collective-permute-start.15 = (bf16[1,1,128,512]{3,2,1,0:T(8,128)(2,1)S(1)}, bf16[1,1,128,512]{3,2,1,0:T(8,128)(2,1)S(1)}, u32[]{:S(2)}, u32[]{:S(2)}) collective-permute-start(bf16[1,1,128,512]{3,2,1,0:T(8,128)(2,1)S(1)} %get-tuple-element.63), channel_id=1, source_target_pairs={{0,2},{1,3},{2,0},{3,1},{4,6},{5,7},{6,4},{7,5},{8,10},{9,11},{10,... | collective-permute-start | bytes 393224 | tf_op jit(solution)/shard_map/ppermute | solution.py:244
  62.3 5.4 %collective-permute-start.16 = (bf16[1,1,128,512]{3,2,1,0:T(8,128)(2,1)S(1)}, bf16[1,1,128,512]{3,2,1,0:T(8,128)(2,1)S(1)}, u32[]{:S(2)}, u32[]{:S(2)}) collective-permute-start(bf16[1,1,128,512]{3,2,1,0:T(8,128)(2,1)S(1)} %get-tuple-element.64), channel_id=1, source_target_pairs={{0,1},{1,0},{2,3},{3,2},{4,5},{5,4},{6,7},{7,6},{8,9},{9,8},{10,11... | collective-permute-start | bytes 393224 | tf_op jit(solution)/shard_map/ppermute | solution.py:244
  67.9 8.0 %collective-permute-start.18 = (bf16[1,128,512]{2,1,0:T(8,128)(2,1)S(1)}, bf16[1,128,512]{2,1,0:T(8,128)(2,1)S(1)}, u32[]{:S(2)}, u32[]{:S(2)}) collective-permute-start(bf16[1,128,512]{2,1,0:T(8,128)(2,1)S(1)} %get-tuple-element.67), channel_id=1, source_target_pairs={{0,3},{1,2},{2,1},{3,0},{4,7},{5,6},{6,5},{7,4},{8,11},{9,10},{10,... | collective-permute-start | bytes 393224 | tf_op jit(solution)/shard_map/ppermute | solution.py:244
  68.8 9.7 %collective-permute-start.19 = (bf16[1,128,512]{2,1,0:T(8,128)(2,1)S(1)}, bf16[1,128,512]{2,1,0:T(8,128)(2,1)S(1)}, u32[]{:S(2)}, u32[]{:S(2)}) collective-permute-start(bf16[1,128,512]{2,1,0:T(8,128)(2,1)S(1)} %get-tuple-element.69), channel_id=1, source_target_pairs={{0,2},{1,3},{2,0},{3,1},{4,6},{5,7},{6,4},{7,5},{8,10},{9,11},{10,... | collective-permute-start | bytes 393224 | tf_op jit(solution)/shard_map/ppermute | solution.py:244
  70.8 7.7 %collective-permute-start.20 = (bf16[1,128,512]{2,1,0:T(8,128)(2,1)S(1)}, bf16[1,128,512]{2,1,0:T(8,128)(2,1)S(1)}, u32[]{:S(2)}, u32[]{:S(2)}) collective-permute-start(bf16[1,128,512]{2,1,0:T(8,128)(2,1)S(1)} %get-tuple-element.71), channel_id=1, source_target_pairs={{0,1},{1,0},{2,3},{3,2},{4,5},{5,4},{6,7},{7,6},{8,9},{9,8},{10,11... | collective-permute-start | bytes 393224 | tf_op jit(solution)/shard_map/ppermute | solution.py:244
  71.5 7.3 %collective-permute-start.17 = (bf16[1,128,512]{2,1,0:T(8,128)(2,1)S(1)}, bf16[1,128,512]{2,1,0:T(8,128)(2,1)S(1)}, u32[]{:S(2)}, u32[]{:S(2)}) collective-permute-start(bf16[1,128,512]{2,1,0:T(8,128)(2,1)S(1)} %sums.1), channel_id=1, source_target_pairs={{0,4},{1,5},{2,6},{3,7},{4,0},{5,1},{6,2},{7,3},{8,12},{9,13},{10,... | collective-permute-start | bytes 393224 | tf_op jit(solution)/shard_map/ppermute | solution.py:250

commit v8 on v7

--- a/solution.py
+++ b/solution.py
@@ -172,6 +172,10 @@
             out[j] = dot(jnp.concatenate(mats, axis=1), slots).astype(BF16)
 
 
+def last_own_kernel(leaf, up_own, *own):
+    put_own(up_own.at[up_own.shape[0] - 1], leaf[...], own, 0)
+
+
 def sum_kernel(radix, *refs):
     got, thirds, outs = take(refs, radix, (len(refs) - radix) // 2, (len(refs) - radix) // 2)
     got = got[::-1]
@@ -190,9 +194,9 @@
 
 
 def middle_kernel(
-    radix, groups, offs, third, rhs, basis, row_mats, up_own, up_other, second_along, second_both, *refs
+    radix, groups, offs, third, rhs, basis, row_mats, up_other, second_along, second_both, *refs
 ):
-    crossed, own_in, (residual_ref,), own, other = take(refs, groups - 1, radix, 1, radix, radix)
+    crossed, own_in, (residual_ref, leaf_ref), other = take(refs, groups - 1, radix, 2, radix)
     coefs = []
     for j in range(offs):
         slots = slots_of([ref[j] for ref in own_in], second_along, second_both, j, 0)
@@ -206,17 +210,22 @@
         residual_ref[rows] = residual
         leaf.append(dot_t(basis[0, offs, k], residual.astype(BF16)).astype(BF16))
     leaf = jnp.concatenate(leaf, axis=0)
+    leaf_ref[...] = leaf
     put_other(up_other.at[offs], leaf, other, 0)
-    put_own(up_own.at[offs], leaf, own, 0)
-
-
-def last_kernel(radix, groups, offs, third, row_mats, residual, *refs):
-    crossed, own_in, (out,) = take(refs, groups - 1, radix, 1)
-    own_in = own_in[::-1]
-    slots = jnp.concatenate([ref[0] for ref in own_in], axis=0)
-    coefs = [group_coef(offs, slots, third, radix)] + [ref[0] for ref in crossed]
-    coefs = jnp.concatenate(coefs, axis=0)
-    out[0] = (residual[...] + dot(row_mats[...], coefs)).astype(BF16)
+
+
+def crossed_kernel(row_mats, residual, *refs):
+    *crossed, out = refs
+    rank = crossed[0].shape[1]
+    coefs = jnp.concatenate([ref[0] for ref in crossed], axis=0)
+    out[...] = residual[...] + dot(row_mats[:, rank:], coefs)
+
+
+def last_kernel(radix, offs, third, row_mats, residual, *refs):
+    own_in, (out,) = take(refs, radix, 1)
+    slots = jnp.concatenate([ref[0] for ref in own_in[::-1]], axis=0)
+    coef = group_coef(offs, slots, third, radix)
+    out[0] = (residual[...] + dot(row_mats[:, : coef.shape[0]], coef)).astype(BF16)
 
 
 def after(array, *others):
@@ -329,7 +338,7 @@
     )
     along = over_members(along, ALONG)
     across = over_members(across, ACROSS)
-    both = over_members(after(along, across, *thirds_last), ACROSS)
+    both = over_members(after(along, across), ACROSS)
     own = call(own_kernel, "own_levels", offs * own_flops, own_out(offs)[:3], leaf, up_own, up_mid)
     own_along = over_members(after(own[2], along), ALONG)
     sums = call(
@@ -347,27 +356,26 @@
     crossed = cross(sums)
     own = [
         own[0],
-        over_members(after(own[1], both), ACROSS),
+        over_members(after(own[1], both, *thirds_last), ACROSS),
         own_along,
     ]
     own.append(over_members(after(own_along, own[1], *sums), ACROSS))
 
-    residual, *levels = call(
+    residual, leaf, *other = call(
         functools.partial(middle_kernel, radix, groups, offs),
         "middle_levels",
         offs * row_flops + leaf_flops + other_flops + own_flops,
-        [((rows, columns), F32)] + own_out(1) + other_out(1),
+        [((rows, columns), F32), ((depth, columns), BF16)] + other_out(1),
         third_level,
         rhs,
         leaf_basis,
         off_rows,
-        up_own,
         up_other,
         *seconds,
         *crossed,
         *own,
     )
-    own, other = levels[:radix], levels[radix:]
+    own = call(last_own_kernel, "last_own_levels", own_flops, own_out(1), leaf, up_own)
     other = [over_members(a, i) for i, a in reversed(list(enumerate(other)))]
     sums = call(
         functools.partial(sum_kernel, radix),
@@ -379,15 +387,23 @@
     )
     crossed = cross(sums)
     own = [over_members(after(a, *sums) if i else a, i) for i, a in enumerate(own)]
+    residual = call(
+        crossed_kernel,
+        "last_crossed",
+        2 * columns * rank * less * rows,
+        [((rows, columns), F32)],
+        last_rows,
+        residual,
+        *crossed,
+    )[0]
     return call(
-        functools.partial(last_kernel, radix, groups, offs),
+        functools.partial(last_kernel, radix, offs),
         "last_levels",
-        row_flops,
+        2 * columns * rank * (rows + depth),
         [((1, rows, columns), BF16)],
         third_level,
         last_rows,
         residual,
-        *crossed,
         *own[::-1],
     )[0]
 

time: 80.7 us -> 82.5 us (1.022)
  waiting for transfers between devices: 39 us -> 43.1 us
  starting transfers between devices: 27.4 us -> 24.6 us
    ppermute x4, starting transfers between devices: 8.59 us -> 4.55 us  [over_groups(): return lax.ppermute(array, 'box', pairs)]
    ppermute x14, waiting for transfers between devices: 24.6 us -> 26.7 us  [over_members(): return array if mask == 0 else lax.ppermute(array, 'box', pairs)]
    ppermute x4, waiting for transfers between devices: 12.6 us -> 14.5 us  [over_groups(): return lax.ppermute(array, 'box', pairs)]
    ppermute x14, starting transfers between devices: 15.9 us -> 17.1 us  [over_members(): return array if mask == 0 else lax.ppermute(array, 'box', pairs)]
    pallas_call x9 -> x11, Pallas kernels: 7.94 us -> 8.52 us  [call(): pl.pallas_call(kernel, out_shape=outs, in_specs=[VMEM] * len(args), out_s...]
  transfers between devices with their start and end apart: 21 -> 21, of which waited for: 14 -> 15; matrix products, arithmetic and copies ran while one was open for 0% -> 0% of each run, Pallas kernels for 3% -> 4%
where the time goes in v8:
time: 82.5 us; the launch traced here: 82.2 us
  waiting for transfers between devices  43.1 us (52%)
  starting transfers between devices  24.6 us (30%)
  Pallas kernels  8.52 us (10%)
  local copies, waits for them, and re-layouts  5.83 us (7%)
    ppermute x14, waiting for transfers between devices, over_members(): return array if mask == 0 else lax.ppermute(array, 'box', pairs)  26.7 us
    ppermute x14, starting transfers between devices, over_members(): return array if mask == 0 else lax.ppermute(array, 'box', pairs)  17.1 us
    ppermute x4, waiting for transfers between devices, over_groups(): return lax.ppermute(array, 'box', pairs)  14.5 us
    pallas_call x11, Pallas kernels, call(): pl.pallas_call(kernel, out_shape=outs, in_specs=[VMEM] * len(args), out_s...  8.52 us
    unnamed x20, local copies, waits for them, and re-layouts  5.83 us
    ppermute x4, starting transfers between devices, over_groups(): return lax.ppermute(array, 'box', pairs)  4.55 us
    ppermute x3, starting transfers between devices, over_row(): return lax.ppermute(array, 'row', [(r, r ^ mask) for r in range(row_size)])  2.97 us
    ppermute x3, waiting for transfers between devices, over_row(): return lax.ppermute(array, 'row', [(r, r ^ mask) for r in range(row_size)])  1.9 us
  transfers between devices with their start and end apart: 21, of which 15 were waited for; matrix products, arithmetic and copies ran while one was open for 0% of the time, Pallas kernels for 4%

profile of v8, /device:TPU:0, one launch (start us, length us, event | category | flops | bytes accessed | tf_op | source)
XLA Modules:
  0.0 82.2 jit_solution(17211844939262711759)
XLA Ops:
  0.0 3.0 %collective-permute-start.3 = (bf16[2,256,512]{2,1,0:T(8,128)(2,1)}, bf16[2,256,512]{2,1,0:T(8,128)(2,1)S(1)}, u32[]{:S(2)}, u32[]{:S(2)}) collective-permute-start(bf16[2,256,512]{2,1,0:T(8,128)(2,1)} %refs_0_.1), channel_id=1, source_target_pairs={{0,16},{8,24},{16,0},{24,8},{1,17},{9,25},{17,1},{25,9},{2,18},{10... | collective-permute-start | bytes 1572872 | tf_op jit(solution)/shard_map/ppermute | solution.py:249
  3.0 0.0 copy-start
  3.0 1.1 %copy-done = bf16[1,3,1,8,128,128]{5,4,3,2,1,0:T(8,128)(2,1)S(1)} copy-done((bf16[1,3,1,8,128,128]{5,4,3,2,1,0:T(8,128)(2,1)S(1)}, bf16[1,3,1,8,128,128]{5,4,3,2,1,0:T(8,128)(2,1)}, u32[]{:S(2)}) %copy-start) | copy-done | bytes 786456
  4.1 2.7 %collective-permute-start.4 = (bf16[2,4,128,128]{3,2,1,0:T(8,128)(2,1)S(1)}, bf16[2,4,128,128]{3,2,1,0:T(8,128)(2,1)S(1)}, u32[]{:S(2)}, u32[]{:S(2)}) collective-permute-start(bf16[2,4,128,128]{3,2,1,0:T(8,128)(2,1)S(1)} %get-tuple-element.47), channel_id=1, source_target_pairs={{0,4},{1,5},{2,6},{3,7},{4,0},{5,1},{6,2},{7,3},{8,12},{9,13},{10,... | collective-permute-start | bytes 786440 | tf_op jit(solution)/shard_map/ppermute | solution.py:259
  6.8 1.1 %copy-done.2 = bf16[1,3,1,8,128,128]{5,4,3,2,1,0:T(8,128)(2,1)S(1)} copy-done((bf16[1,3,1,8,128,128]{5,4,3,2,1,0:T(8,128)(2,1)S(1)}, bf16[1,3,1,8,128,128]{5,4,3,2,1,0:T(8,128)(2,1)}, u32[]{:S(2)}) %copy-start.2) | copy-done | bytes 786456
  7.9 1.6 %collective-permute-start = (bf16[2,2,128,128]{3,2,1,0:T(8,128)(2,1)S(1)}, bf16[2,2,128,128]{3,2,1,0:T(8,128)(2,1)S(1)}, u32[]{:S(2)}, u32[]{:S(2)}) collective-permute-start(bf16[2,2,128,128]{3,2,1,0:T(8,128)(2,1)S(1)} %get-tuple-element.43), channel_id=1, source_target_pairs={{0,2},{1,3},{2,0},{3,1},{4,6},{5,7},{6,4},{7,5},{8,10},{9,11},{10,... | collective-permute-start | bytes 393224 | tf_op jit(solution)/shard_map/ppermute | solution.py:253
  9.6 1.4 %collective-permute-start.1 = (bf16[2,2,128,128]{3,2,1,0:T(8,128)(2,1)S(1)}, bf16[2,2,128,128]{3,2,1,0:T(8,128)(2,1)S(1)}, u32[]{:S(2)}, u32[]{:S(2)}) collective-permute-start(bf16[2,2,128,128]{3,2,1,0:T(8,128)(2,1)S(1)} %get-tuple-element.44), channel_id=1, source_target_pairs={{0,3},{1,2},{2,1},{3,0},{4,7},{5,6},{6,5},{7,4},{8,11},{9,10},{10,... | collective-permute-start | bytes 393224 | tf_op jit(solution)/shard_map/ppermute | solution.py:253
  11.0 0.0 collective-permute-start.2
  11.0 0.0 copy-done.3
  11.0 1.4 %copy-done.5 = bf16[1,3,1,4,4,128,128]{6,5,4,3,2,1,0:T(8,128)(2,1)S(1)} copy-done((bf16[1,3,1,4,4,128,128]{6,5,4,3,2,1,0:T(8,128)(2,1)S(1)}, bf16[1,3,1,4,4,128,128]{6,5,4,3,2,1,0:T(8,128)(2,1)}, u32[]{:S(2)}) %copy-start.5) | copy-done | bytes 1572888
  12.4 1.1 %copy-done.7 = bf16[1,3,2,512,128]{4,3,2,1,0:T(8,128)(2,1)S(1)} copy-done((bf16[1,3,2,512,128]{4,3,2,1,0:T(8,128)(2,1)S(1)}, bf16[1,3,2,512,128]{4,3,2,1,0:T(8,128)(2,1)}, u32[]{:S(2)}) %copy-start.7) | copy-done | bytes 786456
  13.5 1.0 %copy-done.9 = bf16[1,3,1,2,2,128,128]{6,5,4,3,2,1,0:T(8,128)(2,1)S(1)} copy-done((bf16[1,3,1,2,2,128,128]{6,5,4,3,2,1,0:T(8,128)(2,1)S(1)}, bf16[1,3,1,2,2,128,128]{6,5,4,3,2,1,0:T(8,128)(2,1)}, u32[]{:S(2)}) %copy-start.9) | copy-done | bytes 393240
  14.5 1.4 %weights.1 = (bf16[3,4,128,512]{3,2,1,0:T(8,128)(2,1)S(1)}, bf16[3,4,1,128,512]{4,3,2,1,0:T(8,128)(2,1)S(1)}, bf16[2,2,128,512]{3,2,1,0:T(8,128)(2,1)S(1)}, bf16...) custom-call(bf16[1,3,1,4,4,128,128]{6,5,4,3,2,1,0:T(8,128)(2,1)S(1)} %copy-done.5, ...), custom_call_target="tpu_custom_call" | custom-call | flops 603979776 | tf_op jit(solution)/shard_map/weights/pallas_call | solution.py:264
  15.9 0.4 collective-permute-done.second_along
  16.3 4.6 %collective-permute-done.1.second_both = bf16[2,2,128,128]{3,2,1,0:T(8,128)(2,1)S(1)} collective-permute-done((bf16[2,2,128,128]{3,2,1,0:T(8,128)(2,1)S(1)}, bf16[2,2,128,128]{3,2,1,0:T(8,128)(2,1)S(1)}, u32[]{:S(2)}, u32[]{:S(2)}) %collective-permute-start.1) | collective-permute-done | bytes 131104 | tf_op jit(solution)/shard_map/ppermute | solution.py:253
  20.9 0.0 collective-permute-done.4.refs_4_
  20.9 0.0 collective-permute-done.3.refs_2_
  20.9 0.0 collective-permute-start.5
  20.9 0.0 collective-permute-done.2.refs_1_
  21.0 1.9 %collective-permute-done.5.refs_3_ = bf16[2,256,512]{2,1,0:T(8,128)(2,1)S(1)} collective-permute-done((bf16[2,256,512]{2,1,0:T(8,128)(2,1)S(1)}, bf16[2,256,512]{2,1,0:T(8,128)(2,1)S(1)}, u32[]{:S(2)}, u32[]{:S(2)}) %collective-permute-start.5) | collective-permute-done | bytes 524320 | tf_op jit(solution)/shard_map/ppermute | solution.py:249
  22.8 0.0 copy-done.4
  22.8 0.0 copy-done.8
  22.9 1.0 %off_levels.1 = (bf16[2,512,512]{2,1,0:T(8,128)(2,1)S(1)}, bf16[2,1,128,512]{3,2,1,0:T(8,128)(2,1)S(1)}, bf16[2,1,128,512]{3,2,1,0:T(8,128)(2,1)S(1)}, bf16[2,1,128,512]{3,2,1,0:T(8,128)(2,1)S(1)}) custom-call(bf16[1,3,4,256,128]{4,3,2,1,0:T(8,128)(2,1)S(1)} %copy-done.4, bf16[3,4,1,128,512]{4,3,2,1,0:T(8,128)(2,1)S(1)} %get-tuple-element.42.up_other, ...), custom_call_target="tpu_custom_call" | custom-call | flops 805306368 | tf_op jit(solution)/shard_map/off_levels/pallas_call | solution.py:264
  23.9 0.9 %collective-permute-start.6 = (bf16[2,1,128,512]{3,2,1,0:T(8,128)(2,1)S(1)}, bf16[2,1,128,512]{3,2,1,0:T(8,128)(2,1)S(1)}, u32[]{:S(2)}, u32[]{:S(2)}) collective-permute-start(bf16[2,1,128,512]{3,2,1,0:T(8,128)(2,1)S(1)} %get-tuple-element.50), channel_id=1, source_target_pairs={{0,1},{1,0},{2,3},{3,2},{4,5},{5,4},{6,7},{7,6},{8,9},{9,8},{10,11... | collective-permute-start | bytes 786440 | tf_op jit(solution)/shard_map/ppermute | solution.py:253
  24.8 0.0 collective-permute-start.7
  24.8 7.5 %collective-permute-done.6.refs_1_ = bf16[2,1,128,512]{3,2,1,0:T(8,128)(2,1)S(1)} collective-permute-done((bf16[2,1,128,512]{3,2,1,0:T(8,128)(2,1)S(1)}, bf16[2,1,128,512]{3,2,1,0:T(8,128)(2,1)S(1)}, u32[]{:S(2)}, u32[]{:S(2)}) %collective-permute-start.6) | collective-permute-done | bytes 262176 | tf_op jit(solution)/shard_map/ppermute | solution.py:253
  32.3 0.5 collective-permute-done.7.refs_2_
  32.8 1.2 %collective-permute-start.8 = (bf16[2,1,128,512]{3,2,1,0:T(8,128)(2,1)S(1)}, bf16[2,1,128,512]{3,2,1,0:T(8,128)(2,1)S(1)}, u32[]{:S(2)}, u32[]{:S(2)}) collective-permute-start(bf16[2,1,128,512]{3,2,1,0:T(8,128)(2,1)S(1)} %collective-permute-done.7.refs_2_), channel_id=1, source_target_pairs={{0,1},{1,0},{2,3},{3,2},{4,5},{5,4},{6,7},{7,6},{8,9},{9,8},{10,11... | collective-permute-start | bytes 786440 | tf_op jit(solution)/shard_map/ppermute | solution.py:253
  34.1 1.3 %collective-permute-start.10 = (bf16[1,4,128,128]{3,2,1,0:T(8,128)(2,1)S(1)}, bf16[1,4,128,128]{3,2,1,0:T(8,128)(2,1)S(1)}, u32[]{:S(2)}, u32[]{:S(2)}) collective-permute-start(bf16[1,4,128,128]{3,2,1,0:T(8,128)(2,1)S(1)} %get-tuple-element.57), channel_id=1, source_target_pairs={{0,4},{1,5},{2,6},{3,7},{4,0},{5,1},{6,2},{7,3},{8,12},{9,13},{10,... | collective-permute-start | bytes 393224 | tf_op jit(solution)/shard_map/ppermute | solution.py:259
  35.4 0.6 own_levels.1
  35.9 0.0 copy-start.1
  35.9 0.0 copy-start.6
  36.0 1.8 %collective-permute-start.12 = (bf16[2,128,512]{2,1,0:T(8,128)(2,1)S(1)}, bf16[2,128,512]{2,1,0:T(8,128)(2,1)S(1)}, u32[]{:S(2)}, u32[]{:S(2)}) collective-permute-start(bf16[2,128,512]{2,1,0:T(8,128)(2,1)S(1)} %get-tuple-element.60), channel_id=1, source_target_pairs={{0,2},{1,3},{2,0},{3,1},{4,6},{5,7},{6,4},{7,5},{8,10},{9,11},{10,... | collective-permute-start | bytes 786440 | tf_op jit(solution)/shard_map/ppermute | solution.py:253
  37.8 4.0 %collective-permute-done.10.refs_4_ = bf16[1,4,128,128]{3,2,1,0:T(8,128)(2,1)S(1)} collective-permute-done((bf16[1,4,128,128]{3,2,1,0:T(8,128)(2,1)S(1)}, bf16[1,4,128,128]{3,2,1,0:T(8,128)(2,1)S(1)}, u32[]{:S(2)}, u32[]{:S(2)}) %collective-permute-start.10) | collective-permute-done | bytes 131104 | tf_op jit(solution)/shard_map/ppermute | solution.py:259
  41.8 0.0 collective-permute-done.8.refs_3_
  41.8 1.0 %collective-permute-start.11 = (bf16[2,128,512]{2,1,0:T(8,128)(2,1)S(1)}, bf16[2,128,512]{2,1,0:T(8,128)(2,1)S(1)}, u32[]{:S(2)}, u32[]{:S(2)}) collective-permute-start(bf16[2,128,512]{2,1,0:T(8,128)(2,1)S(1)} %get-tuple-element.58), channel_id=1, source_target_pairs={{0,1},{1,0},{2,3},{3,2},{4,5},{5,4},{6,7},{7,6},{8,9},{9,8},{10,11... | collective-permute-start | bytes 786440 | tf_op jit(solution)/shard_map/ppermute | solution.py:253
  42.8 0.6 off_sums.1
  43.4 0.5 collective-permute-start.9
  43.8 1.8 %collective-permute-done.12.refs_3_ = bf16[2,128,512]{2,1,0:T(8,128)(2,1)S(1)} collective-permute-done((bf16[2,128,512]{2,1,0:T(8,128)(2,1)S(1)}, bf16[2,128,512]{2,1,0:T(8,128)(2,1)S(1)}, u32[]{:S(2)}, u32[]{:S(2)}) %collective-permute-start.12) | collective-permute-done | bytes 262176 | tf_op jit(solution)/shard_map/ppermute | solution.py:253
  45.7 3.1 %collective-permute-done.11.refs_2_ = bf16[2,128,512]{2,1,0:T(8,128)(2,1)S(1)} collective-permute-done((bf16[2,128,512]{2,1,0:T(8,128)(2,1)S(1)}, bf16[2,128,512]{2,1,0:T(8,128)(2,1)S(1)}, u32[]{:S(2)}, u32[]{:S(2)}) %collective-permute-start.11) | collective-permute-done | bytes 262176 | tf_op jit(solution)/shard_map/ppermute | solution.py:253
  48.8 1.5 %collective-permute-start.13 = (bf16[2,128,512]{2,1,0:T(8,128)(2,1)S(1)}, bf16[2,128,512]{2,1,0:T(8,128)(2,1)S(1)}, u32[]{:S(2)}, u32[]{:S(2)}) collective-permute-start(bf16[2,128,512]{2,1,0:T(8,128)(2,1)S(1)} %collective-permute-done.12.refs_3_), channel_id=1, source_target_pairs={{0,1},{1,0},{2,3},{3,2},{4,5},{5,4},{6,7},{7,6},{8,9},{9,8},{10,11... | collective-permute-start | bytes 786440 | tf_op jit(solution)/shard_map/ppermute | solution.py:253
  50.3 6.5 %collective-permute-done.9.refs_0_ = bf16[2,128,512]{2,1,0:T(8,128)(2,1)S(1)} collective-permute-done((bf16[2,128,512]{2,1,0:T(8,128)(2,1)S(1)}, bf16[2,128,512]{2,1,0:T(8,128)(2,1)S(1)}, u32[]{:S(2)}, u32[]{:S(2)}) %collective-permute-start.9) | collective-permute-done | bytes 262176 | tf_op jit(solution)/shard_map/ppermute | solution.py:259
  56.7 0.0 collective-permute-done.13.refs_4_
  56.7 0.0 copy-done.1
  56.8 0.0 copy-done.6
  56.8 2.2 %middle_levels.1 = (f32[1024,512]{1,0:T(8,128)S(1)}, bf16[512,512]{1,0:T(8,128)(2,1)S(1)}, bf16[1,1,128,512]{3,2,1,0:T(8,128)(2,1)S(1)}, bf16[1,1,128,512]{3,2,1...) custom-call(bf16[1,3,1,8,128,128]{5,4,3,2,1,0:T(8,128)(2,1)S(1)} %copy-done.1, ...), custom_call_target="tpu_custom_call" | custom-call | flops 1342177280 | tf_op jit(solution)/shard_map/middle_levels/pallas_call | solution.py:264
  59.0 0.1 collective-permute-start.14
  59.1 2.4 %collective-permute-start.15 = (bf16[1,1,128,512]{3,2,1,0:T(8,128)(2,1)S(1)}, bf16[1,1,128,512]{3,2,1,0:T(8,128)(2,1)S(1)}, u32[]{:S(2)}, u32[]{:S(2)}) collective-permute-start(bf16[1,1,128,512]{3,2,1,0:T(8,128)(2,1)S(1)} %get-tuple-element.64), channel_id=1, source_target_pairs={{0,2},{1,3},{2,0},{3,1},{4,6},{5,7},{6,4},{7,5},{8,10},{9,11},{10,... | collective-permute-start | bytes 393224 | tf_op jit(solution)/shard_map/ppermute | solution.py:253
  61.5 1.1 %collective-permute-start.16 = (bf16[1,1,128,512]{3,2,1,0:T(8,128)(2,1)S(1)}, bf16[1,1,128,512]{3,2,1,0:T(8,128)(2,1)S(1)}, u32[]{:S(2)}, u32[]{:S(2)}) collective-permute-start(bf16[1,1,128,512]{3,2,1,0:T(8,128)(2,1)S(1)} %get-tuple-element.65), channel_id=1, source_target_pairs={{0,1},{1,0},{2,3},{3,2},{4,5},{5,4},{6,7},{7,6},{8,9},{9,8},{10,11... | collective-permute-start | bytes 393224 | tf_op jit(solution)/shard_map/ppermute | solution.py:253
  62.5 3.8 %collective-permute-done.14.refs_0_ = bf16[1,1,128,512]{3,2,1,0:T(8,128)(2,1)S(1)} collective-permute-done((bf16[1,1,128,512]{3,2,1,0:T(8,128)(2,1)S(1)}, bf16[1,1,128,512]{3,2,1,0:T(8,128)(2,1)S(1)}, u32[]{:S(2)}, u32[]{:S(2)}) %collective-permute-start.14) | collective-permute-done | bytes 131104 | tf_op jit(solution)/shard_map/ppermute | solution.py:253
  66.3 0.8 %collective-permute-done.15.refs_1_ = bf16[1,1,128,512]{3,2,1,0:T(8,128)(2,1)S(1)} collective-permute-done((bf16[1,1,128,512]{3,2,1,0:T(8,128)(2,1)S(1)}, bf16[1,1,128,512]{3,2,1,0:T(8,128)(2,1)S(1)}, u32[]{:S(2)}, u32[]{:S(2)}) %collective-permute-start.15) | collective-permute-done | bytes 131104 | tf_op jit(solution)/shard_map/ppermute | solution.py:253
  67.1 1.0 %collective-permute-done.16.refs_2_ = bf16[1,1,128,512]{3,2,1,0:T(8,128)(2,1)S(1)} collective-permute-done((bf16[1,1,128,512]{3,2,1,0:T(8,128)(2,1)S(1)}, bf16[1,1,128,512]{3,2,1,0:T(8,128)(2,1)S(1)}, u32[]{:S(2)}, u32[]{:S(2)}) %collective-permute-start.16) | collective-permute-done | bytes 131104 | tf_op jit(solution)/shard_map/ppermute | solution.py:253
  68.2 0.2 sums.1
  68.4 0.1 collective-permute-start.17
  68.5 0.4 last_own_levels.1
  69.0 2.7 %collective-permute-start.18 = (bf16[1,128,512]{2,1,0:T(8,128)(2,1)S(1)}, bf16[1,128,512]{2,1,0:T(8,128)(2,1)S(1)}, u32[]{:S(2)}, u32[]{:S(2)}) collective-permute-start(bf16[1,128,512]{2,1,0:T(8,128)(2,1)S(1)} %get-tuple-element.69), channel_id=1, source_target_pairs={{0,3},{1,2},{2,1},{3,0},{4,7},{5,6},{6,5},{7,4},{8,11},{9,10},{10,... | collective-permute-start | bytes 393224 | tf_op jit(solution)/shard_map/ppermute | solution.py:253
  71.7 0.2 collective-permute-start.19
  71.9 1.2 %collective-permute-start.20 = (bf16[1,128,512]{2,1,0:T(8,128)(2,1)S(1)}, bf16[1,128,512]{2,1,0:T(8,128)(2,1)S(1)}, u32[]{:S(2)}, u32[]{:S(2)}) collective-permute-start(bf16[1,128,512]{2,1,0:T(8,128)(2,1)S(1)} %get-tuple-element.73), channel_id=1, source_target_pairs={{0,1},{1,0},{2,3},{3,2},{4,5},{5,4},{6,7},{7,6},{8,9},{9,8},{10,11... | collective-permute-start | bytes 393224 | tf_op jit(solution)/shard_map/ppermute | solution.py:253
  73.1 4.0 %collective-permute-done.17.refs_0_ = bf16[1,128,512]{2,1,0:T(8,128)(2,1)S(1)} collective-permute-done((bf16[1,128,512]{2,1,0:T(8,128)(2,1)S(1)}, bf16[1,128,512]{2,1,0:T(8,128)(2,1)S(1)}, u32[]{:S(2)}, u32[]{:S(2)}) %collective-permute-start.17) | collective-permute-done | bytes 131104 | tf_op jit(solution)/shard_map/ppermute | solution.py:259
  77.1 0.4 last_crossed.1.residual
  77.5 0.5 collective-permute-done.18.refs_0_
  78.1 2.5 %collective-permute-done.19.refs_1_ = bf16[1,128,512]{2,1,0:T(8,128)(2,1)S(1)} collective-permute-done((bf16[1,128,512]{2,1,0:T(8,128)(2,1)S(1)}, bf16[1,128,512]{2,1,0:T(8,128)(2,1)S(1)}, u32[]{:S(2)}, u32[]{:S(2)}) %collective-permute-start.19) | collective-permute-done | bytes 131104 | tf_op jit(solution)/shard_map/ppermute | solution.py:253
  80.6 0.0 collective-permute-done.20.refs_2_
  80.6 1.6 %last_levels.1 = bf16[1,1024,512]{2,1,0:T(8,128)(2,1)} custom-call(bf16[1,3,1,8,128,128]{5,4,3,2,1,0:T(8,128)(2,1)S(1)} %copy-done.1, bf16[1024,256]{1,0:T(8,128)(2,1)S(1)} %get-tuple-element.40.row_mats, f32[1024,512]{1,0:T(8,128)S(1)} %last_crossed.1.residual, bf16[1,128,512]{2,1,0:T(8,128)(2,1)S(1)} %collective-permute-done.18.refs_0_, ...), custom_call_target="tpu_custom_call" | custom-call | flops 201326592 | tf_op jit(solution)/shard_map/last_levels/pallas_call | solution.py:264
  (9 shorter events, 0.1 us)
Async XLA Ops:
  0.0 20.9 %collective-permute-start.3 = (bf16[2,256,512]{2,1,0:T(8,128)(2,1)}, bf16[2,256,512]{2,1,0:T(8,128)(2,1)S(1)}, u32[]{:S(2)}, u32[]{:S(2)}) collective-permute-start(bf16[2,256,512]{2,1,0:T(8,128)(2,1)} %refs_0_.1), channel_id=1, source_target_pairs={{0,16},{8,24},{16,0},{24,8},{1,17},{9,25},{17,1},{25,9},{2,18},{10... | collective-permute-start | bytes 1572872 | tf_op jit(solution)/shard_map/ppermute | solution.py:249
  3.0 1.1 %copy-start = (bf16[1,3,1,8,128,128]{5,4,3,2,1,0:T(8,128)(2,1)S(1)}, bf16[1,3,1,8,128,128]{5,4,3,2,1,0:T(8,128)(2,1)}, u32[]{:S(2)}) copy-start(bf16[1,3,1,8,128,128]{5,4,3,2,1,0:T(8,128)(2,1)} %third.5) | copy-start | bytes 2359300
  4.1 6.9 %copy-start.3 = (bf16[1,3,1,8,128,128]{5,4,3,2,1,0:T(8,128)(2,1)S(1)}, bf16[1,3,1,8,128,128]{5,4,3,2,1,0:T(8,128)(2,1)}, u32[]{:S(2)}) copy-start(bf16[1,3,1,8,128,128]{5,4,3,2,1,0:T(8,128)(2,1)} %second.3) | copy-start | bytes 2359300
  4.1 16.8 %collective-permute-start.4 = (bf16[2,4,128,128]{3,2,1,0:T(8,128)(2,1)S(1)}, bf16[2,4,128,128]{3,2,1,0:T(8,128)(2,1)S(1)}, u32[]{:S(2)}, u32[]{:S(2)}) collective-permute-start(bf16[2,4,128,128]{3,2,1,0:T(8,128)(2,1)S(1)} %get-tuple-element.47), channel_id=1, source_target_pairs={{0,4},{1,5},{2,6},{3,7},{4,0},{5,1},{6,2},{7,3},{8,12},{9,13},{10,... | collective-permute-start | bytes 786440 | tf_op jit(solution)/shard_map/ppermute | solution.py:259
  6.8 1.1 %copy-start.2 = (bf16[1,3,1,8,128,128]{5,4,3,2,1,0:T(8,128)(2,1)S(1)}, bf16[1,3,1,8,128,128]{5,4,3,2,1,0:T(8,128)(2,1)}, u32[]{:S(2)}) copy-start(bf16[1,3,1,8,128,128]{5,4,3,2,1,0:T(8,128)(2,1)} %second.3) | copy-start | bytes 2359300
  7.9 8.4 %collective-permute-start = (bf16[2,2,128,128]{3,2,1,0:T(8,128)(2,1)S(1)}, bf16[2,2,128,128]{3,2,1,0:T(8,128)(2,1)S(1)}, u32[]{:S(2)}, u32[]{:S(2)}) collective-permute-start(bf16[2,2,128,128]{3,2,1,0:T(8,128)(2,1)S(1)} %get-tuple-element.43), channel_id=1, source_target_pairs={{0,2},{1,3},{2,0},{3,1},{4,6},{5,7},{6,4},{7,5},{8,10},{9,11},{10,... | collective-permute-start | bytes 393224 | tf_op jit(solution)/shard_map/ppermute | solution.py:253
  9.6 13.3 %copy-start.4 = (bf16[1,3,4,256,128]{4,3,2,1,0:T(8,128)(2,1)S(1)}, bf16[1,3,4,256,128]{4,3,2,1,0:T(8,128)(2,1)}, u32[]{:S(2)}) copy-start(bf16[1,3,4,256,128]{4,3,2,1,0:T(8,128)(2,1)} %basis.3) | copy-start | bytes 2359300
  9.6 11.3 %collective-permute-start.1 = (bf16[2,2,128,128]{3,2,1,0:T(8,128)(2,1)S(1)}, bf16[2,2,128,128]{3,2,1,0:T(8,128)(2,1)S(1)}, u32[]{:S(2)}, u32[]{:S(2)}) collective-permute-start(bf16[2,2,128,128]{3,2,1,0:T(8,128)(2,1)S(1)} %get-tuple-element.44), channel_id=1, source_target_pairs={{0,3},{1,2},{2,1},{3,0},{4,7},{5,6},{6,5},{7,4},{8,11},{9,10},{10,... | collective-permute-start | bytes 393224 | tf_op jit(solution)/shard_map/ppermute | solution.py:253
  11.0 10.0 %collective-permute-start.2 = (bf16[2,256,512]{2,1,0:T(8,128)(2,1)}, bf16[2,256,512]{2,1,0:T(8,128)(2,1)S(1)}, u32[]{:S(2)}, u32[]{:S(2)}) collective-permute-start(bf16[2,256,512]{2,1,0:T(8,128)(2,1)} %refs_0_.1), channel_id=1, source_target_pairs={{0,8},{8,0},{16,24},{24,16},{1,9},{9,1},{17,25},{25,17},{2,10},{10... | collective-permute-start | bytes 1572872 | tf_op jit(solution)/shard_map/ppermute | solution.py:249
  11.0 1.4 %copy-start.5 = (bf16[1,3,1,4,4,128,128]{6,5,4,3,2,1,0:T(8,128)(2,1)S(1)}, bf16[1,3,1,4,4,128,128]{6,5,4,3,2,1,0:T(8,128)(2,1)}, u32[]{:S(2)}) copy-start(bf16[1,3,1,4,4,128,128]{6,5,4,3,2,1,0:T(8,128)(2,1)} %first.1) | copy-start | bytes 4718596
  12.4 1.1 %copy-start.7 = (bf16[1,3,2,512,128]{4,3,2,1,0:T(8,128)(2,1)S(1)}, bf16[1,3,2,512,128]{4,3,2,1,0:T(8,128)(2,1)}, u32[]{:S(2)}) copy-start(bf16[1,3,2,512,128]{4,3,2,1,0:T(8,128)(2,1)} %out_basis.1) | copy-start | bytes 2359300
  13.5 1.0 %copy-start.9 = (bf16[1,3,1,2,2,128,128]{6,5,4,3,2,1,0:T(8,128)(2,1)S(1)}, bf16[1,3,1,2,2,128,128]{6,5,4,3,2,1,0:T(8,128)(2,1)}, u32[]{:S(2)}) copy-start(bf16[1,3,1,2,2,128,128]{6,5,4,3,2,1,0:T(8,128)(2,1)} %fourth.1) | copy-start | bytes 1179652
  14.5 8.3 %copy-start.8 = (bf16[2,256,512]{2,1,0:T(8,128)(2,1)S(1)}, bf16[2,256,512]{2,1,0:T(8,128)(2,1)}, u32[]{:S(2)}) copy-start(bf16[2,256,512]{2,1,0:T(8,128)(2,1)} %refs_0_.1) | copy-start | bytes 1572868
  20.9 1.9 %collective-permute-start.5 = (bf16[2,256,512]{2,1,0:T(8,128)(2,1)S(1)}, bf16[2,256,512]{2,1,0:T(8,128)(2,1)S(1)}, u32[]{:S(2)}, u32[]{:S(2)}) collective-permute-start(bf16[2,256,512]{2,1,0:T(8,128)(2,1)S(1)} %collective-permute-done.3.refs_2_), channel_id=1, source_target_pairs={{0,8},{8,0},{16,24},{24,16},{1,9},{9,1},{17,25},{25,17},{2,10},{10... | collective-permute-start | bytes 1572872 | tf_op jit(solution)/shard_map/ppermute | solution.py:249
  23.9 8.4 %collective-permute-start.6 = (bf16[2,1,128,512]{3,2,1,0:T(8,128)(2,1)S(1)}, bf16[2,1,128,512]{3,2,1,0:T(8,128)(2,1)S(1)}, u32[]{:S(2)}, u32[]{:S(2)}) collective-permute-start(bf16[2,1,128,512]{3,2,1,0:T(8,128)(2,1)S(1)} %get-tuple-element.50), channel_id=1, source_target_pairs={{0,1},{1,0},{2,3},{3,2},{4,5},{5,4},{6,7},{7,6},{8,9},{9,8},{10,11... | collective-permute-start | bytes 786440 | tf_op jit(solution)/shard_map/ppermute | solution.py:253
  24.8 8.1 %collective-permute-start.7 = (bf16[2,1,128,512]{3,2,1,0:T(8,128)(2,1)S(1)}, bf16[2,1,128,512]{3,2,1,0:T(8,128)(2,1)S(1)}, u32[]{:S(2)}, u32[]{:S(2)}) collective-permute-start(bf16[2,1,128,512]{3,2,1,0:T(8,128)(2,1)S(1)} %get-tuple-element.51), channel_id=1, source_target_pairs={{0,2},{1,3},{2,0},{3,1},{4,6},{5,7},{6,4},{7,5},{8,10},{9,11},{10,... | collective-permute-start | bytes 786440 | tf_op jit(solution)/shard_map/ppermute | solution.py:253
  32.8 8.9 %collective-permute-start.8 = (bf16[2,1,128,512]{3,2,1,0:T(8,128)(2,1)S(1)}, bf16[2,1,128,512]{3,2,1,0:T(8,128)(2,1)S(1)}, u32[]{:S(2)}, u32[]{:S(2)}) collective-permute-start(bf16[2,1,128,512]{3,2,1,0:T(8,128)(2,1)S(1)} %collective-permute-done.7.refs_2_), channel_id=1, source_target_pairs={{0,1},{1,0},{2,3},{3,2},{4,5},{5,4},{6,7},{7,6},{8,9},{9,8},{10,11... | collective-permute-start | bytes 786440 | tf_op jit(solution)/shard_map/ppermute | solution.py:253
  34.1 7.7 %collective-permute-start.10 = (bf16[1,4,128,128]{3,2,1,0:T(8,128)(2,1)S(1)}, bf16[1,4,128,128]{3,2,1,0:T(8,128)(2,1)S(1)}, u32[]{:S(2)}, u32[]{:S(2)}) collective-permute-start(bf16[1,4,128,128]{3,2,1,0:T(8,128)(2,1)S(1)} %get-tuple-element.57), channel_id=1, source_target_pairs={{0,4},{1,5},{2,6},{3,7},{4,0},{5,1},{6,2},{7,3},{8,12},{9,13},{10,... | collective-permute-start | bytes 393224 | tf_op jit(solution)/shard_map/ppermute | solution.py:259
  35.9 20.8 %copy-start.1 = (bf16[1,3,1,8,128,128]{5,4,3,2,1,0:T(8,128)(2,1)S(1)}, bf16[1,3,1,8,128,128]{5,4,3,2,1,0:T(8,128)(2,1)}, u32[]{:S(2)}) copy-start(bf16[1,3,1,8,128,128]{5,4,3,2,1,0:T(8,128)(2,1)} %third.5) | copy-start | bytes 2359300
  35.9 20.8 %copy-start.6 = (bf16[1,1024,512]{2,1,0:T(8,128)(2,1)S(1)}, bf16[1,1024,512]{2,1,0:T(8,128)(2,1)}, u32[]{:S(2)}) copy-start(bf16[1,1024,512]{2,1,0:T(8,128)(2,1)} %rhs.1) | copy-start | bytes 3145732
  36.0 9.7 %collective-permute-start.12 = (bf16[2,128,512]{2,1,0:T(8,128)(2,1)S(1)}, bf16[2,128,512]{2,1,0:T(8,128)(2,1)S(1)}, u32[]{:S(2)}, u32[]{:S(2)}) collective-permute-start(bf16[2,128,512]{2,1,0:T(8,128)(2,1)S(1)} %get-tuple-element.60), channel_id=1, source_target_pairs={{0,2},{1,3},{2,0},{3,1},{4,6},{5,7},{6,4},{7,5},{8,10},{9,11},{10,... | collective-permute-start | bytes 786440 | tf_op jit(solution)/shard_map/ppermute | solution.py:253
  41.8 7.0 %collective-permute-start.11 = (bf16[2,128,512]{2,1,0:T(8,128)(2,1)S(1)}, bf16[2,128,512]{2,1,0:T(8,128)(2,1)S(1)}, u32[]{:S(2)}, u32[]{:S(2)}) collective-permute-start(bf16[2,128,512]{2,1,0:T(8,128)(2,1)S(1)} %get-tuple-element.58), channel_id=1, source_target_pairs={{0,1},{1,0},{2,3},{3,2},{4,5},{5,4},{6,7},{7,6},{8,9},{9,8},{10,11... | collective-permute-start | bytes 786440 | tf_op jit(solution)/shard_map/ppermute | solution.py:253
  43.4 13.4 %collective-permute-start.9 = (bf16[2,128,512]{2,1,0:T(8,128)(2,1)S(1)}, bf16[2,128,512]{2,1,0:T(8,128)(2,1)S(1)}, u32[]{:S(2)}, u32[]{:S(2)}) collective-permute-start(bf16[2,128,512]{2,1,0:T(8,128)(2,1)S(1)} %off_sums.1), channel_id=1, source_target_pairs={{0,4},{1,5},{2,6},{3,7},{4,0},{5,1},{6,2},{7,3},{8,12},{9,13},{10,... | collective-permute-start | bytes 786440 | tf_op jit(solution)/shard_map/ppermute | solution.py:259
  48.8 8.0 %collective-permute-start.13 = (bf16[2,128,512]{2,1,0:T(8,128)(2,1)S(1)}, bf16[2,128,512]{2,1,0:T(8,128)(2,1)S(1)}, u32[]{:S(2)}, u32[]{:S(2)}) collective-permute-start(bf16[2,128,512]{2,1,0:T(8,128)(2,1)S(1)} %collective-permute-done.12.refs_3_), channel_id=1, source_target_pairs={{0,1},{1,0},{2,3},{3,2},{4,5},{5,4},{6,7},{7,6},{8,9},{9,8},{10,11... | collective-permute-start | bytes 786440 | tf_op jit(solution)/shard_map/ppermute | solution.py:253
  59.0 7.3 %collective-permute-start.14 = (bf16[1,1,128,512]{3,2,1,0:T(8,128)(2,1)S(1)}, bf16[1,1,128,512]{3,2,1,0:T(8,128)(2,1)S(1)}, u32[]{:S(2)}, u32[]{:S(2)}) collective-permute-start(bf16[1,1,128,512]{3,2,1,0:T(8,128)(2,1)S(1)} %get-tuple-element.63), channel_id=1, source_target_pairs={{0,3},{1,2},{2,1},{3,0},{4,7},{5,6},{6,5},{7,4},{8,11},{9,10},{10,... | collective-permute-start | bytes 393224 | tf_op jit(solution)/shard_map/ppermute | solution.py:253
  59.1 8.1 %collective-permute-start.15 = (bf16[1,1,128,512]{3,2,1,0:T(8,128)(2,1)S(1)}, bf16[1,1,128,512]{3,2,1,0:T(8,128)(2,1)S(1)}, u32[]{:S(2)}, u32[]{:S(2)}) collective-permute-start(bf16[1,1,128,512]{3,2,1,0:T(8,128)(2,1)S(1)} %get-tuple-element.64), channel_id=1, source_target_pairs={{0,2},{1,3},{2,0},{3,1},{4,6},{5,7},{6,4},{7,5},{8,10},{9,11},{10,... | collective-permute-start | bytes 393224 | tf_op jit(solution)/shard_map/ppermute | solution.py:253
  61.5 6.7 %collective-permute-start.16 = (bf16[1,1,128,512]{3,2,1,0:T(8,128)(2,1)S(1)}, bf16[1,1,128,512]{3,2,1,0:T(8,128)(2,1)S(1)}, u32[]{:S(2)}, u32[]{:S(2)}) collective-permute-start(bf16[1,1,128,512]{3,2,1,0:T(8,128)(2,1)S(1)} %get-tuple-element.65), channel_id=1, source_target_pairs={{0,1},{1,0},{2,3},{3,2},{4,5},{5,4},{6,7},{7,6},{8,9},{9,8},{10,11... | collective-permute-start | bytes 393224 | tf_op jit(solution)/shard_map/ppermute | solution.py:253
  68.4 8.7 %collective-permute-start.17 = (bf16[1,128,512]{2,1,0:T(8,128)(2,1)S(1)}, bf16[1,128,512]{2,1,0:T(8,128)(2,1)S(1)}, u32[]{:S(2)}, u32[]{:S(2)}) collective-permute-start(bf16[1,128,512]{2,1,0:T(8,128)(2,1)S(1)} %sums.1), channel_id=1, source_target_pairs={{0,4},{1,5},{2,6},{3,7},{4,0},{5,1},{6,2},{7,3},{8,12},{9,13},{10,... | collective-permute-start | bytes 393224 | tf_op jit(solution)/shard_map/ppermute | solution.py:259
  69.0 9.1 %collective-permute-start.18 = (bf16[1,128,512]{2,1,0:T(8,128)(2,1)S(1)}, bf16[1,128,512]{2,1,0:T(8,128)(2,1)S(1)}, u32[]{:S(2)}, u32[]{:S(2)}) collective-permute-start(bf16[1,128,512]{2,1,0:T(8,128)(2,1)S(1)} %get-tuple-element.69), channel_id=1, source_target_pairs={{0,3},{1,2},{2,1},{3,0},{4,7},{5,6},{6,5},{7,4},{8,11},{9,10},{10,... | collective-permute-start | bytes 393224 | tf_op jit(solution)/shard_map/ppermute | solution.py:253
  71.7 8.9 %collective-permute-start.19 = (bf16[1,128,512]{2,1,0:T(8,128)(2,1)S(1)}, bf16[1,128,512]{2,1,0:T(8,128)(2,1)S(1)}, u32[]{:S(2)}, u32[]{:S(2)}) collective-permute-start(bf16[1,128,512]{2,1,0:T(8,128)(2,1)S(1)} %get-tuple-element.71), channel_id=1, source_target_pairs={{0,2},{1,3},{2,0},{3,1},{4,6},{5,7},{6,4},{7,5},{8,10},{9,11},{10,... | collective-permute-start | bytes 393224 | tf_op jit(solution)/shard_map/ppermute | solution.py:253
  71.9 8.7 %collective-permute-start.20 = (bf16[1,128,512]{2,1,0:T(8,128)(2,1)S(1)}, bf16[1,128,512]{2,1,0:T(8,128)(2,1)S(1)}, u32[]{:S(2)}, u32[]{:S(2)}) collective-permute-start(bf16[1,128,512]{2,1,0:T(8,128)(2,1)S(1)} %get-tuple-element.73), channel_id=1, source_target_pairs={{0,1},{1,0},{2,3},{3,2},{4,5},{5,4},{6,7},{7,6},{8,9},{9,8},{10,11... | collective-permute-start | bytes 393224 | tf_op jit(solution)/shard_map/ppermute | solution.py:253

commit v9 on v7

--- a/solution.py
+++ b/solution.py
@@ -110,40 +110,42 @@
         ref[at] = coef[i * rank : (i + 1) * rank]
 
 
-def off_kernel(pieces, basis, up_other, up_mid, *refs):
+def off_kernel(j, pieces, basis, up_other, up_mid, *refs):
     parts, (leaf_ref, keep, across, along) = take(refs, pieces, 4)
     row = lax.axis_index("row")
     leaves, leaf_rows = basis.shape[2], basis.shape[3]
     rows = parts[0].shape[1]
     per_leaf = leaf_rows // rows
     order = leaf_order(row, leaves, pieces)
-    less, rank, columns = keep.shape[1:]
-    for j in range(parts[0].shape[0]):
-        leaf = []
-        for t in range(leaves):
-            total = None
-            for u in range(per_leaf):
-                start = jnp.bitwise_xor(lax.rem(row, per_leaf), u) * rows
-                if per_leaf == 1:
-                    mat = basis[0, j, order[t]]
-                else:
-                    mat = basis[0, j, order[t], pl.ds(pl.multiple_of(start, rows), rows)]
-                part = dot_t(mat, parts[t * per_leaf + u][j])
-                total = part if total is None else total + part
-            leaf.append(total.astype(BF16))
-        leaf = jnp.concatenate(leaf, axis=0)
-        leaf_ref[j] = leaf
-        mats = [up_other[j, 0], up_other[j, ACROSS], up_mid[j, 1:]]
-        mats = jnp.concatenate([m.reshape(less * rank, m.shape[2]) for m in mats], axis=0)
-        coef = dot(mats, leaf).astype(BF16)
-        for i, ref in enumerate((keep, across, along)):
-            ref[j] = coef[i * less * rank : (i + 1) * less * rank].reshape(less, rank, columns)
-
-
-def own_kernel(leaf, up_own, up_mid, *own):
+    less, rank, columns = keep.shape
+    leaf = []
+    for t in range(leaves):
+        total = None
+        for u in range(per_leaf):
+            start = jnp.bitwise_xor(lax.rem(row, per_leaf), u) * rows
+            if per_leaf == 1:
+                mat = basis[0, j, order[t]]
+            else:
+                mat = basis[0, j, order[t], pl.ds(pl.multiple_of(start, rows), rows)]
+            ref = parts[t * per_leaf + u]
+            part = dot_t(mat, ref[j] if ref.shape[0] > 1 else ref[0])
+            total = part if total is None else total + part
+        leaf.append(total.astype(BF16))
+    leaf = jnp.concatenate(leaf, axis=0)
+    leaf_ref[...] = leaf
+    mats = [up_other[j, 0], up_other[j, ACROSS], up_mid[j, 1:]]
+    mats = jnp.concatenate([m.reshape(less * rank, m.shape[2]) for m in mats], axis=0)
+    coef = dot(mats, leaf).astype(BF16)
+    for i, ref in enumerate((keep, across, along)):
+        ref[...] = coef[i * less * rank : (i + 1) * less * rank].reshape(less, rank, columns)
+
+
+def own_kernel(up_own, up_mid, *refs):
     rank = up_mid.shape[2]
-    for j in range(leaf.shape[0]):
-        coef = dot(jnp.concatenate([up_own[j, 0], up_own[j, ACROSS], up_mid[j, 0]], axis=0), leaf[j]).astype(BF16)
+    leaves, own = take(refs, up_mid.shape[0], len(refs) - up_mid.shape[0])
+    for j, leaf in enumerate(leaves):
+        mats = jnp.concatenate([up_own[j, 0], up_own[j, ACROSS], up_mid[j, 0]], axis=0)
+        coef = dot(mats, leaf[...]).astype(BF16)
         for i, ref in enumerate(own):
             ref[j] = coef[i * rank : (i + 1) * rank]
 
@@ -161,15 +163,14 @@
     )
 
 
-def off_sum_kernel(second_along, second_both, *refs):
+def off_sum_kernel(j, second_along, second_both, *refs):
     got, thirds, outs = take(refs, 4, (len(refs) - 4) // 2, (len(refs) - 4) // 2)
     radix = thirds[0].shape[1]
     _, member = place(radix)
     for d, (third, out) in enumerate(zip(thirds, outs)):
-        for j in range(out.shape[0]):
-            mats = [third[j, jnp.bitwise_xor(member, i)] for i in range(radix)]
-            slots = slots_of([ref[j, d] for ref in got], second_along, second_both, j, d + 1)
-            out[j] = dot(jnp.concatenate(mats, axis=1), slots).astype(BF16)
+        mats = [third[0, jnp.bitwise_xor(member, i)] for i in range(radix)]
+        slots = slots_of([ref[d] for ref in got], second_along, second_both, j, d + 1)
+        out[...] = dot(jnp.concatenate(mats, axis=1), slots).astype(BF16)
 
 
 def sum_kernel(radix, *refs):
@@ -192,11 +193,12 @@
 def middle_kernel(
     radix, groups, offs, third, rhs, basis, row_mats, up_own, up_other, second_along, second_both, *refs
 ):
-    crossed, own_in, (residual_ref,), own, other = take(refs, groups - 1, radix, 1, radix, radix)
+    crossed, own_in, (residual_ref,), own, other = take(refs, offs * (groups - 1), radix, 1, radix, radix)
     coefs = []
     for j in range(offs):
         slots = slots_of([ref[j] for ref in own_in], second_along, second_both, j, 0)
-        coefs += [group_coef(j, slots, third, radix)] + [ref[j] for ref in crossed]
+        coefs += [group_coef(j, slots, third, radix)]
+        coefs += [ref[...] for ref in crossed[j * (groups - 1) : (j + 1) * (groups - 1)]]
     coefs = jnp.concatenate(coefs, axis=0)
     leaves, leaf_rows = basis.shape[2], basis.shape[3]
     leaf = []
@@ -266,11 +268,12 @@
         functools.partial(pick_kernel, radix, groups),
         "pick_third",
         0,
-        [((offs, radix, rank, rank), BF16)] * less + [((butterflies - offs, radix, rank, rank), BF16)] * less,
+        [((1, radix, rank, rank), BF16)] * (butterflies * less),
         third_level,
     )
-    thirds = [over_groups(a, d + 1) for d, a in enumerate(picked[:less])]
-    thirds_last = [over_groups(after(a, *thirds), d + 1) for d, a in enumerate(picked[less:])]
+    thirds = [
+        [over_groups(a, d + 1) for d, a in enumerate(picked[j * less : (j + 1) * less])] for j in range(butterflies)
+    ]
 
     up_own, up_other, up_mid, off_rows, last_rows = call(
         functools.partial(weights_kernel, radix, groups, offs, row_size),
@@ -298,11 +301,6 @@
     )
     seconds = [over_members(a, i) for i, a in zip((ALONG, BOTH), seconds)]
 
-    pieces = [solved, over_row(solved, 1)]
-    for mask in range(2, row_size, 2):
-        far = after(over_row(solved, mask), up_own, *thirds, *seconds)
-        pieces += [far, over_row(far, 1)]
-
     other_flops = 2 * columns * rank * radix * less * depth
     own_flops = 2 * columns * rank * radix * depth
     leaf_flops = 2 * columns * rank * rows
@@ -317,39 +315,46 @@
     def cross(sums):
         return [over_groups(a, less - d) for d, a in enumerate(sums)]
 
-    leaf, keep, across, along = call(
-        functools.partial(off_kernel, row_size),
-        "off_levels",
-        offs * (leaf_flops + other_flops),
-        [((offs, depth, columns), BF16)] + other_out(offs)[:3],
-        leaf_basis,
-        up_other,
-        up_mid,
-        *pieces,
-    )
-    along = over_members(along, ALONG)
-    across = over_members(across, ACROSS)
-    both = over_members(after(along, across, *thirds_last), ACROSS)
-    own = call(own_kernel, "own_levels", offs * own_flops, own_out(offs)[:3], leaf, up_own, up_mid)
+    beside = over_row(solved, 1)
+    far, held, leaves, sums, crossed = [], [up_own, *seconds, *thirds[0]], [], [], []
+    for j in range(offs):
+        pieces = [solved, beside]
+        come = far
+        far = [over_row(after(solved[j : j + 1], *come), mask) for mask in range(2, row_size, 2)]
+        for a in far:
+            a = after(a, *held)
+            pieces += [a, over_row(a, 1)]
+        leaf, keep, across, along = call(
+            functools.partial(off_kernel, j, row_size),
+            "off_levels",
+            leaf_flops + other_flops,
+            [((depth, columns), BF16)] + [((less, rank, columns), BF16)] * 3,
+            leaf_basis,
+            up_other,
+            up_mid,
+            *pieces,
+        )
+        leaves.append(leaf)
+        along = over_members(along, ALONG)
+        across = over_members(across, ACROSS)
+        both = over_members(after(along, across, *sums, *(thirds[j] if j else [])), ACROSS)
+        sums = call(
+            functools.partial(off_sum_kernel, j),
+            "off_sums",
+            less * 2 * columns * rank * depth,
+            [((rank, columns), BF16)] * less,
+            *seconds,
+            keep,
+            across,
+            along,
+            both,
+            *thirds[j],
+        )
+        crossed += cross(sums)
+        held = [across, along]
+    own = call(own_kernel, "own_levels", offs * own_flops, own_out(offs)[:3], up_own, up_mid, *leaves)
     own_along = over_members(after(own[2], along), ALONG)
-    sums = call(
-        off_sum_kernel,
-        "off_sums",
-        offs * less * 2 * columns * rank * depth,
-        [((offs, rank, columns), BF16)] * less,
-        *seconds,
-        keep,
-        across,
-        along,
-        both,
-        *thirds,
-    )
-    crossed = cross(sums)
-    own = [
-        own[0],
-        over_members(after(own[1], both), ACROSS),
-        own_along,
-    ]
+    own = [own[0], over_members(after(own[1], both, *thirds[offs], *crossed[:less]), ACROSS), own_along]
     own.append(over_members(after(own_along, own[1], *sums), ACROSS))
 
     residual, *levels = call(
@@ -375,7 +380,7 @@
         less * 2 * columns * rank * depth,
         [((1, rank, columns), BF16)] * less,
         *other,
-        *thirds_last,
+        *thirds[offs],
     )
     crossed = cross(sums)
     own = [over_members(after(a, *sums) if i else a, i) for i, a in enumerate(own)]

time: 80.7 us -> 86.8 us (1.076)
  waiting for transfers between devices: 39 us -> 44.1 us
  starting transfers between devices: 27.4 us -> 30.5 us
  local copies, waits for them, and re-layouts: 5.83 us -> 3.64 us
    ppermute x4 -> x6, waiting for transfers between devices: 12.6 us -> 17.4 us  [over_groups(): return lax.ppermute(array, 'box', pairs)]
    ppermute x14 -> x17, starting transfers between devices: 15.9 us -> 20.2 us  [over_members(): return array if mask == 0 else lax.ppermute(array, 'box', pairs)]
    unnamed x20 -> x16, local copies, waits for them, and re-layouts: 5.83 us -> 2.43 us
    ppermute x3 -> x5, waiting for transfers between devices: 1.9 us -> 4.3 us  [over_row(): return lax.ppermute(array, 'row', [(r, r ^ mask) for r in range(row_size)])]
    ppermute x14 -> x17, waiting for transfers between devices: 24.6 us -> 22.4 us  [over_members(): return array if mask == 0 else lax.ppermute(array, 'box', pairs)]
    ppermute x4 -> x6, starting transfers between devices: 8.59 us -> 6.71 us  [over_groups(): return lax.ppermute(array, 'box', pairs)]
    slice x0 -> x1, local copies, waits for them, and re-layouts: none -> 1.21 us  [on_device(): solved[j:j + 1]]
    ppermute x3 -> x5, starting transfers between devices: 2.97 us -> 3.62 us  [over_row(): return lax.ppermute(array, 'row', [(r, r ^ mask) for r in range(row_size)])]
  transfers between devices with their start and end apart: 21 -> 28, of which waited for: 14 -> 18; matrix products, arithmetic and copies ran while one was open for 0% -> 0% of each run, Pallas kernels for 3% -> 5%
where the time goes in v9:
time: 86.8 us; the launch traced here: 86.6 us
  waiting for transfers between devices  44.1 us (51%)
  starting transfers between devices  30.5 us (35%)
  Pallas kernels  8.29 us (10%)
  local copies, waits for them, and re-layouts  3.64 us (4%)
    ppermute x17, waiting for transfers between devices, over_members(): return array if mask == 0 else lax.ppermute(array, 'box', pairs)  22.4 us
    ppermute x17, starting transfers between devices, over_members(): return array if mask == 0 else lax.ppermute(array, 'box', pairs)  20.2 us
    ppermute x6, waiting for transfers between devices, over_groups(): return lax.ppermute(array, 'box', pairs)  17.4 us
    pallas_call x11, Pallas kernels, call(): pl.pallas_call(kernel, out_shape=outs, in_specs=[VMEM] * len(args), out_s...  8.29 us
    ppermute x6, starting transfers between devices, over_groups(): return lax.ppermute(array, 'box', pairs)  6.71 us
    ppermute x5, waiting for transfers between devices, over_row(): return lax.ppermute(array, 'row', [(r, r ^ mask) for r in range(row_size)])  4.3 us
    ppermute x5, starting transfers between devices, over_row(): return lax.ppermute(array, 'row', [(r, r ^ mask) for r in range(row_size)])  3.62 us
    unnamed x16, local copies, waits for them, and re-layouts  2.43 us
  transfers between devices with their start and end apart: 28, of which 18 were waited for; matrix products, arithmetic and copies ran while one was open for 0% of the time, Pallas kernels for 5%

profile of v9, /device:TPU:0, one launch (start us, length us, event | category | flops | bytes accessed | tf_op | source)
XLA Modules:
  0.0 86.6 jit_solution(15615652955950244131)
XLA Ops:
  0.0 1.2 %fusion = (bf16[1,256,512]{2,1,0:T(8,128)(2,1)S(1)}, bf16[1,256,512]{2,1,0:T(8,128)(2,1)S(1)}) fusion(bf16[2,256,512]{2,1,0:T(8,128)(2,1)} %refs_0_.3), kind=kLoop, calls=%fused_computation | loop fusion | bytes 1048576 | tf_op jit(solution)/shard_map/slice | solution.py:323
  1.2 3.0 %collective-permute-start.3 = (bf16[1,256,512]{2,1,0:T(8,128)(2,1)S(1)}, bf16[1,256,512]{2,1,0:T(8,128)(2,1)S(1)}, u32[]{:S(2)}, u32[]{:S(2)}) collective-permute-start(bf16[1,256,512]{2,1,0:T(8,128)(2,1)S(1)} %get-tuple-element.88), channel_id=1, source_target_pairs={{0,16},{8,24},{16,0},{24,8},{1,17},{9,25},{17,1},{25,9},{2,18},{10... | collective-permute-start | bytes 786440 | tf_op jit(solution)/shard_map/ppermute | solution.py:242
  4.3 0.0 collective-permute-start.2
  4.3 1.6 %collective-permute-start = (bf16[2,2,128,128]{3,2,1,0:T(8,128)(2,1)S(1)}, bf16[2,2,128,128]{3,2,1,0:T(8,128)(2,1)S(1)}, u32[]{:S(2)}, u32[]{:S(2)}) collective-permute-start(bf16[2,2,128,128]{3,2,1,0:T(8,128)(2,1)S(1)} %get-tuple-element.50), channel_id=1, source_target_pairs={{0,2},{1,3},{2,0},{3,1},{4,6},{5,7},{6,4},{7,5},{8,10},{9,11},{10,... | collective-permute-start | bytes 393224 | tf_op jit(solution)/shard_map/ppermute | solution.py:246
  5.9 1.4 %collective-permute-start.1 = (bf16[2,2,128,128]{3,2,1,0:T(8,128)(2,1)S(1)}, bf16[2,2,128,128]{3,2,1,0:T(8,128)(2,1)S(1)}, u32[]{:S(2)}, u32[]{:S(2)}) collective-permute-start(bf16[2,2,128,128]{3,2,1,0:T(8,128)(2,1)S(1)} %get-tuple-element.51), channel_id=1, source_target_pairs={{0,3},{1,2},{2,1},{3,0},{4,7},{5,6},{6,5},{7,4},{8,11},{9,10},{10,... | collective-permute-start | bytes 393224 | tf_op jit(solution)/shard_map/ppermute | solution.py:246
  7.3 0.0 copy-start.1
  7.4 0.0 copy-start.2
  7.4 2.7 %collective-permute-start.4 = (bf16[1,4,128,128]{3,2,1,0:T(8,128)(2,1)S(1)}, bf16[1,4,128,128]{3,2,1,0:T(8,128)(2,1)S(1)}, u32[]{:S(2)}, u32[]{:S(2)}) collective-permute-start(bf16[1,4,128,128]{3,2,1,0:T(8,128)(2,1)S(1)} %get-tuple-element.53), channel_id=1, source_target_pairs={{0,4},{1,5},{2,6},{3,7},{4,0},{5,1},{6,2},{7,3},{8,12},{9,13},{10,... | collective-permute-start | bytes 393224 | tf_op jit(solution)/shard_map/ppermute | solution.py:252
  10.0 1.4 %copy-done.4 = bf16[1,3,1,4,4,128,128]{6,5,4,3,2,1,0:T(8,128)(2,1)S(1)} copy-done((bf16[1,3,1,4,4,128,128]{6,5,4,3,2,1,0:T(8,128)(2,1)S(1)}, bf16[1,3,1,4,4,128,128]{6,5,4,3,2,1,0:T(8,128)(2,1)}, u32[]{:S(2)}) %copy-start.4) | copy-done | bytes 1572888
  11.4 1.0 %copy-done.7 = bf16[1,3,1,2,2,128,128]{6,5,4,3,2,1,0:T(8,128)(2,1)S(1)} copy-done((bf16[1,3,1,2,2,128,128]{6,5,4,3,2,1,0:T(8,128)(2,1)S(1)}, bf16[1,3,1,2,2,128,128]{6,5,4,3,2,1,0:T(8,128)(2,1)}, u32[]{:S(2)}) %copy-start.7) | copy-done | bytes 393240
  12.4 1.4 %weights.1 = (bf16[3,4,128,512]{3,2,1,0:T(8,128)(2,1)S(1)}, bf16[3,4,1,128,512]{4,3,2,1,0:T(8,128)(2,1)S(1)}, bf16[2,2,128,512]{3,2,1,0:T(8,128)(2,1)S(1)}, bf16...) custom-call(bf16[1,3,1,4,4,128,128]{6,5,4,3,2,1,0:T(8,128)(2,1)S(1)} %copy-done.4, ...), custom_call_target="tpu_custom_call" | custom-call | flops 603979776 | tf_op jit(solution)/shard_map/weights/pallas_call | solution.py:257
  13.8 0.0 collective-permute-done.second_along
  13.8 3.0 %collective-permute-done.1.second_both = bf16[2,2,128,128]{3,2,1,0:T(8,128)(2,1)S(1)} collective-permute-done((bf16[2,2,128,128]{3,2,1,0:T(8,128)(2,1)S(1)}, bf16[2,2,128,128]{3,2,1,0:T(8,128)(2,1)S(1)}, u32[]{:S(2)}, u32[]{:S(2)}) %collective-permute-start.1) | collective-permute-done | bytes 131104 | tf_op jit(solution)/shard_map/ppermute | solution.py:246
  16.8 0.0 collective-permute-done.4.refs_4_
  16.8 0.0 collective-permute-done.3.refs_2_
  16.8 0.6 collective-permute-start.10
  17.4 1.0 %collective-permute-done.5.refs_3_ = bf16[1,256,512]{2,1,0:T(8,128)(2,1)S(1)} collective-permute-done((bf16[1,256,512]{2,1,0:T(8,128)(2,1)S(1)}, bf16[1,256,512]{2,1,0:T(8,128)(2,1)S(1)}, u32[]{:S(2)}, u32[]{:S(2)}) %collective-permute-start.5) | collective-permute-done | bytes 262176 | tf_op jit(solution)/shard_map/ppermute | solution.py:242
  18.4 0.6 off_levels.2
  19.0 0.6 collective-permute-start.6
  19.6 2.6 %collective-permute-start.7 = (bf16[1,128,512]{2,1,0:T(8,128)(2,1)S(1)}, bf16[1,128,512]{2,1,0:T(8,128)(2,1)S(1)}, u32[]{:S(2)}, u32[]{:S(2)}) collective-permute-start(bf16[1,128,512]{2,1,0:T(8,128)(2,1)S(1)} %get-tuple-element.57), channel_id=1, source_target_pairs={{0,2},{1,3},{2,0},{3,1},{4,6},{5,7},{6,4},{7,5},{8,10},{9,11},{10,... | collective-permute-start | bytes 393224 | tf_op jit(solution)/shard_map/ppermute | solution.py:246
  22.2 3.3 %collective-permute-done.10.refs_2_ = bf16[1,256,512]{2,1,0:T(8,128)(2,1)S(1)} collective-permute-done((bf16[1,256,512]{2,1,0:T(8,128)(2,1)S(1)}, bf16[1,256,512]{2,1,0:T(8,128)(2,1)S(1)}, u32[]{:S(2)}, u32[]{:S(2)}) %collective-permute-start.10) | collective-permute-done | bytes 262176 | tf_op jit(solution)/shard_map/ppermute | solution.py:242
  25.5 0.0 collective-permute-done.6.refs_1_
  25.5 0.2 collective-permute-done.7.refs_2_
  25.7 1.6 %collective-permute-start.14 = (bf16[1,4,128,128]{3,2,1,0:T(8,128)(2,1)S(1)}, bf16[1,4,128,128]{3,2,1,0:T(8,128)(2,1)S(1)}, u32[]{:S(2)}, u32[]{:S(2)}) collective-permute-start(bf16[1,4,128,128]{3,2,1,0:T(8,128)(2,1)S(1)} %get-tuple-element.64), channel_id=1, source_target_pairs={{0,4},{1,5},{2,6},{3,7},{4,0},{5,1},{6,2},{7,3},{8,12},{9,13},{10,... | collective-permute-start | bytes 393224 | tf_op jit(solution)/shard_map/ppermute | solution.py:252
  27.3 1.4 %collective-permute-start.8 = (bf16[1,128,512]{2,1,0:T(8,128)(2,1)S(1)}, bf16[1,128,512]{2,1,0:T(8,128)(2,1)S(1)}, u32[]{:S(2)}, u32[]{:S(2)}) collective-permute-start(bf16[1,128,512]{2,1,0:T(8,128)(2,1)S(1)} %collective-permute-done.7.refs_2_), channel_id=1, source_target_pairs={{0,1},{1,0},{2,3},{3,2},{4,5},{5,4},{6,7},{7,6},{8,9},{9,8},{10,11... | collective-permute-start | bytes 393224 | tf_op jit(solution)/shard_map/ppermute | solution.py:246
  28.8 0.6 off_levels.3
  29.4 0.7 collective-permute-start.12
  30.1 2.4 %collective-permute-start.13 = (bf16[1,128,512]{2,1,0:T(8,128)(2,1)S(1)}, bf16[1,128,512]{2,1,0:T(8,128)(2,1)S(1)}, u32[]{:S(2)}, u32[]{:S(2)}) collective-permute-start(bf16[1,128,512]{2,1,0:T(8,128)(2,1)S(1)} %get-tuple-element.63), channel_id=1, source_target_pairs={{0,2},{1,3},{2,0},{3,1},{4,6},{5,7},{6,4},{7,5},{8,10},{9,11},{10,... | collective-permute-start | bytes 393224 | tf_op jit(solution)/shard_map/ppermute | solution.py:246
  32.5 0.6 collective-permute-start.17
  33.1 0.6 collective-permute-done.8.refs_3_
  33.7 0.4 off_sums.2
  34.1 1.8 %collective-permute-start.9 = (bf16[128,512]{1,0:T(8,128)(2,1)S(1)}, bf16[128,512]{1,0:T(8,128)(2,1)S(1)}, u32[]{:S(2)}, u32[]{:S(2)}) collective-permute-start(bf16[128,512]{1,0:T(8,128)(2,1)S(1)} %off_sums.2), channel_id=1, source_target_pairs={{0,4},{1,5},{2,6},{3,7},{4,0},{5,1},{6,2},{7,3},{8,12},{9,13},{10,... | collective-permute-start | bytes 393224 | tf_op jit(solution)/shard_map/ppermute | solution.py:252
  35.9 0.0 collective-permute-done.14.refs_4_
  35.9 0.0 collective-permute-done.12.refs_1_
  35.9 2.7 %collective-permute-done.13.refs_2_ = bf16[1,128,512]{2,1,0:T(8,128)(2,1)S(1)} collective-permute-done((bf16[1,128,512]{2,1,0:T(8,128)(2,1)S(1)}, bf16[1,128,512]{2,1,0:T(8,128)(2,1)S(1)}, u32[]{:S(2)}, u32[]{:S(2)}) %collective-permute-start.13) | collective-permute-done | bytes 131104 | tf_op jit(solution)/shard_map/ppermute | solution.py:246
  38.6 0.7 collective-permute-start.15
  39.2 0.6 own_levels.1
  39.8 0.4 collective-permute-start.19
  40.3 4.8 %collective-permute-done.17.refs_4_ = bf16[1,4,128,128]{3,2,1,0:T(8,128)(2,1)S(1)} collective-permute-done((bf16[1,4,128,128]{3,2,1,0:T(8,128)(2,1)S(1)}, bf16[1,4,128,128]{3,2,1,0:T(8,128)(2,1)S(1)}, u32[]{:S(2)}, u32[]{:S(2)}) %collective-permute-start.17) | collective-permute-done | bytes 131104 | tf_op jit(solution)/shard_map/ppermute | solution.py:252
  45.0 1.7 %collective-permute-done.9.refs_0_ = bf16[128,512]{1,0:T(8,128)(2,1)S(1)} collective-permute-done((bf16[128,512]{1,0:T(8,128)(2,1)S(1)}, bf16[128,512]{1,0:T(8,128)(2,1)S(1)}, u32[]{:S(2)}, u32[]{:S(2)}) %collective-permute-start.9) | collective-permute-done | bytes 131104 | tf_op jit(solution)/shard_map/ppermute | solution.py:252
  46.7 0.0 collective-permute-done.15.refs_3_
  46.7 0.7 collective-permute-start.18
  47.5 0.4 off_sums.3
  47.8 3.2 %collective-permute-done.19.refs_4_ = bf16[2,128,512]{2,1,0:T(8,128)(2,1)S(1)} collective-permute-done((bf16[2,128,512]{2,1,0:T(8,128)(2,1)S(1)}, bf16[2,128,512]{2,1,0:T(8,128)(2,1)S(1)}, u32[]{:S(2)}, u32[]{:S(2)}) %collective-permute-start.19) | collective-permute-done | bytes 262176 | tf_op jit(solution)/shard_map/ppermute | solution.py:246
  51.1 2.8 %collective-permute-done.18.refs_3_ = bf16[2,128,512]{2,1,0:T(8,128)(2,1)S(1)} collective-permute-done((bf16[2,128,512]{2,1,0:T(8,128)(2,1)S(1)}, bf16[2,128,512]{2,1,0:T(8,128)(2,1)S(1)}, u32[]{:S(2)}, u32[]{:S(2)}) %collective-permute-start.18) | collective-permute-done | bytes 262176 | tf_op jit(solution)/shard_map/ppermute | solution.py:246
  53.9 0.5 collective-permute-start.20
  54.3 0.0 collective-permute-start.16
  54.3 8.5 %collective-permute-done.16.refs_1_ = bf16[128,512]{1,0:T(8,128)(2,1)S(1)} collective-permute-done((bf16[128,512]{1,0:T(8,128)(2,1)S(1)}, bf16[128,512]{1,0:T(8,128)(2,1)S(1)}, u32[]{:S(2)}, u32[]{:S(2)}) %collective-permute-start.16) | collective-permute-done | bytes 131104 | tf_op jit(solution)/shard_map/ppermute | solution.py:252
  62.8 2.5 %middle_levels.1 = (f32[1024,512]{1,0:T(8,128)S(1)}, bf16[1,128,512]{2,1,0:T(8,128)(2,1)S(1)}, bf16[1,128,512]{2,1,0:T(8,128)(2,1)S(1)}, bf16[1,128,512]{2,1,0:T...) custom-call(bf16[1,3,1,8,128,128]{5,4,3,2,1,0:T(8,128)(2,1)S(1)} %co, ...), custom_call_target="tpu_custom_call" | custom-call | flops 1342177280 | tf_op jit(solution)/shard_map/middle_levels/pallas_call | solution.py:257
  65.3 0.1 collective-permute-start.21
  65.4 2.0 %collective-permute-start.22 = (bf16[1,1,128,512]{3,2,1,0:T(8,128)(2,1)S(1)}, bf16[1,1,128,512]{3,2,1,0:T(8,128)(2,1)S(1)}, u32[]{:S(2)}, u32[]{:S(2)}) collective-permute-start(bf16[1,1,128,512]{3,2,1,0:T(8,128)(2,1)S(1)} %get-tuple-element.77), channel_id=1, source_target_pairs={{0,2},{1,3},{2,0},{3,1},{4,6},{5,7},{6,4},{7,5},{8,10},{9,11},{10,... | collective-permute-start | bytes 393224 | tf_op jit(solution)/shard_map/ppermute | solution.py:246
  67.4 1.4 %collective-permute-start.23 = (bf16[1,1,128,512]{3,2,1,0:T(8,128)(2,1)S(1)}, bf16[1,1,128,512]{3,2,1,0:T(8,128)(2,1)S(1)}, u32[]{:S(2)}, u32[]{:S(2)}) collective-permute-start(bf16[1,1,128,512]{3,2,1,0:T(8,128)(2,1)S(1)} %get-tuple-element.78), channel_id=1, source_target_pairs={{0,1},{1,0},{2,3},{3,2},{4,5},{5,4},{6,7},{7,6},{8,9},{9,8},{10,11... | collective-permute-start | bytes 393224 | tf_op jit(solution)/shard_map/ppermute | solution.py:246
  68.9 2.4 %collective-permute-done.21.refs_0_ = bf16[1,1,128,512]{3,2,1,0:T(8,128)(2,1)S(1)} collective-permute-done((bf16[1,1,128,512]{3,2,1,0:T(8,128)(2,1)S(1)}, bf16[1,1,128,512]{3,2,1,0:T(8,128)(2,1)S(1)}, u32[]{:S(2)}, u32[]{:S(2)}) %collective-permute-start.21) | collective-permute-done | bytes 131104 | tf_op jit(solution)/shard_map/ppermute | solution.py:246
  71.3 1.9 %collective-permute-done.22.refs_1_ = bf16[1,1,128,512]{3,2,1,0:T(8,128)(2,1)S(1)} collective-permute-done((bf16[1,1,128,512]{3,2,1,0:T(8,128)(2,1)S(1)}, bf16[1,1,128,512]{3,2,1,0:T(8,128)(2,1)S(1)}, u32[]{:S(2)}, u32[]{:S(2)}) %collective-permute-start.22) | collective-permute-done | bytes 131104 | tf_op jit(solution)/shard_map/ppermute | solution.py:246
  73.1 1.4 %collective-permute-done.23.refs_2_ = bf16[1,1,128,512]{3,2,1,0:T(8,128)(2,1)S(1)} collective-permute-done((bf16[1,1,128,512]{3,2,1,0:T(8,128)(2,1)S(1)}, bf16[1,1,128,512]{3,2,1,0:T(8,128)(2,1)S(1)}, u32[]{:S(2)}, u32[]{:S(2)}) %collective-permute-start.23) | collective-permute-done | bytes 131104 | tf_op jit(solution)/shard_map/ppermute | solution.py:246
  74.5 0.2 sums.1
  74.8 0.1 collective-permute-start.25
  74.8 2.8 %collective-permute-start.26 = (bf16[1,128,512]{2,1,0:T(8,128)(2,1)S(1)}, bf16[1,128,512]{2,1,0:T(8,128)(2,1)S(1)}, u32[]{:S(2)}, u32[]{:S(2)}) collective-permute-start(bf16[1,128,512]{2,1,0:T(8,128)(2,1)S(1)} %get-tuple-element.83), channel_id=1, source_target_pairs={{0,2},{1,3},{2,0},{3,1},{4,6},{5,7},{6,4},{7,5},{8,10},{9,11},{10,... | collective-permute-start | bytes 393224 | tf_op jit(solution)/shard_map/ppermute | solution.py:246
  77.6 0.7 collective-permute-start.27
  78.3 2.4 %collective-permute-done.25.refs_1_ = bf16[1,128,512]{2,1,0:T(8,128)(2,1)S(1)} collective-permute-done((bf16[1,128,512]{2,1,0:T(8,128)(2,1)S(1)}, bf16[1,128,512]{2,1,0:T(8,128)(2,1)S(1)}, u32[]{:S(2)}, u32[]{:S(2)}) %collective-permute-start.25) | collective-permute-done | bytes 131104 | tf_op jit(solution)/shard_map/ppermute | solution.py:246
  80.7 1.3 %collective-permute-done.26.refs_2_ = bf16[1,128,512]{2,1,0:T(8,128)(2,1)S(1)} collective-permute-done((bf16[1,128,512]{2,1,0:T(8,128)(2,1)S(1)}, bf16[1,128,512]{2,1,0:T(8,128)(2,1)S(1)}, u32[]{:S(2)}, u32[]{:S(2)}) %collective-permute-start.26) | collective-permute-done | bytes 131104 | tf_op jit(solution)/shard_map/ppermute | solution.py:246
  82.0 0.6 collective-permute-done.27.refs_3_
  82.6 2.4 %collective-permute-done.24.refs_0_ = bf16[1,128,512]{2,1,0:T(8,128)(2,1)S(1)} collective-permute-done((bf16[1,128,512]{2,1,0:T(8,128)(2,1)S(1)}, bf16[1,128,512]{2,1,0:T(8,128)(2,1)S(1)}, u32[]{:S(2)}, u32[]{:S(2)}) %collective-permute-start.24) | collective-permute-done | bytes 131104 | tf_op jit(solution)/shard_map/ppermute | solution.py:252
  85.0 1.6 %last_levels.1 = bf16[1,1024,512]{2,1,0:T(8,128)(2,1)} custom-call(bf16[1,3,1,8,128,128]{5,4,3,2,1,0:T(8,128)(2,1)S(1)} %copy-done, bf16[1024,256]{1,0:T(8,128)(2,1)S(1)} %get-tuple-element.46.row_mats, f32[1024,512]{1,0:T(8,128)S(1)} %get-tuple-element.75.residual, bf16[1,128,512]{2,1,0:T(8,128)(2,1)S(1)} %collective-permute-done.24.refs_0_, ...), custom_call_target="tpu_custom_call" | custom-call | flops 335544320 | tf_op jit(solution)/shard_map/last_levels/pallas_call | solution.py:257
  (20 shorter events, 0.1 us)
Async XLA Ops:
  0.0 4.3 %copy-start.3 = (bf16[1,3,1,8,128,128]{5,4,3,2,1,0:T(8,128)(2,1)S(1)}, bf16[1,3,1,8,128,128]{5,4,3,2,1,0:T(8,128)(2,1)}, u32[]{:S(2)}) copy-start(bf16[1,3,1,8,128,128]{5,4,3,2,1,0:T(8,128)(2,1)} %second.3) | copy-start | bytes 2359300
  0.0 7.3 %copy-start = (bf16[1,3,1,8,128,128]{5,4,3,2,1,0:T(8,128)(2,1)S(1)}, bf16[1,3,1,8,128,128]{5,4,3,2,1,0:T(8,128)(2,1)}, u32[]{:S(2)}) copy-start(bf16[1,3,1,8,128,128]{5,4,3,2,1,0:T(8,128)(2,1)} %third.5) | copy-start | bytes 2359300
  0.0 10.0 %copy-start.6 = (bf16[1,3,2,512,128]{4,3,2,1,0:T(8,128)(2,1)S(1)}, bf16[1,3,2,512,128]{4,3,2,1,0:T(8,128)(2,1)}, u32[]{:S(2)}) copy-start(bf16[1,3,2,512,128]{4,3,2,1,0:T(8,128)(2,1)} %out_basis.1) | copy-start | bytes 2359300
  1.2 15.6 %collective-permute-start.3 = (bf16[1,256,512]{2,1,0:T(8,128)(2,1)S(1)}, bf16[1,256,512]{2,1,0:T(8,128)(2,1)S(1)}, u32[]{:S(2)}, u32[]{:S(2)}) collective-permute-start(bf16[1,256,512]{2,1,0:T(8,128)(2,1)S(1)} %get-tuple-element.88), channel_id=1, source_target_pairs={{0,16},{8,24},{16,0},{24,8},{1,17},{9,25},{17,1},{25,9},{2,18},{10... | collective-permute-start | bytes 786440 | tf_op jit(solution)/shard_map/ppermute | solution.py:242
  4.3 13.1 %collective-permute-start.2 = (bf16[2,256,512]{2,1,0:T(8,128)(2,1)}, bf16[2,256,512]{2,1,0:T(8,128)(2,1)S(1)}, u32[]{:S(2)}, u32[]{:S(2)}) collective-permute-start(bf16[2,256,512]{2,1,0:T(8,128)(2,1)} %refs_0_.3), channel_id=1, source_target_pairs={{0,8},{8,0},{16,24},{24,16},{1,9},{9,1},{17,25},{25,17},{2,10},{10... | collective-permute-start | bytes 1572872 | tf_op jit(solution)/shard_map/ppermute | solution.py:242
  4.3 9.5 %collective-permute-start = (bf16[2,2,128,128]{3,2,1,0:T(8,128)(2,1)S(1)}, bf16[2,2,128,128]{3,2,1,0:T(8,128)(2,1)S(1)}, u32[]{:S(2)}, u32[]{:S(2)}) collective-permute-start(bf16[2,2,128,128]{3,2,1,0:T(8,128)(2,1)S(1)} %get-tuple-element.50), channel_id=1, source_target_pairs={{0,2},{1,3},{2,0},{3,1},{4,6},{5,7},{6,4},{7,5},{8,10},{9,11},{10,... | collective-permute-start | bytes 393224 | tf_op jit(solution)/shard_map/ppermute | solution.py:246
  5.9 10.9 %collective-permute-start.1 = (bf16[2,2,128,128]{3,2,1,0:T(8,128)(2,1)S(1)}, bf16[2,2,128,128]{3,2,1,0:T(8,128)(2,1)S(1)}, u32[]{:S(2)}, u32[]{:S(2)}) collective-permute-start(bf16[2,2,128,128]{3,2,1,0:T(8,128)(2,1)S(1)} %get-tuple-element.51), channel_id=1, source_target_pairs={{0,3},{1,2},{2,1},{3,0},{4,7},{5,6},{6,5},{7,4},{8,11},{9,10},{10,... | collective-permute-start | bytes 393224 | tf_op jit(solution)/shard_map/ppermute | solution.py:246
  7.3 11.0 %copy-start.1 = (bf16[1,3,4,256,128]{4,3,2,1,0:T(8,128)(2,1)S(1)}, bf16[1,3,4,256,128]{4,3,2,1,0:T(8,128)(2,1)}, u32[]{:S(2)}) copy-start(bf16[1,3,4,256,128]{4,3,2,1,0:T(8,128)(2,1)} %basis.5) | copy-start | bytes 2359300
  7.4 11.0 %copy-start.2 = (bf16[2,256,512]{2,1,0:T(8,128)(2,1)S(1)}, bf16[2,256,512]{2,1,0:T(8,128)(2,1)}, u32[]{:S(2)}) copy-start(bf16[2,256,512]{2,1,0:T(8,128)(2,1)} %refs_0_.3) | copy-start | bytes 1572868
  7.4 9.4 %collective-permute-start.4 = (bf16[1,4,128,128]{3,2,1,0:T(8,128)(2,1)S(1)}, bf16[1,4,128,128]{3,2,1,0:T(8,128)(2,1)S(1)}, u32[]{:S(2)}, u32[]{:S(2)}) collective-permute-start(bf16[1,4,128,128]{3,2,1,0:T(8,128)(2,1)S(1)} %get-tuple-element.53), channel_id=1, source_target_pairs={{0,4},{1,5},{2,6},{3,7},{4,0},{5,1},{6,2},{7,3},{8,12},{9,13},{10,... | collective-permute-start | bytes 393224 | tf_op jit(solution)/shard_map/ppermute | solution.py:252
  10.0 1.4 %copy-start.4 = (bf16[1,3,1,4,4,128,128]{6,5,4,3,2,1,0:T(8,128)(2,1)S(1)}, bf16[1,3,1,4,4,128,128]{6,5,4,3,2,1,0:T(8,128)(2,1)}, u32[]{:S(2)}) copy-start(bf16[1,3,1,4,4,128,128]{6,5,4,3,2,1,0:T(8,128)(2,1)} %first.1) | copy-start | bytes 4718596
  11.4 1.0 %copy-start.7 = (bf16[1,3,1,2,2,128,128]{6,5,4,3,2,1,0:T(8,128)(2,1)S(1)}, bf16[1,3,1,2,2,128,128]{6,5,4,3,2,1,0:T(8,128)(2,1)}, u32[]{:S(2)}) copy-start(bf16[1,3,1,2,2,128,128]{6,5,4,3,2,1,0:T(8,128)(2,1)} %fourth.1) | copy-start | bytes 1179652
  16.8 1.5 %collective-permute-start.5 = (bf16[1,256,512]{2,1,0:T(8,128)(2,1)S(1)}, bf16[1,256,512]{2,1,0:T(8,128)(2,1)S(1)}, u32[]{:S(2)}, u32[]{:S(2)}) collective-permute-start(bf16[1,256,512]{2,1,0:T(8,128)(2,1)S(1)} %collective-permute-done.3.refs_2_), channel_id=1, source_target_pairs={{0,8},{8,0},{16,24},{24,16},{1,9},{9,1},{17,25},{25,17},{2,10},{10... | collective-permute-start | bytes 786440 | tf_op jit(solution)/shard_map/ppermute | solution.py:242
  16.8 8.7 %collective-permute-start.10 = (bf16[1,256,512]{2,1,0:T(8,128)(2,1)S(1)}, bf16[1,256,512]{2,1,0:T(8,128)(2,1)S(1)}, u32[]{:S(2)}, u32[]{:S(2)}) collective-permute-start(bf16[1,256,512]{2,1,0:T(8,128)(2,1)S(1)} %get-tuple-element.59), channel_id=1, source_target_pairs={{0,16},{8,24},{16,0},{24,8},{1,17},{9,25},{17,1},{25,9},{2,18},{10... | collective-permute-start | bytes 786440 | tf_op jit(solution)/shard_map/ppermute | solution.py:242
  19.0 6.6 %collective-permute-start.6 = (bf16[1,128,512]{2,1,0:T(8,128)(2,1)S(1)}, bf16[1,128,512]{2,1,0:T(8,128)(2,1)S(1)}, u32[]{:S(2)}, u32[]{:S(2)}) collective-permute-start(bf16[1,128,512]{2,1,0:T(8,128)(2,1)S(1)} %get-tuple-element.56), channel_id=1, source_target_pairs={{0,1},{1,0},{2,3},{3,2},{4,5},{5,4},{6,7},{7,6},{8,9},{9,8},{10,11... | collective-permute-start | bytes 393224 | tf_op jit(solution)/shard_map/ppermute | solution.py:246
  19.6 6.1 %collective-permute-start.7 = (bf16[1,128,512]{2,1,0:T(8,128)(2,1)S(1)}, bf16[1,128,512]{2,1,0:T(8,128)(2,1)S(1)}, u32[]{:S(2)}, u32[]{:S(2)}) collective-permute-start(bf16[1,128,512]{2,1,0:T(8,128)(2,1)S(1)} %get-tuple-element.57), channel_id=1, source_target_pairs={{0,2},{1,3},{2,0},{3,1},{4,6},{5,7},{6,4},{7,5},{8,10},{9,11},{10,... | collective-permute-start | bytes 393224 | tf_op jit(solution)/shard_map/ppermute | solution.py:246
  25.7 3.1 %collective-permute-start.11 = (bf16[1,256,512]{2,1,0:T(8,128)(2,1)S(1)}, bf16[1,256,512]{2,1,0:T(8,128)(2,1)S(1)}, u32[]{:S(2)}, u32[]{:S(2)}) collective-permute-start(bf16[1,256,512]{2,1,0:T(8,128)(2,1)S(1)} %collective-permute-done.10.refs_2_), channel_id=1, source_target_pairs={{0,8},{8,0},{16,24},{24,16},{1,9},{9,1},{17,25},{25,17},{2,10},{10... | collective-permute-start | bytes 786440 | tf_op jit(solution)/shard_map/ppermute | solution.py:242
  25.7 10.2 %collective-permute-start.14 = (bf16[1,4,128,128]{3,2,1,0:T(8,128)(2,1)S(1)}, bf16[1,4,128,128]{3,2,1,0:T(8,128)(2,1)S(1)}, u32[]{:S(2)}, u32[]{:S(2)}) collective-permute-start(bf16[1,4,128,128]{3,2,1,0:T(8,128)(2,1)S(1)} %get-tuple-element.64), channel_id=1, source_target_pairs={{0,4},{1,5},{2,6},{3,7},{4,0},{5,1},{6,2},{7,3},{8,12},{9,13},{10,... | collective-permute-start | bytes 393224 | tf_op jit(solution)/shard_map/ppermute | solution.py:252
  27.3 6.3 %collective-permute-start.8 = (bf16[1,128,512]{2,1,0:T(8,128)(2,1)S(1)}, bf16[1,128,512]{2,1,0:T(8,128)(2,1)S(1)}, u32[]{:S(2)}, u32[]{:S(2)}) collective-permute-start(bf16[1,128,512]{2,1,0:T(8,128)(2,1)S(1)} %collective-permute-done.7.refs_2_), channel_id=1, source_target_pairs={{0,1},{1,0},{2,3},{3,2},{4,5},{5,4},{6,7},{7,6},{8,9},{9,8},{10,11... | collective-permute-start | bytes 393224 | tf_op jit(solution)/shard_map/ppermute | solution.py:246
  29.4 6.5 %collective-permute-start.12 = (bf16[1,128,512]{2,1,0:T(8,128)(2,1)S(1)}, bf16[1,128,512]{2,1,0:T(8,128)(2,1)S(1)}, u32[]{:S(2)}, u32[]{:S(2)}) collective-permute-start(bf16[1,128,512]{2,1,0:T(8,128)(2,1)S(1)} %get-tuple-element.62), channel_id=1, source_target_pairs={{0,1},{1,0},{2,3},{3,2},{4,5},{5,4},{6,7},{7,6},{8,9},{9,8},{10,11... | collective-permute-start | bytes 393224 | tf_op jit(solution)/shard_map/ppermute | solution.py:246
  30.1 8.5 %collective-permute-start.13 = (bf16[1,128,512]{2,1,0:T(8,128)(2,1)S(1)}, bf16[1,128,512]{2,1,0:T(8,128)(2,1)S(1)}, u32[]{:S(2)}, u32[]{:S(2)}) collective-permute-start(bf16[1,128,512]{2,1,0:T(8,128)(2,1)S(1)} %get-tuple-element.63), channel_id=1, source_target_pairs={{0,2},{1,3},{2,0},{3,1},{4,6},{5,7},{6,4},{7,5},{8,10},{9,11},{10,... | collective-permute-start | bytes 393224 | tf_op jit(solution)/shard_map/ppermute | solution.py:246
  32.5 12.5 %collective-permute-start.17 = (bf16[1,4,128,128]{3,2,1,0:T(8,128)(2,1)S(1)}, bf16[1,4,128,128]{3,2,1,0:T(8,128)(2,1)S(1)}, u32[]{:S(2)}, u32[]{:S(2)}) collective-permute-start(bf16[1,4,128,128]{3,2,1,0:T(8,128)(2,1)S(1)} %get-tuple-element.70), channel_id=1, source_target_pairs={{0,4},{1,5},{2,6},{3,7},{4,0},{5,1},{6,2},{7,3},{8,12},{9,13},{10,... | collective-permute-start | bytes 393224 | tf_op jit(solution)/shard_map/ppermute | solution.py:252
  34.1 12.7 %collective-permute-start.9 = (bf16[128,512]{1,0:T(8,128)(2,1)S(1)}, bf16[128,512]{1,0:T(8,128)(2,1)S(1)}, u32[]{:S(2)}, u32[]{:S(2)}) collective-permute-start(bf16[128,512]{1,0:T(8,128)(2,1)S(1)} %off_sums.2), channel_id=1, source_target_pairs={{0,4},{1,5},{2,6},{3,7},{4,0},{5,1},{6,2},{7,3},{8,12},{9,13},{10,... | collective-permute-start | bytes 393224 | tf_op jit(solution)/shard_map/ppermute | solution.py:252
  38.6 8.1 %collective-permute-start.15 = (bf16[1,128,512]{2,1,0:T(8,128)(2,1)S(1)}, bf16[1,128,512]{2,1,0:T(8,128)(2,1)S(1)}, u32[]{:S(2)}, u32[]{:S(2)}) collective-permute-start(bf16[1,128,512]{2,1,0:T(8,128)(2,1)S(1)} %collective-permute-done.13.refs_2_), channel_id=1, source_target_pairs={{0,1},{1,0},{2,3},{3,2},{4,5},{5,4},{6,7},{7,6},{8,9},{9,8},{10,11... | collective-permute-start | bytes 393224 | tf_op jit(solution)/shard_map/ppermute | solution.py:246
  39.2 23.6 %copy-start.5 = (bf16[1,1024,512]{2,1,0:T(8,128)(2,1)S(1)}, bf16[1,1024,512]{2,1,0:T(8,128)(2,1)}, u32[]{:S(2)}) copy-start(bf16[1,1024,512]{2,1,0:T(8,128)(2,1)} %rhs.1) | copy-start | bytes 3145732
  39.8 11.3 %collective-permute-start.19 = (bf16[2,128,512]{2,1,0:T(8,128)(2,1)S(1)}, bf16[2,128,512]{2,1,0:T(8,128)(2,1)S(1)}, u32[]{:S(2)}, u32[]{:S(2)}) collective-permute-start(bf16[2,128,512]{2,1,0:T(8,128)(2,1)S(1)} %get-tuple-element.73), channel_id=1, source_target_pairs={{0,2},{1,3},{2,0},{3,1},{4,6},{5,7},{6,4},{7,5},{8,10},{9,11},{10,... | collective-permute-start | bytes 786440 | tf_op jit(solution)/shard_map/ppermute | solution.py:246
  46.7 7.2 %collective-permute-start.18 = (bf16[2,128,512]{2,1,0:T(8,128)(2,1)S(1)}, bf16[2,128,512]{2,1,0:T(8,128)(2,1)S(1)}, u32[]{:S(2)}, u32[]{:S(2)}) collective-permute-start(bf16[2,128,512]{2,1,0:T(8,128)(2,1)S(1)} %get-tuple-element.71), channel_id=1, source_target_pairs={{0,1},{1,0},{2,3},{3,2},{4,5},{5,4},{6,7},{7,6},{8,9},{9,8},{10,11... | collective-permute-start | bytes 786440 | tf_op jit(solution)/shard_map/ppermute | solution.py:246
  53.9 9.0 %collective-permute-start.20 = (bf16[2,128,512]{2,1,0:T(8,128)(2,1)S(1)}, bf16[2,128,512]{2,1,0:T(8,128)(2,1)S(1)}, u32[]{:S(2)}, u32[]{:S(2)}) collective-permute-start(bf16[2,128,512]{2,1,0:T(8,128)(2,1)S(1)} %collective-permute-done.19.refs_4_), channel_id=1, source_target_pairs={{0,1},{1,0},{2,3},{3,2},{4,5},{5,4},{6,7},{7,6},{8,9},{9,8},{10,11... | collective-permute-start | bytes 786440 | tf_op jit(solution)/shard_map/ppermute | solution.py:246
  54.3 8.5 %collective-permute-start.16 = (bf16[128,512]{1,0:T(8,128)(2,1)S(1)}, bf16[128,512]{1,0:T(8,128)(2,1)S(1)}, u32[]{:S(2)}, u32[]{:S(2)}) collective-permute-start(bf16[128,512]{1,0:T(8,128)(2,1)S(1)} %off_sums.3), channel_id=1, source_target_pairs={{0,4},{1,5},{2,6},{3,7},{4,0},{5,1},{6,2},{7,3},{8,12},{9,13},{10,... | collective-permute-start | bytes 393224 | tf_op jit(solution)/shard_map/ppermute | solution.py:252
  65.3 6.0 %collective-permute-start.21 = (bf16[1,1,128,512]{3,2,1,0:T(8,128)(2,1)S(1)}, bf16[1,1,128,512]{3,2,1,0:T(8,128)(2,1)S(1)}, u32[]{:S(2)}, u32[]{:S(2)}) collective-permute-start(bf16[1,1,128,512]{3,2,1,0:T(8,128)(2,1)S(1)} %get-tuple-element.76), channel_id=1, source_target_pairs={{0,3},{1,2},{2,1},{3,0},{4,7},{5,6},{6,5},{7,4},{8,11},{9,10},{10,... | collective-permute-start | bytes 393224 | tf_op jit(solution)/shard_map/ppermute | solution.py:246
  65.4 7.7 %collective-permute-start.22 = (bf16[1,1,128,512]{3,2,1,0:T(8,128)(2,1)S(1)}, bf16[1,1,128,512]{3,2,1,0:T(8,128)(2,1)S(1)}, u32[]{:S(2)}, u32[]{:S(2)}) collective-permute-start(bf16[1,1,128,512]{3,2,1,0:T(8,128)(2,1)S(1)} %get-tuple-element.77), channel_id=1, source_target_pairs={{0,2},{1,3},{2,0},{3,1},{4,6},{5,7},{6,4},{7,5},{8,10},{9,11},{10,... | collective-permute-start | bytes 393224 | tf_op jit(solution)/shard_map/ppermute | solution.py:246
  67.4 7.1 %collective-permute-start.23 = (bf16[1,1,128,512]{3,2,1,0:T(8,128)(2,1)S(1)}, bf16[1,1,128,512]{3,2,1,0:T(8,128)(2,1)S(1)}, u32[]{:S(2)}, u32[]{:S(2)}) collective-permute-start(bf16[1,1,128,512]{3,2,1,0:T(8,128)(2,1)S(1)} %get-tuple-element.78), channel_id=1, source_target_pairs={{0,1},{1,0},{2,3},{3,2},{4,5},{5,4},{6,7},{7,6},{8,9},{9,8},{10,11... | collective-permute-start | bytes 393224 | tf_op jit(solution)/shard_map/ppermute | solution.py:246
  74.8 5.9 %collective-permute-start.25 = (bf16[1,128,512]{2,1,0:T(8,128)(2,1)S(1)}, bf16[1,128,512]{2,1,0:T(8,128)(2,1)S(1)}, u32[]{:S(2)}, u32[]{:S(2)}) collective-permute-start(bf16[1,128,512]{2,1,0:T(8,128)(2,1)S(1)} %get-tuple-element.81), channel_id=1, source_target_pairs={{0,3},{1,2},{2,1},{3,0},{4,7},{5,6},{6,5},{7,4},{8,11},{9,10},{10,... | collective-permute-start | bytes 393224 | tf_op jit(solution)/shard_map/ppermute | solution.py:246
  74.8 7.1 %collective-permute-start.26 = (bf16[1,128,512]{2,1,0:T(8,128)(2,1)S(1)}, bf16[1,128,512]{2,1,0:T(8,128)(2,1)S(1)}, u32[]{:S(2)}, u32[]{:S(2)}) collective-permute-start(bf16[1,128,512]{2,1,0:T(8,128)(2,1)S(1)} %get-tuple-element.83), channel_id=1, source_target_pairs={{0,2},{1,3},{2,0},{3,1},{4,6},{5,7},{6,4},{7,5},{8,10},{9,11},{10,... | collective-permute-start | bytes 393224 | tf_op jit(solution)/shard_map/ppermute | solution.py:246
  77.6 5.0 %collective-permute-start.27 = (bf16[1,128,512]{2,1,0:T(8,128)(2,1)S(1)}, bf16[1,128,512]{2,1,0:T(8,128)(2,1)S(1)}, u32[]{:S(2)}, u32[]{:S(2)}) collective-permute-start(bf16[1,128,512]{2,1,0:T(8,128)(2,1)S(1)} %get-tuple-element.85), channel_id=1, source_target_pairs={{0,1},{1,0},{2,3},{3,2},{4,5},{5,4},{6,7},{7,6},{8,9},{9,8},{10,11... | collective-permute-start | bytes 393224 | tf_op jit(solution)/shard_map/ppermute | solution.py:246
  78.3 6.7 %collective-permute-start.24 = (bf16[1,128,512]{2,1,0:T(8,128)(2,1)S(1)}, bf16[1,128,512]{2,1,0:T(8,128)(2,1)S(1)}, u32[]{:S(2)}, u32[]{:S(2)}) collective-permute-start(bf16[1,128,512]{2,1,0:T(8,128)(2,1)S(1)} %sums.1), channel_id=1, source_target_pairs={{0,4},{1,5},{2,6},{3,7},{4,0},{5,1},{6,2},{7,3},{8,12},{9,13},{10,... | collective-permute-start | bytes 393224 | tf_op jit(solution)/shard_map/ppermute | solution.py:252

commit v10 on v9

--- a/solution.py
+++ b/solution.py
@@ -190,21 +190,33 @@
     return dot(jnp.concatenate(mats, axis=1), slots).astype(BF16)
 
 
-def middle_kernel(
-    radix, groups, offs, third, rhs, basis, row_mats, up_own, up_other, second_along, second_both, *refs
-):
-    crossed, own_in, (residual_ref,), own, other = take(refs, offs * (groups - 1), radix, 1, radix, radix)
+def crossed_kernel(groups, offs, rhs, row_mats, *refs):
+    *crossed, out = refs
+    rank = crossed[0].shape[0]
+    mats = [
+        row_mats[:, (j * groups + delta) * rank : (j * groups + delta + 1) * rank]
+        for j in range(offs)
+        for delta in range(1, groups)
+    ]
+    coefs = jnp.concatenate([ref[...] for ref in crossed], axis=0)
+    out[...] = rhs[0].astype(F32) - dot(jnp.concatenate(mats, axis=1), coefs)
+
+
+def middle_kernel(radix, groups, offs, third, part, basis, row_mats, up_own, up_other, second_along, second_both, *refs):
+    own_in, (residual_ref,), own, other = take(refs, radix, 1, radix, radix)
+    rank = third.shape[5]
     coefs = []
     for j in range(offs):
         slots = slots_of([ref[j] for ref in own_in], second_along, second_both, j, 0)
         coefs += [group_coef(j, slots, third, radix)]
-        coefs += [ref[...] for ref in crossed[j * (groups - 1) : (j + 1) * (groups - 1)]]
     coefs = jnp.concatenate(coefs, axis=0)
+    mats = [row_mats[:, j * groups * rank : (j * groups + 1) * rank] for j in range(offs)]
+    mats = jnp.concatenate(mats, axis=1)
     leaves, leaf_rows = basis.shape[2], basis.shape[3]
     leaf = []
     for k in range(leaves):
         rows = slice(k * leaf_rows, (k + 1) * leaf_rows)
-        residual = rhs[0, rows].astype(F32) - dot(row_mats[rows], coefs)
+        residual = part[rows] - dot(mats[rows], coefs)
         residual_ref[rows] = residual
         leaf.append(dot_t(basis[0, offs, k], residual.astype(BF16)).astype(BF16))
     leaf = jnp.concatenate(leaf, axis=0)
@@ -316,7 +328,7 @@
         return [over_groups(a, less - d) for d, a in enumerate(sums)]
 
     beside = over_row(solved, 1)
-    far, held, leaves, sums, crossed = [], [up_own, *seconds, *thirds[0]], [], [], []
+    far, held, leaves, sums, crossed = [], [up_own, *seconds], [], [], []
     for j in range(offs):
         pieces = [solved, beside]
         come = far
@@ -351,25 +363,33 @@
             *thirds[j],
         )
         crossed += cross(sums)
-        held = [across, along]
+        held = [across, along, *thirds[0]]
     own = call(own_kernel, "own_levels", offs * own_flops, own_out(offs)[:3], up_own, up_mid, *leaves)
     own_along = over_members(after(own[2], along), ALONG)
-    own = [own[0], over_members(after(own[1], both, *thirds[offs], *crossed[:less]), ACROSS), own_along]
-    own.append(over_members(after(own_along, own[1], *sums), ACROSS))
-
+    own = [own[0], over_members(after(own[1], both, *thirds[offs]), ACROSS), own_along]
+    own.append(over_members(after(own_along, *crossed[:less]), ACROSS))
+
+    part = call(
+        functools.partial(crossed_kernel, groups, offs),
+        "middle_crossed",
+        2 * offs * less * columns * rank * rows,
+        [((rows, columns), F32)],
+        rhs,
+        off_rows,
+        *crossed,
+    )[0]
     residual, *levels = call(
         functools.partial(middle_kernel, radix, groups, offs),
         "middle_levels",
         offs * row_flops + leaf_flops + other_flops + own_flops,
         [((rows, columns), F32)] + own_out(1) + other_out(1),
         third_level,
-        rhs,
+        part,
         leaf_basis,
         off_rows,
         up_own,
         up_other,
         *seconds,
-        *crossed,
         *own,
     )
     own, other = levels[:radix], levels[radix:]

time: 86.8 us -> 83 us (0.956)
  waiting for transfers between devices: 44.1 us -> 38.7 us
  starting transfers between devices: 30.5 us -> 31.9 us
    ppermute x17, waiting for transfers between devices: 22.4 us -> 17.1 us  [over_members(): return array if mask == 0 else lax.ppermute(array, 'box', pairs)]
    ppermute x6, starting transfers between devices: 6.71 us -> 9.58 us  [over_groups(): return lax.ppermute(array, 'box', pairs)]
    ppermute x5, waiting for transfers between devices: 4.3 us -> 1.54 us  [over_row(): return lax.ppermute(array, 'row', [(r, r ^ mask) for r in range(row_size)])]
    ppermute x6, waiting for transfers between devices: 17.4 us -> 20.1 us  [over_groups(): return lax.ppermute(array, 'box', pairs)]
    ppermute x17, starting transfers between devices: 20.2 us -> 18.7 us  [over_members(): return array if mask == 0 else lax.ppermute(array, 'box', pairs)]
    pallas_call x11 -> x12, Pallas kernels: 8.29 us -> 8.46 us  [call(): pl.pallas_call(kernel, out_shape=outs, in_specs=[VMEM] * len(args), out_s...]
  transfers between devices with their start and end apart: 28 -> 28, of which waited for: 18 -> 15; matrix products, arithmetic and copies ran while one was open for 0% -> 0% of each run, Pallas kernels for 5% -> 5%
where the time goes in v10:
time: 83 us; the launch traced here: 82.8 us
  waiting for transfers between devices  38.7 us (47%)
  starting transfers between devices  31.9 us (38%)
  Pallas kernels  8.46 us (10%)
  local copies, waits for them, and re-layouts  3.61 us (4%)
    ppermute x6, waiting for transfers between devices, over_groups(): return lax.ppermute(array, 'box', pairs)  20.1 us
    ppermute x17, starting transfers between devices, over_members(): return array if mask == 0 else lax.ppermute(array, 'box', pairs)  18.7 us
    ppermute x17, waiting for transfers between devices, over_members(): return array if mask == 0 else lax.ppermute(array, 'box', pairs)  17.1 us
    ppermute x6, starting transfers between devices, over_groups(): return lax.ppermute(array, 'box', pairs)  9.58 us
    pallas_call x12, Pallas kernels, call(): pl.pallas_call(kernel, out_shape=outs, in_specs=[VMEM] * len(args), out_s...  8.46 us
    ppermute x5, starting transfers between devices, over_row(): return lax.ppermute(array, 'row', [(r, r ^ mask) for r in range(row_size)])  3.55 us
    unnamed x16, local copies, waits for them, and re-layouts  2.43 us
  transfers between devices with their start and end apart: 28, of which 15 were waited for; matrix products, arithmetic and copies ran while one was open for 0% of the time, Pallas kernels for 5%

profile of v10, /device:TPU:0, one launch (start us, length us, event | category | flops | bytes accessed | tf_op | source)
XLA Modules:
  0.0 82.8 jit_solution(2724913336190777755)
XLA Ops:
  0.0 1.2 %fusion = (bf16[1,256,512]{2,1,0:T(8,128)(2,1)S(1)}, bf16[1,256,512]{2,1,0:T(8,128)(2,1)S(1)}) fusion(bf16[2,256,512]{2,1,0:T(8,128)(2,1)} %refs_0_.3), kind=kLoop, calls=%fused_computation | loop fusion | bytes 1048576 | tf_op jit(solution)/shard_map/slice | solution.py:335
  1.2 3.0 %collective-permute-start.3 = (bf16[1,256,512]{2,1,0:T(8,128)(2,1)S(1)}, bf16[1,256,512]{2,1,0:T(8,128)(2,1)S(1)}, u32[]{:S(2)}, u32[]{:S(2)}) collective-permute-start(bf16[1,256,512]{2,1,0:T(8,128)(2,1)S(1)} %get-tuple-element.88), channel_id=1, source_target_pairs={{0,16},{8,24},{16,0},{24,8},{1,17},{9,25},{17,1},{25,9},{2,18},{10... | collective-permute-start | bytes 786440 | tf_op jit(solution)/shard_map/ppermute | solution.py:254
  4.2 0.0 collective-permute-start.2
  4.3 1.6 %collective-permute-start = (bf16[2,2,128,128]{3,2,1,0:T(8,128)(2,1)S(1)}, bf16[2,2,128,128]{3,2,1,0:T(8,128)(2,1)S(1)}, u32[]{:S(2)}, u32[]{:S(2)}) collective-permute-start(bf16[2,2,128,128]{3,2,1,0:T(8,128)(2,1)S(1)} %get-tuple-element.48), channel_id=1, source_target_pairs={{0,2},{1,3},{2,0},{3,1},{4,6},{5,7},{6,4},{7,5},{8,10},{9,11},{10,... | collective-permute-start | bytes 393224 | tf_op jit(solution)/shard_map/ppermute | solution.py:258
  5.9 1.4 %collective-permute-start.1 = (bf16[2,2,128,128]{3,2,1,0:T(8,128)(2,1)S(1)}, bf16[2,2,128,128]{3,2,1,0:T(8,128)(2,1)S(1)}, u32[]{:S(2)}, u32[]{:S(2)}) collective-permute-start(bf16[2,2,128,128]{3,2,1,0:T(8,128)(2,1)S(1)} %get-tuple-element.49), channel_id=1, source_target_pairs={{0,3},{1,2},{2,1},{3,0},{4,7},{5,6},{6,5},{7,4},{8,11},{9,10},{10,... | collective-permute-start | bytes 393224 | tf_op jit(solution)/shard_map/ppermute | solution.py:258
  7.3 1.4 %copy-done.4 = bf16[1,3,1,4,4,128,128]{6,5,4,3,2,1,0:T(8,128)(2,1)S(1)} copy-done((bf16[1,3,1,4,4,128,128]{6,5,4,3,2,1,0:T(8,128)(2,1)S(1)}, bf16[1,3,1,4,4,128,128]{6,5,4,3,2,1,0:T(8,128)(2,1)}, u32[]{:S(2)}) %copy-start.4) | copy-done | bytes 1572888
  8.7 1.0 %copy-done.7 = bf16[1,3,1,2,2,128,128]{6,5,4,3,2,1,0:T(8,128)(2,1)S(1)} copy-done((bf16[1,3,1,2,2,128,128]{6,5,4,3,2,1,0:T(8,128)(2,1)S(1)}, bf16[1,3,1,2,2,128,128]{6,5,4,3,2,1,0:T(8,128)(2,1)}, u32[]{:S(2)}) %copy-start.7) | copy-done | bytes 393240
  9.7 1.4 %weights.1 = (bf16[3,4,128,512]{3,2,1,0:T(8,128)(2,1)S(1)}, bf16[3,4,1,128,512]{4,3,2,1,0:T(8,128)(2,1)S(1)}, bf16[2,2,128,512]{3,2,1,0:T(8,128)(2,1)S(1)}, bf16...) custom-call(bf16[1,3,1,4,4,128,128]{6,5,4,3,2,1,0:T(8,128)(2,1)S(1)} %copy-done.4, ...), custom_call_target="tpu_custom_call" | custom-call | flops 603979776 | tf_op jit(solution)/shard_map/weights/pallas_call | solution.py:269
  11.1 0.0 collective-permute-done.second_along
  11.1 2.9 %collective-permute-done.1.second_both = bf16[2,2,128,128]{3,2,1,0:T(8,128)(2,1)S(1)} collective-permute-done((bf16[2,2,128,128]{3,2,1,0:T(8,128)(2,1)S(1)}, bf16[2,2,128,128]{3,2,1,0:T(8,128)(2,1)S(1)}, u32[]{:S(2)}, u32[]{:S(2)}) %collective-permute-start.1) | collective-permute-done | bytes 131104 | tf_op jit(solution)/shard_map/ppermute | solution.py:258
  14.0 0.0 collective-permute-done.3.refs_2_
  14.0 0.0 collective-permute-start.4
  14.0 0.5 collective-permute-start.10
  14.5 2.7 %collective-permute-start.8 = (bf16[1,4,128,128]{3,2,1,0:T(8,128)(2,1)S(1)}, bf16[1,4,128,128]{3,2,1,0:T(8,128)(2,1)S(1)}, u32[]{:S(2)}, u32[]{:S(2)}) collective-permute-start(bf16[1,4,128,128]{3,2,1,0:T(8,128)(2,1)S(1)} %get-tuple-element.58), channel_id=1, source_target_pairs={{0,4},{1,5},{2,6},{3,7},{4,0},{5,1},{6,2},{7,3},{8,12},{9,13},{10,... | collective-permute-start | bytes 393224 | tf_op jit(solution)/shard_map/ppermute | solution.py:264
  17.2 0.0 collective-permute-done.2.refs_1_
  17.2 0.0 collective-permute-done.4.refs_3_
  17.2 0.6 off_levels.2
  17.8 0.6 collective-permute-start.5
  18.4 1.6 %collective-permute-start.6 = (bf16[1,128,512]{2,1,0:T(8,128)(2,1)S(1)}, bf16[1,128,512]{2,1,0:T(8,128)(2,1)S(1)}, u32[]{:S(2)}, u32[]{:S(2)}) collective-permute-start(bf16[1,128,512]{2,1,0:T(8,128)(2,1)S(1)} %get-tuple-element.56), channel_id=1, source_target_pairs={{0,2},{1,3},{2,0},{3,1},{4,6},{5,7},{6,4},{7,5},{8,10},{9,11},{10,... | collective-permute-start | bytes 393224 | tf_op jit(solution)/shard_map/ppermute | solution.py:258
  20.0 4.0 %collective-permute-done.8.refs_4_ = bf16[1,4,128,128]{3,2,1,0:T(8,128)(2,1)S(1)} collective-permute-done((bf16[1,4,128,128]{3,2,1,0:T(8,128)(2,1)S(1)}, bf16[1,4,128,128]{3,2,1,0:T(8,128)(2,1)S(1)}, u32[]{:S(2)}, u32[]{:S(2)}) %collective-permute-start.8) | collective-permute-done | bytes 131104 | tf_op jit(solution)/shard_map/ppermute | solution.py:264
  24.0 0.0 collective-permute-done.10.refs_2_
  24.0 1.1 %collective-permute-done.6.refs_2_ = bf16[1,128,512]{2,1,0:T(8,128)(2,1)S(1)} collective-permute-done((bf16[1,128,512]{2,1,0:T(8,128)(2,1)S(1)}, bf16[1,128,512]{2,1,0:T(8,128)(2,1)S(1)}, u32[]{:S(2)}, u32[]{:S(2)}) %collective-permute-start.6) | collective-permute-done | bytes 131104 | tf_op jit(solution)/shard_map/ppermute | solution.py:258
  25.2 0.0 collective-permute-start.11
  25.2 1.5 %collective-permute-done.11.refs_3_ = bf16[1,256,512]{2,1,0:T(8,128)(2,1)S(1)} collective-permute-done((bf16[1,256,512]{2,1,0:T(8,128)(2,1)S(1)}, bf16[1,256,512]{2,1,0:T(8,128)(2,1)S(1)}, u32[]{:S(2)}, u32[]{:S(2)}) %collective-permute-start.11) | collective-permute-done | bytes 262176 | tf_op jit(solution)/shard_map/ppermute | solution.py:254
  26.7 0.6 off_levels.3
  27.3 0.5 collective-permute-start.13
  27.9 3.2 %collective-permute-start.14 = (bf16[1,4,128,128]{3,2,1,0:T(8,128)(2,1)S(1)}, bf16[1,4,128,128]{3,2,1,0:T(8,128)(2,1)S(1)}, u32[]{:S(2)}, u32[]{:S(2)}) collective-permute-start(bf16[1,4,128,128]{3,2,1,0:T(8,128)(2,1)S(1)} %get-tuple-element.64), channel_id=1, source_target_pairs={{0,4},{1,5},{2,6},{3,7},{4,0},{5,1},{6,2},{7,3},{8,12},{9,13},{10,... | collective-permute-start | bytes 393224 | tf_op jit(solution)/shard_map/ppermute | solution.py:264
  31.1 1.5 %collective-permute-start.7 = (bf16[1,128,512]{2,1,0:T(8,128)(2,1)S(1)}, bf16[1,128,512]{2,1,0:T(8,128)(2,1)S(1)}, u32[]{:S(2)}, u32[]{:S(2)}) collective-permute-start(bf16[1,128,512]{2,1,0:T(8,128)(2,1)S(1)} %collective-permute-done.6.refs_2_), channel_id=1, source_target_pairs={{0,1},{1,0},{2,3},{3,2},{4,5},{5,4},{6,7},{7,6},{8,9},{9,8},{10,11... | collective-permute-start | bytes 393224 | tf_op jit(solution)/shard_map/ppermute | solution.py:258
  32.6 0.6 collective-permute-start.12
  33.1 0.6 own_levels.1
  33.7 0.0 copy-start.5
  33.7 1.8 %collective-permute-done.13.refs_2_ = bf16[1,128,512]{2,1,0:T(8,128)(2,1)S(1)} collective-permute-done((bf16[1,128,512]{2,1,0:T(8,128)(2,1)S(1)}, bf16[1,128,512]{2,1,0:T(8,128)(2,1)S(1)}, u32[]{:S(2)}, u32[]{:S(2)}) %collective-permute-start.13) | collective-permute-done | bytes 131104 | tf_op jit(solution)/shard_map/ppermute | solution.py:258
  35.5 0.0 collective-permute-start.19
  35.5 2.3 %collective-permute-start.17 = (bf16[1,4,128,128]{3,2,1,0:T(8,128)(2,1)S(1)}, bf16[1,4,128,128]{3,2,1,0:T(8,128)(2,1)S(1)}, u32[]{:S(2)}, u32[]{:S(2)}) collective-permute-start(bf16[1,4,128,128]{3,2,1,0:T(8,128)(2,1)S(1)} %get-tuple-element.70), channel_id=1, source_target_pairs={{0,4},{1,5},{2,6},{3,7},{4,0},{5,1},{6,2},{7,3},{8,12},{9,13},{10,... | collective-permute-start | bytes 393224 | tf_op jit(solution)/shard_map/ppermute | solution.py:264
  37.8 0.4 off_sums.2
  38.2 0.7 collective-permute-done.12.refs_1_
  38.9 1.5 %collective-permute-start.15 = (bf16[1,128,512]{2,1,0:T(8,128)(2,1)S(1)}, bf16[1,128,512]{2,1,0:T(8,128)(2,1)S(1)}, u32[]{:S(2)}, u32[]{:S(2)}) collective-permute-start(bf16[1,128,512]{2,1,0:T(8,128)(2,1)S(1)} %collective-permute-done.13.refs_2_), channel_id=1, source_target_pairs={{0,1},{1,0},{2,3},{3,2},{4,5},{5,4},{6,7},{7,6},{8,9},{9,8},{10,11... | collective-permute-start | bytes 393224 | tf_op jit(solution)/shard_map/ppermute | solution.py:258
  40.4 0.3 collective-permute-start.9
  40.6 4.1 %collective-permute-done.17.refs_4_ = bf16[1,4,128,128]{3,2,1,0:T(8,128)(2,1)S(1)} collective-permute-done((bf16[1,4,128,128]{3,2,1,0:T(8,128)(2,1)S(1)}, bf16[1,4,128,128]{3,2,1,0:T(8,128)(2,1)S(1)}, u32[]{:S(2)}, u32[]{:S(2)}) %collective-permute-start.17) | collective-permute-done | bytes 131104 | tf_op jit(solution)/shard_map/ppermute | solution.py:264
  44.8 1.4 %collective-permute-start.18 = (bf16[2,128,512]{2,1,0:T(8,128)(2,1)S(1)}, bf16[2,128,512]{2,1,0:T(8,128)(2,1)S(1)}, u32[]{:S(2)}, u32[]{:S(2)}) collective-permute-start(bf16[2,128,512]{2,1,0:T(8,128)(2,1)S(1)} %get-tuple-element.71), channel_id=1, source_target_pairs={{0,1},{1,0},{2,3},{3,2},{4,5},{5,4},{6,7},{7,6},{8,9},{9,8},{10,11... | collective-permute-start | bytes 786440 | tf_op jit(solution)/shard_map/ppermute | solution.py:258
  46.2 4.2 %collective-permute-done.9.refs_0_ = bf16[128,512]{1,0:T(8,128)(2,1)S(1)} collective-permute-done((bf16[128,512]{1,0:T(8,128)(2,1)S(1)}, bf16[128,512]{1,0:T(8,128)(2,1)S(1)}, u32[]{:S(2)}, u32[]{:S(2)}) %collective-permute-start.9) | collective-permute-done | bytes 131104 | tf_op jit(solution)/shard_map/ppermute | solution.py:264
  50.3 1.0 %collective-permute-start.20 = (bf16[2,128,512]{2,1,0:T(8,128)(2,1)S(1)}, bf16[2,128,512]{2,1,0:T(8,128)(2,1)S(1)}, u32[]{:S(2)}, u32[]{:S(2)}) collective-permute-start(bf16[2,128,512]{2,1,0:T(8,128)(2,1)S(1)} %collective-permute-done.19.refs_2_), channel_id=1, source_target_pairs={{0,1},{1,0},{2,3},{3,2},{4,5},{5,4},{6,7},{7,6},{8,9},{9,8},{10,11... | collective-permute-start | bytes 786440 | tf_op jit(solution)/shard_map/ppermute | solution.py:258
  51.3 0.4 off_sums.3
  51.7 0.1 collective-permute-start.16
  51.8 6.4 %collective-permute-done.16.refs_1_ = bf16[128,512]{1,0:T(8,128)(2,1)S(1)} collective-permute-done((bf16[128,512]{1,0:T(8,128)(2,1)S(1)}, bf16[128,512]{1,0:T(8,128)(2,1)S(1)}, u32[]{:S(2)}, u32[]{:S(2)}) %collective-permute-start.16) | collective-permute-done | bytes 131104 | tf_op jit(solution)/shard_map/ppermute | solution.py:264
  58.1 0.4 middle_crossed.1.part
  58.6 0.0 collective-permute-done.20.refs_3_
  58.6 2.2 %middle_levels.1 = (f32[1024,512]{1,0:T(8,128)S(1)}, bf16[1,128,512]{2,1,0:T(8,128)(2,1)S(1)}, bf16[1,128,512]{2,1,0:T(8,128)(2,1)S(1)}, bf16[1,128,512]{2,1,0:T...) custom-call(bf16[1,3,1,8,128,128]{5,4,3,2,1,0:T(8,128)(2,1)S(1)} %co, ...), custom_call_target="tpu_custom_call" | custom-call | flops 1342177280 | tf_op jit(solution)/shard_map/middle_levels/pallas_call | solution.py:269
  60.8 1.4 %collective-permute-start.21 = (bf16[1,1,128,512]{3,2,1,0:T(8,128)(2,1)S(1)}, bf16[1,1,128,512]{3,2,1,0:T(8,128)(2,1)S(1)}, u32[]{:S(2)}, u32[]{:S(2)}) collective-permute-start(bf16[1,1,128,512]{3,2,1,0:T(8,128)(2,1)S(1)} %get-tuple-element.76), channel_id=1, source_target_pairs={{0,3},{1,2},{2,1},{3,0},{4,7},{5,6},{6,5},{7,4},{8,11},{9,10},{10,... | collective-permute-start | bytes 393224 | tf_op jit(solution)/shard_map/ppermute | solution.py:258
  62.2 1.5 %collective-permute-start.22 = (bf16[1,1,128,512]{3,2,1,0:T(8,128)(2,1)S(1)}, bf16[1,1,128,512]{3,2,1,0:T(8,128)(2,1)S(1)}, u32[]{:S(2)}, u32[]{:S(2)}) collective-permute-start(bf16[1,1,128,512]{3,2,1,0:T(8,128)(2,1)S(1)} %get-tuple-element.77), channel_id=1, source_target_pairs={{0,2},{1,3},{2,0},{3,1},{4,6},{5,7},{6,4},{7,5},{8,10},{9,11},{10,... | collective-permute-start | bytes 393224 | tf_op jit(solution)/shard_map/ppermute | solution.py:258
  63.7 0.7 collective-permute-start.23
  64.4 3.1 %collective-permute-done.21.refs_0_ = bf16[1,1,128,512]{3,2,1,0:T(8,128)(2,1)S(1)} collective-permute-done((bf16[1,1,128,512]{3,2,1,0:T(8,128)(2,1)S(1)}, bf16[1,1,128,512]{3,2,1,0:T(8,128)(2,1)S(1)}, u32[]{:S(2)}, u32[]{:S(2)}) %collective-permute-start.21) | collective-permute-done | bytes 131104 | tf_op jit(solution)/shard_map/ppermute | solution.py:258
  67.4 1.6 %collective-permute-done.22.refs_1_ = bf16[1,1,128,512]{3,2,1,0:T(8,128)(2,1)S(1)} collective-permute-done((bf16[1,1,128,512]{3,2,1,0:T(8,128)(2,1)S(1)}, bf16[1,1,128,512]{3,2,1,0:T(8,128)(2,1)S(1)}, u32[]{:S(2)}, u32[]{:S(2)}) %collective-permute-start.22) | collective-permute-done | bytes 131104 | tf_op jit(solution)/shard_map/ppermute | solution.py:258
  69.1 0.1 collective-permute-done.23.refs_2_
  69.1 0.2 sums.1
  69.4 0.9 %collective-permute-start.25 = (bf16[1,128,512]{2,1,0:T(8,128)(2,1)S(1)}, bf16[1,128,512]{2,1,0:T(8,128)(2,1)S(1)}, u32[]{:S(2)}, u32[]{:S(2)}) collective-permute-start(bf16[1,128,512]{2,1,0:T(8,128)(2,1)S(1)} %get-tuple-element.81), channel_id=1, source_target_pairs={{0,3},{1,2},{2,1},{3,0},{4,7},{5,6},{6,5},{7,4},{8,11},{9,10},{10,... | collective-permute-start | bytes 393224 | tf_op jit(solution)/shard_map/ppermute | solution.py:258
  70.2 2.1 %collective-permute-start.26 = (bf16[1,128,512]{2,1,0:T(8,128)(2,1)S(1)}, bf16[1,128,512]{2,1,0:T(8,128)(2,1)S(1)}, u32[]{:S(2)}, u32[]{:S(2)}) collective-permute-start(bf16[1,128,512]{2,1,0:T(8,128)(2,1)S(1)} %get-tuple-element.83), channel_id=1, source_target_pairs={{0,2},{1,3},{2,0},{3,1},{4,6},{5,7},{6,4},{7,5},{8,10},{9,11},{10,... | collective-permute-start | bytes 393224 | tf_op jit(solution)/shard_map/ppermute | solution.py:258
  72.3 0.6 collective-permute-start.27
  72.9 1.1 %collective-permute-start.24 = (bf16[1,128,512]{2,1,0:T(8,128)(2,1)S(1)}, bf16[1,128,512]{2,1,0:T(8,128)(2,1)S(1)}, u32[]{:S(2)}, u32[]{:S(2)}) collective-permute-start(bf16[1,128,512]{2,1,0:T(8,128)(2,1)S(1)} %sums.1), channel_id=1, source_target_pairs={{0,4},{1,5},{2,6},{3,7},{4,0},{5,1},{6,2},{7,3},{8,12},{9,13},{10,... | collective-permute-start | bytes 393224 | tf_op jit(solution)/shard_map/ppermute | solution.py:264
  74.0 3.6 %collective-permute-done.25.refs_1_ = bf16[1,128,512]{2,1,0:T(8,128)(2,1)S(1)} collective-permute-done((bf16[1,128,512]{2,1,0:T(8,128)(2,1)S(1)}, bf16[1,128,512]{2,1,0:T(8,128)(2,1)S(1)}, u32[]{:S(2)}, u32[]{:S(2)}) %collective-permute-start.25) | collective-permute-done | bytes 131104 | tf_op jit(solution)/shard_map/ppermute | solution.py:258
  77.6 2.2 %collective-permute-done.26.refs_2_ = bf16[1,128,512]{2,1,0:T(8,128)(2,1)S(1)} collective-permute-done((bf16[1,128,512]{2,1,0:T(8,128)(2,1)S(1)}, bf16[1,128,512]{2,1,0:T(8,128)(2,1)S(1)}, u32[]{:S(2)}, u32[]{:S(2)}) %collective-permute-start.26) | collective-permute-done | bytes 131104 | tf_op jit(solution)/shard_map/ppermute | solution.py:258
  79.8 0.0 collective-permute-done.27.refs_3_
  79.8 1.4 %collective-permute-done.24.refs_0_ = bf16[1,128,512]{2,1,0:T(8,128)(2,1)S(1)} collective-permute-done((bf16[1,128,512]{2,1,0:T(8,128)(2,1)S(1)}, bf16[1,128,512]{2,1,0:T(8,128)(2,1)S(1)}, u32[]{:S(2)}, u32[]{:S(2)}) %collective-permute-start.24) | collective-permute-done | bytes 131104 | tf_op jit(solution)/shard_map/ppermute | solution.py:264
  81.2 1.6 %last_levels.1 = bf16[1,1024,512]{2,1,0:T(8,128)(2,1)} custom-call(bf16[1,3,1,8,128,128]{5,4,3,2,1,0:T(8,128)(2,1)S(1)} %copy-done, bf16[1024,256]{1,0:T(8,128)(2,1)S(1)} %get-tuple-element.46.row_mats, f32[1024,512]{1,0:T(8,128)S(1)} %get-tuple-element.75.residual, bf16[1,128,512]{2,1,0:T(8,128)(2,1)S(1)} %collective-permute-done.24.refs_0_, ...), custom_call_target="tpu_custom_call" | custom-call | flops 335544320 | tf_op jit(solution)/shard_map/last_levels/pallas_call | solution.py:269
  (21 shorter events, 0.1 us)
Async XLA Ops:
  0.0 4.2 %copy-start.3 = (bf16[1,3,1,8,128,128]{5,4,3,2,1,0:T(8,128)(2,1)S(1)}, bf16[1,3,1,8,128,128]{5,4,3,2,1,0:T(8,128)(2,1)}, u32[]{:S(2)}) copy-start(bf16[1,3,1,8,128,128]{5,4,3,2,1,0:T(8,128)(2,1)} %second.3) | copy-start | bytes 2359300
  0.0 7.3 %copy-start.6 = (bf16[1,3,2,512,128]{4,3,2,1,0:T(8,128)(2,1)S(1)}, bf16[1,3,2,512,128]{4,3,2,1,0:T(8,128)(2,1)}, u32[]{:S(2)}) copy-start(bf16[1,3,2,512,128]{4,3,2,1,0:T(8,128)(2,1)} %out_basis.1) | copy-start | bytes 2359300
  1.2 12.8 %collective-permute-start.3 = (bf16[1,256,512]{2,1,0:T(8,128)(2,1)S(1)}, bf16[1,256,512]{2,1,0:T(8,128)(2,1)S(1)}, u32[]{:S(2)}, u32[]{:S(2)}) collective-permute-start(bf16[1,256,512]{2,1,0:T(8,128)(2,1)S(1)} %get-tuple-element.88), channel_id=1, source_target_pairs={{0,16},{8,24},{16,0},{24,8},{1,17},{9,25},{17,1},{25,9},{2,18},{10... | collective-permute-start | bytes 786440 | tf_op jit(solution)/shard_map/ppermute | solution.py:254
  4.2 12.9 %collective-permute-start.2 = (bf16[2,256,512]{2,1,0:T(8,128)(2,1)}, bf16[2,256,512]{2,1,0:T(8,128)(2,1)S(1)}, u32[]{:S(2)}, u32[]{:S(2)}) collective-permute-start(bf16[2,256,512]{2,1,0:T(8,128)(2,1)} %refs_0_.3), channel_id=1, source_target_pairs={{0,8},{8,0},{16,24},{24,16},{1,9},{9,1},{17,25},{25,17},{2,10},{10... | collective-permute-start | bytes 1572872 | tf_op jit(solution)/shard_map/ppermute | solution.py:254
  4.3 6.8 %collective-permute-start = (bf16[2,2,128,128]{3,2,1,0:T(8,128)(2,1)S(1)}, bf16[2,2,128,128]{3,2,1,0:T(8,128)(2,1)S(1)}, u32[]{:S(2)}, u32[]{:S(2)}) collective-permute-start(bf16[2,2,128,128]{3,2,1,0:T(8,128)(2,1)S(1)} %get-tuple-element.48), channel_id=1, source_target_pairs={{0,2},{1,3},{2,0},{3,1},{4,6},{5,7},{6,4},{7,5},{8,10},{9,11},{10,... | collective-permute-start | bytes 393224 | tf_op jit(solution)/shard_map/ppermute | solution.py:258
  5.9 8.6 %copy-start = (bf16[1,3,1,8,128,128]{5,4,3,2,1,0:T(8,128)(2,1)S(1)}, bf16[1,3,1,8,128,128]{5,4,3,2,1,0:T(8,128)(2,1)}, u32[]{:S(2)}) copy-start(bf16[1,3,1,8,128,128]{5,4,3,2,1,0:T(8,128)(2,1)} %third.5) | copy-start | bytes 2359300
  5.9 11.3 %copy-start.1 = (bf16[1,3,4,256,128]{4,3,2,1,0:T(8,128)(2,1)S(1)}, bf16[1,3,4,256,128]{4,3,2,1,0:T(8,128)(2,1)}, u32[]{:S(2)}) copy-start(bf16[1,3,4,256,128]{4,3,2,1,0:T(8,128)(2,1)} %basis.5) | copy-start | bytes 2359300
  5.9 11.3 %copy-start.2 = (bf16[2,256,512]{2,1,0:T(8,128)(2,1)S(1)}, bf16[2,256,512]{2,1,0:T(8,128)(2,1)}, u32[]{:S(2)}) copy-start(bf16[2,256,512]{2,1,0:T(8,128)(2,1)} %refs_0_.3) | copy-start | bytes 1572868
  5.9 8.1 %collective-permute-start.1 = (bf16[2,2,128,128]{3,2,1,0:T(8,128)(2,1)S(1)}, bf16[2,2,128,128]{3,2,1,0:T(8,128)(2,1)S(1)}, u32[]{:S(2)}, u32[]{:S(2)}) collective-permute-start(bf16[2,2,128,128]{3,2,1,0:T(8,128)(2,1)S(1)} %get-tuple-element.49), channel_id=1, source_target_pairs={{0,3},{1,2},{2,1},{3,0},{4,7},{5,6},{6,5},{7,4},{8,11},{9,10},{10,... | collective-permute-start | bytes 393224 | tf_op jit(solution)/shard_map/ppermute | solution.py:258
  7.3 1.4 %copy-start.4 = (bf16[1,3,1,4,4,128,128]{6,5,4,3,2,1,0:T(8,128)(2,1)S(1)}, bf16[1,3,1,4,4,128,128]{6,5,4,3,2,1,0:T(8,128)(2,1)}, u32[]{:S(2)}) copy-start(bf16[1,3,1,4,4,128,128]{6,5,4,3,2,1,0:T(8,128)(2,1)} %first.1) | copy-start | bytes 4718596
  8.7 1.0 %copy-start.7 = (bf16[1,3,1,2,2,128,128]{6,5,4,3,2,1,0:T(8,128)(2,1)S(1)}, bf16[1,3,1,2,2,128,128]{6,5,4,3,2,1,0:T(8,128)(2,1)}, u32[]{:S(2)}) copy-start(bf16[1,3,1,2,2,128,128]{6,5,4,3,2,1,0:T(8,128)(2,1)} %fourth.1) | copy-start | bytes 1179652
  14.0 3.2 %collective-permute-start.4 = (bf16[1,256,512]{2,1,0:T(8,128)(2,1)S(1)}, bf16[1,256,512]{2,1,0:T(8,128)(2,1)S(1)}, u32[]{:S(2)}, u32[]{:S(2)}) collective-permute-start(bf16[1,256,512]{2,1,0:T(8,128)(2,1)S(1)} %collective-permute-done.3.refs_2_), channel_id=1, source_target_pairs={{0,8},{8,0},{16,24},{24,16},{1,9},{9,1},{17,25},{25,17},{2,10},{10... | collective-permute-start | bytes 786440 | tf_op jit(solution)/shard_map/ppermute | solution.py:254
  14.0 10.1 %collective-permute-start.10 = (bf16[1,256,512]{2,1,0:T(8,128)(2,1)S(1)}, bf16[1,256,512]{2,1,0:T(8,128)(2,1)S(1)}, u32[]{:S(2)}, u32[]{:S(2)}) collective-permute-start(bf16[1,256,512]{2,1,0:T(8,128)(2,1)S(1)} %get-tuple-element.59), channel_id=1, source_target_pairs={{0,16},{8,24},{16,0},{24,8},{1,17},{9,25},{17,1},{25,9},{2,18},{10... | collective-permute-start | bytes 786440 | tf_op jit(solution)/shard_map/ppermute | solution.py:254
  14.5 9.5 %collective-permute-start.8 = (bf16[1,4,128,128]{3,2,1,0:T(8,128)(2,1)S(1)}, bf16[1,4,128,128]{3,2,1,0:T(8,128)(2,1)S(1)}, u32[]{:S(2)}, u32[]{:S(2)}) collective-permute-start(bf16[1,4,128,128]{3,2,1,0:T(8,128)(2,1)S(1)} %get-tuple-element.58), channel_id=1, source_target_pairs={{0,4},{1,5},{2,6},{3,7},{4,0},{5,1},{6,2},{7,3},{8,12},{9,13},{10,... | collective-permute-start | bytes 393224 | tf_op jit(solution)/shard_map/ppermute | solution.py:264
  17.8 6.2 %collective-permute-start.5 = (bf16[1,128,512]{2,1,0:T(8,128)(2,1)S(1)}, bf16[1,128,512]{2,1,0:T(8,128)(2,1)S(1)}, u32[]{:S(2)}, u32[]{:S(2)}) collective-permute-start(bf16[1,128,512]{2,1,0:T(8,128)(2,1)S(1)} %get-tuple-element.55), channel_id=1, source_target_pairs={{0,1},{1,0},{2,3},{3,2},{4,5},{5,4},{6,7},{7,6},{8,9},{9,8},{10,11... | collective-permute-start | bytes 393224 | tf_op jit(solution)/shard_map/ppermute | solution.py:258
  18.4 6.8 %collective-permute-start.6 = (bf16[1,128,512]{2,1,0:T(8,128)(2,1)S(1)}, bf16[1,128,512]{2,1,0:T(8,128)(2,1)S(1)}, u32[]{:S(2)}, u32[]{:S(2)}) collective-permute-start(bf16[1,128,512]{2,1,0:T(8,128)(2,1)S(1)} %get-tuple-element.56), channel_id=1, source_target_pairs={{0,2},{1,3},{2,0},{3,1},{4,6},{5,7},{6,4},{7,5},{8,10},{9,11},{10,... | collective-permute-start | bytes 393224 | tf_op jit(solution)/shard_map/ppermute | solution.py:258
  25.2 1.5 %collective-permute-start.11 = (bf16[1,256,512]{2,1,0:T(8,128)(2,1)S(1)}, bf16[1,256,512]{2,1,0:T(8,128)(2,1)S(1)}, u32[]{:S(2)}, u32[]{:S(2)}) collective-permute-start(bf16[1,256,512]{2,1,0:T(8,128)(2,1)S(1)} %collective-permute-done.10.refs_2_), channel_id=1, source_target_pairs={{0,8},{8,0},{16,24},{24,16},{1,9},{9,1},{17,25},{25,17},{2,10},{10... | collective-permute-start | bytes 786440 | tf_op jit(solution)/shard_map/ppermute | solution.py:254
  27.3 8.2 %collective-permute-start.13 = (bf16[1,128,512]{2,1,0:T(8,128)(2,1)S(1)}, bf16[1,128,512]{2,1,0:T(8,128)(2,1)S(1)}, u32[]{:S(2)}, u32[]{:S(2)}) collective-permute-start(bf16[1,128,512]{2,1,0:T(8,128)(2,1)S(1)} %get-tuple-element.63), channel_id=1, source_target_pairs={{0,2},{1,3},{2,0},{3,1},{4,6},{5,7},{6,4},{7,5},{8,10},{9,11},{10,... | collective-permute-start | bytes 393224 | tf_op jit(solution)/shard_map/ppermute | solution.py:258
  27.9 10.3 %collective-permute-start.14 = (bf16[1,4,128,128]{3,2,1,0:T(8,128)(2,1)S(1)}, bf16[1,4,128,128]{3,2,1,0:T(8,128)(2,1)S(1)}, u32[]{:S(2)}, u32[]{:S(2)}) collective-permute-start(bf16[1,4,128,128]{3,2,1,0:T(8,128)(2,1)S(1)} %get-tuple-element.64), channel_id=1, source_target_pairs={{0,4},{1,5},{2,6},{3,7},{4,0},{5,1},{6,2},{7,3},{8,12},{9,13},{10,... | collective-permute-start | bytes 393224 | tf_op jit(solution)/shard_map/ppermute | solution.py:264
  31.1 6.7 %collective-permute-start.7 = (bf16[1,128,512]{2,1,0:T(8,128)(2,1)S(1)}, bf16[1,128,512]{2,1,0:T(8,128)(2,1)S(1)}, u32[]{:S(2)}, u32[]{:S(2)}) collective-permute-start(bf16[1,128,512]{2,1,0:T(8,128)(2,1)S(1)} %collective-permute-done.6.refs_2_), channel_id=1, source_target_pairs={{0,1},{1,0},{2,3},{3,2},{4,5},{5,4},{6,7},{7,6},{8,9},{9,8},{10,11... | collective-permute-start | bytes 393224 | tf_op jit(solution)/shard_map/ppermute | solution.py:258
  32.6 6.3 %collective-permute-start.12 = (bf16[1,128,512]{2,1,0:T(8,128)(2,1)S(1)}, bf16[1,128,512]{2,1,0:T(8,128)(2,1)S(1)}, u32[]{:S(2)}, u32[]{:S(2)}) collective-permute-start(bf16[1,128,512]{2,1,0:T(8,128)(2,1)S(1)} %get-tuple-element.62), channel_id=1, source_target_pairs={{0,1},{1,0},{2,3},{3,2},{4,5},{5,4},{6,7},{7,6},{8,9},{9,8},{10,11... | collective-permute-start | bytes 393224 | tf_op jit(solution)/shard_map/ppermute | solution.py:258
  33.7 24.4 %copy-start.5 = (bf16[1,1024,512]{2,1,0:T(8,128)(2,1)S(1)}, bf16[1,1024,512]{2,1,0:T(8,128)(2,1)}, u32[]{:S(2)}) copy-start(bf16[1,1024,512]{2,1,0:T(8,128)(2,1)} %rhs.1) | copy-start | bytes 3145732
  35.5 14.8 %collective-permute-start.19 = (bf16[2,128,512]{2,1,0:T(8,128)(2,1)S(1)}, bf16[2,128,512]{2,1,0:T(8,128)(2,1)S(1)}, u32[]{:S(2)}, u32[]{:S(2)}) collective-permute-start(bf16[2,128,512]{2,1,0:T(8,128)(2,1)S(1)} %get-tuple-element.73), channel_id=1, source_target_pairs={{0,2},{1,3},{2,0},{3,1},{4,6},{5,7},{6,4},{7,5},{8,10},{9,11},{10,... | collective-permute-start | bytes 786440 | tf_op jit(solution)/shard_map/ppermute | solution.py:258
  35.5 9.3 %collective-permute-start.17 = (bf16[1,4,128,128]{3,2,1,0:T(8,128)(2,1)S(1)}, bf16[1,4,128,128]{3,2,1,0:T(8,128)(2,1)S(1)}, u32[]{:S(2)}, u32[]{:S(2)}) collective-permute-start(bf16[1,4,128,128]{3,2,1,0:T(8,128)(2,1)S(1)} %get-tuple-element.70), channel_id=1, source_target_pairs={{0,4},{1,5},{2,6},{3,7},{4,0},{5,1},{6,2},{7,3},{8,12},{9,13},{10,... | collective-permute-start | bytes 393224 | tf_op jit(solution)/shard_map/ppermute | solution.py:264
  38.9 5.9 %collective-permute-start.15 = (bf16[1,128,512]{2,1,0:T(8,128)(2,1)S(1)}, bf16[1,128,512]{2,1,0:T(8,128)(2,1)S(1)}, u32[]{:S(2)}, u32[]{:S(2)}) collective-permute-start(bf16[1,128,512]{2,1,0:T(8,128)(2,1)S(1)} %collective-permute-done.13.refs_2_), channel_id=1, source_target_pairs={{0,1},{1,0},{2,3},{3,2},{4,5},{5,4},{6,7},{7,6},{8,9},{9,8},{10,11... | collective-permute-start | bytes 393224 | tf_op jit(solution)/shard_map/ppermute | solution.py:258
  40.4 10.0 %collective-permute-start.9 = (bf16[128,512]{1,0:T(8,128)(2,1)S(1)}, bf16[128,512]{1,0:T(8,128)(2,1)S(1)}, u32[]{:S(2)}, u32[]{:S(2)}) collective-permute-start(bf16[128,512]{1,0:T(8,128)(2,1)S(1)} %off_sums.2), channel_id=1, source_target_pairs={{0,4},{1,5},{2,6},{3,7},{4,0},{5,1},{6,2},{7,3},{8,12},{9,13},{10,... | collective-permute-start | bytes 393224 | tf_op jit(solution)/shard_map/ppermute | solution.py:264
  44.8 13.8 %collective-permute-start.18 = (bf16[2,128,512]{2,1,0:T(8,128)(2,1)S(1)}, bf16[2,128,512]{2,1,0:T(8,128)(2,1)S(1)}, u32[]{:S(2)}, u32[]{:S(2)}) collective-permute-start(bf16[2,128,512]{2,1,0:T(8,128)(2,1)S(1)} %get-tuple-element.71), channel_id=1, source_target_pairs={{0,1},{1,0},{2,3},{3,2},{4,5},{5,4},{6,7},{7,6},{8,9},{9,8},{10,11... | collective-permute-start | bytes 786440 | tf_op jit(solution)/shard_map/ppermute | solution.py:258
  50.3 8.2 %collective-permute-start.20 = (bf16[2,128,512]{2,1,0:T(8,128)(2,1)S(1)}, bf16[2,128,512]{2,1,0:T(8,128)(2,1)S(1)}, u32[]{:S(2)}, u32[]{:S(2)}) collective-permute-start(bf16[2,128,512]{2,1,0:T(8,128)(2,1)S(1)} %collective-permute-done.19.refs_2_), channel_id=1, source_target_pairs={{0,1},{1,0},{2,3},{3,2},{4,5},{5,4},{6,7},{7,6},{8,9},{9,8},{10,11... | collective-permute-start | bytes 786440 | tf_op jit(solution)/shard_map/ppermute | solution.py:258
  51.7 6.4 %collective-permute-start.16 = (bf16[128,512]{1,0:T(8,128)(2,1)S(1)}, bf16[128,512]{1,0:T(8,128)(2,1)S(1)}, u32[]{:S(2)}, u32[]{:S(2)}) collective-permute-start(bf16[128,512]{1,0:T(8,128)(2,1)S(1)} %off_sums.3), channel_id=1, source_target_pairs={{0,4},{1,5},{2,6},{3,7},{4,0},{5,1},{6,2},{7,3},{8,12},{9,13},{10,... | collective-permute-start | bytes 393224 | tf_op jit(solution)/shard_map/ppermute | solution.py:264
  60.8 6.6 %collective-permute-start.21 = (bf16[1,1,128,512]{3,2,1,0:T(8,128)(2,1)S(1)}, bf16[1,1,128,512]{3,2,1,0:T(8,128)(2,1)S(1)}, u32[]{:S(2)}, u32[]{:S(2)}) collective-permute-start(bf16[1,1,128,512]{3,2,1,0:T(8,128)(2,1)S(1)} %get-tuple-element.76), channel_id=1, source_target_pairs={{0,3},{1,2},{2,1},{3,0},{4,7},{5,6},{6,5},{7,4},{8,11},{9,10},{10,... | collective-permute-start | bytes 393224 | tf_op jit(solution)/shard_map/ppermute | solution.py:258
  62.2 6.9 %collective-permute-start.22 = (bf16[1,1,128,512]{3,2,1,0:T(8,128)(2,1)S(1)}, bf16[1,1,128,512]{3,2,1,0:T(8,128)(2,1)S(1)}, u32[]{:S(2)}, u32[]{:S(2)}) collective-permute-start(bf16[1,1,128,512]{3,2,1,0:T(8,128)(2,1)S(1)} %get-tuple-element.77), channel_id=1, source_target_pairs={{0,2},{1,3},{2,0},{3,1},{4,6},{5,7},{6,4},{7,5},{8,10},{9,11},{10,... | collective-permute-start | bytes 393224 | tf_op jit(solution)/shard_map/ppermute | solution.py:258
  63.7 5.5 %collective-permute-start.23 = (bf16[1,1,128,512]{3,2,1,0:T(8,128)(2,1)S(1)}, bf16[1,1,128,512]{3,2,1,0:T(8,128)(2,1)S(1)}, u32[]{:S(2)}, u32[]{:S(2)}) collective-permute-start(bf16[1,1,128,512]{3,2,1,0:T(8,128)(2,1)S(1)} %get-tuple-element.78), channel_id=1, source_target_pairs={{0,1},{1,0},{2,3},{3,2},{4,5},{5,4},{6,7},{7,6},{8,9},{9,8},{10,11... | collective-permute-start | bytes 393224 | tf_op jit(solution)/shard_map/ppermute | solution.py:258
  69.4 8.2 %collective-permute-start.25 = (bf16[1,128,512]{2,1,0:T(8,128)(2,1)S(1)}, bf16[1,128,512]{2,1,0:T(8,128)(2,1)S(1)}, u32[]{:S(2)}, u32[]{:S(2)}) collective-permute-start(bf16[1,128,512]{2,1,0:T(8,128)(2,1)S(1)} %get-tuple-element.81), channel_id=1, source_target_pairs={{0,3},{1,2},{2,1},{3,0},{4,7},{5,6},{6,5},{7,4},{8,11},{9,10},{10,... | collective-permute-start | bytes 393224 | tf_op jit(solution)/shard_map/ppermute | solution.py:258
  70.2 9.6 %collective-permute-start.26 = (bf16[1,128,512]{2,1,0:T(8,128)(2,1)S(1)}, bf16[1,128,512]{2,1,0:T(8,128)(2,1)S(1)}, u32[]{:S(2)}, u32[]{:S(2)}) collective-permute-start(bf16[1,128,512]{2,1,0:T(8,128)(2,1)S(1)} %get-tuple-element.83), channel_id=1, source_target_pairs={{0,2},{1,3},{2,0},{3,1},{4,6},{5,7},{6,4},{7,5},{8,10},{9,11},{10,... | collective-permute-start | bytes 393224 | tf_op jit(solution)/shard_map/ppermute | solution.py:258
  72.3 7.5 %collective-permute-start.27 = (bf16[1,128,512]{2,1,0:T(8,128)(2,1)S(1)}, bf16[1,128,512]{2,1,0:T(8,128)(2,1)S(1)}, u32[]{:S(2)}, u32[]{:S(2)}) collective-permute-start(bf16[1,128,512]{2,1,0:T(8,128)(2,1)S(1)} %get-tuple-element.85), channel_id=1, source_target_pairs={{0,1},{1,0},{2,3},{3,2},{4,5},{5,4},{6,7},{7,6},{8,9},{9,8},{10,11... | collective-permute-start | bytes 393224 | tf_op jit(solution)/shard_map/ppermute | solution.py:258
  72.9 8.3 %collective-permute-start.24 = (bf16[1,128,512]{2,1,0:T(8,128)(2,1)S(1)}, bf16[1,128,512]{2,1,0:T(8,128)(2,1)S(1)}, u32[]{:S(2)}, u32[]{:S(2)}) collective-permute-start(bf16[1,128,512]{2,1,0:T(8,128)(2,1)S(1)} %sums.1), channel_id=1, source_target_pairs={{0,4},{1,5},{2,6},{3,7},{4,0},{5,1},{6,2},{7,3},{8,12},{9,13},{10,... | collective-permute-start | bytes 393224 | tf_op jit(solution)/shard_map/ppermute | solution.py:264

commit v11 on v7

--- a/solution.py
+++ b/solution.py
@@ -162,12 +162,14 @@
 
 
 def off_sum_kernel(second_along, second_both, *refs):
-    got, thirds, outs = take(refs, 4, (len(refs) - 4) // 2, (len(refs) - 4) // 2)
+    offs = second_along.shape[0]
+    less = (len(refs) - 4) // (offs + 1)
+    got, thirds, outs = take(refs, 4, offs * less, less)
     radix = thirds[0].shape[1]
     _, member = place(radix)
-    for d, (third, out) in enumerate(zip(thirds, outs)):
-        for j in range(out.shape[0]):
-            mats = [third[j, jnp.bitwise_xor(member, i)] for i in range(radix)]
+    for d, out in enumerate(outs):
+        for j in range(offs):
+            mats = [thirds[j * less + d][0, jnp.bitwise_xor(member, i)] for i in range(radix)]
             slots = slots_of([ref[j, d] for ref in got], second_along, second_both, j, d + 1)
             out[j] = dot(jnp.concatenate(mats, axis=1), slots).astype(BF16)
 
@@ -266,11 +268,13 @@
         functools.partial(pick_kernel, radix, groups),
         "pick_third",
         0,
-        [((offs, radix, rank, rank), BF16)] * less + [((butterflies - offs, radix, rank, rank), BF16)] * less,
+        [((1, radix, rank, rank), BF16)] * (butterflies * less),
         third_level,
     )
-    thirds = [over_groups(a, d + 1) for d, a in enumerate(picked[:less])]
-    thirds_last = [over_groups(after(a, *thirds), d + 1) for d, a in enumerate(picked[less:])]
+    thirds = [
+        [over_groups(a, d + 1) for d, a in enumerate(picked[j * less : (j + 1) * less])]
+        for j in range(butterflies)
+    ]
 
     up_own, up_other, up_mid, off_rows, last_rows = call(
         functools.partial(weights_kernel, radix, groups, offs, row_size),
@@ -300,7 +304,7 @@
 
     pieces = [solved, over_row(solved, 1)]
     for mask in range(2, row_size, 2):
-        far = after(over_row(solved, mask), up_own, *thirds, *seconds)
+        far = after(over_row(solved, mask), up_own, *thirds[0], *seconds)
         pieces += [far, over_row(far, 1)]
 
     other_flops = 2 * columns * rank * radix * less * depth
@@ -329,7 +333,7 @@
     )
     along = over_members(along, ALONG)
     across = over_members(across, ACROSS)
-    both = over_members(after(along, across, *thirds_last), ACROSS)
+    both = over_members(after(along, across, *[a for t in thirds[:offs] for a in t]), ACROSS)
     own = call(own_kernel, "own_levels", offs * own_flops, own_out(offs)[:3], leaf, up_own, up_mid)
     own_along = over_members(after(own[2], along), ALONG)
     sums = call(
@@ -342,12 +346,12 @@
         across,
         along,
         both,
-        *thirds,
+        *[a for j in range(offs) for a in thirds[j]],
     )
     crossed = cross(sums)
     own = [
         own[0],
-        over_members(after(own[1], both), ACROSS),
+        over_members(after(own[1], both, *thirds[-1]), ACROSS),
         own_along,
     ]
     own.append(over_members(after(own_along, own[1], *sums), ACROSS))
@@ -375,7 +379,7 @@
         less * 2 * columns * rank * depth,
         [((1, rank, columns), BF16)] * less,
         *other,
-        *thirds_last,
+        *thirds[offs],
     )
     crossed = cross(sums)
     own = [over_members(after(a, *sums) if i else a, i) for i, a in enumerate(own)]

time: 80.7 us -> 77.4 us (0.959)
  waiting for transfers between devices: 39 us -> 32.1 us
  starting transfers between devices: 27.4 us -> 30.9 us
    ppermute x14, waiting for transfers between devices: 24.6 us -> 14.2 us  [over_members(): return array if mask == 0 else lax.ppermute(array, 'box', pairs)]
    ppermute x4 -> x5, starting transfers between devices: 8.59 us -> 12.1 us  [over_groups(): return lax.ppermute(array, 'box', pairs)]
    ppermute x4 -> x5, waiting for transfers between devices: 12.6 us -> 16 us  [over_groups(): return lax.ppermute(array, 'box', pairs)]
  transfers between devices with their start and end apart: 21 -> 22, of which waited for: 14 -> 13; matrix products, arithmetic and copies ran while one was open for 0% -> 0% of each run, Pallas kernels for 3% -> 3%
where the time goes in v11:
time: 77.4 us; the launch traced here: 76.9 us
  waiting for transfers between devices  32.1 us (41%)
  starting transfers between devices  30.9 us (40%)
  Pallas kernels  7.94 us (10%)
  local copies, waits for them, and re-layouts  5.83 us (8%)
    ppermute x5, waiting for transfers between devices, over_groups(): return lax.ppermute(array, 'box', pairs)  16 us
    ppermute x14, starting transfers between devices, over_members(): return array if mask == 0 else lax.ppermute(array, 'box', pairs)  15.9 us
    ppermute x14, waiting for transfers between devices, over_members(): return array if mask == 0 else lax.ppermute(array, 'box', pairs)  14.2 us
    ppermute x5, starting transfers between devices, over_groups(): return lax.ppermute(array, 'box', pairs)  12.1 us
    pallas_call x9, Pallas kernels, call(): pl.pallas_call(kernel, out_shape=outs, in_specs=[VMEM] * len(args), out_s...  7.94 us
    unnamed x20, local copies, waits for them, and re-layouts  5.83 us
    ppermute x3, starting transfers between devices, over_row(): return lax.ppermute(array, 'row', [(r, r ^ mask) for r in range(row_size)])  2.97 us
    ppermute x3, waiting for transfers between devices, over_row(): return lax.ppermute(array, 'row', [(r, r ^ mask) for r in range(row_size)])  1.91 us
  transfers between devices with their start and end apart: 22, of which 13 were waited for; matrix products, arithmetic and copies ran while one was open for 0% of the time, Pallas kernels for 3%

profile of v11, /device:TPU:0, one launch (start us, length us, event | category | flops | bytes accessed | tf_op | source)
XLA Modules:
  0.0 76.9 jit_solution(14339951104837469919)
XLA Ops:
  0.0 3.0 %collective-permute-start.3 = (bf16[2,256,512]{2,1,0:T(8,128)(2,1)}, bf16[2,256,512]{2,1,0:T(8,128)(2,1)S(1)}, u32[]{:S(2)}, u32[]{:S(2)}) collective-permute-start(bf16[2,256,512]{2,1,0:T(8,128)(2,1)} %refs_0_.1), channel_id=1, source_target_pairs={{0,16},{8,24},{16,0},{24,8},{1,17},{9,25},{17,1},{25,9},{2,18},{10... | collective-permute-start | bytes 1572872 | tf_op jit(solution)/shard_map/ppermute | solution.py:242
  3.0 1.1 %copy-done.3 = bf16[1,3,1,8,128,128]{5,4,3,2,1,0:T(8,128)(2,1)S(1)} copy-done((bf16[1,3,1,8,128,128]{5,4,3,2,1,0:T(8,128)(2,1)S(1)}, bf16[1,3,1,8,128,128]{5,4,3,2,1,0:T(8,128)(2,1)}, u32[]{:S(2)}) %copy-start.3) | copy-done | bytes 786456
  4.1 1.6 %collective-permute-start = (bf16[2,2,128,128]{3,2,1,0:T(8,128)(2,1)S(1)}, bf16[2,2,128,128]{3,2,1,0:T(8,128)(2,1)S(1)}, u32[]{:S(2)}, u32[]{:S(2)}) collective-permute-start(bf16[2,2,128,128]{3,2,1,0:T(8,128)(2,1)S(1)} %get-tuple-element.43), channel_id=1, source_target_pairs={{0,2},{1,3},{2,0},{3,1},{4,6},{5,7},{6,4},{7,5},{8,10},{9,11},{10,... | collective-permute-start | bytes 393224 | tf_op jit(solution)/shard_map/ppermute | solution.py:246
  5.8 1.4 %collective-permute-start.1 = (bf16[2,2,128,128]{3,2,1,0:T(8,128)(2,1)S(1)}, bf16[2,2,128,128]{3,2,1,0:T(8,128)(2,1)S(1)}, u32[]{:S(2)}, u32[]{:S(2)}) collective-permute-start(bf16[2,2,128,128]{3,2,1,0:T(8,128)(2,1)S(1)} %get-tuple-element.44), channel_id=1, source_target_pairs={{0,3},{1,2},{2,1},{3,0},{4,7},{5,6},{6,5},{7,4},{8,11},{9,10},{10,... | collective-permute-start | bytes 393224 | tf_op jit(solution)/shard_map/ppermute | solution.py:246
  7.1 1.1 %copy-done = bf16[1,3,1,8,128,128]{5,4,3,2,1,0:T(8,128)(2,1)S(1)} copy-done((bf16[1,3,1,8,128,128]{5,4,3,2,1,0:T(8,128)(2,1)S(1)}, bf16[1,3,1,8,128,128]{5,4,3,2,1,0:T(8,128)(2,1)}, u32[]{:S(2)}) %copy-start) | copy-done | bytes 786456
  8.3 0.0 copy-start.2
  8.3 2.7 %collective-permute-start.4 = (bf16[1,4,128,128]{3,2,1,0:T(8,128)(2,1)S(1)}, bf16[1,4,128,128]{3,2,1,0:T(8,128)(2,1)S(1)}, u32[]{:S(2)}, u32[]{:S(2)}) collective-permute-start(bf16[1,4,128,128]{3,2,1,0:T(8,128)(2,1)S(1)} %get-tuple-element.46), channel_id=1, source_target_pairs={{0,4},{1,5},{2,6},{3,7},{4,0},{5,1},{6,2},{7,3},{8,12},{9,13},{10,... | collective-permute-start | bytes 393224 | tf_op jit(solution)/shard_map/ppermute | solution.py:252
  11.0 0.0 collective-permute-start.2
  11.0 0.0 copy-done.4
  11.0 1.4 %copy-done.5 = bf16[1,3,1,4,4,128,128]{6,5,4,3,2,1,0:T(8,128)(2,1)S(1)} copy-done((bf16[1,3,1,4,4,128,128]{6,5,4,3,2,1,0:T(8,128)(2,1)S(1)}, bf16[1,3,1,4,4,128,128]{6,5,4,3,2,1,0:T(8,128)(2,1)}, u32[]{:S(2)}) %copy-start.5) | copy-done | bytes 1572888
  12.4 1.1 %copy-done.7 = bf16[1,3,2,512,128]{4,3,2,1,0:T(8,128)(2,1)S(1)} copy-done((bf16[1,3,2,512,128]{4,3,2,1,0:T(8,128)(2,1)S(1)}, bf16[1,3,2,512,128]{4,3,2,1,0:T(8,128)(2,1)}, u32[]{:S(2)}) %copy-start.7) | copy-done | bytes 786456
  13.5 1.0 %copy-done.9 = bf16[1,3,1,2,2,128,128]{6,5,4,3,2,1,0:T(8,128)(2,1)S(1)} copy-done((bf16[1,3,1,2,2,128,128]{6,5,4,3,2,1,0:T(8,128)(2,1)S(1)}, bf16[1,3,1,2,2,128,128]{6,5,4,3,2,1,0:T(8,128)(2,1)}, u32[]{:S(2)}) %copy-start.9) | copy-done | bytes 393240
  14.5 1.4 %weights.1 = (bf16[3,4,128,512]{3,2,1,0:T(8,128)(2,1)S(1)}, bf16[3,4,1,128,512]{4,3,2,1,0:T(8,128)(2,1)S(1)}, bf16[2,2,128,512]{3,2,1,0:T(8,128)(2,1)S(1)}, bf16...) custom-call(bf16[1,3,1,4,4,128,128]{6,5,4,3,2,1,0:T(8,128)(2,1)S(1)} %copy-done.5, ...), custom_call_target="tpu_custom_call" | custom-call | flops 603979776 | tf_op jit(solution)/shard_map/weights/pallas_call | solution.py:257
  15.9 0.0 collective-permute-done.second_along
  15.9 0.0 collective-permute-done.1.second_both
  15.9 1.1 %collective-permute-done.4.refs_4_ = bf16[1,4,128,128]{3,2,1,0:T(8,128)(2,1)S(1)} collective-permute-done((bf16[1,4,128,128]{3,2,1,0:T(8,128)(2,1)S(1)}, bf16[1,4,128,128]{3,2,1,0:T(8,128)(2,1)S(1)}, u32[]{:S(2)}, u32[]{:S(2)}) %collective-permute-start.4) | collective-permute-done | bytes 131104 | tf_op jit(solution)/shard_map/ppermute | solution.py:252
  17.1 0.0 collective-permute-done.3.refs_2_
  17.1 0.0 collective-permute-start.5
  17.1 0.0 collective-permute-done.2.refs_1_
  17.1 1.9 %collective-permute-done.5.refs_3_ = bf16[2,256,512]{2,1,0:T(8,128)(2,1)S(1)} collective-permute-done((bf16[2,256,512]{2,1,0:T(8,128)(2,1)S(1)}, bf16[2,256,512]{2,1,0:T(8,128)(2,1)S(1)}, u32[]{:S(2)}, u32[]{:S(2)}) %collective-permute-start.5) | collective-permute-done | bytes 524320 | tf_op jit(solution)/shard_map/ppermute | solution.py:242
  19.0 0.0 copy-done.2
  19.0 0.0 copy-done.8
  19.0 1.0 %off_levels.1 = (bf16[2,512,512]{2,1,0:T(8,128)(2,1)S(1)}, bf16[2,1,128,512]{3,2,1,0:T(8,128)(2,1)S(1)}, bf16[2,1,128,512]{3,2,1,0:T(8,128)(2,1)S(1)}, bf16[2,1,128,512]{3,2,1,0:T(8,128)(2,1)S(1)}) custom-call(bf16[1,3,4,256,128]{4,3,2,1,0:T(8,128)(2,1)S(1)} %copy-done.2, bf16[3,4,1,128,512]{4,3,2,1,0:T(8,128)(2,1)S(1)} %get-tuple-element.42.up_other, ...), custom_call_target="tpu_custom_call" | custom-call | flops 805306368 | tf_op jit(solution)/shard_map/off_levels/pallas_call | solution.py:257
  20.0 0.1 collective-permute-start.6
  20.1 1.8 %collective-permute-start.7 = (bf16[2,1,128,512]{3,2,1,0:T(8,128)(2,1)S(1)}, bf16[2,1,128,512]{3,2,1,0:T(8,128)(2,1)S(1)}, u32[]{:S(2)}, u32[]{:S(2)}) collective-permute-start(bf16[2,1,128,512]{3,2,1,0:T(8,128)(2,1)S(1)} %get-tuple-element.50), channel_id=1, source_target_pairs={{0,2},{1,3},{2,0},{3,1},{4,6},{5,7},{6,4},{7,5},{8,10},{9,11},{10,... | collective-permute-start | bytes 786440 | tf_op jit(solution)/shard_map/ppermute | solution.py:246
  21.9 2.3 %collective-permute-start.8 = (bf16[1,4,128,128]{3,2,1,0:T(8,128)(2,1)S(1)}, bf16[1,4,128,128]{3,2,1,0:T(8,128)(2,1)S(1)}, u32[]{:S(2)}, u32[]{:S(2)}) collective-permute-start(bf16[1,4,128,128]{3,2,1,0:T(8,128)(2,1)S(1)} %get-tuple-element.51), channel_id=1, source_target_pairs={{0,4},{1,5},{2,6},{3,7},{4,0},{5,1},{6,2},{7,3},{8,12},{9,13},{10,... | collective-permute-start | bytes 393224 | tf_op jit(solution)/shard_map/ppermute | solution.py:252
  24.2 6.1 %collective-permute-done.8.refs_5_ = bf16[1,4,128,128]{3,2,1,0:T(8,128)(2,1)S(1)} collective-permute-done((bf16[1,4,128,128]{3,2,1,0:T(8,128)(2,1)S(1)}, bf16[1,4,128,128]{3,2,1,0:T(8,128)(2,1)S(1)}, u32[]{:S(2)}, u32[]{:S(2)}) %collective-permute-start.8) | collective-permute-done | bytes 131104 | tf_op jit(solution)/shard_map/ppermute | solution.py:252
  30.3 0.0 collective-permute-done.6.refs_1_
  30.3 1.0 %collective-permute-done.7.refs_2_ = bf16[2,1,128,512]{3,2,1,0:T(8,128)(2,1)S(1)} collective-permute-done((bf16[2,1,128,512]{3,2,1,0:T(8,128)(2,1)S(1)}, bf16[2,1,128,512]{3,2,1,0:T(8,128)(2,1)S(1)}, u32[]{:S(2)}, u32[]{:S(2)}) %collective-permute-start.7) | collective-permute-done | bytes 262176 | tf_op jit(solution)/shard_map/ppermute | solution.py:246
  31.3 1.7 %collective-permute-start.9 = (bf16[2,1,128,512]{3,2,1,0:T(8,128)(2,1)S(1)}, bf16[2,1,128,512]{3,2,1,0:T(8,128)(2,1)S(1)}, u32[]{:S(2)}, u32[]{:S(2)}) collective-permute-start(bf16[2,1,128,512]{3,2,1,0:T(8,128)(2,1)S(1)} %collective-permute-done.7.refs_2_), channel_id=1, source_target_pairs={{0,1},{1,0},{2,3},{3,2},{4,5},{5,4},{6,7},{7,6},{8,9},{9,8},{10,11... | collective-permute-start | bytes 786440 | tf_op jit(solution)/shard_map/ppermute | solution.py:246
  33.0 1.8 %collective-permute-start.11 = (bf16[1,4,128,128]{3,2,1,0:T(8,128)(2,1)S(1)}, bf16[1,4,128,128]{3,2,1,0:T(8,128)(2,1)S(1)}, u32[]{:S(2)}, u32[]{:S(2)}) collective-permute-start(bf16[1,4,128,128]{3,2,1,0:T(8,128)(2,1)S(1)} %get-tuple-element.56), channel_id=1, source_target_pairs={{0,4},{1,5},{2,6},{3,7},{4,0},{5,1},{6,2},{7,3},{8,12},{9,13},{10,... | collective-permute-start | bytes 393224 | tf_op jit(solution)/shard_map/ppermute | solution.py:252
  34.8 0.6 own_levels.1
  35.4 0.0 copy-start.1
  35.4 0.0 copy-start.6
  35.4 1.8 %collective-permute-start.13 = (bf16[2,128,512]{2,1,0:T(8,128)(2,1)S(1)}, bf16[2,128,512]{2,1,0:T(8,128)(2,1)S(1)}, u32[]{:S(2)}, u32[]{:S(2)}) collective-permute-start(bf16[2,128,512]{2,1,0:T(8,128)(2,1)S(1)} %get-tuple-element.59), channel_id=1, source_target_pairs={{0,2},{1,3},{2,0},{3,1},{4,6},{5,7},{6,4},{7,5},{8,10},{9,11},{10,... | collective-permute-start | bytes 786440 | tf_op jit(solution)/shard_map/ppermute | solution.py:246
  37.2 3.2 %collective-permute-done.11.refs_4_ = bf16[1,4,128,128]{3,2,1,0:T(8,128)(2,1)S(1)} collective-permute-done((bf16[1,4,128,128]{3,2,1,0:T(8,128)(2,1)S(1)}, bf16[1,4,128,128]{3,2,1,0:T(8,128)(2,1)S(1)}, u32[]{:S(2)}, u32[]{:S(2)}) %collective-permute-start.11) | collective-permute-done | bytes 131104 | tf_op jit(solution)/shard_map/ppermute | solution.py:252
  40.4 0.0 collective-permute-done.9.refs_3_
  40.4 0.4 collective-permute-start.12
  40.8 0.6 off_sums.1
  41.4 2.2 %collective-permute-start.10 = (bf16[2,128,512]{2,1,0:T(8,128)(2,1)S(1)}, bf16[2,128,512]{2,1,0:T(8,128)(2,1)S(1)}, u32[]{:S(2)}, u32[]{:S(2)}) collective-permute-start(bf16[2,128,512]{2,1,0:T(8,128)(2,1)S(1)} %off_sums.1), channel_id=1, source_target_pairs={{0,4},{1,5},{2,6},{3,7},{4,0},{5,1},{6,2},{7,3},{8,12},{9,13},{10,... | collective-permute-start | bytes 786440 | tf_op jit(solution)/shard_map/ppermute | solution.py:252
  43.6 2.9 %collective-permute-done.13.refs_3_ = bf16[2,128,512]{2,1,0:T(8,128)(2,1)S(1)} collective-permute-done((bf16[2,128,512]{2,1,0:T(8,128)(2,1)S(1)}, bf16[2,128,512]{2,1,0:T(8,128)(2,1)S(1)}, u32[]{:S(2)}, u32[]{:S(2)}) %collective-permute-start.13) | collective-permute-done | bytes 262176 | tf_op jit(solution)/shard_map/ppermute | solution.py:246
  46.5 1.6 %collective-permute-done.12.refs_2_ = bf16[2,128,512]{2,1,0:T(8,128)(2,1)S(1)} collective-permute-done((bf16[2,128,512]{2,1,0:T(8,128)(2,1)S(1)}, bf16[2,128,512]{2,1,0:T(8,128)(2,1)S(1)}, u32[]{:S(2)}, u32[]{:S(2)}) %collective-permute-start.12) | collective-permute-done | bytes 262176 | tf_op jit(solution)/shard_map/ppermute | solution.py:246
  48.2 0.0 collective-permute-start.14
  48.2 5.6 %collective-permute-done.10.refs_0_ = bf16[2,128,512]{2,1,0:T(8,128)(2,1)S(1)} collective-permute-done((bf16[2,128,512]{2,1,0:T(8,128)(2,1)S(1)}, bf16[2,128,512]{2,1,0:T(8,128)(2,1)S(1)}, u32[]{:S(2)}, u32[]{:S(2)}) %collective-permute-start.10) | collective-permute-done | bytes 262176 | tf_op jit(solution)/shard_map/ppermute | solution.py:252
  53.8 0.8 collective-permute-done.14.refs_4_
  54.5 0.0 copy-done.1
  54.5 0.0 copy-done.6
  54.5 2.5 %middle_levels.1 = (f32[1024,512]{1,0:T(8,128)S(1)}, bf16[1,128,512]{2,1,0:T(8,128)(2,1)S(1)}, bf16[1,128,512]{2,1,0:T(8,128)(2,1)S(1)}, bf16[1,128,512]{2,1,0:T...) custom-call(bf16[1,3,1,8,128,128]{5,4,3,2,1,0:T(8,128)(2,1)S(1)} %co, ...), custom_call_target="tpu_custom_call" | custom-call | flops 1342177280 | tf_op jit(solution)/shard_map/middle_levels/pallas_call | solution.py:257
  57.0 0.8 %collective-permute-start.15 = (bf16[1,1,128,512]{3,2,1,0:T(8,128)(2,1)S(1)}, bf16[1,1,128,512]{3,2,1,0:T(8,128)(2,1)S(1)}, u32[]{:S(2)}, u32[]{:S(2)}) collective-permute-start(bf16[1,1,128,512]{3,2,1,0:T(8,128)(2,1)S(1)} %get-tuple-element.62), channel_id=1, source_target_pairs={{0,3},{1,2},{2,1},{3,0},{4,7},{5,6},{6,5},{7,4},{8,11},{9,10},{10,... | collective-permute-start | bytes 393224 | tf_op jit(solution)/shard_map/ppermute | solution.py:246
  57.9 0.8 %collective-permute-start.16 = (bf16[1,1,128,512]{3,2,1,0:T(8,128)(2,1)S(1)}, bf16[1,1,128,512]{3,2,1,0:T(8,128)(2,1)S(1)}, u32[]{:S(2)}, u32[]{:S(2)}) collective-permute-start(bf16[1,1,128,512]{3,2,1,0:T(8,128)(2,1)S(1)} %get-tuple-element.63), channel_id=1, source_target_pairs={{0,2},{1,3},{2,0},{3,1},{4,6},{5,7},{6,4},{7,5},{8,10},{9,11},{10,... | collective-permute-start | bytes 393224 | tf_op jit(solution)/shard_map/ppermute | solution.py:246
  58.7 1.9 %collective-permute-start.17 = (bf16[1,1,128,512]{3,2,1,0:T(8,128)(2,1)S(1)}, bf16[1,1,128,512]{3,2,1,0:T(8,128)(2,1)S(1)}, u32[]{:S(2)}, u32[]{:S(2)}) collective-permute-start(bf16[1,1,128,512]{3,2,1,0:T(8,128)(2,1)S(1)} %get-tuple-element.64), channel_id=1, source_target_pairs={{0,1},{1,0},{2,3},{3,2},{4,5},{5,4},{6,7},{7,6},{8,9},{9,8},{10,11... | collective-permute-start | bytes 393224 | tf_op jit(solution)/shard_map/ppermute | solution.py:246
  60.6 2.4 %collective-permute-done.15.refs_0_ = bf16[1,1,128,512]{3,2,1,0:T(8,128)(2,1)S(1)} collective-permute-done((bf16[1,1,128,512]{3,2,1,0:T(8,128)(2,1)S(1)}, bf16[1,1,128,512]{3,2,1,0:T(8,128)(2,1)S(1)}, u32[]{:S(2)}, u32[]{:S(2)}) %collective-permute-start.15) | collective-permute-done | bytes 131104 | tf_op jit(solution)/shard_map/ppermute | solution.py:246
  63.0 1.0 %collective-permute-done.16.refs_1_ = bf16[1,1,128,512]{3,2,1,0:T(8,128)(2,1)S(1)} collective-permute-done((bf16[1,1,128,512]{3,2,1,0:T(8,128)(2,1)S(1)}, bf16[1,1,128,512]{3,2,1,0:T(8,128)(2,1)S(1)}, u32[]{:S(2)}, u32[]{:S(2)}) %collective-permute-start.16) | collective-permute-done | bytes 131104 | tf_op jit(solution)/shard_map/ppermute | solution.py:246
  64.1 0.3 collective-permute-done.17.refs_2_
  64.3 0.2 sums.1
  64.6 2.4 %collective-permute-start.19 = (bf16[1,128,512]{2,1,0:T(8,128)(2,1)S(1)}, bf16[1,128,512]{2,1,0:T(8,128)(2,1)S(1)}, u32[]{:S(2)}, u32[]{:S(2)}) collective-permute-start(bf16[1,128,512]{2,1,0:T(8,128)(2,1)S(1)} %get-tuple-element.67), channel_id=1, source_target_pairs={{0,3},{1,2},{2,1},{3,0},{4,7},{5,6},{6,5},{7,4},{8,11},{9,10},{10,... | collective-permute-start | bytes 393224 | tf_op jit(solution)/shard_map/ppermute | solution.py:246
  66.9 0.4 collective-permute-start.20
  67.3 0.8 %collective-permute-start.21 = (bf16[1,128,512]{2,1,0:T(8,128)(2,1)S(1)}, bf16[1,128,512]{2,1,0:T(8,128)(2,1)S(1)}, u32[]{:S(2)}, u32[]{:S(2)}) collective-permute-start(bf16[1,128,512]{2,1,0:T(8,128)(2,1)S(1)} %get-tuple-element.71), channel_id=1, source_target_pairs={{0,1},{1,0},{2,3},{3,2},{4,5},{5,4},{6,7},{7,6},{8,9},{9,8},{10,11... | collective-permute-start | bytes 393224 | tf_op jit(solution)/shard_map/ppermute | solution.py:246
  68.1 3.0 %collective-permute-start.18 = (bf16[1,128,512]{2,1,0:T(8,128)(2,1)S(1)}, bf16[1,128,512]{2,1,0:T(8,128)(2,1)S(1)}, u32[]{:S(2)}, u32[]{:S(2)}) collective-permute-start(bf16[1,128,512]{2,1,0:T(8,128)(2,1)S(1)} %sums.1), channel_id=1, source_target_pairs={{0,4},{1,5},{2,6},{3,7},{4,0},{5,1},{6,2},{7,3},{8,12},{9,13},{10,... | collective-permute-start | bytes 393224 | tf_op jit(solution)/shard_map/ppermute | solution.py:252
  71.2 0.0 collective-permute-done.19.refs_1_
  71.2 4.1 %collective-permute-done.20.refs_2_ = bf16[1,128,512]{2,1,0:T(8,128)(2,1)S(1)} collective-permute-done((bf16[1,128,512]{2,1,0:T(8,128)(2,1)S(1)}, bf16[1,128,512]{2,1,0:T(8,128)(2,1)S(1)}, u32[]{:S(2)}, u32[]{:S(2)}) %collective-permute-start.20) | collective-permute-done | bytes 131104 | tf_op jit(solution)/shard_map/ppermute | solution.py:246
  75.3 0.0 collective-permute-done.21.refs_3_
  75.3 0.0 collective-permute-done.18.refs_0_
  75.3 1.6 %last_levels.1 = bf16[1,1024,512]{2,1,0:T(8,128)(2,1)} custom-call(bf16[1,3,1,8,128,128]{5,4,3,2,1,0:T(8,128)(2,1)S(1)} %copy-done.1, bf16[1024,256]{1,0:T(8,128)(2,1)S(1)} %get-tuple-element.39.row_mats, f32[1024,512]{1,0:T(8,128)S(1)} %get-tuple-element.61.residual, bf16[1,128,512]{2,1,0:T(8,128)(2,1)S(1)} %collective-permute-done.18.refs_0_, ...), custom_call_target="tpu_custom_call" | custom-call | flops 335544320 | tf_op jit(solution)/shard_map/last_levels/pallas_call | solution.py:257
  (9 shorter events, 0.1 us)
Async XLA Ops:
  0.0 17.1 %collective-permute-start.3 = (bf16[2,256,512]{2,1,0:T(8,128)(2,1)}, bf16[2,256,512]{2,1,0:T(8,128)(2,1)S(1)}, u32[]{:S(2)}, u32[]{:S(2)}) collective-permute-start(bf16[2,256,512]{2,1,0:T(8,128)(2,1)} %refs_0_.1), channel_id=1, source_target_pairs={{0,16},{8,24},{16,0},{24,8},{1,17},{9,25},{17,1},{25,9},{2,18},{10... | collective-permute-start | bytes 1572872 | tf_op jit(solution)/shard_map/ppermute | solution.py:242
  3.0 1.1 %copy-start.3 = (bf16[1,3,1,8,128,128]{5,4,3,2,1,0:T(8,128)(2,1)S(1)}, bf16[1,3,1,8,128,128]{5,4,3,2,1,0:T(8,128)(2,1)}, u32[]{:S(2)}) copy-start(bf16[1,3,1,8,128,128]{5,4,3,2,1,0:T(8,128)(2,1)} %second.3) | copy-start | bytes 2359300
  4.1 6.9 %copy-start.4 = (bf16[1,3,1,8,128,128]{5,4,3,2,1,0:T(8,128)(2,1)S(1)}, bf16[1,3,1,8,128,128]{5,4,3,2,1,0:T(8,128)(2,1)}, u32[]{:S(2)}) copy-start(bf16[1,3,1,8,128,128]{5,4,3,2,1,0:T(8,128)(2,1)} %second.3) | copy-start | bytes 2359300
  4.1 11.8 %collective-permute-start = (bf16[2,2,128,128]{3,2,1,0:T(8,128)(2,1)S(1)}, bf16[2,2,128,128]{3,2,1,0:T(8,128)(2,1)S(1)}, u32[]{:S(2)}, u32[]{:S(2)}) collective-permute-start(bf16[2,2,128,128]{3,2,1,0:T(8,128)(2,1)S(1)} %get-tuple-element.43), channel_id=1, source_target_pairs={{0,2},{1,3},{2,0},{3,1},{4,6},{5,7},{6,4},{7,5},{8,10},{9,11},{10,... | collective-permute-start | bytes 393224 | tf_op jit(solution)/shard_map/ppermute | solution.py:246
  5.8 10.2 %collective-permute-start.1 = (bf16[2,2,128,128]{3,2,1,0:T(8,128)(2,1)S(1)}, bf16[2,2,128,128]{3,2,1,0:T(8,128)(2,1)S(1)}, u32[]{:S(2)}, u32[]{:S(2)}) collective-permute-start(bf16[2,2,128,128]{3,2,1,0:T(8,128)(2,1)S(1)} %get-tuple-element.44), channel_id=1, source_target_pairs={{0,3},{1,2},{2,1},{3,0},{4,7},{5,6},{6,5},{7,4},{8,11},{9,10},{10,... | collective-permute-start | bytes 393224 | tf_op jit(solution)/shard_map/ppermute | solution.py:246
  7.1 1.1 %copy-start = (bf16[1,3,1,8,128,128]{5,4,3,2,1,0:T(8,128)(2,1)S(1)}, bf16[1,3,1,8,128,128]{5,4,3,2,1,0:T(8,128)(2,1)}, u32[]{:S(2)}) copy-start(bf16[1,3,1,8,128,128]{5,4,3,2,1,0:T(8,128)(2,1)} %third.5) | copy-start | bytes 2359300
  8.3 10.7 %copy-start.2 = (bf16[1,3,4,256,128]{4,3,2,1,0:T(8,128)(2,1)S(1)}, bf16[1,3,4,256,128]{4,3,2,1,0:T(8,128)(2,1)}, u32[]{:S(2)}) copy-start(bf16[1,3,4,256,128]{4,3,2,1,0:T(8,128)(2,1)} %basis.3) | copy-start | bytes 2359300
  8.3 8.7 %collective-permute-start.4 = (bf16[1,4,128,128]{3,2,1,0:T(8,128)(2,1)S(1)}, bf16[1,4,128,128]{3,2,1,0:T(8,128)(2,1)S(1)}, u32[]{:S(2)}, u32[]{:S(2)}) collective-permute-start(bf16[1,4,128,128]{3,2,1,0:T(8,128)(2,1)S(1)} %get-tuple-element.46), channel_id=1, source_target_pairs={{0,4},{1,5},{2,6},{3,7},{4,0},{5,1},{6,2},{7,3},{8,12},{9,13},{10,... | collective-permute-start | bytes 393224 | tf_op jit(solution)/shard_map/ppermute | solution.py:252
  11.0 6.1 %collective-permute-start.2 = (bf16[2,256,512]{2,1,0:T(8,128)(2,1)}, bf16[2,256,512]{2,1,0:T(8,128)(2,1)S(1)}, u32[]{:S(2)}, u32[]{:S(2)}) collective-permute-start(bf16[2,256,512]{2,1,0:T(8,128)(2,1)} %refs_0_.1), channel_id=1, source_target_pairs={{0,8},{8,0},{16,24},{24,16},{1,9},{9,1},{17,25},{25,17},{2,10},{10... | collective-permute-start | bytes 1572872 | tf_op jit(solution)/shard_map/ppermute | solution.py:242
  11.0 1.4 %copy-start.5 = (bf16[1,3,1,4,4,128,128]{6,5,4,3,2,1,0:T(8,128)(2,1)S(1)}, bf16[1,3,1,4,4,128,128]{6,5,4,3,2,1,0:T(8,128)(2,1)}, u32[]{:S(2)}) copy-start(bf16[1,3,1,4,4,128,128]{6,5,4,3,2,1,0:T(8,128)(2,1)} %first.1) | copy-start | bytes 4718596
  12.4 1.1 %copy-start.7 = (bf16[1,3,2,512,128]{4,3,2,1,0:T(8,128)(2,1)S(1)}, bf16[1,3,2,512,128]{4,3,2,1,0:T(8,128)(2,1)}, u32[]{:S(2)}) copy-start(bf16[1,3,2,512,128]{4,3,2,1,0:T(8,128)(2,1)} %out_basis.1) | copy-start | bytes 2359300
  13.5 1.0 %copy-start.9 = (bf16[1,3,1,2,2,128,128]{6,5,4,3,2,1,0:T(8,128)(2,1)S(1)}, bf16[1,3,1,2,2,128,128]{6,5,4,3,2,1,0:T(8,128)(2,1)}, u32[]{:S(2)}) copy-start(bf16[1,3,1,2,2,128,128]{6,5,4,3,2,1,0:T(8,128)(2,1)} %fourth.1) | copy-start | bytes 1179652
  14.5 4.5 %copy-start.8 = (bf16[2,256,512]{2,1,0:T(8,128)(2,1)S(1)}, bf16[2,256,512]{2,1,0:T(8,128)(2,1)}, u32[]{:S(2)}) copy-start(bf16[2,256,512]{2,1,0:T(8,128)(2,1)} %refs_0_.1) | copy-start | bytes 1572868
  17.1 1.9 %collective-permute-start.5 = (bf16[2,256,512]{2,1,0:T(8,128)(2,1)S(1)}, bf16[2,256,512]{2,1,0:T(8,128)(2,1)S(1)}, u32[]{:S(2)}, u32[]{:S(2)}) collective-permute-start(bf16[2,256,512]{2,1,0:T(8,128)(2,1)S(1)} %collective-permute-done.3.refs_2_), channel_id=1, source_target_pairs={{0,8},{8,0},{16,24},{24,16},{1,9},{9,1},{17,25},{25,17},{2,10},{10... | collective-permute-start | bytes 1572872 | tf_op jit(solution)/shard_map/ppermute | solution.py:242
  20.0 10.3 %collective-permute-start.6 = (bf16[2,1,128,512]{3,2,1,0:T(8,128)(2,1)S(1)}, bf16[2,1,128,512]{3,2,1,0:T(8,128)(2,1)S(1)}, u32[]{:S(2)}, u32[]{:S(2)}) collective-permute-start(bf16[2,1,128,512]{3,2,1,0:T(8,128)(2,1)S(1)} %get-tuple-element.49), channel_id=1, source_target_pairs={{0,1},{1,0},{2,3},{3,2},{4,5},{5,4},{6,7},{7,6},{8,9},{9,8},{10,11... | collective-permute-start | bytes 786440 | tf_op jit(solution)/shard_map/ppermute | solution.py:246
  20.1 11.2 %collective-permute-start.7 = (bf16[2,1,128,512]{3,2,1,0:T(8,128)(2,1)S(1)}, bf16[2,1,128,512]{3,2,1,0:T(8,128)(2,1)S(1)}, u32[]{:S(2)}, u32[]{:S(2)}) collective-permute-start(bf16[2,1,128,512]{3,2,1,0:T(8,128)(2,1)S(1)} %get-tuple-element.50), channel_id=1, source_target_pairs={{0,2},{1,3},{2,0},{3,1},{4,6},{5,7},{6,4},{7,5},{8,10},{9,11},{10,... | collective-permute-start | bytes 786440 | tf_op jit(solution)/shard_map/ppermute | solution.py:246
  21.9 8.4 %collective-permute-start.8 = (bf16[1,4,128,128]{3,2,1,0:T(8,128)(2,1)S(1)}, bf16[1,4,128,128]{3,2,1,0:T(8,128)(2,1)S(1)}, u32[]{:S(2)}, u32[]{:S(2)}) collective-permute-start(bf16[1,4,128,128]{3,2,1,0:T(8,128)(2,1)S(1)} %get-tuple-element.51), channel_id=1, source_target_pairs={{0,4},{1,5},{2,6},{3,7},{4,0},{5,1},{6,2},{7,3},{8,12},{9,13},{10,... | collective-permute-start | bytes 393224 | tf_op jit(solution)/shard_map/ppermute | solution.py:252
  31.3 9.1 %collective-permute-start.9 = (bf16[2,1,128,512]{3,2,1,0:T(8,128)(2,1)S(1)}, bf16[2,1,128,512]{3,2,1,0:T(8,128)(2,1)S(1)}, u32[]{:S(2)}, u32[]{:S(2)}) collective-permute-start(bf16[2,1,128,512]{3,2,1,0:T(8,128)(2,1)S(1)} %collective-permute-done.7.refs_2_), channel_id=1, source_target_pairs={{0,1},{1,0},{2,3},{3,2},{4,5},{5,4},{6,7},{7,6},{8,9},{9,8},{10,11... | collective-permute-start | bytes 786440 | tf_op jit(solution)/shard_map/ppermute | solution.py:246
  33.0 7.4 %collective-permute-start.11 = (bf16[1,4,128,128]{3,2,1,0:T(8,128)(2,1)S(1)}, bf16[1,4,128,128]{3,2,1,0:T(8,128)(2,1)S(1)}, u32[]{:S(2)}, u32[]{:S(2)}) collective-permute-start(bf16[1,4,128,128]{3,2,1,0:T(8,128)(2,1)S(1)} %get-tuple-element.56), channel_id=1, source_target_pairs={{0,4},{1,5},{2,6},{3,7},{4,0},{5,1},{6,2},{7,3},{8,12},{9,13},{10,... | collective-permute-start | bytes 393224 | tf_op jit(solution)/shard_map/ppermute | solution.py:252
  35.4 19.2 %copy-start.1 = (bf16[1,3,1,8,128,128]{5,4,3,2,1,0:T(8,128)(2,1)S(1)}, bf16[1,3,1,8,128,128]{5,4,3,2,1,0:T(8,128)(2,1)}, u32[]{:S(2)}) copy-start(bf16[1,3,1,8,128,128]{5,4,3,2,1,0:T(8,128)(2,1)} %third.5) | copy-start | bytes 2359300
  35.4 19.2 %copy-start.6 = (bf16[1,1024,512]{2,1,0:T(8,128)(2,1)S(1)}, bf16[1,1024,512]{2,1,0:T(8,128)(2,1)}, u32[]{:S(2)}) copy-start(bf16[1,1024,512]{2,1,0:T(8,128)(2,1)} %rhs.1) | copy-start | bytes 3145732
  35.4 11.1 %collective-permute-start.13 = (bf16[2,128,512]{2,1,0:T(8,128)(2,1)S(1)}, bf16[2,128,512]{2,1,0:T(8,128)(2,1)S(1)}, u32[]{:S(2)}, u32[]{:S(2)}) collective-permute-start(bf16[2,128,512]{2,1,0:T(8,128)(2,1)S(1)} %get-tuple-element.59), channel_id=1, source_target_pairs={{0,2},{1,3},{2,0},{3,1},{4,6},{5,7},{6,4},{7,5},{8,10},{9,11},{10,... | collective-permute-start | bytes 786440 | tf_op jit(solution)/shard_map/ppermute | solution.py:246
  40.4 7.8 %collective-permute-start.12 = (bf16[2,128,512]{2,1,0:T(8,128)(2,1)S(1)}, bf16[2,128,512]{2,1,0:T(8,128)(2,1)S(1)}, u32[]{:S(2)}, u32[]{:S(2)}) collective-permute-start(bf16[2,128,512]{2,1,0:T(8,128)(2,1)S(1)} %get-tuple-element.57), channel_id=1, source_target_pairs={{0,1},{1,0},{2,3},{3,2},{4,5},{5,4},{6,7},{7,6},{8,9},{9,8},{10,11... | collective-permute-start | bytes 786440 | tf_op jit(solution)/shard_map/ppermute | solution.py:246
  41.4 12.3 %collective-permute-start.10 = (bf16[2,128,512]{2,1,0:T(8,128)(2,1)S(1)}, bf16[2,128,512]{2,1,0:T(8,128)(2,1)S(1)}, u32[]{:S(2)}, u32[]{:S(2)}) collective-permute-start(bf16[2,128,512]{2,1,0:T(8,128)(2,1)S(1)} %off_sums.1), channel_id=1, source_target_pairs={{0,4},{1,5},{2,6},{3,7},{4,0},{5,1},{6,2},{7,3},{8,12},{9,13},{10,... | collective-permute-start | bytes 786440 | tf_op jit(solution)/shard_map/ppermute | solution.py:252
  48.2 6.4 %collective-permute-start.14 = (bf16[2,128,512]{2,1,0:T(8,128)(2,1)S(1)}, bf16[2,128,512]{2,1,0:T(8,128)(2,1)S(1)}, u32[]{:S(2)}, u32[]{:S(2)}) collective-permute-start(bf16[2,128,512]{2,1,0:T(8,128)(2,1)S(1)} %collective-permute-done.13.refs_3_), channel_id=1, source_target_pairs={{0,1},{1,0},{2,3},{3,2},{4,5},{5,4},{6,7},{7,6},{8,9},{9,8},{10,11... | collective-permute-start | bytes 786440 | tf_op jit(solution)/shard_map/ppermute | solution.py:246
  57.0 6.0 %collective-permute-start.15 = (bf16[1,1,128,512]{3,2,1,0:T(8,128)(2,1)S(1)}, bf16[1,1,128,512]{3,2,1,0:T(8,128)(2,1)S(1)}, u32[]{:S(2)}, u32[]{:S(2)}) collective-permute-start(bf16[1,1,128,512]{3,2,1,0:T(8,128)(2,1)S(1)} %get-tuple-element.62), channel_id=1, source_target_pairs={{0,3},{1,2},{2,1},{3,0},{4,7},{5,6},{6,5},{7,4},{8,11},{9,10},{10,... | collective-permute-start | bytes 393224 | tf_op jit(solution)/shard_map/ppermute | solution.py:246
  57.9 6.2 %collective-permute-start.16 = (bf16[1,1,128,512]{3,2,1,0:T(8,128)(2,1)S(1)}, bf16[1,1,128,512]{3,2,1,0:T(8,128)(2,1)S(1)}, u32[]{:S(2)}, u32[]{:S(2)}) collective-permute-start(bf16[1,1,128,512]{3,2,1,0:T(8,128)(2,1)S(1)} %get-tuple-element.63), channel_id=1, source_target_pairs={{0,2},{1,3},{2,0},{3,1},{4,6},{5,7},{6,4},{7,5},{8,10},{9,11},{10,... | collective-permute-start | bytes 393224 | tf_op jit(solution)/shard_map/ppermute | solution.py:246
  58.7 5.6 %collective-permute-start.17 = (bf16[1,1,128,512]{3,2,1,0:T(8,128)(2,1)S(1)}, bf16[1,1,128,512]{3,2,1,0:T(8,128)(2,1)S(1)}, u32[]{:S(2)}, u32[]{:S(2)}) collective-permute-start(bf16[1,1,128,512]{3,2,1,0:T(8,128)(2,1)S(1)} %get-tuple-element.64), channel_id=1, source_target_pairs={{0,1},{1,0},{2,3},{3,2},{4,5},{5,4},{6,7},{7,6},{8,9},{9,8},{10,11... | collective-permute-start | bytes 393224 | tf_op jit(solution)/shard_map/ppermute | solution.py:246
  64.6 6.6 %collective-permute-start.19 = (bf16[1,128,512]{2,1,0:T(8,128)(2,1)S(1)}, bf16[1,128,512]{2,1,0:T(8,128)(2,1)S(1)}, u32[]{:S(2)}, u32[]{:S(2)}) collective-permute-start(bf16[1,128,512]{2,1,0:T(8,128)(2,1)S(1)} %get-tuple-element.67), channel_id=1, source_target_pairs={{0,3},{1,2},{2,1},{3,0},{4,7},{5,6},{6,5},{7,4},{8,11},{9,10},{10,... | collective-permute-start | bytes 393224 | tf_op jit(solution)/shard_map/ppermute | solution.py:246
  66.9 8.3 %collective-permute-start.20 = (bf16[1,128,512]{2,1,0:T(8,128)(2,1)S(1)}, bf16[1,128,512]{2,1,0:T(8,128)(2,1)S(1)}, u32[]{:S(2)}, u32[]{:S(2)}) collective-permute-start(bf16[1,128,512]{2,1,0:T(8,128)(2,1)S(1)} %get-tuple-element.69), channel_id=1, source_target_pairs={{0,2},{1,3},{2,0},{3,1},{4,6},{5,7},{6,4},{7,5},{8,10},{9,11},{10,... | collective-permute-start | bytes 393224 | tf_op jit(solution)/shard_map/ppermute | solution.py:246
  67.3 8.0 %collective-permute-start.21 = (bf16[1,128,512]{2,1,0:T(8,128)(2,1)S(1)}, bf16[1,128,512]{2,1,0:T(8,128)(2,1)S(1)}, u32[]{:S(2)}, u32[]{:S(2)}) collective-permute-start(bf16[1,128,512]{2,1,0:T(8,128)(2,1)S(1)} %get-tuple-element.71), channel_id=1, source_target_pairs={{0,1},{1,0},{2,3},{3,2},{4,5},{5,4},{6,7},{7,6},{8,9},{9,8},{10,11... | collective-permute-start | bytes 393224 | tf_op jit(solution)/shard_map/ppermute | solution.py:246
  68.1 7.1 %collective-permute-start.18 = (bf16[1,128,512]{2,1,0:T(8,128)(2,1)S(1)}, bf16[1,128,512]{2,1,0:T(8,128)(2,1)S(1)}, u32[]{:S(2)}, u32[]{:S(2)}) collective-permute-start(bf16[1,128,512]{2,1,0:T(8,128)(2,1)S(1)} %sums.1), channel_id=1, source_target_pairs={{0,4},{1,5},{2,6},{3,7},{4,0},{5,1},{6,2},{7,3},{8,12},{9,13},{10,... | collective-permute-start | bytes 393224 | tf_op jit(solution)/shard_map/ppermute | solution.py:252

commit v12 on v11

--- a/solution.py
+++ b/solution.py
@@ -174,6 +174,10 @@
             out[j] = dot(jnp.concatenate(mats, axis=1), slots).astype(BF16)
 
 
+def last_own_kernel(leaf, up_own, *own):
+    put_own(up_own.at[up_own.shape[0] - 1], leaf[...], own, 0)
+
+
 def sum_kernel(radix, *refs):
     got, thirds, outs = take(refs, radix, (len(refs) - radix) // 2, (len(refs) - radix) // 2)
     got = got[::-1]
@@ -192,9 +196,9 @@
 
 
 def middle_kernel(
-    radix, groups, offs, third, rhs, basis, row_mats, up_own, up_other, second_along, second_both, *refs
+    radix, groups, offs, third, rhs, basis, row_mats, up_other, second_along, second_both, *refs
 ):
-    crossed, own_in, (residual_ref,), own, other = take(refs, groups - 1, radix, 1, radix, radix)
+    crossed, own_in, (residual_ref, leaf_ref), other = take(refs, groups - 1, radix, 2, radix)
     coefs = []
     for j in range(offs):
         slots = slots_of([ref[j] for ref in own_in], second_along, second_both, j, 0)
@@ -208,17 +212,25 @@
         residual_ref[rows] = residual
         leaf.append(dot_t(basis[0, offs, k], residual.astype(BF16)).astype(BF16))
     leaf = jnp.concatenate(leaf, axis=0)
+    leaf_ref[...] = leaf
     put_other(up_other.at[offs], leaf, other, 0)
-    put_own(up_own.at[offs], leaf, own, 0)
 
 
 def last_kernel(radix, groups, offs, third, row_mats, residual, *refs):
-    crossed, own_in, (out,) = take(refs, groups - 1, radix, 1)
-    own_in = own_in[::-1]
-    slots = jnp.concatenate([ref[0] for ref in own_in], axis=0)
+    crossed, own_in, (out, held, sem) = take(refs, groups - 1, radix, 3)
+    slots = jnp.concatenate([ref[0] for ref in own_in[::-1]], axis=0)
     coefs = [group_coef(offs, slots, third, radix)] + [ref[0] for ref in crossed]
     coefs = jnp.concatenate(coefs, axis=0)
-    out[0] = (residual[...] + dot(row_mats[...], coefs)).astype(BF16)
+    count = sem.shape[0]
+    height = residual.shape[0] // count
+    copies = []
+    for i in range(count):
+        rows = pl.ds(i * height, height)
+        held[rows] = (residual[rows] + dot(row_mats[rows], coefs)).astype(BF16)
+        copies.append(pltpu.make_async_copy(held.at[rows], out.at[0, rows], sem.at[i]))
+        copies[-1].start()
+    for copy in copies:
+        copy.wait()
 
 
 def after(array, *others):
@@ -304,7 +316,7 @@
 
     pieces = [solved, over_row(solved, 1)]
     for mask in range(2, row_size, 2):
-        far = after(over_row(solved, mask), up_own, *thirds[0], *seconds)
+        far = after(over_row(solved, mask), up_own, *seconds, *thirds[0])
         pieces += [far, over_row(far, 1)]
 
     other_flops = 2 * columns * rank * radix * less * depth
@@ -356,22 +368,21 @@
     ]
     own.append(over_members(after(own_along, own[1], *sums), ACROSS))
 
-    residual, *levels = call(
+    residual, leaf, *other = call(
         functools.partial(middle_kernel, radix, groups, offs),
         "middle_levels",
         offs * row_flops + leaf_flops + other_flops + own_flops,
-        [((rows, columns), F32)] + own_out(1) + other_out(1),
+        [((rows, columns), F32), ((depth, columns), BF16)] + other_out(1),
         third_level,
         rhs,
         leaf_basis,
         off_rows,
-        up_own,
         up_other,
         *seconds,
         *crossed,
         *own,
     )
-    own, other = levels[:radix], levels[radix:]
+    own = call(last_own_kernel, "last_own_levels", own_flops, own_out(1), leaf, up_own)
     other = [over_members(a, i) for i, a in reversed(list(enumerate(other)))]
     sums = call(
         functools.partial(sum_kernel, radix),
@@ -383,17 +394,17 @@
     )
     crossed = cross(sums)
     own = [over_members(after(a, *sums) if i else a, i) for i, a in enumerate(own)]
-    return call(
+    args = [third_level, last_rows, residual, *crossed, *own[::-1]]
+    return pl.pallas_call(
         functools.partial(last_kernel, radix, groups, offs),
-        "last_levels",
-        row_flops,
-        [((1, rows, columns), BF16)],
-        third_level,
-        last_rows,
-        residual,
-        *crossed,
-        *own[::-1],
-    )[0]
+        out_shape=jax.ShapeDtypeStruct((1, rows, columns), BF16),
+        in_specs=[VMEM] * len(args),
+        out_specs=pl.BlockSpec(memory_space=pltpu.HBM),
+        scratch_shapes=[pltpu.VMEM((rows, columns), BF16), pltpu.SemaphoreType.DMA((4,))],
+        compiler_params=pltpu.CompilerParams(vmem_limit_bytes=32 * MIB),
+        cost_estimate=pl.CostEstimate(flops=row_flops, bytes_accessed=0, transcendentals=0),
+        name="last_levels",
+    )(*args)
 
 
 def solution(mesh):

time: 77.4 us -> 77 us (level)
    pallas_call x9, Pallas kernels: 7.94 us -> 6.47 us  [call(): pl.pallas_call(kernel, out_shape=outs, in_specs=[VMEM] * len(args), out_s...]
    pallas_call x0 -> x1, Pallas kernels: none -> 1.45 us  [on_device(): pl.pallas_call(functools.partial(last_kernel, radix, groups, offs), out_s...]
  transfers between devices with their start and end apart: 22 -> 22, of which waited for: 13 -> 13; matrix products, arithmetic and copies ran while one was open for 0% -> 0% of each run, Pallas kernels for 3% -> 4%
where the time goes in v12:
time: 77 us; the launch traced here: 76.4 us
  waiting for transfers between devices  31.6 us (41%)
  starting transfers between devices  30.9 us (40%)
  Pallas kernels  7.92 us (10%)
  local copies, waits for them, and re-layouts  5.83 us (8%)
    ppermute x5, waiting for transfers between devices, over_groups(): return lax.ppermute(array, 'box', pairs)  16 us
    ppermute x14, starting transfers between devices, over_members(): return array if mask == 0 else lax.ppermute(array, 'box', pairs)  15.9 us
    ppermute x14, waiting for transfers between devices, over_members(): return array if mask == 0 else lax.ppermute(array, 'box', pairs)  13.7 us
    ppermute x5, starting transfers between devices, over_groups(): return lax.ppermute(array, 'box', pairs)  12.1 us
    pallas_call x9, Pallas kernels, call(): pl.pallas_call(kernel, out_shape=outs, in_specs=[VMEM] * len(args), out_s...  6.47 us
    unnamed x20, local copies, waits for them, and re-layouts  5.83 us
    ppermute x3, starting transfers between devices, over_row(): return lax.ppermute(array, 'row', [(r, r ^ mask) for r in range(row_size)])  2.97 us
    ppermute x3, waiting for transfers between devices, over_row(): return lax.ppermute(array, 'row', [(r, r ^ mask) for r in range(row_size)])  1.91 us
  transfers between devices with their start and end apart: 22, of which 13 were waited for; matrix products, arithmetic and copies ran while one was open for 0% of the time, Pallas kernels for 4%

profile of v12, /device:TPU:0, one launch (start us, length us, event | category | flops | bytes accessed | tf_op | source)
XLA Modules:
  0.0 76.4 jit_solution(6380327027948018359)
XLA Ops:
  0.0 3.0 %collective-permute-start.3 = (bf16[2,256,512]{2,1,0:T(8,128)(2,1)}, bf16[2,256,512]{2,1,0:T(8,128)(2,1)S(1)}, u32[]{:S(2)}, u32[]{:S(2)}) collective-permute-start(bf16[2,256,512]{2,1,0:T(8,128)(2,1)} %refs_0_.1), channel_id=1, source_target_pairs={{0,16},{8,24},{16,0},{24,8},{1,17},{9,25},{17,1},{25,9},{2,18},{10... | collective-permute-start | bytes 1572872 | tf_op jit(solution)/shard_map/ppermute | solution.py:254
  3.0 1.1 %copy-done.2 = bf16[1,3,1,8,128,128]{5,4,3,2,1,0:T(8,128)(2,1)S(1)} copy-done((bf16[1,3,1,8,128,128]{5,4,3,2,1,0:T(8,128)(2,1)S(1)}, bf16[1,3,1,8,128,128]{5,4,3,2,1,0:T(8,128)(2,1)}, u32[]{:S(2)}) %copy-start.2) | copy-done | bytes 786456
  4.1 1.6 %collective-permute-start = (bf16[2,2,128,128]{3,2,1,0:T(8,128)(2,1)S(1)}, bf16[2,2,128,128]{3,2,1,0:T(8,128)(2,1)S(1)}, u32[]{:S(2)}, u32[]{:S(2)}) collective-permute-start(bf16[2,2,128,128]{3,2,1,0:T(8,128)(2,1)S(1)} %get-tuple-element.43), channel_id=1, source_target_pairs={{0,2},{1,3},{2,0},{3,1},{4,6},{5,7},{6,4},{7,5},{8,10},{9,11},{10,... | collective-permute-start | bytes 393224 | tf_op jit(solution)/shard_map/ppermute | solution.py:258
  5.8 1.4 %collective-permute-start.1 = (bf16[2,2,128,128]{3,2,1,0:T(8,128)(2,1)S(1)}, bf16[2,2,128,128]{3,2,1,0:T(8,128)(2,1)S(1)}, u32[]{:S(2)}, u32[]{:S(2)}) collective-permute-start(bf16[2,2,128,128]{3,2,1,0:T(8,128)(2,1)S(1)} %get-tuple-element.44), channel_id=1, source_target_pairs={{0,3},{1,2},{2,1},{3,0},{4,7},{5,6},{6,5},{7,4},{8,11},{9,10},{10,... | collective-permute-start | bytes 393224 | tf_op jit(solution)/shard_map/ppermute | solution.py:258
  7.1 1.1 %copy-done = bf16[1,3,1,8,128,128]{5,4,3,2,1,0:T(8,128)(2,1)S(1)} copy-done((bf16[1,3,1,8,128,128]{5,4,3,2,1,0:T(8,128)(2,1)S(1)}, bf16[1,3,1,8,128,128]{5,4,3,2,1,0:T(8,128)(2,1)}, u32[]{:S(2)}) %copy-start) | copy-done | bytes 786456
  8.3 0.0 copy-start.4
  8.3 2.7 %collective-permute-start.4 = (bf16[1,4,128,128]{3,2,1,0:T(8,128)(2,1)S(1)}, bf16[1,4,128,128]{3,2,1,0:T(8,128)(2,1)S(1)}, u32[]{:S(2)}, u32[]{:S(2)}) collective-permute-start(bf16[1,4,128,128]{3,2,1,0:T(8,128)(2,1)S(1)} %get-tuple-element.47), channel_id=1, source_target_pairs={{0,4},{1,5},{2,6},{3,7},{4,0},{5,1},{6,2},{7,3},{8,12},{9,13},{10,... | collective-permute-start | bytes 393224 | tf_op jit(solution)/shard_map/ppermute | solution.py:264
  11.0 0.0 collective-permute-start.2
  11.0 0.0 copy-done.3
  11.0 1.4 %copy-done.5 = bf16[1,3,1,4,4,128,128]{6,5,4,3,2,1,0:T(8,128)(2,1)S(1)} copy-done((bf16[1,3,1,4,4,128,128]{6,5,4,3,2,1,0:T(8,128)(2,1)S(1)}, bf16[1,3,1,4,4,128,128]{6,5,4,3,2,1,0:T(8,128)(2,1)}, u32[]{:S(2)}) %copy-start.5) | copy-done | bytes 1572888
  12.4 1.1 %copy-done.7 = bf16[1,3,2,512,128]{4,3,2,1,0:T(8,128)(2,1)S(1)} copy-done((bf16[1,3,2,512,128]{4,3,2,1,0:T(8,128)(2,1)S(1)}, bf16[1,3,2,512,128]{4,3,2,1,0:T(8,128)(2,1)}, u32[]{:S(2)}) %copy-start.7) | copy-done | bytes 786456
  13.5 1.0 %copy-done.9 = bf16[1,3,1,2,2,128,128]{6,5,4,3,2,1,0:T(8,128)(2,1)S(1)} copy-done((bf16[1,3,1,2,2,128,128]{6,5,4,3,2,1,0:T(8,128)(2,1)S(1)}, bf16[1,3,1,2,2,128,128]{6,5,4,3,2,1,0:T(8,128)(2,1)}, u32[]{:S(2)}) %copy-start.9) | copy-done | bytes 393240
  14.5 1.4 %weights.1 = (bf16[3,4,128,512]{3,2,1,0:T(8,128)(2,1)S(1)}, bf16[3,4,1,128,512]{4,3,2,1,0:T(8,128)(2,1)S(1)}, bf16[2,2,128,512]{3,2,1,0:T(8,128)(2,1)S(1)}, bf16...) custom-call(bf16[1,3,1,4,4,128,128]{6,5,4,3,2,1,0:T(8,128)(2,1)S(1)} %copy-done.5, ...), custom_call_target="tpu_custom_call" | custom-call | flops 603979776 | tf_op jit(solution)/shard_map/weights/pallas_call | solution.py:269
  15.9 0.0 collective-permute-done.second_along
  15.9 0.0 collective-permute-done.1.second_both
  15.9 1.1 %collective-permute-done.4.refs_4_ = bf16[1,4,128,128]{3,2,1,0:T(8,128)(2,1)S(1)} collective-permute-done((bf16[1,4,128,128]{3,2,1,0:T(8,128)(2,1)S(1)}, bf16[1,4,128,128]{3,2,1,0:T(8,128)(2,1)S(1)}, u32[]{:S(2)}, u32[]{:S(2)}) %collective-permute-start.4) | collective-permute-done | bytes 131104 | tf_op jit(solution)/shard_map/ppermute | solution.py:264
  17.1 0.0 collective-permute-done.3.refs_2_
  17.1 0.0 collective-permute-start.5
  17.1 0.0 collective-permute-done.2.refs_1_
  17.1 1.9 %collective-permute-done.5.refs_3_ = bf16[2,256,512]{2,1,0:T(8,128)(2,1)S(1)} collective-permute-done((bf16[2,256,512]{2,1,0:T(8,128)(2,1)S(1)}, bf16[2,256,512]{2,1,0:T(8,128)(2,1)S(1)}, u32[]{:S(2)}, u32[]{:S(2)}) %collective-permute-start.5) | collective-permute-done | bytes 524320 | tf_op jit(solution)/shard_map/ppermute | solution.py:254
  19.0 0.0 copy-done.4
  19.0 0.0 copy-done.8
  19.0 1.0 %off_levels.1 = (bf16[2,512,512]{2,1,0:T(8,128)(2,1)S(1)}, bf16[2,1,128,512]{3,2,1,0:T(8,128)(2,1)S(1)}, bf16[2,1,128,512]{3,2,1,0:T(8,128)(2,1)S(1)}, bf16[2,1,128,512]{3,2,1,0:T(8,128)(2,1)S(1)}) custom-call(bf16[1,3,4,256,128]{4,3,2,1,0:T(8,128)(2,1)S(1)} %copy-done.4, bf16[3,4,1,128,512]{4,3,2,1,0:T(8,128)(2,1)S(1)} %get-tuple-element.42.up_other, ...), custom_call_target="tpu_custom_call" | custom-call | flops 805306368 | tf_op jit(solution)/shard_map/off_levels/pallas_call | solution.py:269
  20.0 0.1 collective-permute-start.6
  20.1 1.8 %collective-permute-start.7 = (bf16[2,1,128,512]{3,2,1,0:T(8,128)(2,1)S(1)}, bf16[2,1,128,512]{3,2,1,0:T(8,128)(2,1)S(1)}, u32[]{:S(2)}, u32[]{:S(2)}) collective-permute-start(bf16[2,1,128,512]{3,2,1,0:T(8,128)(2,1)S(1)} %get-tuple-element.51), channel_id=1, source_target_pairs={{0,2},{1,3},{2,0},{3,1},{4,6},{5,7},{6,4},{7,5},{8,10},{9,11},{10,... | collective-permute-start | bytes 786440 | tf_op jit(solution)/shard_map/ppermute | solution.py:258
  21.9 2.3 %collective-permute-start.8 = (bf16[1,4,128,128]{3,2,1,0:T(8,128)(2,1)S(1)}, bf16[1,4,128,128]{3,2,1,0:T(8,128)(2,1)S(1)}, u32[]{:S(2)}, u32[]{:S(2)}) collective-permute-start(bf16[1,4,128,128]{3,2,1,0:T(8,128)(2,1)S(1)} %get-tuple-element.52), channel_id=1, source_target_pairs={{0,4},{1,5},{2,6},{3,7},{4,0},{5,1},{6,2},{7,3},{8,12},{9,13},{10,... | collective-permute-start | bytes 393224 | tf_op jit(solution)/shard_map/ppermute | solution.py:264
  24.2 6.1 %collective-permute-done.8.refs_5_ = bf16[1,4,128,128]{3,2,1,0:T(8,128)(2,1)S(1)} collective-permute-done((bf16[1,4,128,128]{3,2,1,0:T(8,128)(2,1)S(1)}, bf16[1,4,128,128]{3,2,1,0:T(8,128)(2,1)S(1)}, u32[]{:S(2)}, u32[]{:S(2)}) %collective-permute-start.8) | collective-permute-done | bytes 131104 | tf_op jit(solution)/shard_map/ppermute | solution.py:264
  30.3 0.0 collective-permute-done.6.refs_1_
  30.3 1.0 %collective-permute-done.7.refs_2_ = bf16[2,1,128,512]{3,2,1,0:T(8,128)(2,1)S(1)} collective-permute-done((bf16[2,1,128,512]{3,2,1,0:T(8,128)(2,1)S(1)}, bf16[2,1,128,512]{3,2,1,0:T(8,128)(2,1)S(1)}, u32[]{:S(2)}, u32[]{:S(2)}) %collective-permute-start.7) | collective-permute-done | bytes 262176 | tf_op jit(solution)/shard_map/ppermute | solution.py:258
  31.3 1.7 %collective-permute-start.9 = (bf16[2,1,128,512]{3,2,1,0:T(8,128)(2,1)S(1)}, bf16[2,1,128,512]{3,2,1,0:T(8,128)(2,1)S(1)}, u32[]{:S(2)}, u32[]{:S(2)}) collective-permute-start(bf16[2,1,128,512]{3,2,1,0:T(8,128)(2,1)S(1)} %collective-permute-done.7.refs_2_), channel_id=1, source_target_pairs={{0,1},{1,0},{2,3},{3,2},{4,5},{5,4},{6,7},{7,6},{8,9},{9,8},{10,11... | collective-permute-start | bytes 786440 | tf_op jit(solution)/shard_map/ppermute | solution.py:258
  33.0 1.8 %collective-permute-start.11 = (bf16[1,4,128,128]{3,2,1,0:T(8,128)(2,1)S(1)}, bf16[1,4,128,128]{3,2,1,0:T(8,128)(2,1)S(1)}, u32[]{:S(2)}, u32[]{:S(2)}) collective-permute-start(bf16[1,4,128,128]{3,2,1,0:T(8,128)(2,1)S(1)} %get-tuple-element.57), channel_id=1, source_target_pairs={{0,4},{1,5},{2,6},{3,7},{4,0},{5,1},{6,2},{7,3},{8,12},{9,13},{10,... | collective-permute-start | bytes 393224 | tf_op jit(solution)/shard_map/ppermute | solution.py:264
  34.8 0.6 own_levels.1
  35.4 0.0 copy-start.1
  35.4 0.0 copy-start.6
  35.4 1.8 %collective-permute-start.13 = (bf16[2,128,512]{2,1,0:T(8,128)(2,1)S(1)}, bf16[2,128,512]{2,1,0:T(8,128)(2,1)S(1)}, u32[]{:S(2)}, u32[]{:S(2)}) collective-permute-start(bf16[2,128,512]{2,1,0:T(8,128)(2,1)S(1)} %get-tuple-element.60), channel_id=1, source_target_pairs={{0,2},{1,3},{2,0},{3,1},{4,6},{5,7},{6,4},{7,5},{8,10},{9,11},{10,... | collective-permute-start | bytes 786440 | tf_op jit(solution)/shard_map/ppermute | solution.py:258
  37.2 3.2 %collective-permute-done.11.refs_4_ = bf16[1,4,128,128]{3,2,1,0:T(8,128)(2,1)S(1)} collective-permute-done((bf16[1,4,128,128]{3,2,1,0:T(8,128)(2,1)S(1)}, bf16[1,4,128,128]{3,2,1,0:T(8,128)(2,1)S(1)}, u32[]{:S(2)}, u32[]{:S(2)}) %collective-permute-start.11) | collective-permute-done | bytes 131104 | tf_op jit(solution)/shard_map/ppermute | solution.py:264
  40.4 0.0 collective-permute-done.9.refs_3_
  40.4 0.4 collective-permute-start.12
  40.8 0.6 off_sums.1
  41.4 2.2 %collective-permute-start.10 = (bf16[2,128,512]{2,1,0:T(8,128)(2,1)S(1)}, bf16[2,128,512]{2,1,0:T(8,128)(2,1)S(1)}, u32[]{:S(2)}, u32[]{:S(2)}) collective-permute-start(bf16[2,128,512]{2,1,0:T(8,128)(2,1)S(1)} %off_sums.1), channel_id=1, source_target_pairs={{0,4},{1,5},{2,6},{3,7},{4,0},{5,1},{6,2},{7,3},{8,12},{9,13},{10,... | collective-permute-start | bytes 786440 | tf_op jit(solution)/shard_map/ppermute | solution.py:264
  43.6 2.9 %collective-permute-done.13.refs_3_ = bf16[2,128,512]{2,1,0:T(8,128)(2,1)S(1)} collective-permute-done((bf16[2,128,512]{2,1,0:T(8,128)(2,1)S(1)}, bf16[2,128,512]{2,1,0:T(8,128)(2,1)S(1)}, u32[]{:S(2)}, u32[]{:S(2)}) %collective-permute-start.13) | collective-permute-done | bytes 262176 | tf_op jit(solution)/shard_map/ppermute | solution.py:258
  46.5 1.6 %collective-permute-done.12.refs_2_ = bf16[2,128,512]{2,1,0:T(8,128)(2,1)S(1)} collective-permute-done((bf16[2,128,512]{2,1,0:T(8,128)(2,1)S(1)}, bf16[2,128,512]{2,1,0:T(8,128)(2,1)S(1)}, u32[]{:S(2)}, u32[]{:S(2)}) %collective-permute-start.12) | collective-permute-done | bytes 262176 | tf_op jit(solution)/shard_map/ppermute | solution.py:258
  48.2 0.0 collective-permute-start.14
  48.2 5.6 %collective-permute-done.10.refs_0_ = bf16[2,128,512]{2,1,0:T(8,128)(2,1)S(1)} collective-permute-done((bf16[2,128,512]{2,1,0:T(8,128)(2,1)S(1)}, bf16[2,128,512]{2,1,0:T(8,128)(2,1)S(1)}, u32[]{:S(2)}, u32[]{:S(2)}) %collective-permute-start.10) | collective-permute-done | bytes 262176 | tf_op jit(solution)/shard_map/ppermute | solution.py:264
  53.8 0.8 collective-permute-done.14.refs_4_
  54.5 0.0 copy-done.1
  54.5 2.2 %middle_levels.1 = (f32[1024,512]{1,0:T(8,128)S(1)}, bf16[512,512]{1,0:T(8,128)(2,1)S(1)}, bf16[1,1,128,512]{3,2,1,0:T(8,128)(2,1)S(1)}, bf16[1,1,128,512]{3,2,1...) custom-call(bf16[1,3,1,8,128,128]{5,4,3,2,1,0:T(8,128)(2,1)S(1)} %copy-done.1, ...), custom_call_target="tpu_custom_call" | custom-call | flops 1342177280 | tf_op jit(solution)/shard_map/middle_levels/pallas_call | solution.py:269
  56.7 0.9 %collective-permute-start.15 = (bf16[1,1,128,512]{3,2,1,0:T(8,128)(2,1)S(1)}, bf16[1,1,128,512]{3,2,1,0:T(8,128)(2,1)S(1)}, u32[]{:S(2)}, u32[]{:S(2)}) collective-permute-start(bf16[1,1,128,512]{3,2,1,0:T(8,128)(2,1)S(1)} %get-tuple-element.63), channel_id=1, source_target_pairs={{0,3},{1,2},{2,1},{3,0},{4,7},{5,6},{6,5},{7,4},{8,11},{9,10},{10,... | collective-permute-start | bytes 393224 | tf_op jit(solution)/shard_map/ppermute | solution.py:258
  57.6 0.9 %collective-permute-start.16 = (bf16[1,1,128,512]{3,2,1,0:T(8,128)(2,1)S(1)}, bf16[1,1,128,512]{3,2,1,0:T(8,128)(2,1)S(1)}, u32[]{:S(2)}, u32[]{:S(2)}) collective-permute-start(bf16[1,1,128,512]{3,2,1,0:T(8,128)(2,1)S(1)} %get-tuple-element.64), channel_id=1, source_target_pairs={{0,2},{1,3},{2,0},{3,1},{4,6},{5,7},{6,4},{7,5},{8,10},{9,11},{10,... | collective-permute-start | bytes 393224 | tf_op jit(solution)/shard_map/ppermute | solution.py:258
  58.4 1.8 %collective-permute-start.17 = (bf16[1,1,128,512]{3,2,1,0:T(8,128)(2,1)S(1)}, bf16[1,1,128,512]{3,2,1,0:T(8,128)(2,1)S(1)}, u32[]{:S(2)}, u32[]{:S(2)}) collective-permute-start(bf16[1,1,128,512]{3,2,1,0:T(8,128)(2,1)S(1)} %get-tuple-element.65), channel_id=1, source_target_pairs={{0,1},{1,0},{2,3},{3,2},{4,5},{5,4},{6,7},{7,6},{8,9},{9,8},{10,11... | collective-permute-start | bytes 393224 | tf_op jit(solution)/shard_map/ppermute | solution.py:258
  60.3 0.4 last_own_levels.1
  60.7 2.0 %collective-permute-done.15.refs_0_ = bf16[1,1,128,512]{3,2,1,0:T(8,128)(2,1)S(1)} collective-permute-done((bf16[1,1,128,512]{3,2,1,0:T(8,128)(2,1)S(1)}, bf16[1,1,128,512]{3,2,1,0:T(8,128)(2,1)S(1)}, u32[]{:S(2)}, u32[]{:S(2)}) %collective-permute-start.15) | collective-permute-done | bytes 131104 | tf_op jit(solution)/shard_map/ppermute | solution.py:258
  62.7 1.0 %collective-permute-done.16.refs_1_ = bf16[1,1,128,512]{3,2,1,0:T(8,128)(2,1)S(1)} collective-permute-done((bf16[1,1,128,512]{3,2,1,0:T(8,128)(2,1)S(1)}, bf16[1,1,128,512]{3,2,1,0:T(8,128)(2,1)S(1)}, u32[]{:S(2)}, u32[]{:S(2)}) %collective-permute-start.16) | collective-permute-done | bytes 131104 | tf_op jit(solution)/shard_map/ppermute | solution.py:258
  63.8 0.3 collective-permute-done.17.refs_2_
  64.1 0.2 sums.1
  64.3 2.4 %collective-permute-start.19 = (bf16[1,128,512]{2,1,0:T(8,128)(2,1)S(1)}, bf16[1,128,512]{2,1,0:T(8,128)(2,1)S(1)}, u32[]{:S(2)}, u32[]{:S(2)}) collective-permute-start(bf16[1,128,512]{2,1,0:T(8,128)(2,1)S(1)} %get-tuple-element.69), channel_id=1, source_target_pairs={{0,3},{1,2},{2,1},{3,0},{4,7},{5,6},{6,5},{7,4},{8,11},{9,10},{10,... | collective-permute-start | bytes 393224 | tf_op jit(solution)/shard_map/ppermute | solution.py:258
  66.7 0.4 collective-permute-start.20
  67.0 0.8 %collective-permute-start.21 = (bf16[1,128,512]{2,1,0:T(8,128)(2,1)S(1)}, bf16[1,128,512]{2,1,0:T(8,128)(2,1)S(1)}, u32[]{:S(2)}, u32[]{:S(2)}) collective-permute-start(bf16[1,128,512]{2,1,0:T(8,128)(2,1)S(1)} %get-tuple-element.73), channel_id=1, source_target_pairs={{0,1},{1,0},{2,3},{3,2},{4,5},{5,4},{6,7},{7,6},{8,9},{9,8},{10,11... | collective-permute-start | bytes 393224 | tf_op jit(solution)/shard_map/ppermute | solution.py:258
  67.9 3.0 %collective-permute-start.18 = (bf16[1,128,512]{2,1,0:T(8,128)(2,1)S(1)}, bf16[1,128,512]{2,1,0:T(8,128)(2,1)S(1)}, u32[]{:S(2)}, u32[]{:S(2)}) collective-permute-start(bf16[1,128,512]{2,1,0:T(8,128)(2,1)S(1)} %sums.1), channel_id=1, source_target_pairs={{0,4},{1,5},{2,6},{3,7},{4,0},{5,1},{6,2},{7,3},{8,12},{9,13},{10,... | collective-permute-start | bytes 393224 | tf_op jit(solution)/shard_map/ppermute | solution.py:264
  70.9 0.0 collective-permute-done.19.refs_1_
  70.9 4.1 %collective-permute-done.20.refs_2_ = bf16[1,128,512]{2,1,0:T(8,128)(2,1)S(1)} collective-permute-done((bf16[1,128,512]{2,1,0:T(8,128)(2,1)S(1)}, bf16[1,128,512]{2,1,0:T(8,128)(2,1)S(1)}, u32[]{:S(2)}, u32[]{:S(2)}) %collective-permute-start.20) | collective-permute-done | bytes 131104 | tf_op jit(solution)/shard_map/ppermute | solution.py:258
  75.0 0.0 collective-permute-done.21.refs_3_
  75.0 0.0 collective-permute-done.18.refs_0_
  75.0 1.5 %last_levels.1 = bf16[1,1024,512]{2,1,0:T(8,128)(2,1)} custom-call(bf16[1,3,1,8,128,128]{5,4,3,2,1,0:T(8,128)(2,1)S(1)} %copy-done.1, bf16[1024,256]{1,0:T(8,128)(2,1)S(1)} %get-tuple-element.40.row_mats, f32[1024,512]{1,0:T(8,128)S(1)} %get-tuple-element.62.residual, bf16[1,128,512]{2,1,0:T(8,128)(2,1)S(1)} %collective-permute-done.18.refs_0_, ...), custom_call_target="tpu_custom_call" | custom-call | flops 335544320 | tf_op jit(solution)/shard_map/last_levels/pallas_call | solution.py:398
  (10 shorter events, 0.1 us)
Async XLA Ops:
  0.0 17.1 %collective-permute-start.3 = (bf16[2,256,512]{2,1,0:T(8,128)(2,1)}, bf16[2,256,512]{2,1,0:T(8,128)(2,1)S(1)}, u32[]{:S(2)}, u32[]{:S(2)}) collective-permute-start(bf16[2,256,512]{2,1,0:T(8,128)(2,1)} %refs_0_.1), channel_id=1, source_target_pairs={{0,16},{8,24},{16,0},{24,8},{1,17},{9,25},{17,1},{25,9},{2,18},{10... | collective-permute-start | bytes 1572872 | tf_op jit(solution)/shard_map/ppermute | solution.py:254
  3.0 1.1 %copy-start.2 = (bf16[1,3,1,8,128,128]{5,4,3,2,1,0:T(8,128)(2,1)S(1)}, bf16[1,3,1,8,128,128]{5,4,3,2,1,0:T(8,128)(2,1)}, u32[]{:S(2)}) copy-start(bf16[1,3,1,8,128,128]{5,4,3,2,1,0:T(8,128)(2,1)} %second.3) | copy-start | bytes 2359300
  4.1 6.9 %copy-start.3 = (bf16[1,3,1,8,128,128]{5,4,3,2,1,0:T(8,128)(2,1)S(1)}, bf16[1,3,1,8,128,128]{5,4,3,2,1,0:T(8,128)(2,1)}, u32[]{:S(2)}) copy-start(bf16[1,3,1,8,128,128]{5,4,3,2,1,0:T(8,128)(2,1)} %second.3) | copy-start | bytes 2359300
  4.1 11.8 %collective-permute-start = (bf16[2,2,128,128]{3,2,1,0:T(8,128)(2,1)S(1)}, bf16[2,2,128,128]{3,2,1,0:T(8,128)(2,1)S(1)}, u32[]{:S(2)}, u32[]{:S(2)}) collective-permute-start(bf16[2,2,128,128]{3,2,1,0:T(8,128)(2,1)S(1)} %get-tuple-element.43), channel_id=1, source_target_pairs={{0,2},{1,3},{2,0},{3,1},{4,6},{5,7},{6,4},{7,5},{8,10},{9,11},{10,... | collective-permute-start | bytes 393224 | tf_op jit(solution)/shard_map/ppermute | solution.py:258
  5.8 10.2 %collective-permute-start.1 = (bf16[2,2,128,128]{3,2,1,0:T(8,128)(2,1)S(1)}, bf16[2,2,128,128]{3,2,1,0:T(8,128)(2,1)S(1)}, u32[]{:S(2)}, u32[]{:S(2)}) collective-permute-start(bf16[2,2,128,128]{3,2,1,0:T(8,128)(2,1)S(1)} %get-tuple-element.44), channel_id=1, source_target_pairs={{0,3},{1,2},{2,1},{3,0},{4,7},{5,6},{6,5},{7,4},{8,11},{9,10},{10,... | collective-permute-start | bytes 393224 | tf_op jit(solution)/shard_map/ppermute | solution.py:258
  7.1 1.1 %copy-start = (bf16[1,3,1,8,128,128]{5,4,3,2,1,0:T(8,128)(2,1)S(1)}, bf16[1,3,1,8,128,128]{5,4,3,2,1,0:T(8,128)(2,1)}, u32[]{:S(2)}) copy-start(bf16[1,3,1,8,128,128]{5,4,3,2,1,0:T(8,128)(2,1)} %third.5) | copy-start | bytes 2359300
  8.3 10.7 %copy-start.4 = (bf16[1,3,4,256,128]{4,3,2,1,0:T(8,128)(2,1)S(1)}, bf16[1,3,4,256,128]{4,3,2,1,0:T(8,128)(2,1)}, u32[]{:S(2)}) copy-start(bf16[1,3,4,256,128]{4,3,2,1,0:T(8,128)(2,1)} %basis.3) | copy-start | bytes 2359300
  8.3 8.7 %collective-permute-start.4 = (bf16[1,4,128,128]{3,2,1,0:T(8,128)(2,1)S(1)}, bf16[1,4,128,128]{3,2,1,0:T(8,128)(2,1)S(1)}, u32[]{:S(2)}, u32[]{:S(2)}) collective-permute-start(bf16[1,4,128,128]{3,2,1,0:T(8,128)(2,1)S(1)} %get-tuple-element.47), channel_id=1, source_target_pairs={{0,4},{1,5},{2,6},{3,7},{4,0},{5,1},{6,2},{7,3},{8,12},{9,13},{10,... | collective-permute-start | bytes 393224 | tf_op jit(solution)/shard_map/ppermute | solution.py:264
  11.0 6.1 %collective-permute-start.2 = (bf16[2,256,512]{2,1,0:T(8,128)(2,1)}, bf16[2,256,512]{2,1,0:T(8,128)(2,1)S(1)}, u32[]{:S(2)}, u32[]{:S(2)}) collective-permute-start(bf16[2,256,512]{2,1,0:T(8,128)(2,1)} %refs_0_.1), channel_id=1, source_target_pairs={{0,8},{8,0},{16,24},{24,16},{1,9},{9,1},{17,25},{25,17},{2,10},{10... | collective-permute-start | bytes 1572872 | tf_op jit(solution)/shard_map/ppermute | solution.py:254
  11.0 1.4 %copy-start.5 = (bf16[1,3,1,4,4,128,128]{6,5,4,3,2,1,0:T(8,128)(2,1)S(1)}, bf16[1,3,1,4,4,128,128]{6,5,4,3,2,1,0:T(8,128)(2,1)}, u32[]{:S(2)}) copy-start(bf16[1,3,1,4,4,128,128]{6,5,4,3,2,1,0:T(8,128)(2,1)} %first.1) | copy-start | bytes 4718596
  12.4 1.1 %copy-start.7 = (bf16[1,3,2,512,128]{4,3,2,1,0:T(8,128)(2,1)S(1)}, bf16[1,3,2,512,128]{4,3,2,1,0:T(8,128)(2,1)}, u32[]{:S(2)}) copy-start(bf16[1,3,2,512,128]{4,3,2,1,0:T(8,128)(2,1)} %out_basis.1) | copy-start | bytes 2359300
  13.5 1.0 %copy-start.9 = (bf16[1,3,1,2,2,128,128]{6,5,4,3,2,1,0:T(8,128)(2,1)S(1)}, bf16[1,3,1,2,2,128,128]{6,5,4,3,2,1,0:T(8,128)(2,1)}, u32[]{:S(2)}) copy-start(bf16[1,3,1,2,2,128,128]{6,5,4,3,2,1,0:T(8,128)(2,1)} %fourth.1) | copy-start | bytes 1179652
  14.5 4.5 %copy-start.8 = (bf16[2,256,512]{2,1,0:T(8,128)(2,1)S(1)}, bf16[2,256,512]{2,1,0:T(8,128)(2,1)}, u32[]{:S(2)}) copy-start(bf16[2,256,512]{2,1,0:T(8,128)(2,1)} %refs_0_.1) | copy-start | bytes 1572868
  17.1 1.9 %collective-permute-start.5 = (bf16[2,256,512]{2,1,0:T(8,128)(2,1)S(1)}, bf16[2,256,512]{2,1,0:T(8,128)(2,1)S(1)}, u32[]{:S(2)}, u32[]{:S(2)}) collective-permute-start(bf16[2,256,512]{2,1,0:T(8,128)(2,1)S(1)} %collective-permute-done.3.refs_2_), channel_id=1, source_target_pairs={{0,8},{8,0},{16,24},{24,16},{1,9},{9,1},{17,25},{25,17},{2,10},{10... | collective-permute-start | bytes 1572872 | tf_op jit(solution)/shard_map/ppermute | solution.py:254
  20.0 10.3 %collective-permute-start.6 = (bf16[2,1,128,512]{3,2,1,0:T(8,128)(2,1)S(1)}, bf16[2,1,128,512]{3,2,1,0:T(8,128)(2,1)S(1)}, u32[]{:S(2)}, u32[]{:S(2)}) collective-permute-start(bf16[2,1,128,512]{3,2,1,0:T(8,128)(2,1)S(1)} %get-tuple-element.50), channel_id=1, source_target_pairs={{0,1},{1,0},{2,3},{3,2},{4,5},{5,4},{6,7},{7,6},{8,9},{9,8},{10,11... | collective-permute-start | bytes 786440 | tf_op jit(solution)/shard_map/ppermute | solution.py:258
  20.1 11.2 %collective-permute-start.7 = (bf16[2,1,128,512]{3,2,1,0:T(8,128)(2,1)S(1)}, bf16[2,1,128,512]{3,2,1,0:T(8,128)(2,1)S(1)}, u32[]{:S(2)}, u32[]{:S(2)}) collective-permute-start(bf16[2,1,128,512]{3,2,1,0:T(8,128)(2,1)S(1)} %get-tuple-element.51), channel_id=1, source_target_pairs={{0,2},{1,3},{2,0},{3,1},{4,6},{5,7},{6,4},{7,5},{8,10},{9,11},{10,... | collective-permute-start | bytes 786440 | tf_op jit(solution)/shard_map/ppermute | solution.py:258
  21.9 8.4 %collective-permute-start.8 = (bf16[1,4,128,128]{3,2,1,0:T(8,128)(2,1)S(1)}, bf16[1,4,128,128]{3,2,1,0:T(8,128)(2,1)S(1)}, u32[]{:S(2)}, u32[]{:S(2)}) collective-permute-start(bf16[1,4,128,128]{3,2,1,0:T(8,128)(2,1)S(1)} %get-tuple-element.52), channel_id=1, source_target_pairs={{0,4},{1,5},{2,6},{3,7},{4,0},{5,1},{6,2},{7,3},{8,12},{9,13},{10,... | collective-permute-start | bytes 393224 | tf_op jit(solution)/shard_map/ppermute | solution.py:264
  31.3 9.1 %collective-permute-start.9 = (bf16[2,1,128,512]{3,2,1,0:T(8,128)(2,1)S(1)}, bf16[2,1,128,512]{3,2,1,0:T(8,128)(2,1)S(1)}, u32[]{:S(2)}, u32[]{:S(2)}) collective-permute-start(bf16[2,1,128,512]{3,2,1,0:T(8,128)(2,1)S(1)} %collective-permute-done.7.refs_2_), channel_id=1, source_target_pairs={{0,1},{1,0},{2,3},{3,2},{4,5},{5,4},{6,7},{7,6},{8,9},{9,8},{10,11... | collective-permute-start | bytes 786440 | tf_op jit(solution)/shard_map/ppermute | solution.py:258
  33.0 7.4 %collective-permute-start.11 = (bf16[1,4,128,128]{3,2,1,0:T(8,128)(2,1)S(1)}, bf16[1,4,128,128]{3,2,1,0:T(8,128)(2,1)S(1)}, u32[]{:S(2)}, u32[]{:S(2)}) collective-permute-start(bf16[1,4,128,128]{3,2,1,0:T(8,128)(2,1)S(1)} %get-tuple-element.57), channel_id=1, source_target_pairs={{0,4},{1,5},{2,6},{3,7},{4,0},{5,1},{6,2},{7,3},{8,12},{9,13},{10,... | collective-permute-start | bytes 393224 | tf_op jit(solution)/shard_map/ppermute | solution.py:264
  35.4 19.2 %copy-start.1 = (bf16[1,3,1,8,128,128]{5,4,3,2,1,0:T(8,128)(2,1)S(1)}, bf16[1,3,1,8,128,128]{5,4,3,2,1,0:T(8,128)(2,1)}, u32[]{:S(2)}) copy-start(bf16[1,3,1,8,128,128]{5,4,3,2,1,0:T(8,128)(2,1)} %third.5) | copy-start | bytes 2359300
  35.4 19.2 %copy-start.6 = (bf16[1,1024,512]{2,1,0:T(8,128)(2,1)S(1)}, bf16[1,1024,512]{2,1,0:T(8,128)(2,1)}, u32[]{:S(2)}) copy-start(bf16[1,1024,512]{2,1,0:T(8,128)(2,1)} %rhs.1) | copy-start | bytes 3145732
  35.4 11.1 %collective-permute-start.13 = (bf16[2,128,512]{2,1,0:T(8,128)(2,1)S(1)}, bf16[2,128,512]{2,1,0:T(8,128)(2,1)S(1)}, u32[]{:S(2)}, u32[]{:S(2)}) collective-permute-start(bf16[2,128,512]{2,1,0:T(8,128)(2,1)S(1)} %get-tuple-element.60), channel_id=1, source_target_pairs={{0,2},{1,3},{2,0},{3,1},{4,6},{5,7},{6,4},{7,5},{8,10},{9,11},{10,... | collective-permute-start | bytes 786440 | tf_op jit(solution)/shard_map/ppermute | solution.py:258
  40.4 7.8 %collective-permute-start.12 = (bf16[2,128,512]{2,1,0:T(8,128)(2,1)S(1)}, bf16[2,128,512]{2,1,0:T(8,128)(2,1)S(1)}, u32[]{:S(2)}, u32[]{:S(2)}) collective-permute-start(bf16[2,128,512]{2,1,0:T(8,128)(2,1)S(1)} %get-tuple-element.58), channel_id=1, source_target_pairs={{0,1},{1,0},{2,3},{3,2},{4,5},{5,4},{6,7},{7,6},{8,9},{9,8},{10,11... | collective-permute-start | bytes 786440 | tf_op jit(solution)/shard_map/ppermute | solution.py:258
  41.4 12.3 %collective-permute-start.10 = (bf16[2,128,512]{2,1,0:T(8,128)(2,1)S(1)}, bf16[2,128,512]{2,1,0:T(8,128)(2,1)S(1)}, u32[]{:S(2)}, u32[]{:S(2)}) collective-permute-start(bf16[2,128,512]{2,1,0:T(8,128)(2,1)S(1)} %off_sums.1), channel_id=1, source_target_pairs={{0,4},{1,5},{2,6},{3,7},{4,0},{5,1},{6,2},{7,3},{8,12},{9,13},{10,... | collective-permute-start | bytes 786440 | tf_op jit(solution)/shard_map/ppermute | solution.py:264
  48.2 6.4 %collective-permute-start.14 = (bf16[2,128,512]{2,1,0:T(8,128)(2,1)S(1)}, bf16[2,128,512]{2,1,0:T(8,128)(2,1)S(1)}, u32[]{:S(2)}, u32[]{:S(2)}) collective-permute-start(bf16[2,128,512]{2,1,0:T(8,128)(2,1)S(1)} %collective-permute-done.13.refs_3_), channel_id=1, source_target_pairs={{0,1},{1,0},{2,3},{3,2},{4,5},{5,4},{6,7},{7,6},{8,9},{9,8},{10,11... | collective-permute-start | bytes 786440 | tf_op jit(solution)/shard_map/ppermute | solution.py:258
  56.7 6.0 %collective-permute-start.15 = (bf16[1,1,128,512]{3,2,1,0:T(8,128)(2,1)S(1)}, bf16[1,1,128,512]{3,2,1,0:T(8,128)(2,1)S(1)}, u32[]{:S(2)}, u32[]{:S(2)}) collective-permute-start(bf16[1,1,128,512]{3,2,1,0:T(8,128)(2,1)S(1)} %get-tuple-element.63), channel_id=1, source_target_pairs={{0,3},{1,2},{2,1},{3,0},{4,7},{5,6},{6,5},{7,4},{8,11},{9,10},{10,... | collective-permute-start | bytes 393224 | tf_op jit(solution)/shard_map/ppermute | solution.py:258
  57.6 6.2 %collective-permute-start.16 = (bf16[1,1,128,512]{3,2,1,0:T(8,128)(2,1)S(1)}, bf16[1,1,128,512]{3,2,1,0:T(8,128)(2,1)S(1)}, u32[]{:S(2)}, u32[]{:S(2)}) collective-permute-start(bf16[1,1,128,512]{3,2,1,0:T(8,128)(2,1)S(1)} %get-tuple-element.64), channel_id=1, source_target_pairs={{0,2},{1,3},{2,0},{3,1},{4,6},{5,7},{6,4},{7,5},{8,10},{9,11},{10,... | collective-permute-start | bytes 393224 | tf_op jit(solution)/shard_map/ppermute | solution.py:258
  58.4 5.6 %collective-permute-start.17 = (bf16[1,1,128,512]{3,2,1,0:T(8,128)(2,1)S(1)}, bf16[1,1,128,512]{3,2,1,0:T(8,128)(2,1)S(1)}, u32[]{:S(2)}, u32[]{:S(2)}) collective-permute-start(bf16[1,1,128,512]{3,2,1,0:T(8,128)(2,1)S(1)} %get-tuple-element.65), channel_id=1, source_target_pairs={{0,1},{1,0},{2,3},{3,2},{4,5},{5,4},{6,7},{7,6},{8,9},{9,8},{10,11... | collective-permute-start | bytes 393224 | tf_op jit(solution)/shard_map/ppermute | solution.py:258
  64.3 6.6 %collective-permute-start.19 = (bf16[1,128,512]{2,1,0:T(8,128)(2,1)S(1)}, bf16[1,128,512]{2,1,0:T(8,128)(2,1)S(1)}, u32[]{:S(2)}, u32[]{:S(2)}) collective-permute-start(bf16[1,128,512]{2,1,0:T(8,128)(2,1)S(1)} %get-tuple-element.69), channel_id=1, source_target_pairs={{0,3},{1,2},{2,1},{3,0},{4,7},{5,6},{6,5},{7,4},{8,11},{9,10},{10,... | collective-permute-start | bytes 393224 | tf_op jit(solution)/shard_map/ppermute | solution.py:258
  66.7 8.3 %collective-permute-start.20 = (bf16[1,128,512]{2,1,0:T(8,128)(2,1)S(1)}, bf16[1,128,512]{2,1,0:T(8,128)(2,1)S(1)}, u32[]{:S(2)}, u32[]{:S(2)}) collective-permute-start(bf16[1,128,512]{2,1,0:T(8,128)(2,1)S(1)} %get-tuple-element.71), channel_id=1, source_target_pairs={{0,2},{1,3},{2,0},{3,1},{4,6},{5,7},{6,4},{7,5},{8,10},{9,11},{10,... | collective-permute-start | bytes 393224 | tf_op jit(solution)/shard_map/ppermute | solution.py:258
  67.0 8.0 %collective-permute-start.21 = (bf16[1,128,512]{2,1,0:T(8,128)(2,1)S(1)}, bf16[1,128,512]{2,1,0:T(8,128)(2,1)S(1)}, u32[]{:S(2)}, u32[]{:S(2)}) collective-permute-start(bf16[1,128,512]{2,1,0:T(8,128)(2,1)S(1)} %get-tuple-element.73), channel_id=1, source_target_pairs={{0,1},{1,0},{2,3},{3,2},{4,5},{5,4},{6,7},{7,6},{8,9},{9,8},{10,11... | collective-permute-start | bytes 393224 | tf_op jit(solution)/shard_map/ppermute | solution.py:258
  67.9 7.1 %collective-permute-start.18 = (bf16[1,128,512]{2,1,0:T(8,128)(2,1)S(1)}, bf16[1,128,512]{2,1,0:T(8,128)(2,1)S(1)}, u32[]{:S(2)}, u32[]{:S(2)}) collective-permute-start(bf16[1,128,512]{2,1,0:T(8,128)(2,1)S(1)} %sums.1), channel_id=1, source_target_pairs={{0,4},{1,5},{2,6},{3,7},{4,0},{5,1},{6,2},{7,3},{8,12},{9,13},{10,... | collective-permute-start | bytes 393224 | tf_op jit(solution)/shard_map/ppermute | solution.py:264

commit v13 on v12

--- a/solution.py
+++ b/solution.py
@@ -42,12 +42,14 @@
 def pick_kernel(radix, groups, third, *outs):
     group, _ = place(radix)
     start = 0
-    for at, out in enumerate(outs):
-        base = wrap(group + at % (groups - 1) + 1, groups) * radix
-        for j in range(out.shape[0]):
-            for k in range(radix):
-                out[j, k] = third[0, start + j, 0, base + k]
-        start += out.shape[0] if at % (groups - 1) == groups - 2 else 0
+    for at in range(0, len(outs), groups - 1):
+        count = outs[at].shape[0]
+        for delta in range(1, groups):
+            base = wrap(group + delta, groups) * radix
+            for p in range(count):
+                j, k = divmod(start + p, radix)
+                outs[at + delta - 1][p] = third[0, j, 0, base + k]
+        start += count
 
 
 def second_kernel(radix, groups, second, *outs):
@@ -161,15 +163,16 @@
     )
 
 
-def off_sum_kernel(second_along, second_both, *refs):
-    offs = second_along.shape[0]
-    less = (len(refs) - 4) // (offs + 1)
-    got, thirds, outs = take(refs, 4, offs * less, less)
-    radix = thirds[0].shape[1]
+def off_sum_kernel(radix, second_along, second_both, *refs):
+    less = (len(refs) - 5) // 3
+    got, early, late, outs, (held,) = take(refs, 4, less, less, less, 1)
     _, member = place(radix)
     for d, out in enumerate(outs):
-        for j in range(offs):
-            mats = [thirds[j * less + d][0, jnp.bitwise_xor(member, i)] for i in range(radix)]
+        count = early[d].shape[0]
+        held[:count] = early[d][...]
+        held[count:] = late[d][...]
+        for j in range(out.shape[0]):
+            mats = [held[j * radix + jnp.bitwise_xor(member, i)] for i in range(radix)]
             slots = slots_of([ref[j, d] for ref in got], second_along, second_both, j, d + 1)
             out[j] = dot(jnp.concatenate(mats, axis=1), slots).astype(BF16)
 
@@ -184,7 +187,7 @@
     _, member = place(radix)
     for d, (third, out) in enumerate(zip(thirds, outs)):
         for j in range(out.shape[0]):
-            mats = [third[j, jnp.bitwise_xor(member, i)] for i in range(radix)]
+            mats = [third[jnp.bitwise_xor(member, i)] for i in range(radix)]
             slots = jnp.concatenate([ref[j, d] for ref in got], axis=0)
             out[j] = dot(jnp.concatenate(mats, axis=1), slots).astype(BF16)
 
@@ -263,7 +266,7 @@
         ]
         return lax.ppermute(array, "box", pairs)
 
-    def call(kernel, name, flops, outs, *args):
+    def call(kernel, name, flops, outs, *args, scratch=()):
         outs = [jax.ShapeDtypeStruct(shape, dtype) for shape, dtype in outs]
         size = sum(a.size * a.dtype.itemsize for a in [*args, *outs])
         return pl.pallas_call(
@@ -271,21 +274,23 @@
             out_shape=outs,
             in_specs=[VMEM] * len(args),
             out_specs=[VMEM] * len(outs),
+            scratch_shapes=list(scratch),
             compiler_params=pltpu.CompilerParams(vmem_limit_bytes=min(16 * MIB + 2 * size, 56 * MIB)),
             cost_estimate=pl.CostEstimate(flops=int(flops), bytes_accessed=0, transcendentals=0),
             name=name,
         )(*args)
 
+    early = radix + (offs - 1) * radix // 4
+    counts = [early, offs * radix - early, (butterflies - offs) * radix]
     picked = call(
         functools.partial(pick_kernel, radix, groups),
         "pick_third",
         0,
-        [((1, radix, rank, rank), BF16)] * (butterflies * less),
+        [((count, rank, rank), BF16) for count in counts for _ in range(less)],
         third_level,
     )
     thirds = [
-        [over_groups(a, d + 1) for d, a in enumerate(picked[j * less : (j + 1) * less])]
-        for j in range(butterflies)
+        [over_groups(a, d + 1) for d, a in enumerate(picked[at : at + less])] for at in range(0, len(picked), less)
     ]
 
     up_own, up_other, up_mid, off_rows, last_rows = call(
@@ -345,11 +350,11 @@
     )
     along = over_members(along, ALONG)
     across = over_members(across, ACROSS)
-    both = over_members(after(along, across, *[a for t in thirds[:offs] for a in t]), ACROSS)
+    both = over_members(after(along, across, *thirds[0], *thirds[1]), ACROSS)
     own = call(own_kernel, "own_levels", offs * own_flops, own_out(offs)[:3], leaf, up_own, up_mid)
     own_along = over_members(after(own[2], along), ALONG)
     sums = call(
-        off_sum_kernel,
+        functools.partial(off_sum_kernel, radix),
         "off_sums",
         offs * less * 2 * columns * rank * depth,
         [((offs, rank, columns), BF16)] * less,
@@ -358,12 +363,14 @@
         across,
         along,
         both,
-        *[a for j in range(offs) for a in thirds[j]],
+        *thirds[0],
+        *thirds[1],
+        scratch=[pltpu.VMEM((offs * radix, rank, rank), BF16)],
     )
     crossed = cross(sums)
     own = [
         own[0],
-        over_members(after(own[1], both, *thirds[-1]), ACROSS),
+        over_members(after(own[1], both, *thirds[2]), ACROSS),
         own_along,
     ]
     own.append(over_members(after(own_along, own[1], *sums), ACROSS))
@@ -390,7 +397,7 @@
         less * 2 * columns * rank * depth,
         [((1, rank, columns), BF16)] * less,
         *other,
-        *thirds[offs],
+        *thirds[2],
     )
     crossed = cross(sums)
     own = [over_members(after(a, *sums) if i else a, i) for i, a in enumerate(own)]

time: 77 us -> 78.4 us (1.018)
  waiting for transfers between devices: 31.6 us -> 37.3 us
  starting transfers between devices: 30.9 us -> 27 us
    ppermute x14, waiting for transfers between devices: 13.7 us -> 19.1 us  [over_members(): return array if mask == 0 else lax.ppermute(array, 'box', pairs)]
    ppermute x5, starting transfers between devices: 12.1 us -> 8.56 us  [over_groups(): return lax.ppermute(array, 'box', pairs)]
  transfers between devices with their start and end apart: 22 -> 22, of which waited for: 13 -> 15; matrix products, arithmetic and copies ran while one was open for 0% -> 0% of each run, Pallas kernels for 4% -> 4%
where the time goes in v13:
time: 78.4 us; the launch traced here: 78.1 us
  waiting for transfers between devices  37.3 us (48%)
  starting transfers between devices  27 us (34%)
  Pallas kernels  7.93 us (10%)
  local copies, waits for them, and re-layouts  5.83 us (7%)
    ppermute x14, waiting for transfers between devices, over_members(): return array if mask == 0 else lax.ppermute(array, 'box', pairs)  19.1 us
    ppermute x5, waiting for transfers between devices, over_groups(): return lax.ppermute(array, 'box', pairs)  16.3 us
    ppermute x14, starting transfers between devices, over_members(): return array if mask == 0 else lax.ppermute(array, 'box', pairs)  15.5 us
    ppermute x5, starting transfers between devices, over_groups(): return lax.ppermute(array, 'box', pairs)  8.56 us
    pallas_call x9, Pallas kernels, call(): pl.pallas_call(kernel, out_shape=outs, in_specs=[VMEM] * len(args), out_s...  6.48 us
    unnamed x20, local copies, waits for them, and re-layouts  5.83 us
    ppermute x3, starting transfers between devices, over_row(): return lax.ppermute(array, 'row', [(r, r ^ mask) for r in range(row_size)])  2.97 us
    ppermute x3, waiting for transfers between devices, over_row(): return lax.ppermute(array, 'row', [(r, r ^ mask) for r in range(row_size)])  1.9 us
  transfers between devices with their start and end apart: 22, of which 15 were waited for; matrix products, arithmetic and copies ran while one was open for 0% of the time, Pallas kernels for 4%

profile of v13, /device:TPU:0, one launch (start us, length us, event | category | flops | bytes accessed | tf_op | source)
XLA Modules:
  0.0 78.1 jit_solution(13979468426792328678)
XLA Ops:
  0.0 3.0 %collective-permute-start.3 = (bf16[2,256,512]{2,1,0:T(8,128)(2,1)}, bf16[2,256,512]{2,1,0:T(8,128)(2,1)S(1)}, u32[]{:S(2)}, u32[]{:S(2)}) collective-permute-start(bf16[2,256,512]{2,1,0:T(8,128)(2,1)} %refs_0_.1), channel_id=1, source_target_pairs={{0,16},{8,24},{16,0},{24,8},{1,17},{9,25},{17,1},{25,9},{2,18},{10... | collective-permute-start | bytes 1572872 | tf_op jit(solution)/shard_map/ppermute | solution.py:257
  3.0 1.1 %copy-done = bf16[1,3,1,8,128,128]{5,4,3,2,1,0:T(8,128)(2,1)S(1)} copy-done((bf16[1,3,1,8,128,128]{5,4,3,2,1,0:T(8,128)(2,1)S(1)}, bf16[1,3,1,8,128,128]{5,4,3,2,1,0:T(8,128)(2,1)}, u32[]{:S(2)}) %copy-start) | copy-done | bytes 786456
  4.1 2.7 %collective-permute-start.4 = (bf16[5,128,128]{2,1,0:T(8,128)(2,1)S(1)}, bf16[5,128,128]{2,1,0:T(8,128)(2,1)S(1)}, u32[]{:S(2)}, u32[]{:S(2)}) collective-permute-start(bf16[5,128,128]{2,1,0:T(8,128)(2,1)S(1)} %get-tuple-element.47), channel_id=1, source_target_pairs={{0,4},{1,5},{2,6},{3,7},{4,0},{5,1},{6,2},{7,3},{8,12},{9,13},{10,... | collective-permute-start | bytes 491528 | tf_op jit(solution)/shard_map/ppermute | solution.py:267
  6.8 1.1 %copy-done.2 = bf16[1,3,1,8,128,128]{5,4,3,2,1,0:T(8,128)(2,1)S(1)} copy-done((bf16[1,3,1,8,128,128]{5,4,3,2,1,0:T(8,128)(2,1)S(1)}, bf16[1,3,1,8,128,128]{5,4,3,2,1,0:T(8,128)(2,1)}, u32[]{:S(2)}) %copy-start.2) | copy-done | bytes 786456
  7.9 1.6 %collective-permute-start = (bf16[2,2,128,128]{3,2,1,0:T(8,128)(2,1)S(1)}, bf16[2,2,128,128]{3,2,1,0:T(8,128)(2,1)S(1)}, u32[]{:S(2)}, u32[]{:S(2)}) collective-permute-start(bf16[2,2,128,128]{3,2,1,0:T(8,128)(2,1)S(1)} %get-tuple-element.43), channel_id=1, source_target_pairs={{0,2},{1,3},{2,0},{3,1},{4,6},{5,7},{6,4},{7,5},{8,10},{9,11},{10,... | collective-permute-start | bytes 393224 | tf_op jit(solution)/shard_map/ppermute | solution.py:261
  9.6 1.4 %collective-permute-start.1 = (bf16[2,2,128,128]{3,2,1,0:T(8,128)(2,1)S(1)}, bf16[2,2,128,128]{3,2,1,0:T(8,128)(2,1)S(1)}, u32[]{:S(2)}, u32[]{:S(2)}) collective-permute-start(bf16[2,2,128,128]{3,2,1,0:T(8,128)(2,1)S(1)} %get-tuple-element.44), channel_id=1, source_target_pairs={{0,3},{1,2},{2,1},{3,0},{4,7},{5,6},{6,5},{7,4},{8,11},{9,10},{10,... | collective-permute-start | bytes 393224 | tf_op jit(solution)/shard_map/ppermute | solution.py:261
  11.0 0.0 collective-permute-start.2
  11.0 0.0 copy-done.3
  11.0 1.4 %copy-done.5 = bf16[1,3,1,4,4,128,128]{6,5,4,3,2,1,0:T(8,128)(2,1)S(1)} copy-done((bf16[1,3,1,4,4,128,128]{6,5,4,3,2,1,0:T(8,128)(2,1)S(1)}, bf16[1,3,1,4,4,128,128]{6,5,4,3,2,1,0:T(8,128)(2,1)}, u32[]{:S(2)}) %copy-start.5) | copy-done | bytes 1572888
  12.4 1.1 %copy-done.7 = bf16[1,3,2,512,128]{4,3,2,1,0:T(8,128)(2,1)S(1)} copy-done((bf16[1,3,2,512,128]{4,3,2,1,0:T(8,128)(2,1)S(1)}, bf16[1,3,2,512,128]{4,3,2,1,0:T(8,128)(2,1)}, u32[]{:S(2)}) %copy-start.7) | copy-done | bytes 786456
  13.5 1.0 %copy-done.9 = bf16[1,3,1,2,2,128,128]{6,5,4,3,2,1,0:T(8,128)(2,1)S(1)} copy-done((bf16[1,3,1,2,2,128,128]{6,5,4,3,2,1,0:T(8,128)(2,1)S(1)}, bf16[1,3,1,2,2,128,128]{6,5,4,3,2,1,0:T(8,128)(2,1)}, u32[]{:S(2)}) %copy-start.9) | copy-done | bytes 393240
  14.5 1.4 %weights.1 = (bf16[3,4,128,512]{3,2,1,0:T(8,128)(2,1)S(1)}, bf16[3,4,1,128,512]{4,3,2,1,0:T(8,128)(2,1)S(1)}, bf16[2,2,128,512]{3,2,1,0:T(8,128)(2,1)S(1)}, bf16...) custom-call(bf16[1,3,1,4,4,128,128]{6,5,4,3,2,1,0:T(8,128)(2,1)S(1)} %copy-done.5, ...), custom_call_target="tpu_custom_call" | custom-call | flops 603979776 | tf_op jit(solution)/shard_map/weights/pallas_call | solution.py:272
  15.9 0.4 collective-permute-done.second_along
  16.3 2.5 %collective-permute-done.1.second_both = bf16[2,2,128,128]{3,2,1,0:T(8,128)(2,1)S(1)} collective-permute-done((bf16[2,2,128,128]{3,2,1,0:T(8,128)(2,1)S(1)}, bf16[2,2,128,128]{3,2,1,0:T(8,128)(2,1)S(1)}, u32[]{:S(2)}, u32[]{:S(2)}) %collective-permute-start.1) | collective-permute-done | bytes 131104 | tf_op jit(solution)/shard_map/ppermute | solution.py:261
  18.8 0.0 collective-permute-done.4.refs_4_
  18.8 0.0 collective-permute-done.3.refs_2_
  18.8 0.0 collective-permute-start.5
  18.8 0.0 collective-permute-done.2.refs_1_
  18.8 1.9 %collective-permute-done.5.refs_3_ = bf16[2,256,512]{2,1,0:T(8,128)(2,1)S(1)} collective-permute-done((bf16[2,256,512]{2,1,0:T(8,128)(2,1)S(1)}, bf16[2,256,512]{2,1,0:T(8,128)(2,1)S(1)}, u32[]{:S(2)}, u32[]{:S(2)}) %collective-permute-start.5) | collective-permute-done | bytes 524320 | tf_op jit(solution)/shard_map/ppermute | solution.py:257
  20.7 0.0 copy-done.4
  20.7 0.0 copy-done.8
  20.7 1.0 %off_levels.1 = (bf16[2,512,512]{2,1,0:T(8,128)(2,1)S(1)}, bf16[2,1,128,512]{3,2,1,0:T(8,128)(2,1)S(1)}, bf16[2,1,128,512]{3,2,1,0:T(8,128)(2,1)S(1)}, bf16[2,1,128,512]{3,2,1,0:T(8,128)(2,1)S(1)}) custom-call(bf16[1,3,4,256,128]{4,3,2,1,0:T(8,128)(2,1)S(1)} %copy-done.4, bf16[3,4,1,128,512]{4,3,2,1,0:T(8,128)(2,1)S(1)} %get-tuple-element.42.up_other, ...), custom_call_target="tpu_custom_call" | custom-call | flops 805306368 | tf_op jit(solution)/shard_map/off_levels/pallas_call | solution.py:272
  21.8 0.6 collective-permute-start.6
  22.4 0.2 collective-permute-start.7
  22.6 2.8 %collective-permute-start.8 = (bf16[3,128,128]{2,1,0:T(8,128)(2,1)S(1)}, bf16[3,128,128]{2,1,0:T(8,128)(2,1)S(1)}, u32[]{:S(2)}, u32[]{:S(2)}) collective-permute-start(bf16[3,128,128]{2,1,0:T(8,128)(2,1)S(1)} %get-tuple-element.52), channel_id=1, source_target_pairs={{0,4},{1,5},{2,6},{3,7},{4,0},{5,1},{6,2},{7,3},{8,12},{9,13},{10,... | collective-permute-start | bytes 294920 | tf_op jit(solution)/shard_map/ppermute | solution.py:267
  25.4 4.9 %collective-permute-done.8.refs_5_ = bf16[3,128,128]{2,1,0:T(8,128)(2,1)S(1)} collective-permute-done((bf16[3,128,128]{2,1,0:T(8,128)(2,1)S(1)}, bf16[3,128,128]{2,1,0:T(8,128)(2,1)S(1)}, u32[]{:S(2)}, u32[]{:S(2)}) %collective-permute-start.8) | collective-permute-done | bytes 98336 | tf_op jit(solution)/shard_map/ppermute | solution.py:267
  30.4 0.0 collective-permute-done.6.refs_1_
  30.4 2.2 %collective-permute-done.7.refs_2_ = bf16[2,1,128,512]{3,2,1,0:T(8,128)(2,1)S(1)} collective-permute-done((bf16[2,1,128,512]{3,2,1,0:T(8,128)(2,1)S(1)}, bf16[2,1,128,512]{3,2,1,0:T(8,128)(2,1)S(1)}, u32[]{:S(2)}, u32[]{:S(2)}) %collective-permute-start.7) | collective-permute-done | bytes 262176 | tf_op jit(solution)/shard_map/ppermute | solution.py:261
  32.5 1.5 %collective-permute-start.9 = (bf16[2,1,128,512]{3,2,1,0:T(8,128)(2,1)S(1)}, bf16[2,1,128,512]{3,2,1,0:T(8,128)(2,1)S(1)}, u32[]{:S(2)}, u32[]{:S(2)}) collective-permute-start(bf16[2,1,128,512]{3,2,1,0:T(8,128)(2,1)S(1)} %collective-permute-done.7.refs_2_), channel_id=1, source_target_pairs={{0,1},{1,0},{2,3},{3,2},{4,5},{5,4},{6,7},{7,6},{8,9},{9,8},{10,11... | collective-permute-start | bytes 786440 | tf_op jit(solution)/shard_map/ppermute | solution.py:261
  34.0 1.2 %collective-permute-start.11 = (bf16[4,128,128]{2,1,0:T(8,128)(2,1)S(1)}, bf16[4,128,128]{2,1,0:T(8,128)(2,1)S(1)}, u32[]{:S(2)}, u32[]{:S(2)}) collective-permute-start(bf16[4,128,128]{2,1,0:T(8,128)(2,1)S(1)} %get-tuple-element.57), channel_id=1, source_target_pairs={{0,4},{1,5},{2,6},{3,7},{4,0},{5,1},{6,2},{7,3},{8,12},{9,13},{10,... | collective-permute-start | bytes 393224 | tf_op jit(solution)/shard_map/ppermute | solution.py:267
  35.2 0.6 own_levels.1
  35.8 0.0 copy-start.1
  35.8 0.0 copy-start.6
  35.8 1.9 %collective-permute-start.13 = (bf16[2,128,512]{2,1,0:T(8,128)(2,1)S(1)}, bf16[2,128,512]{2,1,0:T(8,128)(2,1)S(1)}, u32[]{:S(2)}, u32[]{:S(2)}) collective-permute-start(bf16[2,128,512]{2,1,0:T(8,128)(2,1)S(1)} %get-tuple-element.60), channel_id=1, source_target_pairs={{0,2},{1,3},{2,0},{3,1},{4,6},{5,7},{6,4},{7,5},{8,10},{9,11},{10,... | collective-permute-start | bytes 786440 | tf_op jit(solution)/shard_map/ppermute | solution.py:261
  37.8 3.8 %collective-permute-done.11.refs_4_ = bf16[4,128,128]{2,1,0:T(8,128)(2,1)S(1)} collective-permute-done((bf16[4,128,128]{2,1,0:T(8,128)(2,1)S(1)}, bf16[4,128,128]{2,1,0:T(8,128)(2,1)S(1)}, u32[]{:S(2)}, u32[]{:S(2)}) %collective-permute-start.11) | collective-permute-done | bytes 131104 | tf_op jit(solution)/shard_map/ppermute | solution.py:267
  41.6 0.0 collective-permute-done.9.refs_3_
  41.6 0.5 collective-permute-start.12
  42.1 0.6 off_sums.1
  42.7 0.9 %collective-permute-start.10 = (bf16[2,128,512]{2,1,0:T(8,128)(2,1)S(1)}, bf16[2,128,512]{2,1,0:T(8,128)(2,1)S(1)}, u32[]{:S(2)}, u32[]{:S(2)}) collective-permute-start(bf16[2,128,512]{2,1,0:T(8,128)(2,1)S(1)} %off_sums.1), channel_id=1, source_target_pairs={{0,4},{1,5},{2,6},{3,7},{4,0},{5,1},{6,2},{7,3},{8,12},{9,13},{10,... | collective-permute-start | bytes 786440 | tf_op jit(solution)/shard_map/ppermute | solution.py:267
  43.6 2.9 %collective-permute-done.13.refs_3_ = bf16[2,128,512]{2,1,0:T(8,128)(2,1)S(1)} collective-permute-done((bf16[2,128,512]{2,1,0:T(8,128)(2,1)S(1)}, bf16[2,128,512]{2,1,0:T(8,128)(2,1)S(1)}, u32[]{:S(2)}, u32[]{:S(2)}) %collective-permute-start.13) | collective-permute-done | bytes 262176 | tf_op jit(solution)/shard_map/ppermute | solution.py:261
  46.5 1.9 %collective-permute-done.12.refs_2_ = bf16[2,128,512]{2,1,0:T(8,128)(2,1)S(1)} collective-permute-done((bf16[2,128,512]{2,1,0:T(8,128)(2,1)S(1)}, bf16[2,128,512]{2,1,0:T(8,128)(2,1)S(1)}, u32[]{:S(2)}, u32[]{:S(2)}) %collective-permute-start.12) | collective-permute-done | bytes 262176 | tf_op jit(solution)/shard_map/ppermute | solution.py:261
  48.4 0.6 collective-permute-start.14
  49.0 6.0 %collective-permute-done.10.refs_0_ = bf16[2,128,512]{2,1,0:T(8,128)(2,1)S(1)} collective-permute-done((bf16[2,128,512]{2,1,0:T(8,128)(2,1)S(1)}, bf16[2,128,512]{2,1,0:T(8,128)(2,1)S(1)}, u32[]{:S(2)}, u32[]{:S(2)}) %collective-permute-start.10) | collective-permute-done | bytes 262176 | tf_op jit(solution)/shard_map/ppermute | solution.py:267
  55.0 0.0 collective-permute-done.14.refs_4_
  55.0 0.0 copy-done.1
  55.0 0.0 copy-done.6
  55.0 2.2 %middle_levels.1 = (f32[1024,512]{1,0:T(8,128)S(1)}, bf16[512,512]{1,0:T(8,128)(2,1)S(1)}, bf16[1,1,128,512]{3,2,1,0:T(8,128)(2,1)S(1)}, bf16[1,1,128,512]{3,2,1...) custom-call(bf16[1,3,1,8,128,128]{5,4,3,2,1,0:T(8,128)(2,1)S(1)} %copy-done.1, ...), custom_call_target="tpu_custom_call" | custom-call | flops 1342177280 | tf_op jit(solution)/shard_map/middle_levels/pallas_call | solution.py:272
  57.2 1.1 %collective-permute-start.15 = (bf16[1,1,128,512]{3,2,1,0:T(8,128)(2,1)S(1)}, bf16[1,1,128,512]{3,2,1,0:T(8,128)(2,1)S(1)}, u32[]{:S(2)}, u32[]{:S(2)}) collective-permute-start(bf16[1,1,128,512]{3,2,1,0:T(8,128)(2,1)S(1)} %get-tuple-element.63), channel_id=1, source_target_pairs={{0,3},{1,2},{2,1},{3,0},{4,7},{5,6},{6,5},{7,4},{8,11},{9,10},{10,... | collective-permute-start | bytes 393224 | tf_op jit(solution)/shard_map/ppermute | solution.py:261
  58.3 1.9 %collective-permute-start.16 = (bf16[1,1,128,512]{3,2,1,0:T(8,128)(2,1)S(1)}, bf16[1,1,128,512]{3,2,1,0:T(8,128)(2,1)S(1)}, u32[]{:S(2)}, u32[]{:S(2)}) collective-permute-start(bf16[1,1,128,512]{3,2,1,0:T(8,128)(2,1)S(1)} %get-tuple-element.64), channel_id=1, source_target_pairs={{0,2},{1,3},{2,0},{3,1},{4,6},{5,7},{6,4},{7,5},{8,10},{9,11},{10,... | collective-permute-start | bytes 393224 | tf_op jit(solution)/shard_map/ppermute | solution.py:261
  60.2 0.6 collective-permute-start.17
  60.8 0.4 last_own_levels.1
  61.2 2.0 %collective-permute-done.15.refs_0_ = bf16[1,1,128,512]{3,2,1,0:T(8,128)(2,1)S(1)} collective-permute-done((bf16[1,1,128,512]{3,2,1,0:T(8,128)(2,1)S(1)}, bf16[1,1,128,512]{3,2,1,0:T(8,128)(2,1)S(1)}, u32[]{:S(2)}, u32[]{:S(2)}) %collective-permute-start.15) | collective-permute-done | bytes 131104 | tf_op jit(solution)/shard_map/ppermute | solution.py:261
  63.3 2.0 %collective-permute-done.16.refs_1_ = bf16[1,1,128,512]{3,2,1,0:T(8,128)(2,1)S(1)} collective-permute-done((bf16[1,1,128,512]{3,2,1,0:T(8,128)(2,1)S(1)}, bf16[1,1,128,512]{3,2,1,0:T(8,128)(2,1)S(1)}, u32[]{:S(2)}, u32[]{:S(2)}) %collective-permute-start.16) | collective-permute-done | bytes 131104 | tf_op jit(solution)/shard_map/ppermute | solution.py:261
  65.2 0.1 collective-permute-done.17.refs_2_
  65.3 0.2 sums.1
  65.5 1.5 %collective-permute-start.19 = (bf16[1,128,512]{2,1,0:T(8,128)(2,1)S(1)}, bf16[1,128,512]{2,1,0:T(8,128)(2,1)S(1)}, u32[]{:S(2)}, u32[]{:S(2)}) collective-permute-start(bf16[1,128,512]{2,1,0:T(8,128)(2,1)S(1)} %get-tuple-element.69), channel_id=1, source_target_pairs={{0,3},{1,2},{2,1},{3,0},{4,7},{5,6},{6,5},{7,4},{8,11},{9,10},{10,... | collective-permute-start | bytes 393224 | tf_op jit(solution)/shard_map/ppermute | solution.py:261
  67.0 1.4 %collective-permute-start.20 = (bf16[1,128,512]{2,1,0:T(8,128)(2,1)S(1)}, bf16[1,128,512]{2,1,0:T(8,128)(2,1)S(1)}, u32[]{:S(2)}, u32[]{:S(2)}) collective-permute-start(bf16[1,128,512]{2,1,0:T(8,128)(2,1)S(1)} %get-tuple-element.71), channel_id=1, source_target_pairs={{0,2},{1,3},{2,0},{3,1},{4,6},{5,7},{6,4},{7,5},{8,10},{9,11},{10,... | collective-permute-start | bytes 393224 | tf_op jit(solution)/shard_map/ppermute | solution.py:261
  68.5 0.6 collective-permute-start.21
  69.1 1.0 %collective-permute-start.18 = (bf16[1,128,512]{2,1,0:T(8,128)(2,1)S(1)}, bf16[1,128,512]{2,1,0:T(8,128)(2,1)S(1)}, u32[]{:S(2)}, u32[]{:S(2)}) collective-permute-start(bf16[1,128,512]{2,1,0:T(8,128)(2,1)S(1)} %sums.1), channel_id=1, source_target_pairs={{0,4},{1,5},{2,6},{3,7},{4,0},{5,1},{6,2},{7,3},{8,12},{9,13},{10,... | collective-permute-start | bytes 393224 | tf_op jit(solution)/shard_map/ppermute | solution.py:267
  70.1 3.5 %collective-permute-done.19.refs_1_ = bf16[1,128,512]{2,1,0:T(8,128)(2,1)S(1)} collective-permute-done((bf16[1,128,512]{2,1,0:T(8,128)(2,1)S(1)}, bf16[1,128,512]{2,1,0:T(8,128)(2,1)S(1)}, u32[]{:S(2)}, u32[]{:S(2)}) %collective-permute-start.19) | collective-permute-done | bytes 131104 | tf_op jit(solution)/shard_map/ppermute | solution.py:261
  73.6 1.6 %collective-permute-done.20.refs_2_ = bf16[1,128,512]{2,1,0:T(8,128)(2,1)S(1)} collective-permute-done((bf16[1,128,512]{2,1,0:T(8,128)(2,1)S(1)}, bf16[1,128,512]{2,1,0:T(8,128)(2,1)S(1)}, u32[]{:S(2)}, u32[]{:S(2)}) %collective-permute-start.20) | collective-permute-done | bytes 131104 | tf_op jit(solution)/shard_map/ppermute | solution.py:261
  75.2 0.0 collective-permute-done.21.refs_3_
  75.2 1.5 %collective-permute-done.18.refs_0_ = bf16[1,128,512]{2,1,0:T(8,128)(2,1)S(1)} collective-permute-done((bf16[1,128,512]{2,1,0:T(8,128)(2,1)S(1)}, bf16[1,128,512]{2,1,0:T(8,128)(2,1)S(1)}, u32[]{:S(2)}, u32[]{:S(2)}) %collective-permute-start.18) | collective-permute-done | bytes 131104 | tf_op jit(solution)/shard_map/ppermute | solution.py:267
  76.7 1.5 %last_levels.1 = bf16[1,1024,512]{2,1,0:T(8,128)(2,1)} custom-call(bf16[1,3,1,8,128,128]{5,4,3,2,1,0:T(8,128)(2,1)S(1)} %copy-done.1, bf16[1024,256]{1,0:T(8,128)(2,1)S(1)} %get-tuple-element.40.row_mats, f32[1024,512]{1,0:T(8,128)S(1)} %get-tuple-element.62.residual, bf16[1,128,512]{2,1,0:T(8,128)(2,1)S(1)} %collective-permute-done.18.refs_0_, ...), custom_call_target="tpu_custom_call" | custom-call | flops 335544320 | tf_op jit(solution)/shard_map/last_levels/pallas_call | solution.py:405
  (10 shorter events, 0.1 us)
Async XLA Ops:
  0.0 18.8 %collective-permute-start.3 = (bf16[2,256,512]{2,1,0:T(8,128)(2,1)}, bf16[2,256,512]{2,1,0:T(8,128)(2,1)S(1)}, u32[]{:S(2)}, u32[]{:S(2)}) collective-permute-start(bf16[2,256,512]{2,1,0:T(8,128)(2,1)} %refs_0_.1), channel_id=1, source_target_pairs={{0,16},{8,24},{16,0},{24,8},{1,17},{9,25},{17,1},{25,9},{2,18},{10... | collective-permute-start | bytes 1572872 | tf_op jit(solution)/shard_map/ppermute | solution.py:257
  3.0 1.1 %copy-start = (bf16[1,3,1,8,128,128]{5,4,3,2,1,0:T(8,128)(2,1)S(1)}, bf16[1,3,1,8,128,128]{5,4,3,2,1,0:T(8,128)(2,1)}, u32[]{:S(2)}) copy-start(bf16[1,3,1,8,128,128]{5,4,3,2,1,0:T(8,128)(2,1)} %third.5) | copy-start | bytes 2359300
  4.1 6.9 %copy-start.3 = (bf16[1,3,1,8,128,128]{5,4,3,2,1,0:T(8,128)(2,1)S(1)}, bf16[1,3,1,8,128,128]{5,4,3,2,1,0:T(8,128)(2,1)}, u32[]{:S(2)}) copy-start(bf16[1,3,1,8,128,128]{5,4,3,2,1,0:T(8,128)(2,1)} %second.3) | copy-start | bytes 2359300
  4.1 14.7 %collective-permute-start.4 = (bf16[5,128,128]{2,1,0:T(8,128)(2,1)S(1)}, bf16[5,128,128]{2,1,0:T(8,128)(2,1)S(1)}, u32[]{:S(2)}, u32[]{:S(2)}) collective-permute-start(bf16[5,128,128]{2,1,0:T(8,128)(2,1)S(1)} %get-tuple-element.47), channel_id=1, source_target_pairs={{0,4},{1,5},{2,6},{3,7},{4,0},{5,1},{6,2},{7,3},{8,12},{9,13},{10,... | collective-permute-start | bytes 491528 | tf_op jit(solution)/shard_map/ppermute | solution.py:267
  6.8 1.1 %copy-start.2 = (bf16[1,3,1,8,128,128]{5,4,3,2,1,0:T(8,128)(2,1)S(1)}, bf16[1,3,1,8,128,128]{5,4,3,2,1,0:T(8,128)(2,1)}, u32[]{:S(2)}) copy-start(bf16[1,3,1,8,128,128]{5,4,3,2,1,0:T(8,128)(2,1)} %second.3) | copy-start | bytes 2359300
  7.9 8.4 %collective-permute-start = (bf16[2,2,128,128]{3,2,1,0:T(8,128)(2,1)S(1)}, bf16[2,2,128,128]{3,2,1,0:T(8,128)(2,1)S(1)}, u32[]{:S(2)}, u32[]{:S(2)}) collective-permute-start(bf16[2,2,128,128]{3,2,1,0:T(8,128)(2,1)S(1)} %get-tuple-element.43), channel_id=1, source_target_pairs={{0,2},{1,3},{2,0},{3,1},{4,6},{5,7},{6,4},{7,5},{8,10},{9,11},{10,... | collective-permute-start | bytes 393224 | tf_op jit(solution)/shard_map/ppermute | solution.py:261
  9.6 11.2 %copy-start.4 = (bf16[1,3,4,256,128]{4,3,2,1,0:T(8,128)(2,1)S(1)}, bf16[1,3,4,256,128]{4,3,2,1,0:T(8,128)(2,1)}, u32[]{:S(2)}) copy-start(bf16[1,3,4,256,128]{4,3,2,1,0:T(8,128)(2,1)} %basis.3) | copy-start | bytes 2359300
  9.6 9.2 %collective-permute-start.1 = (bf16[2,2,128,128]{3,2,1,0:T(8,128)(2,1)S(1)}, bf16[2,2,128,128]{3,2,1,0:T(8,128)(2,1)S(1)}, u32[]{:S(2)}, u32[]{:S(2)}) collective-permute-start(bf16[2,2,128,128]{3,2,1,0:T(8,128)(2,1)S(1)} %get-tuple-element.44), channel_id=1, source_target_pairs={{0,3},{1,2},{2,1},{3,0},{4,7},{5,6},{6,5},{7,4},{8,11},{9,10},{10,... | collective-permute-start | bytes 393224 | tf_op jit(solution)/shard_map/ppermute | solution.py:261
  11.0 7.9 %collective-permute-start.2 = (bf16[2,256,512]{2,1,0:T(8,128)(2,1)}, bf16[2,256,512]{2,1,0:T(8,128)(2,1)S(1)}, u32[]{:S(2)}, u32[]{:S(2)}) collective-permute-start(bf16[2,256,512]{2,1,0:T(8,128)(2,1)} %refs_0_.1), channel_id=1, source_target_pairs={{0,8},{8,0},{16,24},{24,16},{1,9},{9,1},{17,25},{25,17},{2,10},{10... | collective-permute-start | bytes 1572872 | tf_op jit(solution)/shard_map/ppermute | solution.py:257
  11.0 1.4 %copy-start.5 = (bf16[1,3,1,4,4,128,128]{6,5,4,3,2,1,0:T(8,128)(2,1)S(1)}, bf16[1,3,1,4,4,128,128]{6,5,4,3,2,1,0:T(8,128)(2,1)}, u32[]{:S(2)}) copy-start(bf16[1,3,1,4,4,128,128]{6,5,4,3,2,1,0:T(8,128)(2,1)} %first.1) | copy-start | bytes 4718596
  12.4 1.1 %copy-start.7 = (bf16[1,3,2,512,128]{4,3,2,1,0:T(8,128)(2,1)S(1)}, bf16[1,3,2,512,128]{4,3,2,1,0:T(8,128)(2,1)}, u32[]{:S(2)}) copy-start(bf16[1,3,2,512,128]{4,3,2,1,0:T(8,128)(2,1)} %out_basis.1) | copy-start | bytes 2359300
  13.5 1.0 %copy-start.9 = (bf16[1,3,1,2,2,128,128]{6,5,4,3,2,1,0:T(8,128)(2,1)S(1)}, bf16[1,3,1,2,2,128,128]{6,5,4,3,2,1,0:T(8,128)(2,1)}, u32[]{:S(2)}) copy-start(bf16[1,3,1,2,2,128,128]{6,5,4,3,2,1,0:T(8,128)(2,1)} %fourth.1) | copy-start | bytes 1179652
  14.5 6.2 %copy-start.8 = (bf16[2,256,512]{2,1,0:T(8,128)(2,1)S(1)}, bf16[2,256,512]{2,1,0:T(8,128)(2,1)}, u32[]{:S(2)}) copy-start(bf16[2,256,512]{2,1,0:T(8,128)(2,1)} %refs_0_.1) | copy-start | bytes 1572868
  18.8 1.9 %collective-permute-start.5 = (bf16[2,256,512]{2,1,0:T(8,128)(2,1)S(1)}, bf16[2,256,512]{2,1,0:T(8,128)(2,1)S(1)}, u32[]{:S(2)}, u32[]{:S(2)}) collective-permute-start(bf16[2,256,512]{2,1,0:T(8,128)(2,1)S(1)} %collective-permute-done.3.refs_2_), channel_id=1, source_target_pairs={{0,8},{8,0},{16,24},{24,16},{1,9},{9,1},{17,25},{25,17},{2,10},{10... | collective-permute-start | bytes 1572872 | tf_op jit(solution)/shard_map/ppermute | solution.py:257
  21.8 8.6 %collective-permute-start.6 = (bf16[2,1,128,512]{3,2,1,0:T(8,128)(2,1)S(1)}, bf16[2,1,128,512]{3,2,1,0:T(8,128)(2,1)S(1)}, u32[]{:S(2)}, u32[]{:S(2)}) collective-permute-start(bf16[2,1,128,512]{3,2,1,0:T(8,128)(2,1)S(1)} %get-tuple-element.50), channel_id=1, source_target_pairs={{0,1},{1,0},{2,3},{3,2},{4,5},{5,4},{6,7},{7,6},{8,9},{9,8},{10,11... | collective-permute-start | bytes 786440 | tf_op jit(solution)/shard_map/ppermute | solution.py:261
  22.4 10.2 %collective-permute-start.7 = (bf16[2,1,128,512]{3,2,1,0:T(8,128)(2,1)S(1)}, bf16[2,1,128,512]{3,2,1,0:T(8,128)(2,1)S(1)}, u32[]{:S(2)}, u32[]{:S(2)}) collective-permute-start(bf16[2,1,128,512]{3,2,1,0:T(8,128)(2,1)S(1)} %get-tuple-element.51), channel_id=1, source_target_pairs={{0,2},{1,3},{2,0},{3,1},{4,6},{5,7},{6,4},{7,5},{8,10},{9,11},{10,... | collective-permute-start | bytes 786440 | tf_op jit(solution)/shard_map/ppermute | solution.py:261
  22.6 7.8 %collective-permute-start.8 = (bf16[3,128,128]{2,1,0:T(8,128)(2,1)S(1)}, bf16[3,128,128]{2,1,0:T(8,128)(2,1)S(1)}, u32[]{:S(2)}, u32[]{:S(2)}) collective-permute-start(bf16[3,128,128]{2,1,0:T(8,128)(2,1)S(1)} %get-tuple-element.52), channel_id=1, source_target_pairs={{0,4},{1,5},{2,6},{3,7},{4,0},{5,1},{6,2},{7,3},{8,12},{9,13},{10,... | collective-permute-start | bytes 294920 | tf_op jit(solution)/shard_map/ppermute | solution.py:267
  32.5 9.1 %collective-permute-start.9 = (bf16[2,1,128,512]{3,2,1,0:T(8,128)(2,1)S(1)}, bf16[2,1,128,512]{3,2,1,0:T(8,128)(2,1)S(1)}, u32[]{:S(2)}, u32[]{:S(2)}) collective-permute-start(bf16[2,1,128,512]{3,2,1,0:T(8,128)(2,1)S(1)} %collective-permute-done.7.refs_2_), channel_id=1, source_target_pairs={{0,1},{1,0},{2,3},{3,2},{4,5},{5,4},{6,7},{7,6},{8,9},{9,8},{10,11... | collective-permute-start | bytes 786440 | tf_op jit(solution)/shard_map/ppermute | solution.py:261
  34.0 7.6 %collective-permute-start.11 = (bf16[4,128,128]{2,1,0:T(8,128)(2,1)S(1)}, bf16[4,128,128]{2,1,0:T(8,128)(2,1)S(1)}, u32[]{:S(2)}, u32[]{:S(2)}) collective-permute-start(bf16[4,128,128]{2,1,0:T(8,128)(2,1)S(1)} %get-tuple-element.57), channel_id=1, source_target_pairs={{0,4},{1,5},{2,6},{3,7},{4,0},{5,1},{6,2},{7,3},{8,12},{9,13},{10,... | collective-permute-start | bytes 393224 | tf_op jit(solution)/shard_map/ppermute | solution.py:267
  35.8 19.2 %copy-start.1 = (bf16[1,3,1,8,128,128]{5,4,3,2,1,0:T(8,128)(2,1)S(1)}, bf16[1,3,1,8,128,128]{5,4,3,2,1,0:T(8,128)(2,1)}, u32[]{:S(2)}) copy-start(bf16[1,3,1,8,128,128]{5,4,3,2,1,0:T(8,128)(2,1)} %third.5) | copy-start | bytes 2359300
  35.8 19.2 %copy-start.6 = (bf16[1,1024,512]{2,1,0:T(8,128)(2,1)S(1)}, bf16[1,1024,512]{2,1,0:T(8,128)(2,1)}, u32[]{:S(2)}) copy-start(bf16[1,1024,512]{2,1,0:T(8,128)(2,1)} %rhs.1) | copy-start | bytes 3145732
  35.8 10.7 %collective-permute-start.13 = (bf16[2,128,512]{2,1,0:T(8,128)(2,1)S(1)}, bf16[2,128,512]{2,1,0:T(8,128)(2,1)S(1)}, u32[]{:S(2)}, u32[]{:S(2)}) collective-permute-start(bf16[2,128,512]{2,1,0:T(8,128)(2,1)S(1)} %get-tuple-element.60), channel_id=1, source_target_pairs={{0,2},{1,3},{2,0},{3,1},{4,6},{5,7},{6,4},{7,5},{8,10},{9,11},{10,... | collective-permute-start | bytes 786440 | tf_op jit(solution)/shard_map/ppermute | solution.py:261
  41.6 6.8 %collective-permute-start.12 = (bf16[2,128,512]{2,1,0:T(8,128)(2,1)S(1)}, bf16[2,128,512]{2,1,0:T(8,128)(2,1)S(1)}, u32[]{:S(2)}, u32[]{:S(2)}) collective-permute-start(bf16[2,128,512]{2,1,0:T(8,128)(2,1)S(1)} %get-tuple-element.58), channel_id=1, source_target_pairs={{0,1},{1,0},{2,3},{3,2},{4,5},{5,4},{6,7},{7,6},{8,9},{9,8},{10,11... | collective-permute-start | bytes 786440 | tf_op jit(solution)/shard_map/ppermute | solution.py:261
  42.7 12.3 %collective-permute-start.10 = (bf16[2,128,512]{2,1,0:T(8,128)(2,1)S(1)}, bf16[2,128,512]{2,1,0:T(8,128)(2,1)S(1)}, u32[]{:S(2)}, u32[]{:S(2)}) collective-permute-start(bf16[2,128,512]{2,1,0:T(8,128)(2,1)S(1)} %off_sums.1), channel_id=1, source_target_pairs={{0,4},{1,5},{2,6},{3,7},{4,0},{5,1},{6,2},{7,3},{8,12},{9,13},{10,... | collective-permute-start | bytes 786440 | tf_op jit(solution)/shard_map/ppermute | solution.py:267
  48.4 6.6 %collective-permute-start.14 = (bf16[2,128,512]{2,1,0:T(8,128)(2,1)S(1)}, bf16[2,128,512]{2,1,0:T(8,128)(2,1)S(1)}, u32[]{:S(2)}, u32[]{:S(2)}) collective-permute-start(bf16[2,128,512]{2,1,0:T(8,128)(2,1)S(1)} %collective-permute-done.13.refs_3_), channel_id=1, source_target_pairs={{0,1},{1,0},{2,3},{3,2},{4,5},{5,4},{6,7},{7,6},{8,9},{9,8},{10,11... | collective-permute-start | bytes 786440 | tf_op jit(solution)/shard_map/ppermute | solution.py:261
  57.2 6.0 %collective-permute-start.15 = (bf16[1,1,128,512]{3,2,1,0:T(8,128)(2,1)S(1)}, bf16[1,1,128,512]{3,2,1,0:T(8,128)(2,1)S(1)}, u32[]{:S(2)}, u32[]{:S(2)}) collective-permute-start(bf16[1,1,128,512]{3,2,1,0:T(8,128)(2,1)S(1)} %get-tuple-element.63), channel_id=1, source_target_pairs={{0,3},{1,2},{2,1},{3,0},{4,7},{5,6},{6,5},{7,4},{8,11},{9,10},{10,... | collective-permute-start | bytes 393224 | tf_op jit(solution)/shard_map/ppermute | solution.py:261
  58.3 6.9 %collective-permute-start.16 = (bf16[1,1,128,512]{3,2,1,0:T(8,128)(2,1)S(1)}, bf16[1,1,128,512]{3,2,1,0:T(8,128)(2,1)S(1)}, u32[]{:S(2)}, u32[]{:S(2)}) collective-permute-start(bf16[1,1,128,512]{3,2,1,0:T(8,128)(2,1)S(1)} %get-tuple-element.64), channel_id=1, source_target_pairs={{0,2},{1,3},{2,0},{3,1},{4,6},{5,7},{6,4},{7,5},{8,10},{9,11},{10,... | collective-permute-start | bytes 393224 | tf_op jit(solution)/shard_map/ppermute | solution.py:261
  60.2 5.1 %collective-permute-start.17 = (bf16[1,1,128,512]{3,2,1,0:T(8,128)(2,1)S(1)}, bf16[1,1,128,512]{3,2,1,0:T(8,128)(2,1)S(1)}, u32[]{:S(2)}, u32[]{:S(2)}) collective-permute-start(bf16[1,1,128,512]{3,2,1,0:T(8,128)(2,1)S(1)} %get-tuple-element.65), channel_id=1, source_target_pairs={{0,1},{1,0},{2,3},{3,2},{4,5},{5,4},{6,7},{7,6},{8,9},{9,8},{10,11... | collective-permute-start | bytes 393224 | tf_op jit(solution)/shard_map/ppermute | solution.py:261
  65.5 8.1 %collective-permute-start.19 = (bf16[1,128,512]{2,1,0:T(8,128)(2,1)S(1)}, bf16[1,128,512]{2,1,0:T(8,128)(2,1)S(1)}, u32[]{:S(2)}, u32[]{:S(2)}) collective-permute-start(bf16[1,128,512]{2,1,0:T(8,128)(2,1)S(1)} %get-tuple-element.69), channel_id=1, source_target_pairs={{0,3},{1,2},{2,1},{3,0},{4,7},{5,6},{6,5},{7,4},{8,11},{9,10},{10,... | collective-permute-start | bytes 393224 | tf_op jit(solution)/shard_map/ppermute | solution.py:261
  67.0 8.1 %collective-permute-start.20 = (bf16[1,128,512]{2,1,0:T(8,128)(2,1)S(1)}, bf16[1,128,512]{2,1,0:T(8,128)(2,1)S(1)}, u32[]{:S(2)}, u32[]{:S(2)}) collective-permute-start(bf16[1,128,512]{2,1,0:T(8,128)(2,1)S(1)} %get-tuple-element.71), channel_id=1, source_target_pairs={{0,2},{1,3},{2,0},{3,1},{4,6},{5,7},{6,4},{7,5},{8,10},{9,11},{10,... | collective-permute-start | bytes 393224 | tf_op jit(solution)/shard_map/ppermute | solution.py:261
  68.5 6.7 %collective-permute-start.21 = (bf16[1,128,512]{2,1,0:T(8,128)(2,1)S(1)}, bf16[1,128,512]{2,1,0:T(8,128)(2,1)S(1)}, u32[]{:S(2)}, u32[]{:S(2)}) collective-permute-start(bf16[1,128,512]{2,1,0:T(8,128)(2,1)S(1)} %get-tuple-element.73), channel_id=1, source_target_pairs={{0,1},{1,0},{2,3},{3,2},{4,5},{5,4},{6,7},{7,6},{8,9},{9,8},{10,11... | collective-permute-start | bytes 393224 | tf_op jit(solution)/shard_map/ppermute | solution.py:261
  69.1 7.6 %collective-permute-start.18 = (bf16[1,128,512]{2,1,0:T(8,128)(2,1)S(1)}, bf16[1,128,512]{2,1,0:T(8,128)(2,1)S(1)}, u32[]{:S(2)}, u32[]{:S(2)}) collective-permute-start(bf16[1,128,512]{2,1,0:T(8,128)(2,1)S(1)} %sums.1), channel_id=1, source_target_pairs={{0,4},{1,5},{2,6},{3,7},{4,0},{5,1},{6,2},{7,3},{8,12},{9,13},{10,... | collective-permute-start | bytes 393224 | tf_op jit(solution)/shard_map/ppermute | solution.py:267

commit v14 on v12

--- a/solution.py
+++ b/solution.py
@@ -393,7 +393,7 @@
         *thirds[offs],
     )
     crossed = cross(sums)
-    own = [over_members(after(a, *sums) if i else a, i) for i, a in enumerate(own)]
+    own = [over_members(after(a, *([other[0]] if i == ACROSS else sums)) if i else a, i) for i, a in enumerate(own)]
     args = [third_level, last_rows, residual, *crossed, *own[::-1]]
     return pl.pallas_call(
         functools.partial(last_kernel, radix, groups, offs),

time: 77 us -> 77.5 us (level)
  no operation moved by 1% of the time
where the time goes in v14:
time: 77.5 us; the launch traced here: 76.5 us
  waiting for transfers between devices  32.1 us (41%)
  starting transfers between devices  30.6 us (39%)
  Pallas kernels  7.92 us (10%)
  local copies, waits for them, and re-layouts  5.83 us (8%)
    ppermute x5, waiting for transfers between devices, over_groups(): return lax.ppermute(array, 'box', pairs)  16 us
    ppermute x14, starting transfers between devices, over_members(): return array if mask == 0 else lax.ppermute(array, 'box', pairs)  15.7 us
    ppermute x14, waiting for transfers between devices, over_members(): return array if mask == 0 else lax.ppermute(array, 'box', pairs)  14.2 us
    ppermute x5, starting transfers between devices, over_groups(): return lax.ppermute(array, 'box', pairs)  11.9 us
    pallas_call x9, Pallas kernels, call(): pl.pallas_call(kernel, out_shape=outs, in_specs=[VMEM] * len(args), out_s...  6.47 us
    unnamed x20, local copies, waits for them, and re-layouts  5.83 us
    ppermute x3, starting transfers between devices, over_row(): return lax.ppermute(array, 'row', [(r, r ^ mask) for r in range(row_size)])  2.97 us
    ppermute x3, waiting for transfers between devices, over_row(): return lax.ppermute(array, 'row', [(r, r ^ mask) for r in range(row_size)])  1.91 us
  transfers between devices with their start and end apart: 22, of which 13 were waited for; matrix products, arithmetic and copies ran while one was open for 0% of the time, Pallas kernels for 4%

profile of v14, /device:TPU:0, one launch (start us, length us, event | category | flops | bytes accessed | tf_op | source)
XLA Modules:
  0.0 76.5 jit_solution(5609826235954788672)
XLA Ops:
  0.0 3.0 %collective-permute-start.3 = (bf16[2,256,512]{2,1,0:T(8,128)(2,1)}, bf16[2,256,512]{2,1,0:T(8,128)(2,1)S(1)}, u32[]{:S(2)}, u32[]{:S(2)}) collective-permute-start(bf16[2,256,512]{2,1,0:T(8,128)(2,1)} %refs_0_.1), channel_id=1, source_target_pairs={{0,16},{8,24},{16,0},{24,8},{1,17},{9,25},{17,1},{25,9},{2,18},{10... | collective-permute-start | bytes 1572872 | tf_op jit(solution)/shard_map/ppermute | solution.py:254
  3.0 1.1 %copy-done.2 = bf16[1,3,1,8,128,128]{5,4,3,2,1,0:T(8,128)(2,1)S(1)} copy-done((bf16[1,3,1,8,128,128]{5,4,3,2,1,0:T(8,128)(2,1)S(1)}, bf16[1,3,1,8,128,128]{5,4,3,2,1,0:T(8,128)(2,1)}, u32[]{:S(2)}) %copy-start.2) | copy-done | bytes 786456
  4.1 1.6 %collective-permute-start = (bf16[2,2,128,128]{3,2,1,0:T(8,128)(2,1)S(1)}, bf16[2,2,128,128]{3,2,1,0:T(8,128)(2,1)S(1)}, u32[]{:S(2)}, u32[]{:S(2)}) collective-permute-start(bf16[2,2,128,128]{3,2,1,0:T(8,128)(2,1)S(1)} %get-tuple-element.43), channel_id=1, source_target_pairs={{0,2},{1,3},{2,0},{3,1},{4,6},{5,7},{6,4},{7,5},{8,10},{9,11},{10,... | collective-permute-start | bytes 393224 | tf_op jit(solution)/shard_map/ppermute | solution.py:258
  5.8 1.4 %collective-permute-start.1 = (bf16[2,2,128,128]{3,2,1,0:T(8,128)(2,1)S(1)}, bf16[2,2,128,128]{3,2,1,0:T(8,128)(2,1)S(1)}, u32[]{:S(2)}, u32[]{:S(2)}) collective-permute-start(bf16[2,2,128,128]{3,2,1,0:T(8,128)(2,1)S(1)} %get-tuple-element.44), channel_id=1, source_target_pairs={{0,3},{1,2},{2,1},{3,0},{4,7},{5,6},{6,5},{7,4},{8,11},{9,10},{10,... | collective-permute-start | bytes 393224 | tf_op jit(solution)/shard_map/ppermute | solution.py:258
  7.1 1.1 %copy-done = bf16[1,3,1,8,128,128]{5,4,3,2,1,0:T(8,128)(2,1)S(1)} copy-done((bf16[1,3,1,8,128,128]{5,4,3,2,1,0:T(8,128)(2,1)S(1)}, bf16[1,3,1,8,128,128]{5,4,3,2,1,0:T(8,128)(2,1)}, u32[]{:S(2)}) %copy-start) | copy-done | bytes 786456
  8.3 0.0 copy-start.4
  8.3 2.7 %collective-permute-start.4 = (bf16[1,4,128,128]{3,2,1,0:T(8,128)(2,1)S(1)}, bf16[1,4,128,128]{3,2,1,0:T(8,128)(2,1)S(1)}, u32[]{:S(2)}, u32[]{:S(2)}) collective-permute-start(bf16[1,4,128,128]{3,2,1,0:T(8,128)(2,1)S(1)} %get-tuple-element.47), channel_id=1, source_target_pairs={{0,4},{1,5},{2,6},{3,7},{4,0},{5,1},{6,2},{7,3},{8,12},{9,13},{10,... | collective-permute-start | bytes 393224 | tf_op jit(solution)/shard_map/ppermute | solution.py:264
  11.0 0.0 collective-permute-start.2
  11.0 0.0 copy-done.3
  11.0 1.4 %copy-done.5 = bf16[1,3,1,4,4,128,128]{6,5,4,3,2,1,0:T(8,128)(2,1)S(1)} copy-done((bf16[1,3,1,4,4,128,128]{6,5,4,3,2,1,0:T(8,128)(2,1)S(1)}, bf16[1,3,1,4,4,128,128]{6,5,4,3,2,1,0:T(8,128)(2,1)}, u32[]{:S(2)}) %copy-start.5) | copy-done | bytes 1572888
  12.4 1.1 %copy-done.7 = bf16[1,3,2,512,128]{4,3,2,1,0:T(8,128)(2,1)S(1)} copy-done((bf16[1,3,2,512,128]{4,3,2,1,0:T(8,128)(2,1)S(1)}, bf16[1,3,2,512,128]{4,3,2,1,0:T(8,128)(2,1)}, u32[]{:S(2)}) %copy-start.7) | copy-done | bytes 786456
  13.5 1.0 %copy-done.9 = bf16[1,3,1,2,2,128,128]{6,5,4,3,2,1,0:T(8,128)(2,1)S(1)} copy-done((bf16[1,3,1,2,2,128,128]{6,5,4,3,2,1,0:T(8,128)(2,1)S(1)}, bf16[1,3,1,2,2,128,128]{6,5,4,3,2,1,0:T(8,128)(2,1)}, u32[]{:S(2)}) %copy-start.9) | copy-done | bytes 393240
  14.5 1.4 %weights.1 = (bf16[3,4,128,512]{3,2,1,0:T(8,128)(2,1)S(1)}, bf16[3,4,1,128,512]{4,3,2,1,0:T(8,128)(2,1)S(1)}, bf16[2,2,128,512]{3,2,1,0:T(8,128)(2,1)S(1)}, bf16...) custom-call(bf16[1,3,1,4,4,128,128]{6,5,4,3,2,1,0:T(8,128)(2,1)S(1)} %copy-done.5, ...), custom_call_target="tpu_custom_call" | custom-call | flops 603979776 | tf_op jit(solution)/shard_map/weights/pallas_call | solution.py:269
  15.9 0.0 collective-permute-done.second_along
  15.9 0.0 collective-permute-done.1.second_both
  15.9 1.1 %collective-permute-done.4.refs_4_ = bf16[1,4,128,128]{3,2,1,0:T(8,128)(2,1)S(1)} collective-permute-done((bf16[1,4,128,128]{3,2,1,0:T(8,128)(2,1)S(1)}, bf16[1,4,128,128]{3,2,1,0:T(8,128)(2,1)S(1)}, u32[]{:S(2)}, u32[]{:S(2)}) %collective-permute-start.4) | collective-permute-done | bytes 131104 | tf_op jit(solution)/shard_map/ppermute | solution.py:264
  17.1 0.0 collective-permute-done.3.refs_2_
  17.1 0.0 collective-permute-start.5
  17.1 0.0 collective-permute-done.2.refs_1_
  17.1 1.9 %collective-permute-done.5.refs_3_ = bf16[2,256,512]{2,1,0:T(8,128)(2,1)S(1)} collective-permute-done((bf16[2,256,512]{2,1,0:T(8,128)(2,1)S(1)}, bf16[2,256,512]{2,1,0:T(8,128)(2,1)S(1)}, u32[]{:S(2)}, u32[]{:S(2)}) %collective-permute-start.5) | collective-permute-done | bytes 524320 | tf_op jit(solution)/shard_map/ppermute | solution.py:254
  19.0 0.0 copy-done.4
  19.0 0.0 copy-done.8
  19.0 1.0 %off_levels.1 = (bf16[2,512,512]{2,1,0:T(8,128)(2,1)S(1)}, bf16[2,1,128,512]{3,2,1,0:T(8,128)(2,1)S(1)}, bf16[2,1,128,512]{3,2,1,0:T(8,128)(2,1)S(1)}, bf16[2,1,128,512]{3,2,1,0:T(8,128)(2,1)S(1)}) custom-call(bf16[1,3,4,256,128]{4,3,2,1,0:T(8,128)(2,1)S(1)} %copy-done.4, bf16[3,4,1,128,512]{4,3,2,1,0:T(8,128)(2,1)S(1)} %get-tuple-element.42.up_other, ...), custom_call_target="tpu_custom_call" | custom-call | flops 805306368 | tf_op jit(solution)/shard_map/off_levels/pallas_call | solution.py:269
  20.0 0.1 collective-permute-start.6
  20.1 1.8 %collective-permute-start.7 = (bf16[2,1,128,512]{3,2,1,0:T(8,128)(2,1)S(1)}, bf16[2,1,128,512]{3,2,1,0:T(8,128)(2,1)S(1)}, u32[]{:S(2)}, u32[]{:S(2)}) collective-permute-start(bf16[2,1,128,512]{3,2,1,0:T(8,128)(2,1)S(1)} %get-tuple-element.51), channel_id=1, source_target_pairs={{0,2},{1,3},{2,0},{3,1},{4,6},{5,7},{6,4},{7,5},{8,10},{9,11},{10,... | collective-permute-start | bytes 786440 | tf_op jit(solution)/shard_map/ppermute | solution.py:258
  21.9 2.3 %collective-permute-start.8 = (bf16[1,4,128,128]{3,2,1,0:T(8,128)(2,1)S(1)}, bf16[1,4,128,128]{3,2,1,0:T(8,128)(2,1)S(1)}, u32[]{:S(2)}, u32[]{:S(2)}) collective-permute-start(bf16[1,4,128,128]{3,2,1,0:T(8,128)(2,1)S(1)} %get-tuple-element.52), channel_id=1, source_target_pairs={{0,4},{1,5},{2,6},{3,7},{4,0},{5,1},{6,2},{7,3},{8,12},{9,13},{10,... | collective-permute-start | bytes 393224 | tf_op jit(solution)/shard_map/ppermute | solution.py:264
  24.2 6.1 %collective-permute-done.8.refs_5_ = bf16[1,4,128,128]{3,2,1,0:T(8,128)(2,1)S(1)} collective-permute-done((bf16[1,4,128,128]{3,2,1,0:T(8,128)(2,1)S(1)}, bf16[1,4,128,128]{3,2,1,0:T(8,128)(2,1)S(1)}, u32[]{:S(2)}, u32[]{:S(2)}) %collective-permute-start.8) | collective-permute-done | bytes 131104 | tf_op jit(solution)/shard_map/ppermute | solution.py:264
  30.3 0.0 collective-permute-done.6.refs_1_
  30.3 1.0 %collective-permute-done.7.refs_2_ = bf16[2,1,128,512]{3,2,1,0:T(8,128)(2,1)S(1)} collective-permute-done((bf16[2,1,128,512]{3,2,1,0:T(8,128)(2,1)S(1)}, bf16[2,1,128,512]{3,2,1,0:T(8,128)(2,1)S(1)}, u32[]{:S(2)}, u32[]{:S(2)}) %collective-permute-start.7) | collective-permute-done | bytes 262176 | tf_op jit(solution)/shard_map/ppermute | solution.py:258
  31.3 1.7 %collective-permute-start.9 = (bf16[2,1,128,512]{3,2,1,0:T(8,128)(2,1)S(1)}, bf16[2,1,128,512]{3,2,1,0:T(8,128)(2,1)S(1)}, u32[]{:S(2)}, u32[]{:S(2)}) collective-permute-start(bf16[2,1,128,512]{3,2,1,0:T(8,128)(2,1)S(1)} %collective-permute-done.7.refs_2_), channel_id=1, source_target_pairs={{0,1},{1,0},{2,3},{3,2},{4,5},{5,4},{6,7},{7,6},{8,9},{9,8},{10,11... | collective-permute-start | bytes 786440 | tf_op jit(solution)/shard_map/ppermute | solution.py:258
  33.0 1.8 %collective-permute-start.11 = (bf16[1,4,128,128]{3,2,1,0:T(8,128)(2,1)S(1)}, bf16[1,4,128,128]{3,2,1,0:T(8,128)(2,1)S(1)}, u32[]{:S(2)}, u32[]{:S(2)}) collective-permute-start(bf16[1,4,128,128]{3,2,1,0:T(8,128)(2,1)S(1)} %get-tuple-element.57), channel_id=1, source_target_pairs={{0,4},{1,5},{2,6},{3,7},{4,0},{5,1},{6,2},{7,3},{8,12},{9,13},{10,... | collective-permute-start | bytes 393224 | tf_op jit(solution)/shard_map/ppermute | solution.py:264
  34.8 0.6 own_levels.1
  35.4 0.0 copy-start.1
  35.4 0.0 copy-start.6
  35.4 1.8 %collective-permute-start.13 = (bf16[2,128,512]{2,1,0:T(8,128)(2,1)S(1)}, bf16[2,128,512]{2,1,0:T(8,128)(2,1)S(1)}, u32[]{:S(2)}, u32[]{:S(2)}) collective-permute-start(bf16[2,128,512]{2,1,0:T(8,128)(2,1)S(1)} %get-tuple-element.60), channel_id=1, source_target_pairs={{0,2},{1,3},{2,0},{3,1},{4,6},{5,7},{6,4},{7,5},{8,10},{9,11},{10,... | collective-permute-start | bytes 786440 | tf_op jit(solution)/shard_map/ppermute | solution.py:258
  37.2 3.2 %collective-permute-done.11.refs_4_ = bf16[1,4,128,128]{3,2,1,0:T(8,128)(2,1)S(1)} collective-permute-done((bf16[1,4,128,128]{3,2,1,0:T(8,128)(2,1)S(1)}, bf16[1,4,128,128]{3,2,1,0:T(8,128)(2,1)S(1)}, u32[]{:S(2)}, u32[]{:S(2)}) %collective-permute-start.11) | collective-permute-done | bytes 131104 | tf_op jit(solution)/shard_map/ppermute | solution.py:264
  40.4 0.0 collective-permute-done.9.refs_3_
  40.4 0.4 collective-permute-start.12
  40.8 0.6 off_sums.1
  41.4 2.2 %collective-permute-start.10 = (bf16[2,128,512]{2,1,0:T(8,128)(2,1)S(1)}, bf16[2,128,512]{2,1,0:T(8,128)(2,1)S(1)}, u32[]{:S(2)}, u32[]{:S(2)}) collective-permute-start(bf16[2,128,512]{2,1,0:T(8,128)(2,1)S(1)} %off_sums.1), channel_id=1, source_target_pairs={{0,4},{1,5},{2,6},{3,7},{4,0},{5,1},{6,2},{7,3},{8,12},{9,13},{10,... | collective-permute-start | bytes 786440 | tf_op jit(solution)/shard_map/ppermute | solution.py:264
  43.6 2.9 %collective-permute-done.13.refs_3_ = bf16[2,128,512]{2,1,0:T(8,128)(2,1)S(1)} collective-permute-done((bf16[2,128,512]{2,1,0:T(8,128)(2,1)S(1)}, bf16[2,128,512]{2,1,0:T(8,128)(2,1)S(1)}, u32[]{:S(2)}, u32[]{:S(2)}) %collective-permute-start.13) | collective-permute-done | bytes 262176 | tf_op jit(solution)/shard_map/ppermute | solution.py:258
  46.5 1.6 %collective-permute-done.12.refs_2_ = bf16[2,128,512]{2,1,0:T(8,128)(2,1)S(1)} collective-permute-done((bf16[2,128,512]{2,1,0:T(8,128)(2,1)S(1)}, bf16[2,128,512]{2,1,0:T(8,128)(2,1)S(1)}, u32[]{:S(2)}, u32[]{:S(2)}) %collective-permute-start.12) | collective-permute-done | bytes 262176 | tf_op jit(solution)/shard_map/ppermute | solution.py:258
  48.2 0.0 collective-permute-start.14
  48.2 5.6 %collective-permute-done.10.refs_0_ = bf16[2,128,512]{2,1,0:T(8,128)(2,1)S(1)} collective-permute-done((bf16[2,128,512]{2,1,0:T(8,128)(2,1)S(1)}, bf16[2,128,512]{2,1,0:T(8,128)(2,1)S(1)}, u32[]{:S(2)}, u32[]{:S(2)}) %collective-permute-start.10) | collective-permute-done | bytes 262176 | tf_op jit(solution)/shard_map/ppermute | solution.py:264
  53.8 0.8 collective-permute-done.14.refs_4_
  54.5 0.0 copy-done.1
  54.5 2.2 %middle_levels.1 = (f32[1024,512]{1,0:T(8,128)S(1)}, bf16[512,512]{1,0:T(8,128)(2,1)S(1)}, bf16[1,1,128,512]{3,2,1,0:T(8,128)(2,1)S(1)}, bf16[1,1,128,512]{3,2,1...) custom-call(bf16[1,3,1,8,128,128]{5,4,3,2,1,0:T(8,128)(2,1)S(1)} %copy-done.1, ...), custom_call_target="tpu_custom_call" | custom-call | flops 1342177280 | tf_op jit(solution)/shard_map/middle_levels/pallas_call | solution.py:269
  56.7 0.9 %collective-permute-start.15 = (bf16[1,1,128,512]{3,2,1,0:T(8,128)(2,1)S(1)}, bf16[1,1,128,512]{3,2,1,0:T(8,128)(2,1)S(1)}, u32[]{:S(2)}, u32[]{:S(2)}) collective-permute-start(bf16[1,1,128,512]{3,2,1,0:T(8,128)(2,1)S(1)} %get-tuple-element.63), channel_id=1, source_target_pairs={{0,3},{1,2},{2,1},{3,0},{4,7},{5,6},{6,5},{7,4},{8,11},{9,10},{10,... | collective-permute-start | bytes 393224 | tf_op jit(solution)/shard_map/ppermute | solution.py:258
  57.6 0.9 %collective-permute-start.16 = (bf16[1,1,128,512]{3,2,1,0:T(8,128)(2,1)S(1)}, bf16[1,1,128,512]{3,2,1,0:T(8,128)(2,1)S(1)}, u32[]{:S(2)}, u32[]{:S(2)}) collective-permute-start(bf16[1,1,128,512]{3,2,1,0:T(8,128)(2,1)S(1)} %get-tuple-element.64), channel_id=1, source_target_pairs={{0,2},{1,3},{2,0},{3,1},{4,6},{5,7},{6,4},{7,5},{8,10},{9,11},{10,... | collective-permute-start | bytes 393224 | tf_op jit(solution)/shard_map/ppermute | solution.py:258
  58.4 1.8 %collective-permute-start.17 = (bf16[1,1,128,512]{3,2,1,0:T(8,128)(2,1)S(1)}, bf16[1,1,128,512]{3,2,1,0:T(8,128)(2,1)S(1)}, u32[]{:S(2)}, u32[]{:S(2)}) collective-permute-start(bf16[1,1,128,512]{3,2,1,0:T(8,128)(2,1)S(1)} %get-tuple-element.65), channel_id=1, source_target_pairs={{0,1},{1,0},{2,3},{3,2},{4,5},{5,4},{6,7},{7,6},{8,9},{9,8},{10,11... | collective-permute-start | bytes 393224 | tf_op jit(solution)/shard_map/ppermute | solution.py:258
  60.3 0.4 last_own_levels.1
  60.7 2.0 %collective-permute-done.15.refs_0_ = bf16[1,1,128,512]{3,2,1,0:T(8,128)(2,1)S(1)} collective-permute-done((bf16[1,1,128,512]{3,2,1,0:T(8,128)(2,1)S(1)}, bf16[1,1,128,512]{3,2,1,0:T(8,128)(2,1)S(1)}, u32[]{:S(2)}, u32[]{:S(2)}) %collective-permute-start.15) | collective-permute-done | bytes 131104 | tf_op jit(solution)/shard_map/ppermute | solution.py:258
  62.7 1.1 %collective-permute-start.21 = (bf16[1,128,512]{2,1,0:T(8,128)(2,1)S(1)}, bf16[1,128,512]{2,1,0:T(8,128)(2,1)S(1)}, u32[]{:S(2)}, u32[]{:S(2)}) collective-permute-start(bf16[1,128,512]{2,1,0:T(8,128)(2,1)S(1)} %get-tuple-element.73), channel_id=1, source_target_pairs={{0,1},{1,0},{2,3},{3,2},{4,5},{5,4},{6,7},{7,6},{8,9},{9,8},{10,11... | collective-permute-start | bytes 393224 | tf_op jit(solution)/shard_map/ppermute | solution.py:258
  63.9 0.0 collective-permute-done.16.refs_1_
  63.9 1.6 %collective-permute-done.17.refs_2_ = bf16[1,1,128,512]{3,2,1,0:T(8,128)(2,1)S(1)} collective-permute-done((bf16[1,1,128,512]{3,2,1,0:T(8,128)(2,1)S(1)}, bf16[1,1,128,512]{3,2,1,0:T(8,128)(2,1)S(1)}, u32[]{:S(2)}, u32[]{:S(2)}) %collective-permute-start.17) | collective-permute-done | bytes 131104 | tf_op jit(solution)/shard_map/ppermute | solution.py:258
  65.5 0.2 sums.1
  65.7 2.1 %collective-permute-start.19 = (bf16[1,128,512]{2,1,0:T(8,128)(2,1)S(1)}, bf16[1,128,512]{2,1,0:T(8,128)(2,1)S(1)}, u32[]{:S(2)}, u32[]{:S(2)}) collective-permute-start(bf16[1,128,512]{2,1,0:T(8,128)(2,1)S(1)} %get-tuple-element.69), channel_id=1, source_target_pairs={{0,3},{1,2},{2,1},{3,0},{4,7},{5,6},{6,5},{7,4},{8,11},{9,10},{10,... | collective-permute-start | bytes 393224 | tf_op jit(solution)/shard_map/ppermute | solution.py:258
  67.8 0.1 collective-permute-start.20
  67.9 2.9 %collective-permute-start.18 = (bf16[1,128,512]{2,1,0:T(8,128)(2,1)S(1)}, bf16[1,128,512]{2,1,0:T(8,128)(2,1)S(1)}, u32[]{:S(2)}, u32[]{:S(2)}) collective-permute-start(bf16[1,128,512]{2,1,0:T(8,128)(2,1)S(1)} %sums.1), channel_id=1, source_target_pairs={{0,4},{1,5},{2,6},{3,7},{4,0},{5,1},{6,2},{7,3},{8,12},{9,13},{10,... | collective-permute-start | bytes 393224 | tf_op jit(solution)/shard_map/ppermute | solution.py:264
  70.8 0.0 collective-permute-done.21.refs_3_
  70.8 2.0 %collective-permute-done.19.refs_1_ = bf16[1,128,512]{2,1,0:T(8,128)(2,1)S(1)} collective-permute-done((bf16[1,128,512]{2,1,0:T(8,128)(2,1)S(1)}, bf16[1,128,512]{2,1,0:T(8,128)(2,1)S(1)}, u32[]{:S(2)}, u32[]{:S(2)}) %collective-permute-start.19) | collective-permute-done | bytes 131104 | tf_op jit(solution)/shard_map/ppermute | solution.py:258
  72.8 2.2 %collective-permute-done.20.refs_2_ = bf16[1,128,512]{2,1,0:T(8,128)(2,1)S(1)} collective-permute-done((bf16[1,128,512]{2,1,0:T(8,128)(2,1)S(1)}, bf16[1,128,512]{2,1,0:T(8,128)(2,1)S(1)}, u32[]{:S(2)}, u32[]{:S(2)}) %collective-permute-start.20) | collective-permute-done | bytes 131104 | tf_op jit(solution)/shard_map/ppermute | solution.py:258
  75.1 0.0 collective-permute-done.18.refs_0_
  75.1 1.4 %last_levels.1 = bf16[1,1024,512]{2,1,0:T(8,128)(2,1)} custom-call(bf16[1,3,1,8,128,128]{5,4,3,2,1,0:T(8,128)(2,1)S(1)} %copy-done.1, bf16[1024,256]{1,0:T(8,128)(2,1)S(1)} %get-tuple-element.40.row_mats, f32[1024,512]{1,0:T(8,128)S(1)} %get-tuple-element.62.residual, bf16[1,128,512]{2,1,0:T(8,128)(2,1)S(1)} %collective-permute-done.18.refs_0_, ...), custom_call_target="tpu_custom_call" | custom-call | flops 335544320 | tf_op jit(solution)/shard_map/last_levels/pallas_call | solution.py:398
  (10 shorter events, 0.1 us)
Async XLA Ops:
  0.0 17.1 %collective-permute-start.3 = (bf16[2,256,512]{2,1,0:T(8,128)(2,1)}, bf16[2,256,512]{2,1,0:T(8,128)(2,1)S(1)}, u32[]{:S(2)}, u32[]{:S(2)}) collective-permute-start(bf16[2,256,512]{2,1,0:T(8,128)(2,1)} %refs_0_.1), channel_id=1, source_target_pairs={{0,16},{8,24},{16,0},{24,8},{1,17},{9,25},{17,1},{25,9},{2,18},{10... | collective-permute-start | bytes 1572872 | tf_op jit(solution)/shard_map/ppermute | solution.py:254
  3.0 1.1 %copy-start.2 = (bf16[1,3,1,8,128,128]{5,4,3,2,1,0:T(8,128)(2,1)S(1)}, bf16[1,3,1,8,128,128]{5,4,3,2,1,0:T(8,128)(2,1)}, u32[]{:S(2)}) copy-start(bf16[1,3,1,8,128,128]{5,4,3,2,1,0:T(8,128)(2,1)} %second.3) | copy-start | bytes 2359300
  4.1 6.9 %copy-start.3 = (bf16[1,3,1,8,128,128]{5,4,3,2,1,0:T(8,128)(2,1)S(1)}, bf16[1,3,1,8,128,128]{5,4,3,2,1,0:T(8,128)(2,1)}, u32[]{:S(2)}) copy-start(bf16[1,3,1,8,128,128]{5,4,3,2,1,0:T(8,128)(2,1)} %second.3) | copy-start | bytes 2359300
  4.1 11.8 %collective-permute-start = (bf16[2,2,128,128]{3,2,1,0:T(8,128)(2,1)S(1)}, bf16[2,2,128,128]{3,2,1,0:T(8,128)(2,1)S(1)}, u32[]{:S(2)}, u32[]{:S(2)}) collective-permute-start(bf16[2,2,128,128]{3,2,1,0:T(8,128)(2,1)S(1)} %get-tuple-element.43), channel_id=1, source_target_pairs={{0,2},{1,3},{2,0},{3,1},{4,6},{5,7},{6,4},{7,5},{8,10},{9,11},{10,... | collective-permute-start | bytes 393224 | tf_op jit(solution)/shard_map/ppermute | solution.py:258
  5.8 10.2 %collective-permute-start.1 = (bf16[2,2,128,128]{3,2,1,0:T(8,128)(2,1)S(1)}, bf16[2,2,128,128]{3,2,1,0:T(8,128)(2,1)S(1)}, u32[]{:S(2)}, u32[]{:S(2)}) collective-permute-start(bf16[2,2,128,128]{3,2,1,0:T(8,128)(2,1)S(1)} %get-tuple-element.44), channel_id=1, source_target_pairs={{0,3},{1,2},{2,1},{3,0},{4,7},{5,6},{6,5},{7,4},{8,11},{9,10},{10,... | collective-permute-start | bytes 393224 | tf_op jit(solution)/shard_map/ppermute | solution.py:258
  7.1 1.1 %copy-start = (bf16[1,3,1,8,128,128]{5,4,3,2,1,0:T(8,128)(2,1)S(1)}, bf16[1,3,1,8,128,128]{5,4,3,2,1,0:T(8,128)(2,1)}, u32[]{:S(2)}) copy-start(bf16[1,3,1,8,128,128]{5,4,3,2,1,0:T(8,128)(2,1)} %third.5) | copy-start | bytes 2359300
  8.3 10.7 %copy-start.4 = (bf16[1,3,4,256,128]{4,3,2,1,0:T(8,128)(2,1)S(1)}, bf16[1,3,4,256,128]{4,3,2,1,0:T(8,128)(2,1)}, u32[]{:S(2)}) copy-start(bf16[1,3,4,256,128]{4,3,2,1,0:T(8,128)(2,1)} %basis.3) | copy-start | bytes 2359300
  8.3 8.7 %collective-permute-start.4 = (bf16[1,4,128,128]{3,2,1,0:T(8,128)(2,1)S(1)}, bf16[1,4,128,128]{3,2,1,0:T(8,128)(2,1)S(1)}, u32[]{:S(2)}, u32[]{:S(2)}) collective-permute-start(bf16[1,4,128,128]{3,2,1,0:T(8,128)(2,1)S(1)} %get-tuple-element.47), channel_id=1, source_target_pairs={{0,4},{1,5},{2,6},{3,7},{4,0},{5,1},{6,2},{7,3},{8,12},{9,13},{10,... | collective-permute-start | bytes 393224 | tf_op jit(solution)/shard_map/ppermute | solution.py:264
  11.0 6.1 %collective-permute-start.2 = (bf16[2,256,512]{2,1,0:T(8,128)(2,1)}, bf16[2,256,512]{2,1,0:T(8,128)(2,1)S(1)}, u32[]{:S(2)}, u32[]{:S(2)}) collective-permute-start(bf16[2,256,512]{2,1,0:T(8,128)(2,1)} %refs_0_.1), channel_id=1, source_target_pairs={{0,8},{8,0},{16,24},{24,16},{1,9},{9,1},{17,25},{25,17},{2,10},{10... | collective-permute-start | bytes 1572872 | tf_op jit(solution)/shard_map/ppermute | solution.py:254
  11.0 1.4 %copy-start.5 = (bf16[1,3,1,4,4,128,128]{6,5,4,3,2,1,0:T(8,128)(2,1)S(1)}, bf16[1,3,1,4,4,128,128]{6,5,4,3,2,1,0:T(8,128)(2,1)}, u32[]{:S(2)}) copy-start(bf16[1,3,1,4,4,128,128]{6,5,4,3,2,1,0:T(8,128)(2,1)} %first.1) | copy-start | bytes 4718596
  12.4 1.1 %copy-start.7 = (bf16[1,3,2,512,128]{4,3,2,1,0:T(8,128)(2,1)S(1)}, bf16[1,3,2,512,128]{4,3,2,1,0:T(8,128)(2,1)}, u32[]{:S(2)}) copy-start(bf16[1,3,2,512,128]{4,3,2,1,0:T(8,128)(2,1)} %out_basis.1) | copy-start | bytes 2359300
  13.5 1.0 %copy-start.9 = (bf16[1,3,1,2,2,128,128]{6,5,4,3,2,1,0:T(8,128)(2,1)S(1)}, bf16[1,3,1,2,2,128,128]{6,5,4,3,2,1,0:T(8,128)(2,1)}, u32[]{:S(2)}) copy-start(bf16[1,3,1,2,2,128,128]{6,5,4,3,2,1,0:T(8,128)(2,1)} %fourth.1) | copy-start | bytes 1179652
  14.5 4.5 %copy-start.8 = (bf16[2,256,512]{2,1,0:T(8,128)(2,1)S(1)}, bf16[2,256,512]{2,1,0:T(8,128)(2,1)}, u32[]{:S(2)}) copy-start(bf16[2,256,512]{2,1,0:T(8,128)(2,1)} %refs_0_.1) | copy-start | bytes 1572868
  17.1 1.9 %collective-permute-start.5 = (bf16[2,256,512]{2,1,0:T(8,128)(2,1)S(1)}, bf16[2,256,512]{2,1,0:T(8,128)(2,1)S(1)}, u32[]{:S(2)}, u32[]{:S(2)}) collective-permute-start(bf16[2,256,512]{2,1,0:T(8,128)(2,1)S(1)} %collective-permute-done.3.refs_2_), channel_id=1, source_target_pairs={{0,8},{8,0},{16,24},{24,16},{1,9},{9,1},{17,25},{25,17},{2,10},{10... | collective-permute-start | bytes 1572872 | tf_op jit(solution)/shard_map/ppermute | solution.py:254
  20.0 10.3 %collective-permute-start.6 = (bf16[2,1,128,512]{3,2,1,0:T(8,128)(2,1)S(1)}, bf16[2,1,128,512]{3,2,1,0:T(8,128)(2,1)S(1)}, u32[]{:S(2)}, u32[]{:S(2)}) collective-permute-start(bf16[2,1,128,512]{3,2,1,0:T(8,128)(2,1)S(1)} %get-tuple-element.50), channel_id=1, source_target_pairs={{0,1},{1,0},{2,3},{3,2},{4,5},{5,4},{6,7},{7,6},{8,9},{9,8},{10,11... | collective-permute-start | bytes 786440 | tf_op jit(solution)/shard_map/ppermute | solution.py:258
  20.1 11.2 %collective-permute-start.7 = (bf16[2,1,128,512]{3,2,1,0:T(8,128)(2,1)S(1)}, bf16[2,1,128,512]{3,2,1,0:T(8,128)(2,1)S(1)}, u32[]{:S(2)}, u32[]{:S(2)}) collective-permute-start(bf16[2,1,128,512]{3,2,1,0:T(8,128)(2,1)S(1)} %get-tuple-element.51), channel_id=1, source_target_pairs={{0,2},{1,3},{2,0},{3,1},{4,6},{5,7},{6,4},{7,5},{8,10},{9,11},{10,... | collective-permute-start | bytes 786440 | tf_op jit(solution)/shard_map/ppermute | solution.py:258
  21.9 8.4 %collective-permute-start.8 = (bf16[1,4,128,128]{3,2,1,0:T(8,128)(2,1)S(1)}, bf16[1,4,128,128]{3,2,1,0:T(8,128)(2,1)S(1)}, u32[]{:S(2)}, u32[]{:S(2)}) collective-permute-start(bf16[1,4,128,128]{3,2,1,0:T(8,128)(2,1)S(1)} %get-tuple-element.52), channel_id=1, source_target_pairs={{0,4},{1,5},{2,6},{3,7},{4,0},{5,1},{6,2},{7,3},{8,12},{9,13},{10,... | collective-permute-start | bytes 393224 | tf_op jit(solution)/shard_map/ppermute | solution.py:264
  31.3 9.1 %collective-permute-start.9 = (bf16[2,1,128,512]{3,2,1,0:T(8,128)(2,1)S(1)}, bf16[2,1,128,512]{3,2,1,0:T(8,128)(2,1)S(1)}, u32[]{:S(2)}, u32[]{:S(2)}) collective-permute-start(bf16[2,1,128,512]{3,2,1,0:T(8,128)(2,1)S(1)} %collective-permute-done.7.refs_2_), channel_id=1, source_target_pairs={{0,1},{1,0},{2,3},{3,2},{4,5},{5,4},{6,7},{7,6},{8,9},{9,8},{10,11... | collective-permute-start | bytes 786440 | tf_op jit(solution)/shard_map/ppermute | solution.py:258
  33.0 7.4 %collective-permute-start.11 = (bf16[1,4,128,128]{3,2,1,0:T(8,128)(2,1)S(1)}, bf16[1,4,128,128]{3,2,1,0:T(8,128)(2,1)S(1)}, u32[]{:S(2)}, u32[]{:S(2)}) collective-permute-start(bf16[1,4,128,128]{3,2,1,0:T(8,128)(2,1)S(1)} %get-tuple-element.57), channel_id=1, source_target_pairs={{0,4},{1,5},{2,6},{3,7},{4,0},{5,1},{6,2},{7,3},{8,12},{9,13},{10,... | collective-permute-start | bytes 393224 | tf_op jit(solution)/shard_map/ppermute | solution.py:264
  35.4 19.2 %copy-start.1 = (bf16[1,3,1,8,128,128]{5,4,3,2,1,0:T(8,128)(2,1)S(1)}, bf16[1,3,1,8,128,128]{5,4,3,2,1,0:T(8,128)(2,1)}, u32[]{:S(2)}) copy-start(bf16[1,3,1,8,128,128]{5,4,3,2,1,0:T(8,128)(2,1)} %third.5) | copy-start | bytes 2359300
  35.4 19.2 %copy-start.6 = (bf16[1,1024,512]{2,1,0:T(8,128)(2,1)S(1)}, bf16[1,1024,512]{2,1,0:T(8,128)(2,1)}, u32[]{:S(2)}) copy-start(bf16[1,1024,512]{2,1,0:T(8,128)(2,1)} %rhs.1) | copy-start | bytes 3145732
  35.4 11.1 %collective-permute-start.13 = (bf16[2,128,512]{2,1,0:T(8,128)(2,1)S(1)}, bf16[2,128,512]{2,1,0:T(8,128)(2,1)S(1)}, u32[]{:S(2)}, u32[]{:S(2)}) collective-permute-start(bf16[2,128,512]{2,1,0:T(8,128)(2,1)S(1)} %get-tuple-element.60), channel_id=1, source_target_pairs={{0,2},{1,3},{2,0},{3,1},{4,6},{5,7},{6,4},{7,5},{8,10},{9,11},{10,... | collective-permute-start | bytes 786440 | tf_op jit(solution)/shard_map/ppermute | solution.py:258
  40.4 7.8 %collective-permute-start.12 = (bf16[2,128,512]{2,1,0:T(8,128)(2,1)S(1)}, bf16[2,128,512]{2,1,0:T(8,128)(2,1)S(1)}, u32[]{:S(2)}, u32[]{:S(2)}) collective-permute-start(bf16[2,128,512]{2,1,0:T(8,128)(2,1)S(1)} %get-tuple-element.58), channel_id=1, source_target_pairs={{0,1},{1,0},{2,3},{3,2},{4,5},{5,4},{6,7},{7,6},{8,9},{9,8},{10,11... | collective-permute-start | bytes 786440 | tf_op jit(solution)/shard_map/ppermute | solution.py:258
  41.4 12.3 %collective-permute-start.10 = (bf16[2,128,512]{2,1,0:T(8,128)(2,1)S(1)}, bf16[2,128,512]{2,1,0:T(8,128)(2,1)S(1)}, u32[]{:S(2)}, u32[]{:S(2)}) collective-permute-start(bf16[2,128,512]{2,1,0:T(8,128)(2,1)S(1)} %off_sums.1), channel_id=1, source_target_pairs={{0,4},{1,5},{2,6},{3,7},{4,0},{5,1},{6,2},{7,3},{8,12},{9,13},{10,... | collective-permute-start | bytes 786440 | tf_op jit(solution)/shard_map/ppermute | solution.py:264
  48.2 6.4 %collective-permute-start.14 = (bf16[2,128,512]{2,1,0:T(8,128)(2,1)S(1)}, bf16[2,128,512]{2,1,0:T(8,128)(2,1)S(1)}, u32[]{:S(2)}, u32[]{:S(2)}) collective-permute-start(bf16[2,128,512]{2,1,0:T(8,128)(2,1)S(1)} %collective-permute-done.13.refs_3_), channel_id=1, source_target_pairs={{0,1},{1,0},{2,3},{3,2},{4,5},{5,4},{6,7},{7,6},{8,9},{9,8},{10,11... | collective-permute-start | bytes 786440 | tf_op jit(solution)/shard_map/ppermute | solution.py:258
  56.7 6.0 %collective-permute-start.15 = (bf16[1,1,128,512]{3,2,1,0:T(8,128)(2,1)S(1)}, bf16[1,1,128,512]{3,2,1,0:T(8,128)(2,1)S(1)}, u32[]{:S(2)}, u32[]{:S(2)}) collective-permute-start(bf16[1,1,128,512]{3,2,1,0:T(8,128)(2,1)S(1)} %get-tuple-element.63), channel_id=1, source_target_pairs={{0,3},{1,2},{2,1},{3,0},{4,7},{5,6},{6,5},{7,4},{8,11},{9,10},{10,... | collective-permute-start | bytes 393224 | tf_op jit(solution)/shard_map/ppermute | solution.py:258
  57.6 6.3 %collective-permute-start.16 = (bf16[1,1,128,512]{3,2,1,0:T(8,128)(2,1)S(1)}, bf16[1,1,128,512]{3,2,1,0:T(8,128)(2,1)S(1)}, u32[]{:S(2)}, u32[]{:S(2)}) collective-permute-start(bf16[1,1,128,512]{3,2,1,0:T(8,128)(2,1)S(1)} %get-tuple-element.64), channel_id=1, source_target_pairs={{0,2},{1,3},{2,0},{3,1},{4,6},{5,7},{6,4},{7,5},{8,10},{9,11},{10,... | collective-permute-start | bytes 393224 | tf_op jit(solution)/shard_map/ppermute | solution.py:258
  58.4 7.0 %collective-permute-start.17 = (bf16[1,1,128,512]{3,2,1,0:T(8,128)(2,1)S(1)}, bf16[1,1,128,512]{3,2,1,0:T(8,128)(2,1)S(1)}, u32[]{:S(2)}, u32[]{:S(2)}) collective-permute-start(bf16[1,1,128,512]{3,2,1,0:T(8,128)(2,1)S(1)} %get-tuple-element.65), channel_id=1, source_target_pairs={{0,1},{1,0},{2,3},{3,2},{4,5},{5,4},{6,7},{7,6},{8,9},{9,8},{10,11... | collective-permute-start | bytes 393224 | tf_op jit(solution)/shard_map/ppermute | solution.py:258
  62.7 8.1 %collective-permute-start.21 = (bf16[1,128,512]{2,1,0:T(8,128)(2,1)S(1)}, bf16[1,128,512]{2,1,0:T(8,128)(2,1)S(1)}, u32[]{:S(2)}, u32[]{:S(2)}) collective-permute-start(bf16[1,128,512]{2,1,0:T(8,128)(2,1)S(1)} %get-tuple-element.73), channel_id=1, source_target_pairs={{0,1},{1,0},{2,3},{3,2},{4,5},{5,4},{6,7},{7,6},{8,9},{9,8},{10,11... | collective-permute-start | bytes 393224 | tf_op jit(solution)/shard_map/ppermute | solution.py:258
  65.7 7.1 %collective-permute-start.19 = (bf16[1,128,512]{2,1,0:T(8,128)(2,1)S(1)}, bf16[1,128,512]{2,1,0:T(8,128)(2,1)S(1)}, u32[]{:S(2)}, u32[]{:S(2)}) collective-permute-start(bf16[1,128,512]{2,1,0:T(8,128)(2,1)S(1)} %get-tuple-element.69), channel_id=1, source_target_pairs={{0,3},{1,2},{2,1},{3,0},{4,7},{5,6},{6,5},{7,4},{8,11},{9,10},{10,... | collective-permute-start | bytes 393224 | tf_op jit(solution)/shard_map/ppermute | solution.py:258
  67.8 7.3 %collective-permute-start.20 = (bf16[1,128,512]{2,1,0:T(8,128)(2,1)S(1)}, bf16[1,128,512]{2,1,0:T(8,128)(2,1)S(1)}, u32[]{:S(2)}, u32[]{:S(2)}) collective-permute-start(bf16[1,128,512]{2,1,0:T(8,128)(2,1)S(1)} %get-tuple-element.71), channel_id=1, source_target_pairs={{0,2},{1,3},{2,0},{3,1},{4,6},{5,7},{6,4},{7,5},{8,10},{9,11},{10,... | collective-permute-start | bytes 393224 | tf_op jit(solution)/shard_map/ppermute | solution.py:258
  67.9 7.2 %collective-permute-start.18 = (bf16[1,128,512]{2,1,0:T(8,128)(2,1)S(1)}, bf16[1,128,512]{2,1,0:T(8,128)(2,1)S(1)}, u32[]{:S(2)}, u32[]{:S(2)}) collective-permute-start(bf16[1,128,512]{2,1,0:T(8,128)(2,1)S(1)} %sums.1), channel_id=1, source_target_pairs={{0,4},{1,5},{2,6},{3,7},{4,0},{5,1},{6,2},{7,3},{8,12},{9,13},{10,... | collective-permute-start | bytes 393224 | tf_op jit(solution)/shard_map/ppermute | solution.py:264
